TPU v7x, 32 devices: a whole 2x2x4 slice. The times are simulated.
32 devices in a mesh: kp: 4 (over y, x), ga: 8 (over z, core).
Axes of the slice: x: 2, y: 2, z: 4, core: 2. Of those that a mesh axis runs over, the one named last changes fastest.
Arguments:
- densities: bfloat16 [8, 2, 3072, 256], P('kp', None, 'ga'), may hold values from -6 to 6
- screened: bfloat16 [8, 2, 3072, 3072], P('kp', None, 'ga'), may hold values from -3 to 3, as said below
- coulomb: float32 [3072], P('ga'), may hold values from 0.05 to 1
- block_rows: int32 [4, 2], P('kp'), may hold values from 0 to 6, as said below
Outputs:
- kernel: float32 [8, 2, 2, 256, 256], P('kp', None, None, 'ga')
- mirror: float32 [8, 2, 2, 256, 256], P('kp', None, None, 'ga')
Inputs may be any that keep to these rules, and one draw needn't show every extreme that they name: block_rows[o, j] + 2 o + 1 <= 7, so every column k-point exists. Each panel screened[q] is Hermitian: its real part symmetric, its imaginary part antisymmetric.
All inputs are finite; a program needn't handle non-finite values.
Results may differ from a plain program's by a relative error of at most 0.0032.
Values may be sent and summed in bfloat16 or wider, within the bound.
No kernel may reach another device: no remote copies, remote signals or barrier semaphores. Data moves between devices by JAX's collectives and lax.ppermute only.
A program may use at most 64 MiB of HBM per device.

v0:
```python
import math

import jax
import jax.numpy as jnp
from jax import lax
from jax.sharding import PartitionSpec as P


def shards(densities, screened, coulomb, block_rows):
    owner = lax.axis_index("kp")
    g_slot = lax.axis_index("ga")
    k_held = densities.shape[0]
    g_local = densities.shape[2]
    g_total = screened.shape[3]
    rows = block_rows[0]
    transfers = owner * k_held + jnp.arange(k_held, dtype=jnp.int32)
    far_rows = rows[:, None] + transfers[None, :]
    piece = lax.all_gather(densities, "kp", axis=0, tiled=True)
    labels = jnp.arange(piece.shape[0], dtype=jnp.int32)
    pick_near = (rows[:, None] == labels[None, :]).astype(jnp.bfloat16)
    pick_far = (far_rows[:, :, None] == labels[None, None, :]).astype(jnp.bfloat16)
    near_acc = jnp.einsum(
        "jp,pcgt->jcgt", pick_near, piece, preferred_element_type=jnp.float32
    ).astype(jnp.bfloat16)
    far_acc = jnp.einsum(
        "jsp,pcgt->jscgt", pick_far, piece, preferred_element_type=jnp.float32
    ).astype(jnp.bfloat16)
    columns = jnp.arange(g_total, dtype=jnp.int32)
    own_rows = g_slot * g_local + jnp.arange(g_local, dtype=jnp.int32)
    diag_mask = own_rows[:, None] == columns[None, :]
    coulomb_diag = jnp.where(diag_mask, 2.0 * coulomb[:, None], 0.0)
    screen_real = (coulomb_diag[None] - screened[:, 0].astype(jnp.float32)).astype(jnp.bfloat16)
    screen_imag = -screened[:, 1]
    near_all = lax.all_gather(near_acc, "ga", axis=2, tiled=True)
    piece_real = near_all[:, 0]
    piece_imag = near_all[:, 1]
    real_term = jnp.einsum(
        "sgh,jht->jsgt", screen_real, piece_real, preferred_element_type=jnp.float32
    ) - jnp.einsum("sgh,jht->jsgt", screen_imag, piece_imag, preferred_element_type=jnp.float32)
    imag_term = jnp.einsum(
        "sgh,jht->jsgt", screen_real, piece_imag, preferred_element_type=jnp.float32
    ) + jnp.einsum("sgh,jht->jsgt", screen_imag, piece_real, preferred_element_type=jnp.float32)
    image = jnp.stack([real_term, imag_term], 2)
    image = image.astype(jnp.bfloat16)
    image_real = image[:, :, 0]
    image_imag = image[:, :, 1]
    far_real = far_acc[:, :, 0]
    far_imag = far_acc[:, :, 1]
    lower_real = jnp.einsum(
        "jsga,jsgb->jsab", far_real, image_real, preferred_element_type=jnp.float32
    ) + jnp.einsum("jsga,jsgb->jsab", far_imag, image_imag, preferred_element_type=jnp.float32)
    lower_imag = jnp.einsum(
        "jsga,jsgb->jsab", far_real, image_imag, preferred_element_type=jnp.float32
    ) - jnp.einsum("jsga,jsgb->jsab", far_imag, image_real, preferred_element_type=jnp.float32)
    partial_lower = jnp.stack([lower_real, lower_imag], 2)
    inverse = 1.0 / math.sqrt(g_total)
    mirror = lax.psum_scatter(partial_lower, "ga", scatter_dimension=3, tiled=True) * inverse
    partial_upper = jnp.stack([jnp.swapaxes(lower_real, 2, 3), -jnp.swapaxes(lower_imag, 2, 3)], 2)
    kernel = lax.psum_scatter(partial_upper, "ga", scatter_dimension=3, tiled=True) * inverse
    return (kernel, mirror)


def solution(mesh):
    placed = (P("kp", None, "ga", None), P("kp", None, "ga", None), P("ga"), P("kp", None))
    return jax.shard_map(
        shards,
        mesh=mesh,
        in_specs=placed,
        out_specs=(P("kp", None, None, "ga", None), P("kp", None, None, "ga", None)),
        check_vma=False,
    )
```

profile of v0, /device:TPU:0, one launch (start us, length us, event | category | flops | bytes accessed | tf_op | source)
XLA Modules:
  0.0 252.7 jit_solution(8219982747424281753)
XLA Ops:
  7.2 0.7 all-gather.3.cloned.1.call-update
  8.0 48.6 %all-gather.3.cloned.1.call-done = bf16[8,2,384,256]{3,2,1,0:T(8,128)(2,1)} async-done(((bf16[2,2,384,256]{3,2,1,0:T(8,128)(2,1)}), bf16[8,2,384,256]{3,2,1,0:T(8,128)(2,1)}) %all-gather.3.cloned.1.call-update) | async-done | bytes 3145744 | tf_op jit(solution)/shard_map/all_gather | solution.py:18
  56.6 4.9 %fusion.19 = bf16[2,2,384,256]{3,0,2,1:T(2,128)(2,1)} fusion(bf16[8,2,384,256]{3,2,1,0:T(8,128)(2,1)} %all-gather.3.cloned.1.call-done, s32[2]{0:T(128)} %bitcast.90), kind=kOutput, calls=%fused_computation.20 | convolution fusion | flops 6684688 | bytes 3932168 | tf_op jit(solution)/shard_map/jp,pcgt->jcgt/dot_general | solution.py:22
  61.7 3.0 %fusion.2 = f32[384,3072]{1,0:T(8,128)} fusion(f32[384]{0:T(512)S(1)} %broadcast_multiply_fusion.2, s32[384]{0:T(512)S(1)} %iota_add_fusion), kind=kLoop, calls=%fused_computation.5 | loop fusion | flops 2359296 | bytes 4721664 | tf_op jit(solution)/shard_map/jit(_where)/select_n | solution.py:31
  64.7 2.5 fusion.12
  67.2 1.1 slice_bitcast_fusion.2
  68.3 2.1 copy.35
  70.4 1.8 copy.31
  72.1 54.2 %all-gather.5.cloned.1.call-done = bf16[2,2,3072,256]{3,0,2,1:T(2,128)(2,1)} async-done(((bf16[2,2,384,256]{3,0,2,1:T(2,128)(2,1)}), bf16[2,2,3072,256]{3,0,2,1:T(2,128)(2,1)}) %all-gather.5.cloned.1.call-update) | async-done | bytes 6291472 | tf_op jit(solution)/shard_map/all_gather | solution.py:34
  126.4 7.9 %slice_bitcast_fusion.1 = (bf16[2,3072,256,1]{2,0,1,3:T(2,128)(2,1)}, bf16[2,3072,256,1]{2,0,1,3:T(2,128)(2,1)S(1)}) fusion(bf16[2,2,3072,256]{3,0,2,1:T(2,128)(2,1)} %all-gather.5.cloned.1.call-done), kind=kLoop, calls=%fused_computation.9 | loop fusion | bytes 12582912 | tf_op jit(solution)/shard_map/squeeze | solution.py:35
  134.2 8.8 %copy.49 = bf16[2,3072,256,1]{1,2,3,0:T(8,128)(2,1)} copy(bf16[2,3072,256,1]{2,0,1,3:T(2,128)(2,1)} %get-tuple-element.6) | data formatting | bytes 6291456 | tf_op jit(solution)/shard_map/squeeze | solution.py:35
  143.0 6.9 %copy.50 = bf16[2,3072,256,1]{1,2,3,0:T(8,128)(2,1)} copy(bf16[2,3072,256,1]{2,0,1,3:T(2,128)(2,1)S(1)} %get-tuple-element.7) | data formatting | bytes 6291456 | tf_op jit(solution)/shard_map/squeeze | solution.py:36
  149.9 7.4 %fusion.28 = f32[2,256,2,384]{3,1,2,0:T(8,128)S(1)} fusion(bf16[2,3072,256,1]{1,2,3,0:T(8,128)(2,1)} %copy.50, bf16[2,2,384,3072]{3,2,1,0:T(8,128)(2,1)} %param.5, f32[384,3072]{1,0:T(8,128)} %fusion.2), kind=kOutput, calls=%fused_computation.25 | convolution fusion | flops 2422996992 | bytes 14155776 | tf_op jit(solution)/shard_map/sgh,jht->jsgt/dot_general | solution.py:40
  157.4 6.5 %fusion.30 = f32[2,256,2,384]{3,1,2,0:T(8,128)S(1)} fusion(bf16[2,3072,256,1]{1,2,3,0:T(8,128)(2,1)S(1)} %copy-done.3, bf16[2,2,384,3072]{3,2,1,0:T(8,128)(2,1)} %param.5, f32[384,3072]{1,0:T(8,128)} %fusion.2), kind=kOutput, calls=%fused_computation.26 | convolution fusion | flops 2422996992 | bytes 14155776 | tf_op jit(solution)/shard_map/sgh,jht->jsgt/dot_general | solution.py:37
  163.9 2.6 %fusion.25 = bf16[2,2,384,256]{2,3,1,0:T(8,128)(2,1)S(1)} fusion(f32[2,256,2,384]{3,1,2,0:T(8,128)S(1)} %fusion.28, bf16[2,3072,256,1]{1,2,3,0:T(8,128)(2,1)S(1)} %copy-done.3, bf16[2,2,384,3072]{3,2,1,0:T(8,128)(2,1)S(1)} %bitcast.93), kind=kOutput, calls=%fused_computation.24 | convolution fusion | flops 2423783424 | bytes 10223616 | tf_op jit(solution)/shard_map/sgh,jht->jsgt/dot_general | solution.py:42
  166.6 2.7 %fusion.22 = bf16[2,2,384,256]{2,3,1,0:T(8,128)(2,1)S(1)} fusion(f32[2,256,2,384]{3,1,2,0:T(8,128)S(1)} %fusion.30, bf16[2,3072,256,1]{1,2,3,0:T(8,128)(2,1)S(1)} %copy-done.4, bf16[2,2,384,3072]{3,2,1,0:T(8,128)(2,1)S(1)} %bitcast.93), kind=kOutput, calls=%fused_computation.23 | convolution fusion | flops 2423783424 | bytes 10223616 | tf_op jit(solution)/shard_map/sgh,jht->jsgt/dot_general | solution.py:39
  171.7 1.5 pad_maximum_fusion.1
  173.8 1.6 pad_maximum_fusion
  175.3 32.5 %reduce-scatter.5.cloned.1.call-done = f32[2,2,2,32,256]{4,3,1,0,2:T(8,128)} async-done(((f32[2,2,2,256,256]{4,3,1,0,2:T(8,128)}), f32[2,2,2,32,256]{4,3,1,0,2:T(8,128)}) %reduce-scatter.5.cloned.1.call-update) | async-done | bytes 262160 | tf_op jit(solution)/shard_map/reduce_scatter | solution.py:57
  207.9 1.0 broadcast_multiply_fusion
  208.8 0.7 copy.46
  209.6 34.9 %reduce-scatter.3.cloned.1.call-done = f32[2,2,2,32,256]{4,3,1,0,2:T(8,128)} async-done(((f32[2,2,2,256,256]{4,3,1,0,2:T(8,128)}), f32[2,2,2,32,256]{4,3,1,0,2:T(8,128)}) %reduce-scatter.3.cloned.1.call-update) | async-done | bytes 262160 | tf_op jit(solution)/shard_map/reduce_scatter | solution.py:59
  244.5 1.0 broadcast_multiply_fusion.1
  245.5 0.7 copy.45
  (39 shorter events, 3.1 us)
Async XLA Ops:
  7.2 54.4 %copy-start.5 = (s32[1,2]{1,0:T(1,128)S(1)}, s32[1,2]{1,0:T(1,128)}, u32[]{:S(2)}) copy-start(s32[1,2]{1,0:T(1,128)} %param.7) | copy-start | bytes 28
  7.2 54.5 %copy-start.6 = (f32[384]{0:T(512)S(1)}, f32[384]{0:T(512)}, u32[]{:S(2)}) copy-start(f32[384]{0:T(512)} %param.6) | copy-start | bytes 4612
  7.2 49.4 %all-gather.3.cloned.1.call-start = ((), (), s32[]{:S(2)}) async-start(), calls=%async_computation.2 | async-start | bytes 3932160 | tf_op jit(solution)/shard_map/all_gather | solution.py:18
  7.9 118.5 %all-gather.5.cloned.1.call-start = ((), (), s32[]{:S(2)}) async-start(), calls=%async_computation.3 | async-start | bytes 7077888 | tf_op jit(solution)/shard_map/all_gather | solution.py:34
  61.5 3.2 %copy-start = (bf16[8,2,384,256]{3,2,1,0:T(8,128)(2,1)S(1)}, bf16[8,2,384,256]{3,2,1,0:T(8,128)(2,1)}, u32[]{:S(2)}) copy-start(bf16[8,2,384,256]{3,2,1,0:T(8,128)(2,1)} %all-gather.3.cloned.1.call-done) | copy-start | bytes 9437188
  61.5 146.3 %reduce-scatter.5.cloned.1.call-start = ((), (), s32[]{:S(2)}) async-start(), calls=%async_computation.5 | async-start | bytes 2359296 | tf_op jit(solution)/shard_map/reduce_scatter | solution.py:57
  149.9 7.4 %copy-start.3 = (bf16[2,3072,256,1]{1,2,3,0:T(8,128)(2,1)S(1)}, bf16[2,3072,256,1]{1,2,3,0:T(8,128)(2,1)}, u32[]{:S(2)}) copy-start(bf16[2,3072,256,1]{1,2,3,0:T(8,128)(2,1)} %copy.49) | copy-start | bytes 9437188
  149.9 14.0 %slice-start = ((s8[9437184]{0:T(1024)(128)(4,1)}), s8[4194304]{0:T(1024)(128)(4,1)S(1)}, s32[]{:S(2)}) async-start(s8[9437184]{0:T(1024)(128)(4,1)} %bitcast.92), calls=%async_computation.6 | async-start | bytes 8388608
  149.9 14.0 %slice-start.1 = ((s8[9437184]{0:T(1024)(128)(4,1)}), s8[4194304]{0:T(1024)(128)(4,1)S(1)}, s32[]{:S(2)}) async-start(s8[9437184]{0:T(1024)(128)(4,1)} %bitcast.92), calls=%async_computation.7 | async-start | bytes 8388608
  157.4 6.5 %slice-start.2 = ((s8[9437184]{0:T(1024)(128)(4,1)}), s8[1048576]{0:T(1024)(128)(4,1)S(1)}, s32[]{:S(2)}) async-start(s8[9437184]{0:T(1024)(128)(4,1)} %bitcast.92), calls=%async_computation.8 | async-start | bytes 2097152
  163.9 2.7 %copy-start.4 = (bf16[2,3072,256,1]{1,2,3,0:T(8,128)(2,1)S(1)}, bf16[2,3072,256,1]{1,2,3,0:T(8,128)(2,1)}, u32[]{:S(2)}) copy-start(bf16[2,3072,256,1]{1,2,3,0:T(8,128)(2,1)} %copy.50) | copy-start | bytes 9437188
  166.6 2.7 %copy-start.2 = (bf16[2,2,384,256]{2,3,1,0:T(8,128)(2,1)S(1)}, bf16[2,2,384,256]{2,3,1,0:T(8,128)(2,1)}, u32[]{:S(2)}) copy-start(bf16[2,2,384,256]{2,3,1,0:T(8,128)(2,1)} %copy.31) | copy-start | bytes 2359300
  169.3 1.1 copy-start.1
  173.3 71.2 %reduce-scatter.3.cloned.1.call-start = ((), (), s32[]{:S(2)}) async-start(), calls=%async_computation.4 | async-start | bytes 2359296 | tf_op jit(solution)/shard_map/reduce_scatter | solution.py:59
Sparse Core Ops, SparseCore 0:
  9.9 46.6 all-gather.2
  61.6 64.7 all-gather.4
  173.4 34.4 reduce-scatter.4
  210.0 34.4 reduce-scatter.2
where the time goes:
time: 253 us
  waiting for transfers between devices  171 us (68%)
  local copies, waits for them, and re-layouts  30.8 us (12%)
  matrix products  28.5 us (11%)
  between operations  14 us (6%)
  other arithmetic  8.26 us (3%)
    all_gather x1, waiting for transfers between devices, shards(): near_all = lax.all_gather(near_acc, 'ga', axis=2, tiled=True)  54.2 us
    all_gather x1, waiting for transfers between devices, shards(): piece = lax.all_gather(densities, 'kp', axis=0, tiled=True)  48.6 us
    reduce_scatter x1, waiting for transfers between devices, shards(): lax.psum_scatter(partial_upper, 'ga', scatter_dimension=3, tiled=True)  34.9 us
    reduce_scatter x1, waiting for transfers between devices, shards(): lax.psum_scatter(partial_lower, 'ga', scatter_dimension=3, tiled=True)  32.5 us
    squeeze x2, local copies, waits for them, and re-layouts, shards(): piece_real = near_all[:, 0]  16.7 us
    dot_general x1, matrix products, shards(): jnp.einsum('sgh,jht->jsgt', screen_real, piece_imag, preferred_element_ty...  7.42 us
    squeeze x1, local copies, waits for them, and re-layouts, shards(): piece_imag = near_all[:, 1]  6.87 us
    dot_general x1, matrix products, shards(): jnp.einsum('sgh,jht->jsgt', screen_real, piece_real, preferred_element_ty...  6.49 us
  transfers between devices with their start and end apart: 4, of which 4 were waited for; matrix products, arithmetic and copies ran while one was open for 6% of the time, Pallas kernels for 0%

commit v1 on v0

--- a/solution.py
+++ b/solution.py
@@ -1,12 +1,446 @@
+import functools
 import math
 
 import jax
 import jax.numpy as jnp
 from jax import lax
+from jax.experimental import pallas as pl
+from jax.experimental.pallas import tpu as pltpu
 from jax.sharding import PartitionSpec as P
 
-
-def shards(densities, screened, coulomb, block_rows):
+F32 = jnp.float32
+BF16 = jnp.bfloat16
+LABELS = 16
+VMEM = pl.BlockSpec(memory_space=pltpu.VMEM)
+SMEM = pl.BlockSpec(memory_space=pltpu.SMEM)
+HBM = pl.BlockSpec(memory_space=pltpu.HBM)
+
+
+def dot(a, b):
+    return jnp.dot(a, b, preferred_element_type=F32)
+
+
+def tdot(a, b):
+    return lax.dot_general(a, b, (((0,), (0,)), ((), ())), preferred_element_type=F32)
+
+
+def run(body, out, *args, specs=None, scratch=(), name=None, aliases=None, mib=16):
+    outs = out if isinstance(out, (list, tuple)) else [out]
+    result = pl.pallas_call(
+        body,
+        in_specs=specs or [VMEM] * len(args),
+        out_specs=[VMEM] * len(outs),
+        out_shape=list(outs),
+        scratch_shapes=list(scratch),
+        input_output_aliases=aliases or {},
+        compiler_params=pltpu.CompilerParams(vmem_limit_bytes=mib * 2**20),
+        cost_estimate=pl.CostEstimate(flops=0, bytes_accessed=0, transcendentals=0),
+        name=name,
+    )(*args)
+    return list(result) if isinstance(out, (list, tuple)) else result[0]
+
+
+BITS = ((1, 2), (2, 1))
+
+
+def pack_kernel(rows, densities, *sends):
+    held, _, g_local, t = densities.shape
+    half = g_local // 2
+    for h in range(2):
+        for k in range(held):
+            for part in range(2):
+                at = (2 * k + part) * half
+                sends[h][at : at + half] = densities[k, part, h * half : (h + 1) * half]
+        line = lax.broadcasted_iota(jnp.int32, (LABELS, t), 0)
+        tile = jnp.zeros((LABELS, t), F32)
+        for j in range(rows.shape[1]):
+            tile = jnp.where(line == j, rows[0, j].astype(F32), tile)
+        sends[h][2 * held * half :] = tile.astype(BF16)
+
+
+def label_of(message, held, half, j):
+    tail = message[2 * held * half :].astype(F32)
+    return jnp.max(tail[j : j + 1]).astype(jnp.int32)
+
+
+def entries(message, owner, held, half):
+    return [(owner * held + k, message, 2 * k * half, (2 * k + 1) * half) for k in range(held)]
+
+
+def copy_if(label, found, out):
+    half = out.shape[1]
+    hit = None
+    for name, message, real, imag in found:
+        match = label == name
+        hit = match if hit is None else hit | match
+
+        @pl.when(match)
+        def _(message=message, real=real, imag=imag):
+            out[0] = message[real : real + half]
+            out[1] = message[imag : imag + half]
+
+    return hit
+
+
+def pick_kernel(held, packed_0, packed_1, came_0, came_1, *sends):
+    owner = lax.axis_index("kp")
+    packed, came = (packed_0, packed_1), (came_0, came_1)
+    half = sends[0].shape[2]
+    for j in range(sends[0].shape[0]):
+        for h in range(2):
+            found = entries(packed[h], owner, held, half)
+            found += entries(came[h], owner ^ BITS[h][0], held, half)
+            copy_if(label_of(came[1 - h], held, half, j), found, sends[h].at[j])
+
+
+def near_kernel(held, packed_0, packed_1, came_0, came_1, picked_0, picked_1, near, *each):
+    owner = lax.axis_index("kp")
+    packed, came, picked = (packed_0, packed_1), (came_0, came_1), (picked_0, picked_1)
+    half = picked_0.shape[2]
+    for j in range(near.shape[0]):
+        label = label_of(packed_0, held, half, j)
+        for h in range(2):
+            out = near.at[j, :, h * half : (h + 1) * half]
+            found = entries(packed[h], owner, held, half)
+            found += entries(came[h], owner ^ BITS[h][0], held, half)
+            hit = copy_if(label, found, out)
+
+            @pl.when(jnp.logical_not(hit))
+            def _(h=h, j=j, out=out):
+                out[...] = picked[h][j]
+
+    for j, out in enumerate(each):
+        out[...] = near[j]
+
+
+def stack_kernel(*refs):
+    for i, ref in enumerate(refs[:-1]):
+        refs[-1][i] = ref[...]
+
+
+def rest_kernel(held, packed_0, packed_1, came_0, came_1, *sends):
+    owner = lax.axis_index("kp")
+    packed, came = (packed_0, packed_1), (came_0, came_1)
+    transfers, _, half, _ = sends[0].shape
+    for j in range(len(sends) // 2):
+        for h in range(2):
+            first, second = BITS[h]
+            found = entries(packed[h], owner, held, half)
+            found += entries(came[h], owner ^ first, held, half)
+            row = label_of(came[1 - h], held, half, j)
+            for s in range(transfers):
+                label = row + (owner ^ second) * transfers + s
+                copy_if(label, found, sends[2 * j + h].at[s])
+
+
+def far_kernel(held, j, packed_0, packed_1, came_0, came_1, rest_0, rest_1, far):
+    owner = lax.axis_index("kp")
+    packed, came, rest = (packed_0, packed_1), (came_0, came_1), (rest_0, rest_1)
+    transfers, _, half, _ = rest_0.shape
+    row = label_of(packed_0, held, half, j)
+    for h in range(2):
+        found = entries(packed[h], owner, held, half)
+        found += entries(came[h], owner ^ BITS[h][0], held, half)
+        for s in range(transfers):
+            out = far.at[s, :, h * half : (h + 1) * half]
+            hit = copy_if(row + owner * transfers + s, found, out)
+
+            @pl.when(jnp.logical_not(hit))
+            def _(h=h, s=s, out=out):
+                out[...] = rest[h][s]
+
+
+def load_kernel(source, panels, sems):
+    copies = []
+    for s in range(source.shape[0]):
+        for part in range(2):
+            copy = pltpu.make_async_copy(source.at[s, part], panels.at[s, part], sems.at[2 * s + part])
+            copy.start()
+            copies.append(copy)
+    for copy in copies:
+        copy.wait()
+
+
+FORTH = (1, 3, 0, 2)
+BACK = (2, 0, 3, 1)
+
+
+def chip_at(z, steps):
+    if steps == 1:
+        return jnp.where(z < 2, 2 * z + 1, 2 * z - 4)
+    if steps == -1:
+        return jnp.where(lax.rem(z, 2) == 0, 2 + z // 2, z // 2)
+    return z if steps == 0 else 3 - z
+
+
+def lay(terms, upper, lower):
+    for ref, first in terms:
+        *count, _, g_local, t = ref.shape
+        rows = pl.ds(first if isinstance(first, int) else pl.multiple_of(first, 128), g_local)
+        for j, panel in enumerate([ref.at[j] for j in range(count[0])] if count else [ref]):
+            real, imag = slice(2 * j * t, (2 * j + 1) * t), slice((2 * j + 1) * t, (2 * j + 2) * t)
+            upper[rows, real] = panel[0]
+            upper[rows, imag] = panel[1]
+            lower[rows, real] = -panel[1]
+            lower[rows, imag] = panel[0]
+
+
+def place():
+    slot = lax.axis_index("ga")
+    return slot // 2, lax.rem(slot, 2)
+
+
+def multiply(screened, s, span, width, upper, lower, first=0):
+    span = pl.ds(pl.multiple_of(span, 128), width)
+    rows = slice(first, first + width)
+    return dot(screened[s, 0, :, span], upper[rows]) + dot(screened[s, 1, :, span], lower[rows])
+
+
+def first_kernel(screened, own, coulomb, total, upper, lower):
+    z, core = place()
+    g = screened.shape[2]
+    lay([(own, 0)], upper, lower)
+    span = pl.ds(pl.multiple_of((2 * z + core) * g, 128), g)
+    line = lax.broadcasted_iota(jnp.int32, (g, g), 0)
+    on = line == lax.broadcasted_iota(jnp.int32, (g, g), 1)
+    for s in range(screened.shape[0]):
+        real = screened[s, 0, :, span]
+        real = jnp.where(on, (real.astype(F32) - 2.0 * coulomb[...]).astype(BF16), real)
+        total[s] = dot(real, upper[...]) + dot(screened[s, 1, :, span], lower[...])
+
+
+def step_kernel(steps, screened, own, pair, before, total, upper, lower):
+    z, core = place()
+    g = screened.shape[2]
+    lay([(own, core * g), (pair, (1 - core) * g)], upper, lower)
+    span = 2 * chip_at(z, steps) * g
+    for s in range(screened.shape[0]):
+        total[s] = before[s] + multiply(screened, s, span, 2 * g, upper, lower)
+
+
+def second_kernel(steps, screened, own, pairs, before, total, upper, lower):
+    z, core = place()
+    g = screened.shape[2]
+    lay([(own, core * g), (pairs.at[1], (1 - core) * g), (pairs.at[0], 2 * g)], upper, lower)
+    span = 2 * chip_at(z, steps) * g
+    left = (2 * z + 1 - core) * g
+    for s in range(screened.shape[0]):
+        value = before[s] + multiply(screened, s, span, 2 * g, upper, lower)
+        total[s] = value + multiply(screened, s, left, g, upper, lower, 2 * g)
+
+
+def last_kernel(chips, steps, j, screened, own, pair, before, far, keep, give_0, give_1, upper, lower):
+    z, core = place()
+    g = screened.shape[2]
+    t = far.shape[-1]
+    lay([(own, core * g), (pair, (1 - core) * g)], upper, lower)
+    span = 2 * chip_at(z, steps) * g
+    first = core == 0
+    for s in range(screened.shape[0]):
+        value = before[s, :, 2 * j * t : 2 * (j + 1) * t]
+        image = (value + multiply(screened, s, span, 2 * g, upper, lower)).astype(BF16)
+        by_real, by_imag = tdot(far[s, 0], image), tdot(far[s, 1], image)
+        real = by_real[:, :t] + by_imag[:, t:]
+        imag = by_real[:, t:] - by_imag[:, :t]
+        parts = ((real, imag), (real.T, -imag.T))
+        for which in range(2):
+            for part in range(2):
+                block = parts[which][part]
+                block = block.reshape(chips, 2, t // (2 * chips), t)
+                keep[:, s, which, part] = jnp.where(first, block[:, 0], block[:, 1])
+                give = (give_0, give_1)[which]
+                give[:, s, part] = jnp.where(first, block[:, 1], block[:, 0]).astype(BF16)
+
+
+def split_kernel(keep, came_0, came_1, own, cross, sends):
+    z = lax.axis_index("ga") // 2
+    for which, came in enumerate((came_0, came_1)):
+
+        def chip(at):
+            return keep[at, :, which] + came[at].astype(F32)
+
+        own[:, which] = chip(z)
+        cross[:, which] = chip(z ^ 2)
+        for i, at in enumerate((z ^ 1, z ^ 3)):
+            sends[i, :, which] = chip(at).astype(BF16)
+
+
+def merge_kernel(own, cross, came, total, sends):
+    total[...] = own[...] + came[0].astype(F32)
+    sends[...] = (cross[...] + came[1].astype(F32)).astype(BF16)
+
+
+def finish_kernel(count, chips, scale, *refs):
+    kernel, mirror = refs[-2:]
+    for j in range(count):
+        terms = refs[j * chips : (j + 1) * chips]
+        total = terms[0][...]
+        for term in terms[1:]:
+            total = total + term[...].astype(F32)
+        mirror[j] = total[:, 0] * scale
+        kernel[j] = total[:, 1] * scale
+
+
+def quick(n_kp, n_ga, densities, screened, coulomb, block_rows):
+    held, _, g_local, t = densities.shape
+    transfers, g_total = screened.shape[0], screened.shape[3]
+    count = block_rows.shape[1]
+    chips = n_ga // 2
+    half = g_local // 2
+    shape = jax.ShapeDtypeStruct
+    tie = lax.optimization_barrier
+
+    def across(x, bit):
+        return lax.ppermute(x, "kp", [(i, i ^ bit) for i in range(n_kp)])
+
+    def other_core(x):
+        return lax.ppermute(x, "ga", [(i, i ^ 1) for i in range(n_ga)])
+
+    def along(x, chips_on):
+        return lax.ppermute(x, "ga", [(i, 2 * chips_on[i // 2] + i % 2) for i in range(n_ga)])
+
+    message = shape((2 * held * half + LABELS, t), BF16)
+
+    def pack(panels):
+        return run(pack_kernel, [message] * 2, block_rows, panels, specs=[SMEM, VMEM], name="pack")
+
+    sums = shape((transfers, g_local, 2 * count * t), F32)
+
+    def product(body, terms, *args):
+        return run(
+            body,
+            sums,
+            screened,
+            *args,
+            scratch=[pltpu.VMEM((terms * g_local, 2 * count * t), BF16)] * 2,
+            aliases={} if terms == 1 else {3: 0},
+            name="product",
+            mib=24,
+        )
+
+    def pick(packed, came):
+        sends = run(
+            functools.partial(pick_kernel, held),
+            [shape((count, 2, half, t), BF16)] * 2,
+            *packed,
+            *came,
+            name="pick",
+        )
+        return [across(sends[h], BITS[h][1]) for h in range(2)]
+
+    slices = shape((count, 2, g_local, t), BF16)
+
+    def near_of(packed, came, picked, apart=False):
+        kernel = functools.partial(near_kernel, held)
+        outs = [slices] + [shape(slices.shape[1:], BF16)] * (count if apart else 0)
+        near, *each = run(kernel, outs, *packed, *came, *picked, name="near")
+        return (near, each) if apart else near
+
+    packed = pack(densities)
+    before = along(tie((densities, packed))[0], FORTH)
+    came = [across(packed[h], BITS[h][0]) for h in range(2)]
+    source, packed = tie((screened, packed))
+    screened = run(
+        load_kernel,
+        shape(screened.shape, screened.dtype),
+        source,
+        specs=[HBM],
+        scratch=[pltpu.SemaphoreType.DMA((2 * transfers,))],
+        name="load",
+        mib=40,
+    )
+    came, screened = tie((came, screened))
+    picked = pick(packed, came)
+    packed_before = pack(before)
+    picked, _ = tie((picked, packed_before))
+    near = near_of(packed, came, picked)
+    ahead = along(near, BACK)
+    total = product(first_kernel, 1, near, coulomb[None, :])
+
+    came_before = [across(packed_before[h], BITS[h][0]) for h in range(2)]
+    rest_sends = run(
+        functools.partial(rest_kernel, held),
+        [shape((transfers, 2, half, t), BF16)] * (2 * count),
+        *packed,
+        *came,
+        name="rest",
+    )
+    came_before, total, rest_sends = tie((came_before, total, rest_sends))
+    picked_before = pick(packed_before, came_before)
+    near_before, before_each = near_of(packed_before, came_before, picked_before, True)
+
+    behind = [along(x, FORTH) for x in before_each]
+    rest_sends, ahead, _ = tie((rest_sends, ahead, near_before))
+    rest = [across(x, BITS[i % 2][1]) for i, x in enumerate(rest_sends)]
+
+    stack, _ = tie(((near, near_before), ahead))
+    both = run(stack_kernel, shape((2, *slices.shape), BF16), *stack, name="stack")
+    total = product(functools.partial(step_kernel, 1), 2, ahead, other_core(ahead), total)
+    total = product(
+        functools.partial(second_kernel, -1), 3, near_before, other_core(both), total
+    )
+
+    parts = shape((chips, transfers, 2, 2, t // n_ga, t), F32)
+    part = parts.shape[1:]
+    sums_of = []
+    done = total
+    for j in range(count):
+        came_j = rest[2 * j : 2 * j + 2]
+        if j:
+            behind[j], came_j, _ = tie((behind[j], came_j, done))
+        else:
+            behind[j] = tie((behind[j], done))[0]
+            came_j = [tie((x, done))[0] for x in came_j]
+        far = run(
+            functools.partial(far_kernel, held, j),
+            shape((transfers, 2, g_local, t), BF16),
+            *packed,
+            *came,
+            *came_j,
+            name="far",
+        )
+        if j:
+            far = tie((far, halves))[0]
+        keep, *give = run(
+            functools.partial(last_kernel, chips, -2, j),
+            [parts] + [shape((chips, transfers, 2, t // n_ga, t), BF16)] * 2,
+            screened,
+            behind[j],
+            other_core(behind[j]),
+            total,
+            far,
+            scratch=[pltpu.VMEM((2 * g_local, 2 * t), BF16)] * 2,
+            name="last",
+            mib=24,
+        )
+        own, cross, sends = run(
+            split_kernel,
+            [shape(part, F32), shape(part, F32), shape((2, *part), BF16)],
+            keep,
+            *[other_core(x) for x in give],
+            name="split",
+        )
+        done = sends
+        halves = lax.ppermute(sends, "ga", [(i, i ^ 2) for i in range(n_ga)])
+        sums_of.append((own, cross, halves))
+    groups = []
+    for own, cross, halves in sums_of:
+        own, sends = run(
+            merge_kernel, [shape(part, F32), shape(part, BF16)], own, cross, halves, name="merge"
+        )
+        groups += [own, lax.ppermute(sends, "ga", [(i, i ^ 4) for i in range(n_ga)])]
+    result = shape((count, transfers, 2, t // n_ga, t), F32)
+    return tuple(
+        run(
+            functools.partial(finish_kernel, count, 2, -1.0 / math.sqrt(g_total)),
+            [result] * 2,
+            *groups,
+            name="finish",
+        )
+    )
+
+
+def plain(densities, screened, coulomb, block_rows):
     owner = lax.axis_index("kp")
     g_slot = lax.axis_index("ga")
     k_held = densities.shape[0]
@@ -62,6 +496,17 @@
 
 def solution(mesh):
     placed = (P("kp", None, "ga", None), P("kp", None, "ga", None), P("ga"), P("kp", None))
+    n_kp, n_ga = mesh.shape["kp"], mesh.shape["ga"]
+
+    def shards(densities, screened, coulomb, block_rows):
+        g_local, t = densities.shape[2], densities.shape[3]
+        fits = n_kp == 2 * 2 and n_ga == 4 * 2
+        fits = fits and g_local % 128 == 0 and t % (8 * n_ga) == 0
+        fits = fits and n_kp * densities.shape[0] <= 256
+        if fits:
+            return quick(n_kp, n_ga, densities, screened, coulomb, block_rows)
+        return plain(densities, screened, coulomb, block_rows)
+
     return jax.shard_map(
         shards,
         mesh=mesh,

time: 253 us -> 109 us (0.43)
  waiting for transfers between devices: 171 us -> 57.5 us
  local copies, waits for them, and re-layouts: 30.8 us -> 0.67 us
  matrix products: 28.5 us -> 0 us
  starting transfers between devices: 0.16 us -> 25.4 us
  Pallas kernels: 0 us -> 24.5 us
  between operations: 14 us -> 0.87 us
  other arithmetic: 8.26 us -> 0 us
    all_gather x2 -> x0, waiting for transfers between devices: 103 us -> none  [the longest x1 54.2 us: shards(): near_all = lax.all_gather(near_acc, 'ga', axis=2, tiled=True)]
    reduce_scatter x2 -> x0, waiting for transfers between devices: 67.5 us -> none  [the longest x1 34.9 us: shards(): lax.psum_scatter(partial_upper, 'ga', scatter_dimension=3, tiled=True)]
    ppermute x0 -> x28, waiting for transfers between devices: none -> 57.5 us  [the longest x12 23.3 us: across(): return lax.ppermute(x, 'kp', [(i, i ^ bit) for i in range(n_kp)])]
    dot_general x10 -> x0, matrix products: 28.5 us -> none  [the longest x1 7.42 us: shards(): jnp.einsum('sgh,jht->jsgt', screen_real, piece_imag, preferred_element_ty...]
    squeeze x6 -> x0, local copies, waits for them, and re-layouts: 28.4 us -> none  [the longest x2 16.7 us: shards(): piece_real = near_all[:, 0]]
    ppermute x0 -> x28, starting transfers between devices: none -> 25.4 us  [the longest x12 12.4 us: across(): return lax.ppermute(x, 'kp', [(i, i ^ bit) for i in range(n_kp)])]
    pallas_call x0 -> x21, Pallas kernels: none -> 24.5 us  [run(): pl.pallas_call(body, in_specs=specs or [VMEM] * len(args), out_specs=[VME...]
    another operation x3 -> x0, other arithmetic: 3.18 us -> none  [the longest x2 1.64 us: shards(): jnp.stack([jnp.swapaxes(lower_real, 2, 3), -jnp.swapaxes(lower_imag, 2, 3...]
  transfers between devices with their start and end apart: 4 -> 28, of which waited for: 4 -> 19; matrix products, arithmetic and copies ran while one was open for 6% -> 0% of each run, Pallas kernels for 0% -> 18%
where the time goes in v1:
time: 109 us
  waiting for transfers between devices  57.5 us (53%)
  starting transfers between devices  25.4 us (23%)
  Pallas kernels  24.5 us (22%)
    pallas_call x21, Pallas kernels, run(): pl.pallas_call(body, in_specs=specs or [VMEM] * len(args), out_specs=[VME...  24.5 us
    ppermute x12, waiting for transfers between devices, across(): return lax.ppermute(x, 'kp', [(i, i ^ bit) for i in range(n_kp)])  23.3 us
    ppermute x2, waiting for transfers between devices, quick(): halves = lax.ppermute(sends, 'ga', [(i, i ^ 2) for i in range(n_ga)])  16.6 us
    ppermute x12, starting transfers between devices, across(): return lax.ppermute(x, 'kp', [(i, i ^ bit) for i in range(n_kp)])  12.4 us
    ppermute x4, starting transfers between devices, along(): lax.ppermute(x, 'ga', [(i, 2 * chips_on[i // 2] + i % 2) for i in range(n...  7.71 us
    ppermute x2, waiting for transfers between devices, quick(): lax.ppermute(sends, 'ga', [(i, i ^ 4) for i in range(n_ga)])  7.7 us
    ppermute x4, waiting for transfers between devices, along(): lax.ppermute(x, 'ga', [(i, 2 * chips_on[i // 2] + i % 2) for i in range(n...  6.23 us
    ppermute x8, waiting for transfers between devices, other_core(): return lax.ppermute(x, 'ga', [(i, i ^ 1) for i in range(n_ga)])  3.69 us
  transfers between devices with their start and end apart: 28, of which 19 were waited for; matrix products, arithmetic and copies ran while one was open for 0% of the time, Pallas kernels for 18%

profile of v1, /device:TPU:0, one launch (start us, length us, event | category | flops | bytes accessed | tf_op | source)
XLA Modules:
  0.0 108.9 jit_solution(14507612294878969151)
XLA Ops:
  2.5 3.1 %collective-permute-start.2 = (bf16[2,2,384,256]{3,2,1,0:T(8,128)(2,1)}, bf16[2,2,384,256]{3,2,1,0:T(8,128)(2,1)S(1)}, u32[]{:S(2)}, u32[]{:S(2)}) collective-permute-start(bf16[2,2,384,256]{3,2,1,0:T(8,128)(2,1)} %densities.1), channel_id=1, source_target_pairs={{0,2},{1,3},{2,6},{3,7},{4,0},{5,1},{6,4},{7,5},{8,10},{9,11},{10,... | collective-permute-start | bytes 2359304 | tf_op jit(solution)/shard_map/ppermute | solution.py:300
  5.6 1.5 %collective-permute-start = (bf16[784,256]{1,0:T(8,128)(2,1)S(1)}, bf16[784,256]{1,0:T(8,128)(2,1)S(1)}, u32[]{:S(2)}, u32[]{:S(2)}) collective-permute-start(bf16[784,256]{1,0:T(8,128)(2,1)S(1)} %get-tuple-element.70.packed_0), channel_id=1, source_target_pairs={{0,8},{8,0},{16,24},{24,16},{1,9},{9,1},{17,25},{25,17},{2,10},{10... | collective-permute-start | bytes 1204232 | tf_op jit(solution)/shard_map/ppermute | solution.py:294
  7.1 1.5 %collective-permute-start.1 = (bf16[784,256]{1,0:T(8,128)(2,1)S(1)}, bf16[784,256]{1,0:T(8,128)(2,1)S(1)}, u32[]{:S(2)}, u32[]{:S(2)}) collective-permute-start(bf16[784,256]{1,0:T(8,128)(2,1)S(1)} %get-tuple-element.71.packed_1), channel_id=1, source_target_pairs={{0,16},{8,24},{16,0},{24,8},{1,17},{9,25},{17,1},{25,9},{2,18},{10... | collective-permute-start | bytes 1204232 | tf_op jit(solution)/shard_map/ppermute | solution.py:294
  8.6 3.8 %load.1.screened = bf16[2,2,384,3072]{3,2,1,0:T(8,128)(2,1)S(1)} custom-call(bf16[2,2,384,3072]{3,2,1,0:T(8,128)(2,1)} %source), custom_call_target="tpu_custom_call" | custom-call | tf_op jit(solution)/shard_map/load/pallas_call | solution.py:29
  12.4 3.9 %collective-permute-done.came_0 = bf16[784,256]{1,0:T(8,128)(2,1)S(1)} collective-permute-done((bf16[784,256]{1,0:T(8,128)(2,1)S(1)}, bf16[784,256]{1,0:T(8,128)(2,1)S(1)}, u32[]{:S(2)}, u32[]{:S(2)}) %collective-permute-start) | collective-permute-done | bytes 401440 | tf_op jit(solution)/shard_map/ppermute | solution.py:294
  18.1 1.6 %collective-permute-start.5 = (bf16[2,2,192,256]{3,2,1,0:T(8,128)(2,1)S(1)}, bf16[2,2,192,256]{3,2,1,0:T(8,128)(2,1)S(1)}, u32[]{:S(2)}, u32[]{:S(2)}) collective-permute-start(bf16[2,2,192,256]{3,2,1,0:T(8,128)(2,1)S(1)} %get-tuple-element.74), channel_id=1, source_target_pairs={{0,16},{8,24},{16,0},{24,8},{1,17},{9,25},{17,1},{25,9},{2,18},{10... | collective-permute-start | bytes 1179656 | tf_op jit(solution)/shard_map/ppermute | solution.py:294
  20.2 4.1 %collective-permute-done.2.densities = bf16[2,2,384,256]{3,2,1,0:T(8,128)(2,1)S(1)} collective-permute-done((bf16[2,2,384,256]{3,2,1,0:T(8,128)(2,1)}, bf16[2,2,384,256]{3,2,1,0:T(8,128)(2,1)S(1)}, u32[]{:S(2)}, u32[]{:S(2)}) %collective-permute-start.2) | collective-permute-done | bytes 786464 | tf_op jit(solution)/shard_map/ppermute | solution.py:300
  24.9 1.6 %collective-permute-start.3 = (bf16[784,256]{1,0:T(8,128)(2,1)S(1)}, bf16[784,256]{1,0:T(8,128)(2,1)S(1)}, u32[]{:S(2)}, u32[]{:S(2)}) collective-permute-start(bf16[784,256]{1,0:T(8,128)(2,1)S(1)} %get-tuple-element.68.packed_0), channel_id=1, source_target_pairs={{0,8},{8,0},{16,24},{24,16},{1,9},{9,1},{17,25},{25,17},{2,10},{10... | collective-permute-start | bytes 1204232 | tf_op jit(solution)/shard_map/ppermute | solution.py:294
  26.6 1.5 %collective-permute-start.4 = (bf16[784,256]{1,0:T(8,128)(2,1)S(1)}, bf16[784,256]{1,0:T(8,128)(2,1)S(1)}, u32[]{:S(2)}, u32[]{:S(2)}) collective-permute-start(bf16[784,256]{1,0:T(8,128)(2,1)S(1)} %get-tuple-element.69.packed_1), channel_id=1, source_target_pairs={{0,16},{8,24},{16,0},{24,8},{1,17},{9,25},{17,1},{25,9},{2,18},{10... | collective-permute-start | bytes 1204232 | tf_op jit(solution)/shard_map/ppermute | solution.py:294
  28.1 2.6 %collective-permute-done.6.picked_1 = bf16[2,2,192,256]{3,2,1,0:T(8,128)(2,1)S(1)} collective-permute-done((bf16[2,2,192,256]{3,2,1,0:T(8,128)(2,1)S(1)}, bf16[2,2,192,256]{3,2,1,0:T(8,128)(2,1)S(1)}, u32[]{:S(2)}, u32[]{:S(2)}) %collective-permute-start.6) | collective-permute-done | bytes 393248 | tf_op jit(solution)/shard_map/ppermute | solution.py:294
  33.1 1.8 %product.3.before = f32[2,384,1024]{2,1,0:T(8,128)S(1)} custom-call(bf16[2,2,384,3072]{3,2,1,0:T(8,128)(2,1)S(1)} %load.1.screened, bf16[2,2,384,256]{3,2,1,0:T(8,128)(2,1)S(1)} %near.2.own.refs_0_, f32[1,384]{1,0:T(1,128)S(1)} %broadcast_in_dim.3.coulomb), custom_call_target="tpu_custom_call" | custom-call | tf_op jit(solution)/shard_map/product/pallas_call | solution.py:29
  34.9 2.5 %collective-permute-done.3.came_0 = bf16[784,256]{1,0:T(8,128)(2,1)S(1)} collective-permute-done((bf16[784,256]{1,0:T(8,128)(2,1)S(1)}, bf16[784,256]{1,0:T(8,128)(2,1)S(1)}, u32[]{:S(2)}, u32[]{:S(2)}) %collective-permute-start.3) | collective-permute-done | bytes 401440 | tf_op jit(solution)/shard_map/ppermute | solution.py:294
  39.1 8.2 %collective-permute-done.7.picked_0 = bf16[2,2,192,256]{3,2,1,0:T(8,128)(2,1)S(1)} collective-permute-done((bf16[2,2,192,256]{3,2,1,0:T(8,128)(2,1)S(1)}, bf16[2,2,192,256]{3,2,1,0:T(8,128)(2,1)S(1)}, u32[]{:S(2)}, u32[]{:S(2)}) %collective-permute-start.7) | collective-permute-done | bytes 393248 | tf_op jit(solution)/shard_map/ppermute | solution.py:294
  49.4 2.1 %collective-permute-start.9 = (bf16[2,384,256]{2,1,0:T(8,128)(2,1)S(1)}, bf16[2,384,256]{2,1,0:T(8,128)(2,1)S(1)}, u32[]{:S(2)}, u32[]{:S(2)}) collective-permute-start(bf16[2,384,256]{2,1,0:T(8,128)(2,1)S(1)} %get-tuple-element.86), channel_id=1, source_target_pairs={{0,2},{1,3},{2,6},{3,7},{4,0},{5,1},{6,4},{7,5},{8,10},{9,11},{10,... | collective-permute-start | bytes 1179656 | tf_op jit(solution)/shard_map/ppermute | solution.py:300
  53.5 3.0 %product.4.before = f32[2,384,1024]{2,1,0:T(8,128)S(1)} custom-call(bf16[2,2,384,3072]{3,2,1,0:T(8,128)(2,1)S(1)} %load.1.screened, bf16[2,2,384,256]{3,2,1,0:T(8,128)(2,1)S(1)} %collective-permute-done.10.own, bf16[2,2,384,256]{3,2,1,0:T(8,128)(2,1)S(1)} %collective-permute-done.12.pair, ...), custom_call_target="tpu_custom_call", output_to_operand_aliasing={{}: (3, {})} | custom-call | tf_op jit(solution)/shard_map/product/pallas_call | solution.py:29
  56.5 4.6 %product.5.before = f32[2,384,1024]{2,1,0:T(8,128)S(1)} custom-call(bf16[2,2,384,3072]{3,2,1,0:T(8,128)(2,1)S(1)} %load.1.screened, bf16[2,2,384,256]{3,2,1,0:T(8,128)(2,1)S(1)} %get-tuple-element.94.refs_1_.own, bf16[2,2,2,384,256]{4,3,2,1,0:T(8,128)(2,1)S(1)} %collective-permute-done.11.pairs, ...), custom_call_target="tpu_custom_call", output_to_operand_aliasing={{}: (3, {})} | custom-call | tf_op jit(solution)/shard_map/product/pallas_call | solution.py:29
  65.0 2.5 %last.2 = (f32[4,2,2,2,32,256]{5,4,3,2,1,0:T(8,128)S(1)}, bf16[4,2,2,32,256]{4,3,2,1,0:T(8,128)(2,1)S(1)}, bf16[4,2,2,32,256]{4,3,2,1,0:T(8,128)(2,1)S(1)}) custom-call(bf16[2,2,384,3072]{3,2,1,0:T(8,128)(2,1)S(1)} %load.1.screened, bf16[2,384,256]{2,1,0:T(8,128)(2,1)S(1)} %collective-permute-done.9.own, ...), custom_call_target="tpu_custom_call" | custom-call | tf_op jit(solution)/shard_map/last/pallas_call | solution.py:29
  69.6 3.4 %collective-permute-done.21.rest_0 = bf16[2,2,192,256]{3,2,1,0:T(8,128)(2,1)S(1)} collective-permute-done((bf16[2,2,192,256]{3,2,1,0:T(8,128)(2,1)S(1)}, bf16[2,2,192,256]{3,2,1,0:T(8,128)(2,1)S(1)}, u32[]{:S(2)}, u32[]{:S(2)}) %collective-permute-start.21) | collective-permute-done | bytes 393248 | tf_op jit(solution)/shard_map/ppermute | solution.py:294
  73.5 1.8 %collective-permute-done.20.own = bf16[2,384,256]{2,1,0:T(8,128)(2,1)S(1)} collective-permute-done((bf16[2,384,256]{2,1,0:T(8,128)(2,1)S(1)}, bf16[2,384,256]{2,1,0:T(8,128)(2,1)S(1)}, u32[]{:S(2)}, u32[]{:S(2)}) %collective-permute-start.20) | collective-permute-done | bytes 393248 | tf_op jit(solution)/shard_map/ppermute | solution.py:300
  75.6 8.5 %collective-permute-done.18.came = bf16[2,2,2,2,32,256]{5,4,3,2,1,0:T(8,128)(2,1)S(1)} collective-permute-done((bf16[2,2,2,2,32,256]{5,4,3,2,1,0:T(8,128)(2,1)S(1)}, bf16[2,2,2,2,32,256]{5,4,3,2,1,0:T(8,128)(2,1)S(1)}, u32[]{:S(2)}, u32[]{:S(2)}) %collective-permute-start.18) | collective-permute-done | bytes 262176 | tf_op jit(solution)/shard_map/ppermute | solution.py:424
  84.0 2.5 %last.3 = (f32[4,2,2,2,32,256]{5,4,3,2,1,0:T(8,128)S(1)}, bf16[4,2,2,32,256]{4,3,2,1,0:T(8,128)(2,1)S(1)}, bf16[4,2,2,32,256]{4,3,2,1,0:T(8,128)(2,1)S(1)}) custom-call(bf16[2,2,384,3072]{3,2,1,0:T(8,128)(2,1)S(1)} %load.1.screened, bf16[2,384,256]{2,1,0:T(8,128)(2,1)S(1)} %collective-permute-done.20.own, ...), custom_call_target="tpu_custom_call" | custom-call | tf_op jit(solution)/shard_map/last/pallas_call | solution.py:29
  89.0 2.7 %collective-permute-start.19 = (bf16[2,2,2,32,256]{4,3,2,1,0:T(8,128)(2,1)S(1)}, bf16[2,2,2,32,256]{4,3,2,1,0:T(8,128)(2,1)S(1)}, u32[]{:S(2)}, u32[]{:S(2)}) collective-permute-start(bf16[2,2,2,32,256]{4,3,2,1,0:T(8,128)(2,1)S(1)} %get-tuple-element.108), channel_id=1, source_target_pairs={{0,4},{1,5},{2,6},{3,7},{4,0},{5,1},{6,2},{7,3},{8,12},{9,13},{10,... | collective-permute-start | bytes 393224 | tf_op jit(solution)/shard_map/ppermute | solution.py:431
  91.7 8.1 %collective-permute-done.26.came = bf16[2,2,2,2,32,256]{5,4,3,2,1,0:T(8,128)(2,1)S(1)} collective-permute-done((bf16[2,2,2,2,32,256]{5,4,3,2,1,0:T(8,128)(2,1)S(1)}, bf16[2,2,2,2,32,256]{5,4,3,2,1,0:T(8,128)(2,1)S(1)}, u32[]{:S(2)}, u32[]{:S(2)}) %collective-permute-start.26) | collective-permute-done | bytes 262176 | tf_op jit(solution)/shard_map/ppermute | solution.py:424
  100.4 7.7 %collective-permute-done.27.refs_3_ = bf16[2,2,2,32,256]{4,3,2,1,0:T(8,128)(2,1)S(1)} collective-permute-done((bf16[2,2,2,32,256]{4,3,2,1,0:T(8,128)(2,1)S(1)}, bf16[2,2,2,32,256]{4,3,2,1,0:T(8,128)(2,1)S(1)}, u32[]{:S(2)}, u32[]{:S(2)}) %collective-permute-start.27) | collective-permute-done | bytes 131104 | tf_op jit(solution)/shard_map/ppermute | solution.py:431
  (60 shorter events, 23.4 us)
Async XLA Ops:
  2.5 21.8 %collective-permute-start.2 = (bf16[2,2,384,256]{3,2,1,0:T(8,128)(2,1)}, bf16[2,2,384,256]{3,2,1,0:T(8,128)(2,1)S(1)}, u32[]{:S(2)}, u32[]{:S(2)}) collective-permute-start(bf16[2,2,384,256]{3,2,1,0:T(8,128)(2,1)} %densities.1), channel_id=1, source_target_pairs={{0,2},{1,3},{2,6},{3,7},{4,0},{5,1},{6,4},{7,5},{8,10},{9,11},{10,... | collective-permute-start | bytes 2359304 | tf_op jit(solution)/shard_map/ppermute | solution.py:300
  5.6 10.8 %collective-permute-start = (bf16[784,256]{1,0:T(8,128)(2,1)S(1)}, bf16[784,256]{1,0:T(8,128)(2,1)S(1)}, u32[]{:S(2)}, u32[]{:S(2)}) collective-permute-start(bf16[784,256]{1,0:T(8,128)(2,1)S(1)} %get-tuple-element.70.packed_0), channel_id=1, source_target_pairs={{0,8},{8,0},{16,24},{24,16},{1,9},{9,1},{17,25},{25,17},{2,10},{10... | collective-permute-start | bytes 1204232 | tf_op jit(solution)/shard_map/ppermute | solution.py:294
  7.1 10.5 %collective-permute-start.1 = (bf16[784,256]{1,0:T(8,128)(2,1)S(1)}, bf16[784,256]{1,0:T(8,128)(2,1)S(1)}, u32[]{:S(2)}, u32[]{:S(2)}) collective-permute-start(bf16[784,256]{1,0:T(8,128)(2,1)S(1)} %get-tuple-element.71.packed_1), channel_id=1, source_target_pairs={{0,16},{8,24},{16,0},{24,8},{1,17},{9,25},{17,1},{25,9},{2,18},{10... | collective-permute-start | bytes 1204232 | tf_op jit(solution)/shard_map/ppermute | solution.py:294
  18.1 9.9 %collective-permute-start.5 = (bf16[2,2,192,256]{3,2,1,0:T(8,128)(2,1)S(1)}, bf16[2,2,192,256]{3,2,1,0:T(8,128)(2,1)S(1)}, u32[]{:S(2)}, u32[]{:S(2)}) collective-permute-start(bf16[2,2,192,256]{3,2,1,0:T(8,128)(2,1)S(1)} %get-tuple-element.74), channel_id=1, source_target_pairs={{0,16},{8,24},{16,0},{24,8},{1,17},{9,25},{17,1},{25,9},{2,18},{10... | collective-permute-start | bytes 1179656 | tf_op jit(solution)/shard_map/ppermute | solution.py:294
  19.7 10.9 %collective-permute-start.6 = (bf16[2,2,192,256]{3,2,1,0:T(8,128)(2,1)S(1)}, bf16[2,2,192,256]{3,2,1,0:T(8,128)(2,1)S(1)}, u32[]{:S(2)}, u32[]{:S(2)}) collective-permute-start(bf16[2,2,192,256]{3,2,1,0:T(8,128)(2,1)S(1)} %get-tuple-element.75), channel_id=1, source_target_pairs={{0,8},{8,0},{16,24},{24,16},{1,9},{9,1},{17,25},{25,17},{2,10},{10... | collective-permute-start | bytes 1179656 | tf_op jit(solution)/shard_map/ppermute | solution.py:294
  24.9 12.5 %collective-permute-start.3 = (bf16[784,256]{1,0:T(8,128)(2,1)S(1)}, bf16[784,256]{1,0:T(8,128)(2,1)S(1)}, u32[]{:S(2)}, u32[]{:S(2)}) collective-permute-start(bf16[784,256]{1,0:T(8,128)(2,1)S(1)} %get-tuple-element.68.packed_0), channel_id=1, source_target_pairs={{0,8},{8,0},{16,24},{24,16},{1,9},{9,1},{17,25},{25,17},{2,10},{10... | collective-permute-start | bytes 1204232 | tf_op jit(solution)/shard_map/ppermute | solution.py:294
  26.6 10.9 %collective-permute-start.4 = (bf16[784,256]{1,0:T(8,128)(2,1)S(1)}, bf16[784,256]{1,0:T(8,128)(2,1)S(1)}, u32[]{:S(2)}, u32[]{:S(2)}) collective-permute-start(bf16[784,256]{1,0:T(8,128)(2,1)S(1)} %get-tuple-element.69.packed_1), channel_id=1, source_target_pairs={{0,16},{8,24},{16,0},{24,8},{1,17},{9,25},{17,1},{25,9},{2,18},{10... | collective-permute-start | bytes 1204232 | tf_op jit(solution)/shard_map/ppermute | solution.py:294
  31.0 17.7 %collective-permute-start.10 = (bf16[2,2,384,256]{3,2,1,0:T(8,128)(2,1)S(1)}, bf16[2,2,384,256]{3,2,1,0:T(8,128)(2,1)S(1)}, u32[]{:S(2)}, u32[]{:S(2)}) collective-permute-start(bf16[2,2,384,256]{3,2,1,0:T(8,128)(2,1)S(1)} %near.2.own.refs_0_), channel_id=1, source_target_pairs={{0,4},{1,5},{2,0},{3,1},{4,6},{5,7},{6,2},{7,3},{8,12},{9,13},{10,... | collective-permute-start | bytes 2359304 | tf_op jit(solution)/shard_map/ppermute | solution.py:300
  38.0 9.3 %collective-permute-start.7 = (bf16[2,2,192,256]{3,2,1,0:T(8,128)(2,1)S(1)}, bf16[2,2,192,256]{3,2,1,0:T(8,128)(2,1)S(1)}, u32[]{:S(2)}, u32[]{:S(2)}) collective-permute-start(bf16[2,2,192,256]{3,2,1,0:T(8,128)(2,1)S(1)} %get-tuple-element.84), channel_id=1, source_target_pairs={{0,16},{8,24},{16,0},{24,8},{1,17},{9,25},{17,1},{25,9},{2,18},{10... | collective-permute-start | bytes 1179656 | tf_op jit(solution)/shard_map/ppermute | solution.py:294
  38.6 9.7 %collective-permute-start.8 = (bf16[2,2,192,256]{3,2,1,0:T(8,128)(2,1)S(1)}, bf16[2,2,192,256]{3,2,1,0:T(8,128)(2,1)S(1)}, u32[]{:S(2)}, u32[]{:S(2)}) collective-permute-start(bf16[2,2,192,256]{3,2,1,0:T(8,128)(2,1)S(1)} %get-tuple-element.85), channel_id=1, source_target_pairs={{0,8},{8,0},{16,24},{24,16},{1,9},{9,1},{17,25},{25,17},{2,10},{10... | collective-permute-start | bytes 1179656 | tf_op jit(solution)/shard_map/ppermute | solution.py:294
  48.9 7.7 %collective-permute-start.11 = (bf16[2,2,2,384,256]{4,3,2,1,0:T(8,128)(2,1)S(1)}, bf16[2,2,2,384,256]{4,3,2,1,0:T(8,128)(2,1)S(1)}, u32[]{:S(2)}, u32[]{:S(2)}) collective-permute-start(bf16[2,2,2,384,256]{4,3,2,1,0:T(8,128)(2,1)S(1)} %stack.1), channel_id=1, source_target_pairs={{0,1},{1,0},{2,3},{3,2},{4,5},{5,4},{6,7},{7,6},{8,9},{9,8},{10,11... | collective-permute-start | bytes 4718600 | tf_op jit(solution)/shard_map/ppermute | solution.py:297
  48.9 4.5 %collective-permute-start.12 = (bf16[2,2,384,256]{3,2,1,0:T(8,128)(2,1)S(1)}, bf16[2,2,384,256]{3,2,1,0:T(8,128)(2,1)S(1)}, u32[]{:S(2)}, u32[]{:S(2)}) collective-permute-start(bf16[2,2,384,256]{3,2,1,0:T(8,128)(2,1)S(1)} %collective-permute-done.10.own), channel_id=1, source_target_pairs={{0,1},{1,0},{2,3},{3,2},{4,5},{5,4},{6,7},{7,6},{8,9},{9,8},{10,11... | collective-permute-start | bytes 2359304 | tf_op jit(solution)/shard_map/ppermute | solution.py:297
  49.4 12.0 %collective-permute-start.9 = (bf16[2,384,256]{2,1,0:T(8,128)(2,1)S(1)}, bf16[2,384,256]{2,1,0:T(8,128)(2,1)S(1)}, u32[]{:S(2)}, u32[]{:S(2)}) collective-permute-start(bf16[2,384,256]{2,1,0:T(8,128)(2,1)S(1)} %get-tuple-element.86), channel_id=1, source_target_pairs={{0,2},{1,3},{2,6},{3,7},{4,0},{5,1},{6,4},{7,5},{8,10},{9,11},{10,... | collective-permute-start | bytes 1179656 | tf_op jit(solution)/shard_map/ppermute | solution.py:300
  51.5 11.9 %collective-permute-start.15 = (bf16[2,2,192,256]{3,2,1,0:T(8,128)(2,1)S(1)}, bf16[2,2,192,256]{3,2,1,0:T(8,128)(2,1)S(1)}, u32[]{:S(2)}, u32[]{:S(2)}) collective-permute-start(bf16[2,2,192,256]{3,2,1,0:T(8,128)(2,1)S(1)} %get-tuple-element.99), channel_id=1, source_target_pairs={{0,8},{8,0},{16,24},{24,16},{1,9},{9,1},{17,25},{25,17},{2,10},{10... | collective-permute-start | bytes 1179656 | tf_op jit(solution)/shard_map/ppermute | solution.py:294
  52.1 12.5 %collective-permute-start.14 = (bf16[2,2,192,256]{3,2,1,0:T(8,128)(2,1)S(1)}, bf16[2,2,192,256]{3,2,1,0:T(8,128)(2,1)S(1)}, u32[]{:S(2)}, u32[]{:S(2)}) collective-permute-start(bf16[2,2,192,256]{3,2,1,0:T(8,128)(2,1)S(1)} %get-tuple-element.97), channel_id=1, source_target_pairs={{0,16},{8,24},{16,0},{24,8},{1,17},{9,25},{17,1},{25,9},{2,18},{10... | collective-permute-start | bytes 1179656 | tf_op jit(solution)/shard_map/ppermute | solution.py:294
  61.4 3.5 %collective-permute-start.13 = (bf16[2,384,256]{2,1,0:T(8,128)(2,1)S(1)}, bf16[2,384,256]{2,1,0:T(8,128)(2,1)S(1)}, u32[]{:S(2)}, u32[]{:S(2)}) collective-permute-start(bf16[2,384,256]{2,1,0:T(8,128)(2,1)S(1)} %collective-permute-done.9.own), channel_id=1, source_target_pairs={{0,1},{1,0},{2,3},{3,2},{4,5},{5,4},{6,7},{7,6},{8,9},{9,8},{10,11... | collective-permute-start | bytes 1179656 | tf_op jit(solution)/shard_map/ppermute | solution.py:297
  61.4 11.5 %collective-permute-start.21 = (bf16[2,2,192,256]{3,2,1,0:T(8,128)(2,1)S(1)}, bf16[2,2,192,256]{3,2,1,0:T(8,128)(2,1)S(1)}, u32[]{:S(2)}, u32[]{:S(2)}) collective-permute-start(bf16[2,2,192,256]{3,2,1,0:T(8,128)(2,1)S(1)} %get-tuple-element.110), channel_id=1, source_target_pairs={{0,16},{8,24},{16,0},{24,8},{1,17},{9,25},{17,1},{25,9},{2,18},{10... | collective-permute-start | bytes 1179656 | tf_op jit(solution)/shard_map/ppermute | solution.py:294
  62.2 11.2 %collective-permute-start.22 = (bf16[2,2,192,256]{3,2,1,0:T(8,128)(2,1)S(1)}, bf16[2,2,192,256]{3,2,1,0:T(8,128)(2,1)S(1)}, u32[]{:S(2)}, u32[]{:S(2)}) collective-permute-start(bf16[2,2,192,256]{3,2,1,0:T(8,128)(2,1)S(1)} %get-tuple-element.111), channel_id=1, source_target_pairs={{0,8},{8,0},{16,24},{24,16},{1,9},{9,1},{17,25},{25,17},{2,10},{10... | collective-permute-start | bytes 1179656 | tf_op jit(solution)/shard_map/ppermute | solution.py:294
  63.4 11.9 %collective-permute-start.20 = (bf16[2,384,256]{2,1,0:T(8,128)(2,1)S(1)}, bf16[2,384,256]{2,1,0:T(8,128)(2,1)S(1)}, u32[]{:S(2)}, u32[]{:S(2)}) collective-permute-start(bf16[2,384,256]{2,1,0:T(8,128)(2,1)S(1)} %get-tuple-element.109), channel_id=1, source_target_pairs={{0,2},{1,3},{2,6},{3,7},{4,0},{5,1},{6,4},{7,5},{8,10},{9,11},{10,... | collective-permute-start | bytes 1179656 | tf_op jit(solution)/shard_map/ppermute | solution.py:300
  75.3 8.7 %collective-permute-start.23 = (bf16[2,384,256]{2,1,0:T(8,128)(2,1)S(1)}, bf16[2,384,256]{2,1,0:T(8,128)(2,1)S(1)}, u32[]{:S(2)}, u32[]{:S(2)}) collective-permute-start(bf16[2,384,256]{2,1,0:T(8,128)(2,1)S(1)} %collective-permute-done.20.own), channel_id=1, source_target_pairs={{0,1},{1,0},{2,3},{3,2},{4,5},{5,4},{6,7},{7,6},{8,9},{9,8},{10,11... | collective-permute-start | bytes 1179656 | tf_op jit(solution)/shard_map/ppermute | solution.py:297
  75.3 8.7 %collective-permute-start.18 = (bf16[2,2,2,2,32,256]{5,4,3,2,1,0:T(8,128)(2,1)S(1)}, bf16[2,2,2,2,32,256]{5,4,3,2,1,0:T(8,128)(2,1)S(1)}, u32[]{:S(2)}, u32[]{:S(2)}) collective-permute-start(bf16[2,2,2,2,32,256]{5,4,3,2,1,0:T(8,128)(2,1)S(1)} %get-tuple-element.106), channel_id=1, source_target_pairs={{0,2},{1,3},{2,0},{3,1},{4,6},{5,7},{6,4},{7,5},{8,10},{9,11},{10,... | collective-permute-start | bytes 786440 | tf_op jit(solution)/shard_map/ppermute | solution.py:424
  88.6 11.2 %collective-permute-start.26 = (bf16[2,2,2,2,32,256]{5,4,3,2,1,0:T(8,128)(2,1)S(1)}, bf16[2,2,2,2,32,256]{5,4,3,2,1,0:T(8,128)(2,1)S(1)}, u32[]{:S(2)}, u32[]{:S(2)}) collective-permute-start(bf16[2,2,2,2,32,256]{5,4,3,2,1,0:T(8,128)(2,1)S(1)} %get-tuple-element.121), channel_id=1, source_target_pairs={{0,2},{1,3},{2,0},{3,1},{4,6},{5,7},{6,4},{7,5},{8,10},{9,11},{10,... | collective-permute-start | bytes 786440 | tf_op jit(solution)/shard_map/ppermute | solution.py:424
  89.0 11.4 %collective-permute-start.19 = (bf16[2,2,2,32,256]{4,3,2,1,0:T(8,128)(2,1)S(1)}, bf16[2,2,2,32,256]{4,3,2,1,0:T(8,128)(2,1)S(1)}, u32[]{:S(2)}, u32[]{:S(2)}) collective-permute-start(bf16[2,2,2,32,256]{4,3,2,1,0:T(8,128)(2,1)S(1)} %get-tuple-element.108), channel_id=1, source_target_pairs={{0,4},{1,5},{2,6},{3,7},{4,0},{5,1},{6,2},{7,3},{8,12},{9,13},{10,... | collective-permute-start | bytes 393224 | tf_op jit(solution)/shard_map/ppermute | solution.py:431
  99.9 8.2 %collective-permute-start.27 = (bf16[2,2,2,32,256]{4,3,2,1,0:T(8,128)(2,1)S(1)}, bf16[2,2,2,32,256]{4,3,2,1,0:T(8,128)(2,1)S(1)}, u32[]{:S(2)}, u32[]{:S(2)}) collective-permute-start(bf16[2,2,2,32,256]{4,3,2,1,0:T(8,128)(2,1)S(1)} %get-tuple-element.123), channel_id=1, source_target_pairs={{0,4},{1,5},{2,6},{3,7},{4,0},{5,1},{6,2},{7,3},{8,12},{9,13},{10,... | collective-permute-start | bytes 393224 | tf_op jit(solution)/shard_map/ppermute | solution.py:431
  (7 other events, 49.6 us)

commit v2 on v1

--- a/solution.py
+++ b/solution.py
@@ -1,4 +1,5 @@
 import functools
+import itertools
 import math
 
 import jax
@@ -93,7 +94,7 @@
             copy_if(label_of(came[1 - h], held, half, j), found, sends[h].at[j])
 
 
-def near_kernel(held, packed_0, packed_1, came_0, came_1, picked_0, picked_1, near, *each):
+def near_kernel(held, packed_0, packed_1, came_0, came_1, picked_0, picked_1, near):
     owner = lax.axis_index("kp")
     packed, came, picked = (packed_0, packed_1), (came_0, came_1), (picked_0, picked_1)
     half = picked_0.shape[2]
@@ -109,45 +110,95 @@
             def _(h=h, j=j, out=out):
                 out[...] = picked[h][j]
 
-    for j, out in enumerate(each):
-        out[...] = near[j]
-
 
 def stack_kernel(*refs):
     for i, ref in enumerate(refs[:-1]):
         refs[-1][i] = ref[...]
 
 
-def rest_kernel(held, packed_0, packed_1, came_0, came_1, *sends):
+def left_over(n_kp, held, transfers, count):
+    most = []
+    for first, second in BITS:
+        worst = 0
+        for owner in range(n_kp):
+            side = {who * held + k for who in (owner ^ second, owner ^ second ^ first) for k in range(held)}
+            rows = range(n_kp * held - transfers * (owner + 1) + 1)
+            for chosen in itertools.product(rows, repeat=count):
+                need = {r + owner * transfers + s for r in chosen for s in range(transfers)}
+                worst = max(worst, len((need & side) - set(chosen)))
+        most.append(max(worst, 1))
+    return most
+
+
+def slots(labels, rows, owner, transfers):
+    found, place = [], jnp.int32(0)
+    for label in labels:
+        need, sent = jnp.bool_(False), jnp.bool_(False)
+        for row in rows:
+            first = row + owner * transfers
+            need = need | ((label >= first) & (label < first + transfers))
+            sent = sent | (label == row)
+        need = need & jnp.logical_not(sent)
+        found.append((need, place))
+        place = place + need.astype(jnp.int32)
+    return found
+
+
+def rest_kernel(held, transfers, count, packed_0, packed_1, came_0, came_1, *sends):
     owner = lax.axis_index("kp")
     packed, came = (packed_0, packed_1), (came_0, came_1)
-    transfers, _, half, _ = sends[0].shape
-    for j in range(len(sends) // 2):
-        for h in range(2):
-            first, second = BITS[h]
-            found = entries(packed[h], owner, held, half)
-            found += entries(came[h], owner ^ first, held, half)
-            row = label_of(came[1 - h], held, half, j)
+    for h in range(2):
+        first, second = BITS[h]
+        room, _, half, _ = sends[h].shape
+        found = entries(packed[h], owner, held, half)
+        found += entries(came[h], owner ^ first, held, half)
+        rows = [label_of(came[1 - h], held, half, j) for j in range(count)]
+        places = slots([label for label, *_ in found], rows, owner ^ second, transfers)
+        for (_, message, real, imag), (need, place) in zip(found, places):
+            for i in range(room):
+
+                @pl.when(need & (place == i))
+                def _(h=h, i=i, message=message, real=real, imag=imag, half=half):
+                    sends[h][i, 0] = message[real : real + half]
+                    sends[h][i, 1] = message[imag : imag + half]
+
+
+def far_kernel(
+    held, packed_0, packed_1, came_0, came_1, picked_0, picked_1, rest_0, rest_1, far
+):
+    owner = lax.axis_index("kp")
+    packed, came = (packed_0, packed_1), (came_0, came_1)
+    picked, rest = (picked_0, picked_1), (rest_0, rest_1)
+    count, transfers, _, g_local, _ = far.shape
+    half = g_local // 2
+    rows = [label_of(packed_0, held, half, j) for j in range(count)]
+    for h in range(2):
+        first, second = BITS[h]
+        found = entries(packed[h], owner, held, half)
+        found += entries(came[h], owner ^ first, held, half)
+        side = [
+            who * held + k for who in (owner ^ second, owner ^ second ^ first) for k in range(held)
+        ]
+        places = slots(side, rows, owner, transfers)
+        for j in range(count):
             for s in range(transfers):
-                label = row + (owner ^ second) * transfers + s
-                copy_if(label, found, sends[2 * j + h].at[s])
-
-
-def far_kernel(held, j, packed_0, packed_1, came_0, came_1, rest_0, rest_1, far):
-    owner = lax.axis_index("kp")
-    packed, came, rest = (packed_0, packed_1), (came_0, came_1), (rest_0, rest_1)
-    transfers, _, half, _ = rest_0.shape
-    row = label_of(packed_0, held, half, j)
-    for h in range(2):
-        found = entries(packed[h], owner, held, half)
-        found += entries(came[h], owner ^ BITS[h][0], held, half)
-        for s in range(transfers):
-            out = far.at[s, :, h * half : (h + 1) * half]
-            hit = copy_if(row + owner * transfers + s, found, out)
-
-            @pl.when(jnp.logical_not(hit))
-            def _(h=h, s=s, out=out):
-                out[...] = rest[h][s]
+                label = rows[j] + owner * transfers + s
+                out = far.at[j, s, :, h * half : (h + 1) * half]
+                hit = copy_if(label, found, out)
+                for i in range(count):
+                    match = (label == rows[i]) & jnp.logical_not(hit)
+                    hit = hit | match
+
+                    @pl.when(match)
+                    def _(h=h, i=i, out=out):
+                        out[...] = picked[h][i]
+
+                for name, (need, place) in zip(side, places):
+                    for i in range(rest[h].shape[0]):
+
+                        @pl.when((label == name) & need & (place == i))
+                        def _(h=h, i=i, out=out):
+                            out[...] = rest[h][i]
 
 
 def load_kernel(source, panels, sems):
@@ -175,14 +226,14 @@
 
 def lay(terms, upper, lower):
     for ref, first in terms:
-        *count, _, g_local, t = ref.shape
+        count, _, g_local, t = ref.shape
         rows = pl.ds(first if isinstance(first, int) else pl.multiple_of(first, 128), g_local)
-        for j, panel in enumerate([ref.at[j] for j in range(count[0])] if count else [ref]):
+        for j in range(count):
             real, imag = slice(2 * j * t, (2 * j + 1) * t), slice((2 * j + 1) * t, (2 * j + 2) * t)
-            upper[rows, real] = panel[0]
-            upper[rows, imag] = panel[1]
-            lower[rows, real] = -panel[1]
-            lower[rows, imag] = panel[0]
+            upper[rows, real] = ref[j, 0]
+            upper[rows, imag] = ref[j, 1]
+            lower[rows, real] = -ref[j, 1]
+            lower[rows, imag] = ref[j, 0]
 
 
 def place():
@@ -229,17 +280,17 @@
         total[s] = value + multiply(screened, s, left, g, upper, lower, 2 * g)
 
 
-def last_kernel(chips, steps, j, screened, own, pair, before, far, keep, give_0, give_1, upper, lower):
+def last_kernel(chips, steps, j, screened, own, pair, before, far, keep, give, upper, lower):
     z, core = place()
     g = screened.shape[2]
     t = far.shape[-1]
-    lay([(own, core * g), (pair, (1 - core) * g)], upper, lower)
+    lay([(own.at[j : j + 1], core * g), (pair.at[j : j + 1], (1 - core) * g)], upper, lower)
     span = 2 * chip_at(z, steps) * g
     first = core == 0
     for s in range(screened.shape[0]):
         value = before[s, :, 2 * j * t : 2 * (j + 1) * t]
         image = (value + multiply(screened, s, span, 2 * g, upper, lower)).astype(BF16)
-        by_real, by_imag = tdot(far[s, 0], image), tdot(far[s, 1], image)
+        by_real, by_imag = tdot(far[j, s, 0], image), tdot(far[j, s, 1], image)
         real = by_real[:, :t] + by_imag[:, t:]
         imag = by_real[:, t:] - by_imag[:, :t]
         parts = ((real, imag), (real.T, -imag.T))
@@ -248,21 +299,15 @@
                 block = parts[which][part]
                 block = block.reshape(chips, 2, t // (2 * chips), t)
                 keep[:, s, which, part] = jnp.where(first, block[:, 0], block[:, 1])
-                give = (give_0, give_1)[which]
-                give[:, s, part] = jnp.where(first, block[:, 1], block[:, 0]).astype(BF16)
-
-
-def split_kernel(keep, came_0, came_1, own, cross, sends):
+                give[:, s, which, part] = jnp.where(first, block[:, 1], block[:, 0]).astype(BF16)
+
+
+def split_kernel(keep, came, own, cross, sends):
     z = lax.axis_index("ga") // 2
-    for which, came in enumerate((came_0, came_1)):
-
-        def chip(at):
-            return keep[at, :, which] + came[at].astype(F32)
-
-        own[:, which] = chip(z)
-        cross[:, which] = chip(z ^ 2)
-        for i, at in enumerate((z ^ 1, z ^ 3)):
-            sends[i, :, which] = chip(at).astype(BF16)
+    own[...] = keep[z] + came[z].astype(F32)
+    cross[...] = keep[z ^ 2] + came[z ^ 2].astype(F32)
+    for i, at in enumerate((z ^ 1, z ^ 3)):
+        sends[i] = (keep[at] + came[at].astype(F32)).astype(BF16)
 
 
 def merge_kernel(own, cross, came, total, sends):
@@ -330,14 +375,12 @@
 
     slices = shape((count, 2, g_local, t), BF16)
 
-    def near_of(packed, came, picked, apart=False):
+    def near_of(packed, came, picked):
         kernel = functools.partial(near_kernel, held)
-        outs = [slices] + [shape(slices.shape[1:], BF16)] * (count if apart else 0)
-        near, *each = run(kernel, outs, *packed, *came, *picked, name="near")
-        return (near, each) if apart else near
-
+        return run(kernel, slices, *packed, *came, *picked, name="near")
+
+    before = along(densities, FORTH)
     packed = pack(densities)
-    before = along(tie((densities, packed))[0], FORTH)
     came = [across(packed[h], BITS[h][0]) for h in range(2)]
     source, packed = tie((screened, packed))
     screened = run(
@@ -352,81 +395,80 @@
     came, screened = tie((came, screened))
     picked = pick(packed, came)
     packed_before = pack(before)
-    picked, _ = tie((picked, packed_before))
+    rest_sends = run(
+        functools.partial(rest_kernel, held, transfers, count),
+        [shape((room, 2, half, t), BF16) for room in left_over(n_kp, held, transfers, count)],
+        *packed,
+        *came,
+        name="rest",
+    )
+    picked = list(tie((picked, (packed_before, rest_sends)))[0])
     near = near_of(packed, came, picked)
     ahead = along(near, BACK)
     total = product(first_kernel, 1, near, coulomb[None, :])
 
     came_before = [across(packed_before[h], BITS[h][0]) for h in range(2)]
-    rest_sends = run(
-        functools.partial(rest_kernel, held),
-        [shape((transfers, 2, half, t), BF16)] * (2 * count),
+    came_before, total = tie((came_before, total))
+    picked_before = pick(packed_before, came_before)
+    near_before = near_of(packed_before, came_before, picked_before)
+    behind = along(near_before, FORTH)
+
+    rest_sends, ahead, _ = tie((rest_sends, ahead, near_before))
+    rest = [across(rest_sends[h], BITS[h][1]) for h in range(2)]
+
+    stack, _ = tie(((near, near_before), ahead))
+    both = run(stack_kernel, shape((2, *slices.shape), BF16), *stack, name="stack")
+    total = product(
+        functools.partial(step_kernel, 1), 2, ahead, other_core(ahead), total
+    )
+    total = product(
+        functools.partial(second_kernel, -1), 3, near_before, other_core(both), total
+    )
+    behind, rest, total = tie((behind, rest, total))
+    far = run(
+        functools.partial(far_kernel, held),
+        shape((count, transfers, 2, g_local, t), BF16),
         *packed,
         *came,
-        name="rest",
-    )
-    came_before, total, rest_sends = tie((came_before, total, rest_sends))
-    picked_before = pick(packed_before, came_before)
-    near_before, before_each = near_of(packed_before, came_before, picked_before, True)
-
-    behind = [along(x, FORTH) for x in before_each]
-    rest_sends, ahead, _ = tie((rest_sends, ahead, near_before))
-    rest = [across(x, BITS[i % 2][1]) for i, x in enumerate(rest_sends)]
-
-    stack, _ = tie(((near, near_before), ahead))
-    both = run(stack_kernel, shape((2, *slices.shape), BF16), *stack, name="stack")
-    total = product(functools.partial(step_kernel, 1), 2, ahead, other_core(ahead), total)
-    total = product(
-        functools.partial(second_kernel, -1), 3, near_before, other_core(both), total
+        *picked,
+        *rest,
+        name="far",
     )
 
     parts = shape((chips, transfers, 2, 2, t // n_ga, t), F32)
     part = parts.shape[1:]
-    sums_of = []
-    done = total
+    pair = other_core(behind)
+    swaps = []
     for j in range(count):
-        came_j = rest[2 * j : 2 * j + 2]
-        if j:
-            behind[j], came_j, _ = tie((behind[j], came_j, done))
-        else:
-            behind[j] = tie((behind[j], done))[0]
-            came_j = [tie((x, done))[0] for x in came_j]
-        far = run(
-            functools.partial(far_kernel, held, j),
-            shape((transfers, 2, g_local, t), BF16),
-            *packed,
-            *came,
-            *came_j,
-            name="far",
-        )
-        if j:
-            far = tie((far, halves))[0]
-        keep, *give = run(
+        keep, give = run(
             functools.partial(last_kernel, chips, -2, j),
-            [parts] + [shape((chips, transfers, 2, t // n_ga, t), BF16)] * 2,
+            [parts, shape(parts.shape, BF16)],
             screened,
-            behind[j],
-            other_core(behind[j]),
+            behind,
+            pair,
             total,
             far,
             scratch=[pltpu.VMEM((2 * g_local, 2 * t), BF16)] * 2,
             name="last",
             mib=24,
         )
+        swaps.append((keep, other_core(give)))
+    groups = []
+    for keep, came_j in swaps:
         own, cross, sends = run(
             split_kernel,
             [shape(part, F32), shape(part, F32), shape((2, *part), BF16)],
             keep,
-            *[other_core(x) for x in give],
+            came_j,
             name="split",
         )
-        done = sends
-        halves = lax.ppermute(sends, "ga", [(i, i ^ 2) for i in range(n_ga)])
-        sums_of.append((own, cross, halves))
-    groups = []
-    for own, cross, halves in sums_of:
         own, sends = run(
-            merge_kernel, [shape(part, F32), shape(part, BF16)], own, cross, halves, name="merge"
+            merge_kernel,
+            [shape(part, F32), shape(part, BF16)],
+            own,
+            cross,
+            lax.ppermute(sends, "ga", [(i, i ^ 2) for i in range(n_ga)]),
+            name="merge",
         )
         groups += [own, lax.ppermute(sends, "ga", [(i, i ^ 4) for i in range(n_ga)])]
     result = shape((count, transfers, 2, t // n_ga, t), F32)

time: 109 us -> 102 us (0.936)
  waiting for transfers between devices: 57.5 us -> 53.1 us
  starting transfers between devices: 25.4 us -> 22.6 us
    ppermute x4 -> x3, waiting for transfers between devices: 6.23 us -> 11.5 us  [along(): lax.ppermute(x, 'ga', [(i, 2 * chips_on[i // 2] + i % 2) for i in range(n...]
    ppermute x12 -> x10, waiting for transfers between devices: 23.3 us -> 19.5 us  [across(): return lax.ppermute(x, 'kp', [(i, i ^ bit) for i in range(n_kp)])]
    ppermute x2, waiting for transfers between devices: 16.6 us -> 12.8 us  [quick(): lax.ppermute(sends, 'ga', [(i, i ^ 2) for i in range(n_ga)])]
    ppermute x4 -> x3, starting transfers between devices: 7.71 us -> 5.13 us  [along(): lax.ppermute(x, 'ga', [(i, 2 * chips_on[i // 2] + i % 2) for i in range(n...]
    ppermute x8 -> x5, waiting for transfers between devices: 3.69 us -> 1.57 us  [other_core(): return lax.ppermute(x, 'ga', [(i, i ^ 1) for i in range(n_ga)])]
    ppermute x2, starting transfers between devices: 3.23 us -> 1.71 us  [quick(): lax.ppermute(sends, 'ga', [(i, i ^ 4) for i in range(n_ga)])]
    ppermute x2, starting transfers between devices: 0.33 us -> 1.72 us  [quick(): lax.ppermute(sends, 'ga', [(i, i ^ 2) for i in range(n_ga)])]
    ppermute x12 -> x10, starting transfers between devices: 12.4 us -> 12.8 us  [across(): return lax.ppermute(x, 'kp', [(i, i ^ bit) for i in range(n_kp)])]
  transfers between devices with their start and end apart: 28 -> 22, of which waited for: 19 -> 15; matrix products, arithmetic and copies ran while one was open for 0% -> 0% of each run, Pallas kernels for 18% -> 20%
where the time goes in v2:
time: 102 us
  waiting for transfers between devices  53.1 us (52%)
  Pallas kernels  24.8 us (24%)
  starting transfers between devices  22.6 us (22%)
    pallas_call x20, Pallas kernels, run(): pl.pallas_call(body, in_specs=specs or [VMEM] * len(args), out_specs=[VME...  24.8 us
    ppermute x10, waiting for transfers between devices, across(): return lax.ppermute(x, 'kp', [(i, i ^ bit) for i in range(n_kp)])  19.5 us
    ppermute x2, waiting for transfers between devices, quick(): lax.ppermute(sends, 'ga', [(i, i ^ 2) for i in range(n_ga)])  12.8 us
    ppermute x10, starting transfers between devices, across(): return lax.ppermute(x, 'kp', [(i, i ^ bit) for i in range(n_kp)])  12.8 us
    ppermute x3, waiting for transfers between devices, along(): lax.ppermute(x, 'ga', [(i, 2 * chips_on[i // 2] + i % 2) for i in range(n...  11.5 us
    ppermute x2, waiting for transfers between devices, quick(): lax.ppermute(sends, 'ga', [(i, i ^ 4) for i in range(n_ga)])  7.69 us
    ppermute x3, starting transfers between devices, along(): lax.ppermute(x, 'ga', [(i, 2 * chips_on[i // 2] + i % 2) for i in range(n...  5.13 us
  transfers between devices with their start and end apart: 22, of which 15 were waited for; matrix products, arithmetic and copies ran while one was open for 0% of the time, Pallas kernels for 20%

profile of v2, /device:TPU:0, one launch (start us, length us, event | category | flops | bytes accessed | tf_op | source)
XLA Modules:
  0.0 102.0 jit_solution(13437641775084073144)
XLA Ops:
  2.5 3.0 %collective-permute-start = (bf16[784,256]{1,0:T(8,128)(2,1)S(1)}, bf16[784,256]{1,0:T(8,128)(2,1)S(1)}, u32[]{:S(2)}, u32[]{:S(2)}) collective-permute-start(bf16[784,256]{1,0:T(8,128)(2,1)S(1)} %get-tuple-element.52.packed_0), channel_id=1, source_target_pairs={{0,8},{8,0},{16,24},{24,16},{1,9},{9,1},{17,25},{25,17},{2,10},{10... | collective-permute-start | bytes 1204232 | tf_op jit(solution)/shard_map/ppermute | solution.py:339
  5.5 1.5 %collective-permute-start.1 = (bf16[784,256]{1,0:T(8,128)(2,1)S(1)}, bf16[784,256]{1,0:T(8,128)(2,1)S(1)}, u32[]{:S(2)}, u32[]{:S(2)}) collective-permute-start(bf16[784,256]{1,0:T(8,128)(2,1)S(1)} %get-tuple-element.53.packed_1), channel_id=1, source_target_pairs={{0,16},{8,24},{16,0},{24,8},{1,17},{9,25},{17,1},{25,9},{2,18},{10... | collective-permute-start | bytes 1204232 | tf_op jit(solution)/shard_map/ppermute | solution.py:339
  7.0 1.6 %collective-permute-start.2 = (bf16[2,2,384,256]{3,2,1,0:T(8,128)(2,1)}, bf16[2,2,384,256]{3,2,1,0:T(8,128)(2,1)S(1)}, u32[]{:S(2)}, u32[]{:S(2)}) collective-permute-start(bf16[2,2,384,256]{3,2,1,0:T(8,128)(2,1)} %densities.1), channel_id=1, source_target_pairs={{0,2},{1,3},{2,6},{3,7},{4,0},{5,1},{6,4},{7,5},{8,10},{9,11},{10,... | collective-permute-start | bytes 2359304 | tf_op jit(solution)/shard_map/ppermute | solution.py:345
  8.6 3.8 %load.1.screened = bf16[2,2,384,3072]{3,2,1,0:T(8,128)(2,1)S(1)} custom-call(bf16[2,2,384,3072]{3,2,1,0:T(8,128)(2,1)} %source), custom_call_target="tpu_custom_call" | custom-call | tf_op jit(solution)/shard_map/load/pallas_call | solution.py:30
  12.4 2.4 %collective-permute-done.came_0 = bf16[784,256]{1,0:T(8,128)(2,1)S(1)} collective-permute-done((bf16[784,256]{1,0:T(8,128)(2,1)S(1)}, bf16[784,256]{1,0:T(8,128)(2,1)S(1)}, u32[]{:S(2)}, u32[]{:S(2)}) %collective-permute-start) | collective-permute-done | bytes 401440 | tf_op jit(solution)/shard_map/ppermute | solution.py:339
  16.8 1.6 %collective-permute-start.5 = (bf16[2,2,192,256]{3,2,1,0:T(8,128)(2,1)S(1)}, bf16[2,2,192,256]{3,2,1,0:T(8,128)(2,1)S(1)}, u32[]{:S(2)}, u32[]{:S(2)}) collective-permute-start(bf16[2,2,192,256]{3,2,1,0:T(8,128)(2,1)S(1)} %get-tuple-element.56), channel_id=1, source_target_pairs={{0,16},{8,24},{16,0},{24,8},{1,17},{9,25},{17,1},{25,9},{2,18},{10... | collective-permute-start | bytes 1179656 | tf_op jit(solution)/shard_map/ppermute | solution.py:339
  19.0 7.9 %collective-permute-done.2.densities = bf16[2,2,384,256]{3,2,1,0:T(8,128)(2,1)S(1)} collective-permute-done((bf16[2,2,384,256]{3,2,1,0:T(8,128)(2,1)}, bf16[2,2,384,256]{3,2,1,0:T(8,128)(2,1)S(1)}, u32[]{:S(2)}, u32[]{:S(2)}) %collective-permute-start.2) | collective-permute-done | bytes 786464 | tf_op jit(solution)/shard_map/ppermute | solution.py:345
  29.3 1.8 %collective-permute-start.10 = (bf16[2,2,384,256]{3,2,1,0:T(8,128)(2,1)S(1)}, bf16[2,2,384,256]{3,2,1,0:T(8,128)(2,1)S(1)}, u32[]{:S(2)}, u32[]{:S(2)}) collective-permute-start(bf16[2,2,384,256]{3,2,1,0:T(8,128)(2,1)S(1)} %near.2.own.refs_0_), channel_id=1, source_target_pairs={{0,4},{1,5},{2,0},{3,1},{4,6},{5,7},{6,2},{7,3},{8,12},{9,13},{10,... | collective-permute-start | bytes 2359304 | tf_op jit(solution)/shard_map/ppermute | solution.py:345
  31.1 1.8 %product.3.before = f32[2,384,1024]{2,1,0:T(8,128)S(1)} custom-call(bf16[2,2,384,3072]{3,2,1,0:T(8,128)(2,1)S(1)} %load.1.screened, bf16[2,2,384,256]{3,2,1,0:T(8,128)(2,1)S(1)} %near.2.own.refs_0_, f32[1,384]{1,0:T(1,128)S(1)} %broadcast_in_dim.3.coulomb), custom_call_target="tpu_custom_call" | custom-call | tf_op jit(solution)/shard_map/product/pallas_call | solution.py:30
  32.9 4.2 %collective-permute-done.3.came_0 = bf16[784,256]{1,0:T(8,128)(2,1)S(1)} collective-permute-done((bf16[784,256]{1,0:T(8,128)(2,1)S(1)}, bf16[784,256]{1,0:T(8,128)(2,1)S(1)}, u32[]{:S(2)}, u32[]{:S(2)}) %collective-permute-start.3) | collective-permute-done | bytes 401440 | tf_op jit(solution)/shard_map/ppermute | solution.py:339
  40.0 6.2 %collective-permute-done.7.picked_0 = bf16[2,2,192,256]{3,2,1,0:T(8,128)(2,1)S(1)} collective-permute-done((bf16[2,2,192,256]{3,2,1,0:T(8,128)(2,1)S(1)}, bf16[2,2,192,256]{3,2,1,0:T(8,128)(2,1)S(1)}, u32[]{:S(2)}, u32[]{:S(2)}) %collective-permute-start.7) | collective-permute-done | bytes 393248 | tf_op jit(solution)/shard_map/ppermute | solution.py:339
  48.0 1.8 %collective-permute-start.9 = (bf16[2,2,384,256]{3,2,1,0:T(8,128)(2,1)S(1)}, bf16[2,2,384,256]{3,2,1,0:T(8,128)(2,1)S(1)}, u32[]{:S(2)}, u32[]{:S(2)}) collective-permute-start(bf16[2,2,384,256]{3,2,1,0:T(8,128)(2,1)S(1)} %near.3.refs_1_.own), channel_id=1, source_target_pairs={{0,2},{1,3},{2,6},{3,7},{4,0},{5,1},{6,4},{7,5},{8,10},{9,11},{10,... | collective-permute-start | bytes 2359304 | tf_op jit(solution)/shard_map/ppermute | solution.py:345
  49.7 1.5 %collective-permute-start.11 = (bf16[3,2,192,256]{3,2,1,0:T(8,128)(2,1)S(1)}, bf16[3,2,192,256]{3,2,1,0:T(8,128)(2,1)S(1)}, u32[]{:S(2)}, u32[]{:S(2)}) collective-permute-start(bf16[3,2,192,256]{3,2,1,0:T(8,128)(2,1)S(1)} %get-tuple-element.66), channel_id=1, source_target_pairs={{0,16},{8,24},{16,0},{24,8},{1,17},{9,25},{17,1},{25,9},{2,18},{10... | collective-permute-start | bytes 1769480 | tf_op jit(solution)/shard_map/ppermute | solution.py:339
  51.3 1.5 %collective-permute-start.12 = (bf16[2,2,192,256]{3,2,1,0:T(8,128)(2,1)S(1)}, bf16[2,2,192,256]{3,2,1,0:T(8,128)(2,1)S(1)}, u32[]{:S(2)}, u32[]{:S(2)}) collective-permute-start(bf16[2,2,192,256]{3,2,1,0:T(8,128)(2,1)S(1)} %get-tuple-element.67), channel_id=1, source_target_pairs={{0,8},{8,0},{16,24},{24,16},{1,9},{9,1},{17,25},{25,17},{2,10},{10... | collective-permute-start | bytes 1179656 | tf_op jit(solution)/shard_map/ppermute | solution.py:339
  52.8 3.0 %product.4.before = f32[2,384,1024]{2,1,0:T(8,128)S(1)} custom-call(bf16[2,2,384,3072]{3,2,1,0:T(8,128)(2,1)S(1)} %load.1.screened, bf16[2,2,384,256]{3,2,1,0:T(8,128)(2,1)S(1)} %collective-permute-done.10.own, bf16[2,2,384,256]{3,2,1,0:T(8,128)(2,1)S(1)} %collective-permute-done.14.pair, ...), custom_call_target="tpu_custom_call", output_to_operand_aliasing={{}: (3, {})} | custom-call | tf_op jit(solution)/shard_map/product/pallas_call | solution.py:30
  55.9 4.6 %product.5.before = f32[2,384,1024]{2,1,0:T(8,128)S(1)} custom-call(bf16[2,2,384,3072]{3,2,1,0:T(8,128)(2,1)S(1)} %load.1.screened, bf16[2,2,384,256]{3,2,1,0:T(8,128)(2,1)S(1)} %near.3.refs_1_.own, bf16[2,2,2,384,256]{4,3,2,1,0:T(8,128)(2,1)S(1)} %collective-permute-done.13.pairs, f32[2,384,1024]{2,1,0:T(8,128)S(1)} %product.4.before), custom_call_target="tpu_custom_call", output_to_operand_aliasing={{}: (3, {})} | custom-call | tf_op jit(solution)/shard_map/product/pallas_call | solution.py:30
  61.8 3.0 %collective-permute-done.11.rest_0 = bf16[3,2,192,256]{3,2,1,0:T(8,128)(2,1)S(1)} collective-permute-done((bf16[3,2,192,256]{3,2,1,0:T(8,128)(2,1)S(1)}, bf16[3,2,192,256]{3,2,1,0:T(8,128)(2,1)S(1)}, u32[]{:S(2)}, u32[]{:S(2)}) %collective-permute-start.11) | collective-permute-done | bytes 589856 | tf_op jit(solution)/shard_map/ppermute | solution.py:339
  64.8 3.6 %collective-permute-done.9.own = bf16[2,2,384,256]{3,2,1,0:T(8,128)(2,1)S(1)} collective-permute-done((bf16[2,2,384,256]{3,2,1,0:T(8,128)(2,1)S(1)}, bf16[2,2,384,256]{3,2,1,0:T(8,128)(2,1)S(1)}, u32[]{:S(2)}, u32[]{:S(2)}) %collective-permute-start.9) | collective-permute-done | bytes 786464 | tf_op jit(solution)/shard_map/ppermute | solution.py:345
  70.7 2.5 %last.3 = (f32[4,2,2,2,32,256]{5,4,3,2,1,0:T(8,128)S(1)}, bf16[4,2,2,2,32,256]{5,4,3,2,1,0:T(8,128)(2,1)S(1)}) custom-call(bf16[2,2,384,3072]{3,2,1,0:T(8,128)(2,1)S(1)} %load.1.screened, bf16[2,2,384,256]{3,2,1,0:T(8,128)(2,1)S(1)} %collective-permute-done.9.own, bf16[2,2,384,256]{3,2,1,0:T(8,128)(2,1)S(1)} %collective-permute-done.15.pair, ...), custom_call_target="tpu_custom_call" | custom-call | tf_op jit(solution)/shard_map/last/pallas_call | solution.py:30
  73.4 2.5 %last.2 = (f32[4,2,2,2,32,256]{5,4,3,2,1,0:T(8,128)S(1)}, bf16[4,2,2,2,32,256]{5,4,3,2,1,0:T(8,128)(2,1)S(1)}) custom-call(bf16[2,2,384,3072]{3,2,1,0:T(8,128)(2,1)S(1)} %load.1.screened, bf16[2,2,384,256]{3,2,1,0:T(8,128)(2,1)S(1)} %collective-permute-done.9.own, bf16[2,2,384,256]{3,2,1,0:T(8,128)(2,1)S(1)} %collective-permute-done.15.pair, ...), custom_call_target="tpu_custom_call" | custom-call | tf_op jit(solution)/shard_map/last/pallas_call | solution.py:30
  78.8 6.8 %collective-permute-done.20.came = bf16[2,2,2,2,32,256]{5,4,3,2,1,0:T(8,128)(2,1)S(1)} collective-permute-done((bf16[2,2,2,2,32,256]{5,4,3,2,1,0:T(8,128)(2,1)S(1)}, bf16[2,2,2,2,32,256]{5,4,3,2,1,0:T(8,128)(2,1)S(1)}, u32[]{:S(2)}, u32[]{:S(2)}) %collective-permute-start.20) | collective-permute-done | bytes 262176 | tf_op jit(solution)/shard_map/ppermute | solution.py:470
  85.7 1.5 %collective-permute-start.21 = (bf16[2,2,2,32,256]{4,3,2,1,0:T(8,128)(2,1)S(1)}, bf16[2,2,2,32,256]{4,3,2,1,0:T(8,128)(2,1)S(1)}, u32[]{:S(2)}, u32[]{:S(2)}) collective-permute-start(bf16[2,2,2,32,256]{4,3,2,1,0:T(8,128)(2,1)S(1)} %get-tuple-element.89), channel_id=1, source_target_pairs={{0,4},{1,5},{2,6},{3,7},{4,0},{5,1},{6,2},{7,3},{8,12},{9,13},{10,... | collective-permute-start | bytes 393224 | tf_op jit(solution)/shard_map/ppermute | solution.py:473
  87.3 6.0 %collective-permute-done.17.came = bf16[2,2,2,2,32,256]{5,4,3,2,1,0:T(8,128)(2,1)S(1)} collective-permute-done((bf16[2,2,2,2,32,256]{5,4,3,2,1,0:T(8,128)(2,1)S(1)}, bf16[2,2,2,2,32,256]{5,4,3,2,1,0:T(8,128)(2,1)S(1)}, u32[]{:S(2)}, u32[]{:S(2)}) %collective-permute-start.17) | collective-permute-done | bytes 262176 | tf_op jit(solution)/shard_map/ppermute | solution.py:470
  93.5 7.7 %collective-permute-done.18.refs_1_ = bf16[2,2,2,32,256]{4,3,2,1,0:T(8,128)(2,1)S(1)} collective-permute-done((bf16[2,2,2,32,256]{4,3,2,1,0:T(8,128)(2,1)S(1)}, bf16[2,2,2,32,256]{4,3,2,1,0:T(8,128)(2,1)S(1)}, u32[]{:S(2)}, u32[]{:S(2)}) %collective-permute-start.18) | collective-permute-done | bytes 131104 | tf_op jit(solution)/shard_map/ppermute | solution.py:473
  (47 shorter events, 19.3 us)
Async XLA Ops:
  2.5 12.3 %collective-permute-start = (bf16[784,256]{1,0:T(8,128)(2,1)S(1)}, bf16[784,256]{1,0:T(8,128)(2,1)S(1)}, u32[]{:S(2)}, u32[]{:S(2)}) collective-permute-start(bf16[784,256]{1,0:T(8,128)(2,1)S(1)} %get-tuple-element.52.packed_0), channel_id=1, source_target_pairs={{0,8},{8,0},{16,24},{24,16},{1,9},{9,1},{17,25},{25,17},{2,10},{10... | collective-permute-start | bytes 1204232 | tf_op jit(solution)/shard_map/ppermute | solution.py:339
  5.5 21.4 %copy-start.1 = (s32[1,2]{1,0:T(1,128)S(1)}, s32[1,2]{1,0:T(1,128)}, u32[]{:S(2)}) copy-start(s32[1,2]{1,0:T(1,128)} %rows.3) | copy-start | bytes 28
  5.5 10.8 %collective-permute-start.1 = (bf16[784,256]{1,0:T(8,128)(2,1)S(1)}, bf16[784,256]{1,0:T(8,128)(2,1)S(1)}, u32[]{:S(2)}, u32[]{:S(2)}) collective-permute-start(bf16[784,256]{1,0:T(8,128)(2,1)S(1)} %get-tuple-element.53.packed_1), channel_id=1, source_target_pairs={{0,16},{8,24},{16,0},{24,8},{1,17},{9,25},{17,1},{25,9},{2,18},{10... | collective-permute-start | bytes 1204232 | tf_op jit(solution)/shard_map/ppermute | solution.py:339
  7.0 19.8 %collective-permute-start.2 = (bf16[2,2,384,256]{3,2,1,0:T(8,128)(2,1)}, bf16[2,2,384,256]{3,2,1,0:T(8,128)(2,1)S(1)}, u32[]{:S(2)}, u32[]{:S(2)}) collective-permute-start(bf16[2,2,384,256]{3,2,1,0:T(8,128)(2,1)} %densities.1), channel_id=1, source_target_pairs={{0,2},{1,3},{2,6},{3,7},{4,0},{5,1},{6,4},{7,5},{8,10},{9,11},{10,... | collective-permute-start | bytes 2359304 | tf_op jit(solution)/shard_map/ppermute | solution.py:345
  16.8 14.3 %copy-start.2 = (f32[384]{0:T(512)S(1)}, f32[384]{0:T(512)}, u32[]{:S(2)}) copy-start(f32[384]{0:T(512)} %param.6) | copy-start | bytes 4612
  16.8 12.1 %collective-permute-start.5 = (bf16[2,2,192,256]{3,2,1,0:T(8,128)(2,1)S(1)}, bf16[2,2,192,256]{3,2,1,0:T(8,128)(2,1)S(1)}, u32[]{:S(2)}, u32[]{:S(2)}) collective-permute-start(bf16[2,2,192,256]{3,2,1,0:T(8,128)(2,1)S(1)} %get-tuple-element.56), channel_id=1, source_target_pairs={{0,16},{8,24},{16,0},{24,8},{1,17},{9,25},{17,1},{25,9},{2,18},{10... | collective-permute-start | bytes 1179656 | tf_op jit(solution)/shard_map/ppermute | solution.py:339
  18.4 10.5 %collective-permute-start.6 = (bf16[2,2,192,256]{3,2,1,0:T(8,128)(2,1)S(1)}, bf16[2,2,192,256]{3,2,1,0:T(8,128)(2,1)S(1)}, u32[]{:S(2)}, u32[]{:S(2)}) collective-permute-start(bf16[2,2,192,256]{3,2,1,0:T(8,128)(2,1)S(1)} %get-tuple-element.57), channel_id=1, source_target_pairs={{0,8},{8,0},{16,24},{24,16},{1,9},{9,1},{17,25},{25,17},{2,10},{10... | collective-permute-start | bytes 1179656 | tf_op jit(solution)/shard_map/ppermute | solution.py:339
  27.4 9.6 %collective-permute-start.3 = (bf16[784,256]{1,0:T(8,128)(2,1)S(1)}, bf16[784,256]{1,0:T(8,128)(2,1)S(1)}, u32[]{:S(2)}, u32[]{:S(2)}) collective-permute-start(bf16[784,256]{1,0:T(8,128)(2,1)S(1)} %get-tuple-element.50.packed_0), channel_id=1, source_target_pairs={{0,8},{8,0},{16,24},{24,16},{1,9},{9,1},{17,25},{25,17},{2,10},{10... | collective-permute-start | bytes 1204232 | tf_op jit(solution)/shard_map/ppermute | solution.py:339
  28.1 9.3 %collective-permute-start.4 = (bf16[784,256]{1,0:T(8,128)(2,1)S(1)}, bf16[784,256]{1,0:T(8,128)(2,1)S(1)}, u32[]{:S(2)}, u32[]{:S(2)}) collective-permute-start(bf16[784,256]{1,0:T(8,128)(2,1)S(1)} %get-tuple-element.51.packed_1), channel_id=1, source_target_pairs={{0,16},{8,24},{16,0},{24,8},{1,17},{9,25},{17,1},{25,9},{2,18},{10... | collective-permute-start | bytes 1204232 | tf_op jit(solution)/shard_map/ppermute | solution.py:339
  29.3 18.0 %collective-permute-start.10 = (bf16[2,2,384,256]{3,2,1,0:T(8,128)(2,1)S(1)}, bf16[2,2,384,256]{3,2,1,0:T(8,128)(2,1)S(1)}, u32[]{:S(2)}, u32[]{:S(2)}) collective-permute-start(bf16[2,2,384,256]{3,2,1,0:T(8,128)(2,1)S(1)} %near.2.own.refs_0_), channel_id=1, source_target_pairs={{0,4},{1,5},{2,0},{3,1},{4,6},{5,7},{6,2},{7,3},{8,12},{9,13},{10,... | collective-permute-start | bytes 2359304 | tf_op jit(solution)/shard_map/ppermute | solution.py:345
  37.9 8.3 %collective-permute-start.7 = (bf16[2,2,192,256]{3,2,1,0:T(8,128)(2,1)S(1)}, bf16[2,2,192,256]{3,2,1,0:T(8,128)(2,1)S(1)}, u32[]{:S(2)}, u32[]{:S(2)}) collective-permute-start(bf16[2,2,192,256]{3,2,1,0:T(8,128)(2,1)S(1)} %get-tuple-element.64), channel_id=1, source_target_pairs={{0,16},{8,24},{16,0},{24,8},{1,17},{9,25},{17,1},{25,9},{2,18},{10... | collective-permute-start | bytes 1179656 | tf_op jit(solution)/shard_map/ppermute | solution.py:339
  38.7 8.2 %collective-permute-start.8 = (bf16[2,2,192,256]{3,2,1,0:T(8,128)(2,1)S(1)}, bf16[2,2,192,256]{3,2,1,0:T(8,128)(2,1)S(1)}, u32[]{:S(2)}, u32[]{:S(2)}) collective-permute-start(bf16[2,2,192,256]{3,2,1,0:T(8,128)(2,1)S(1)} %get-tuple-element.65), channel_id=1, source_target_pairs={{0,8},{8,0},{16,24},{24,16},{1,9},{9,1},{17,25},{25,17},{2,10},{10... | collective-permute-start | bytes 1179656 | tf_op jit(solution)/shard_map/ppermute | solution.py:339
  47.4 8.4 %collective-permute-start.13 = (bf16[2,2,2,384,256]{4,3,2,1,0:T(8,128)(2,1)S(1)}, bf16[2,2,2,384,256]{4,3,2,1,0:T(8,128)(2,1)S(1)}, u32[]{:S(2)}, u32[]{:S(2)}) collective-permute-start(bf16[2,2,2,384,256]{4,3,2,1,0:T(8,128)(2,1)S(1)} %stack.1), channel_id=1, source_target_pairs={{0,1},{1,0},{2,3},{3,2},{4,5},{5,4},{6,7},{7,6},{8,9},{9,8},{10,11... | collective-permute-start | bytes 4718600 | tf_op jit(solution)/shard_map/ppermute | solution.py:342
  47.5 5.3 %collective-permute-start.14 = (bf16[2,2,384,256]{3,2,1,0:T(8,128)(2,1)S(1)}, bf16[2,2,384,256]{3,2,1,0:T(8,128)(2,1)S(1)}, u32[]{:S(2)}, u32[]{:S(2)}) collective-permute-start(bf16[2,2,384,256]{3,2,1,0:T(8,128)(2,1)S(1)} %collective-permute-done.10.own), channel_id=1, source_target_pairs={{0,1},{1,0},{2,3},{3,2},{4,5},{5,4},{6,7},{7,6},{8,9},{9,8},{10,11... | collective-permute-start | bytes 2359304 | tf_op jit(solution)/shard_map/ppermute | solution.py:342
  48.0 20.4 %collective-permute-start.9 = (bf16[2,2,384,256]{3,2,1,0:T(8,128)(2,1)S(1)}, bf16[2,2,384,256]{3,2,1,0:T(8,128)(2,1)S(1)}, u32[]{:S(2)}, u32[]{:S(2)}) collective-permute-start(bf16[2,2,384,256]{3,2,1,0:T(8,128)(2,1)S(1)} %near.3.refs_1_.own), channel_id=1, source_target_pairs={{0,2},{1,3},{2,6},{3,7},{4,0},{5,1},{6,4},{7,5},{8,10},{9,11},{10,... | collective-permute-start | bytes 2359304 | tf_op jit(solution)/shard_map/ppermute | solution.py:345
  49.7 15.0 %collective-permute-start.11 = (bf16[3,2,192,256]{3,2,1,0:T(8,128)(2,1)S(1)}, bf16[3,2,192,256]{3,2,1,0:T(8,128)(2,1)S(1)}, u32[]{:S(2)}, u32[]{:S(2)}) collective-permute-start(bf16[3,2,192,256]{3,2,1,0:T(8,128)(2,1)S(1)} %get-tuple-element.66), channel_id=1, source_target_pairs={{0,16},{8,24},{16,0},{24,8},{1,17},{9,25},{17,1},{25,9},{2,18},{10... | collective-permute-start | bytes 1769480 | tf_op jit(solution)/shard_map/ppermute | solution.py:339
  51.3 10.5 %collective-permute-start.12 = (bf16[2,2,192,256]{3,2,1,0:T(8,128)(2,1)S(1)}, bf16[2,2,192,256]{3,2,1,0:T(8,128)(2,1)S(1)}, u32[]{:S(2)}, u32[]{:S(2)}) collective-permute-start(bf16[2,2,192,256]{3,2,1,0:T(8,128)(2,1)S(1)} %get-tuple-element.67), channel_id=1, source_target_pairs={{0,8},{8,0},{16,24},{24,16},{1,9},{9,1},{17,25},{25,17},{2,10},{10... | collective-permute-start | bytes 1179656 | tf_op jit(solution)/shard_map/ppermute | solution.py:339
  68.4 2.3 %collective-permute-start.15 = (bf16[2,2,384,256]{3,2,1,0:T(8,128)(2,1)S(1)}, bf16[2,2,384,256]{3,2,1,0:T(8,128)(2,1)S(1)}, u32[]{:S(2)}, u32[]{:S(2)}) collective-permute-start(bf16[2,2,384,256]{3,2,1,0:T(8,128)(2,1)S(1)} %collective-permute-done.9.own), channel_id=1, source_target_pairs={{0,1},{1,0},{2,3},{3,2},{4,5},{5,4},{6,7},{7,6},{8,9},{9,8},{10,11... | collective-permute-start | bytes 2359304 | tf_op jit(solution)/shard_map/ppermute | solution.py:342
  73.2 3.1 %collective-permute-start.19 = (bf16[4,2,2,2,32,256]{5,4,3,2,1,0:T(8,128)(2,1)S(1)}, bf16[4,2,2,2,32,256]{5,4,3,2,1,0:T(8,128)(2,1)S(1)}, u32[]{:S(2)}, u32[]{:S(2)}) collective-permute-start(bf16[4,2,2,2,32,256]{5,4,3,2,1,0:T(8,128)(2,1)S(1)} %get-tuple-element.84), channel_id=1, source_target_pairs={{0,1},{1,0},{2,3},{3,2},{4,5},{5,4},{6,7},{7,6},{8,9},{9,8},{10,11... | collective-permute-start | bytes 1572872 | tf_op jit(solution)/shard_map/ppermute | solution.py:342
  75.9 2.0 %collective-permute-start.16 = (bf16[4,2,2,2,32,256]{5,4,3,2,1,0:T(8,128)(2,1)S(1)}, bf16[4,2,2,2,32,256]{5,4,3,2,1,0:T(8,128)(2,1)S(1)}, u32[]{:S(2)}, u32[]{:S(2)}) collective-permute-start(bf16[4,2,2,2,32,256]{5,4,3,2,1,0:T(8,128)(2,1)S(1)} %get-tuple-element.77), channel_id=1, source_target_pairs={{0,1},{1,0},{2,3},{3,2},{4,5},{5,4},{6,7},{7,6},{8,9},{9,8},{10,11... | collective-permute-start | bytes 1572872 | tf_op jit(solution)/shard_map/ppermute | solution.py:342
  76.4 9.2 %collective-permute-start.20 = (bf16[2,2,2,2,32,256]{5,4,3,2,1,0:T(8,128)(2,1)S(1)}, bf16[2,2,2,2,32,256]{5,4,3,2,1,0:T(8,128)(2,1)S(1)}, u32[]{:S(2)}, u32[]{:S(2)}) collective-permute-start(bf16[2,2,2,2,32,256]{5,4,3,2,1,0:T(8,128)(2,1)S(1)} %get-tuple-element.87), channel_id=1, source_target_pairs={{0,2},{1,3},{2,0},{3,1},{4,6},{5,7},{6,4},{7,5},{8,10},{9,11},{10,... | collective-permute-start | bytes 786440 | tf_op jit(solution)/shard_map/ppermute | solution.py:470
  78.0 15.3 %collective-permute-start.17 = (bf16[2,2,2,2,32,256]{5,4,3,2,1,0:T(8,128)(2,1)S(1)}, bf16[2,2,2,2,32,256]{5,4,3,2,1,0:T(8,128)(2,1)S(1)}, u32[]{:S(2)}, u32[]{:S(2)}) collective-permute-start(bf16[2,2,2,2,32,256]{5,4,3,2,1,0:T(8,128)(2,1)S(1)} %get-tuple-element.80), channel_id=1, source_target_pairs={{0,2},{1,3},{2,0},{3,1},{4,6},{5,7},{6,4},{7,5},{8,10},{9,11},{10,... | collective-permute-start | bytes 786440 | tf_op jit(solution)/shard_map/ppermute | solution.py:470
  85.7 7.8 %collective-permute-start.21 = (bf16[2,2,2,32,256]{4,3,2,1,0:T(8,128)(2,1)S(1)}, bf16[2,2,2,32,256]{4,3,2,1,0:T(8,128)(2,1)S(1)}, u32[]{:S(2)}, u32[]{:S(2)}) collective-permute-start(bf16[2,2,2,32,256]{4,3,2,1,0:T(8,128)(2,1)S(1)} %get-tuple-element.89), channel_id=1, source_target_pairs={{0,4},{1,5},{2,6},{3,7},{4,0},{5,1},{6,2},{7,3},{8,12},{9,13},{10,... | collective-permute-start | bytes 393224 | tf_op jit(solution)/shard_map/ppermute | solution.py:473
  93.3 7.9 %collective-permute-start.18 = (bf16[2,2,2,32,256]{4,3,2,1,0:T(8,128)(2,1)S(1)}, bf16[2,2,2,32,256]{4,3,2,1,0:T(8,128)(2,1)S(1)}, u32[]{:S(2)}, u32[]{:S(2)}) collective-permute-start(bf16[2,2,2,32,256]{4,3,2,1,0:T(8,128)(2,1)S(1)} %get-tuple-element.82), channel_id=1, source_target_pairs={{0,4},{1,5},{2,6},{3,7},{4,0},{5,1},{6,2},{7,3},{8,12},{9,13},{10,... | collective-permute-start | bytes 393224 | tf_op jit(solution)/shard_map/ppermute | solution.py:473
  (1 other events, 0.7 us)

commit v3 on v2

--- a/solution.py
+++ b/solution.py
@@ -302,11 +302,11 @@
                 give[:, s, which, part] = jnp.where(first, block[:, 1], block[:, 0]).astype(BF16)
 
 
-def split_kernel(keep, came, own, cross, sends):
+def split_kernel(near, far, keep, came, own, cross, sends):
     z = lax.axis_index("ga") // 2
     own[...] = keep[z] + came[z].astype(F32)
-    cross[...] = keep[z ^ 2] + came[z ^ 2].astype(F32)
-    for i, at in enumerate((z ^ 1, z ^ 3)):
+    cross[...] = keep[z ^ far] + came[z ^ far].astype(F32)
+    for i, at in enumerate((z ^ near, z ^ 3)):
         sends[i] = (keep[at] + came[at].astype(F32)).astype(BF16)
 
 
@@ -454,9 +454,10 @@
         )
         swaps.append((keep, other_core(give)))
     groups = []
-    for keep, came_j in swaps:
+    for j, (keep, came_j) in enumerate(swaps):
+        near_z, far_z = ((1, 2), (2, 1))[j % 2]
         own, cross, sends = run(
-            split_kernel,
+            functools.partial(split_kernel, near_z, far_z),
             [shape(part, F32), shape(part, F32), shape((2, *part), BF16)],
             keep,
             came_j,
@@ -467,10 +468,10 @@
             [shape(part, F32), shape(part, BF16)],
             own,
             cross,
-            lax.ppermute(sends, "ga", [(i, i ^ 2) for i in range(n_ga)]),
+            lax.ppermute(sends, "ga", [(i, i ^ (2 * near_z)) for i in range(n_ga)]),
             name="merge",
         )
-        groups += [own, lax.ppermute(sends, "ga", [(i, i ^ 4) for i in range(n_ga)])]
+        groups += [own, lax.ppermute(sends, "ga", [(i, i ^ (2 * far_z)) for i in range(n_ga)])]
     result = shape((count, transfers, 2, t // n_ga, t), F32)
     return tuple(
         run(

time: 102 us -> 102 us (level)
  waiting for transfers between devices: 53.1 us -> 50.2 us
  starting transfers between devices: 22.6 us -> 24.9 us
    ppermute x4, waiting for transfers between devices: 20.5 us -> 17.8 us  [the longest x2 11.4 us: quick(): lax.ppermute(sends, 'ga', [(i, i ^ 2 * near_z) for i in range(n_ga)])]
    ppermute x4, starting transfers between devices: 3.43 us -> 5.78 us  [the longest x2 3.33 us: quick(): lax.ppermute(sends, 'ga', [(i, i ^ 2 * near_z) for i in range(n_ga)])]
  transfers between devices with their start and end apart: 22 -> 22, of which waited for: 15 -> 16; matrix products, arithmetic and copies ran while one was open for 0% -> 0% of each run, Pallas kernels for 20% -> 20%
where the time goes in v3:
time: 102 us; the launch traced here: 101 us
  waiting for transfers between devices  50.2 us (49%)
  starting transfers between devices  24.9 us (24%)
  Pallas kernels  24.8 us (24%)
    pallas_call x20, Pallas kernels, run(): pl.pallas_call(body, in_specs=specs or [VMEM] * len(args), out_specs=[VME...  24.8 us
    ppermute x10, waiting for transfers between devices, across(): return lax.ppermute(x, 'kp', [(i, i ^ bit) for i in range(n_kp)])  19.5 us
    ppermute x10, starting transfers between devices, across(): return lax.ppermute(x, 'kp', [(i, i ^ bit) for i in range(n_kp)])  12.8 us
    ppermute x3, waiting for transfers between devices, along(): lax.ppermute(x, 'ga', [(i, 2 * chips_on[i // 2] + i % 2) for i in range(n...  11.5 us
    ppermute x2, waiting for transfers between devices, quick(): lax.ppermute(sends, 'ga', [(i, i ^ 2 * near_z) for i in range(n_ga)])  11.4 us
    ppermute x2, waiting for transfers between devices, quick(): lax.ppermute(sends, 'ga', [(i, i ^ 2 * far_z) for i in range(n_ga)])  6.35 us
    ppermute x3, starting transfers between devices, along(): lax.ppermute(x, 'ga', [(i, 2 * chips_on[i // 2] + i % 2) for i in range(n...  5.13 us
    ppermute x2, starting transfers between devices, quick(): lax.ppermute(sends, 'ga', [(i, i ^ 2 * near_z) for i in range(n_ga)])  3.33 us
  transfers between devices with their start and end apart: 22, of which 16 were waited for; matrix products, arithmetic and copies ran while one was open for 0% of the time, Pallas kernels for 20%

profile of v3, /device:TPU:0, one launch (start us, length us, event | category | flops | bytes accessed | tf_op | source)
XLA Modules:
  0.0 101.4 jit_solution(2642818512252951164)
XLA Ops:
  2.5 3.0 %collective-permute-start = (bf16[784,256]{1,0:T(8,128)(2,1)S(1)}, bf16[784,256]{1,0:T(8,128)(2,1)S(1)}, u32[]{:S(2)}, u32[]{:S(2)}) collective-permute-start(bf16[784,256]{1,0:T(8,128)(2,1)S(1)} %get-tuple-element.52.packed_0), channel_id=1, source_target_pairs={{0,8},{8,0},{16,24},{24,16},{1,9},{9,1},{17,25},{25,17},{2,10},{10... | collective-permute-start | bytes 1204232 | tf_op jit(solution)/shard_map/ppermute | solution.py:339
  5.5 1.5 %collective-permute-start.1 = (bf16[784,256]{1,0:T(8,128)(2,1)S(1)}, bf16[784,256]{1,0:T(8,128)(2,1)S(1)}, u32[]{:S(2)}, u32[]{:S(2)}) collective-permute-start(bf16[784,256]{1,0:T(8,128)(2,1)S(1)} %get-tuple-element.53.packed_1), channel_id=1, source_target_pairs={{0,16},{8,24},{16,0},{24,8},{1,17},{9,25},{17,1},{25,9},{2,18},{10... | collective-permute-start | bytes 1204232 | tf_op jit(solution)/shard_map/ppermute | solution.py:339
  7.0 1.6 %collective-permute-start.2 = (bf16[2,2,384,256]{3,2,1,0:T(8,128)(2,1)}, bf16[2,2,384,256]{3,2,1,0:T(8,128)(2,1)S(1)}, u32[]{:S(2)}, u32[]{:S(2)}) collective-permute-start(bf16[2,2,384,256]{3,2,1,0:T(8,128)(2,1)} %densities.1), channel_id=1, source_target_pairs={{0,2},{1,3},{2,6},{3,7},{4,0},{5,1},{6,4},{7,5},{8,10},{9,11},{10,... | collective-permute-start | bytes 2359304 | tf_op jit(solution)/shard_map/ppermute | solution.py:345
  8.6 3.8 %load.1.screened = bf16[2,2,384,3072]{3,2,1,0:T(8,128)(2,1)S(1)} custom-call(bf16[2,2,384,3072]{3,2,1,0:T(8,128)(2,1)} %source), custom_call_target="tpu_custom_call" | custom-call | tf_op jit(solution)/shard_map/load/pallas_call | solution.py:30
  12.4 2.4 %collective-permute-done.came_0 = bf16[784,256]{1,0:T(8,128)(2,1)S(1)} collective-permute-done((bf16[784,256]{1,0:T(8,128)(2,1)S(1)}, bf16[784,256]{1,0:T(8,128)(2,1)S(1)}, u32[]{:S(2)}, u32[]{:S(2)}) %collective-permute-start) | collective-permute-done | bytes 401440 | tf_op jit(solution)/shard_map/ppermute | solution.py:339
  16.8 1.6 %collective-permute-start.5 = (bf16[2,2,192,256]{3,2,1,0:T(8,128)(2,1)S(1)}, bf16[2,2,192,256]{3,2,1,0:T(8,128)(2,1)S(1)}, u32[]{:S(2)}, u32[]{:S(2)}) collective-permute-start(bf16[2,2,192,256]{3,2,1,0:T(8,128)(2,1)S(1)} %get-tuple-element.56), channel_id=1, source_target_pairs={{0,16},{8,24},{16,0},{24,8},{1,17},{9,25},{17,1},{25,9},{2,18},{10... | collective-permute-start | bytes 1179656 | tf_op jit(solution)/shard_map/ppermute | solution.py:339
  19.0 7.9 %collective-permute-done.2.densities = bf16[2,2,384,256]{3,2,1,0:T(8,128)(2,1)S(1)} collective-permute-done((bf16[2,2,384,256]{3,2,1,0:T(8,128)(2,1)}, bf16[2,2,384,256]{3,2,1,0:T(8,128)(2,1)S(1)}, u32[]{:S(2)}, u32[]{:S(2)}) %collective-permute-start.2) | collective-permute-done | bytes 786464 | tf_op jit(solution)/shard_map/ppermute | solution.py:345
  29.3 1.8 %collective-permute-start.10 = (bf16[2,2,384,256]{3,2,1,0:T(8,128)(2,1)S(1)}, bf16[2,2,384,256]{3,2,1,0:T(8,128)(2,1)S(1)}, u32[]{:S(2)}, u32[]{:S(2)}) collective-permute-start(bf16[2,2,384,256]{3,2,1,0:T(8,128)(2,1)S(1)} %near.2.own.refs_0_), channel_id=1, source_target_pairs={{0,4},{1,5},{2,0},{3,1},{4,6},{5,7},{6,2},{7,3},{8,12},{9,13},{10,... | collective-permute-start | bytes 2359304 | tf_op jit(solution)/shard_map/ppermute | solution.py:345
  31.1 1.8 %product.3.before = f32[2,384,1024]{2,1,0:T(8,128)S(1)} custom-call(bf16[2,2,384,3072]{3,2,1,0:T(8,128)(2,1)S(1)} %load.1.screened, bf16[2,2,384,256]{3,2,1,0:T(8,128)(2,1)S(1)} %near.2.own.refs_0_, f32[1,384]{1,0:T(1,128)S(1)} %broadcast_in_dim.3.coulomb), custom_call_target="tpu_custom_call" | custom-call | tf_op jit(solution)/shard_map/product/pallas_call | solution.py:30
  32.9 4.2 %collective-permute-done.3.came_0 = bf16[784,256]{1,0:T(8,128)(2,1)S(1)} collective-permute-done((bf16[784,256]{1,0:T(8,128)(2,1)S(1)}, bf16[784,256]{1,0:T(8,128)(2,1)S(1)}, u32[]{:S(2)}, u32[]{:S(2)}) %collective-permute-start.3) | collective-permute-done | bytes 401440 | tf_op jit(solution)/shard_map/ppermute | solution.py:339
  40.0 6.2 %collective-permute-done.7.picked_0 = bf16[2,2,192,256]{3,2,1,0:T(8,128)(2,1)S(1)} collective-permute-done((bf16[2,2,192,256]{3,2,1,0:T(8,128)(2,1)S(1)}, bf16[2,2,192,256]{3,2,1,0:T(8,128)(2,1)S(1)}, u32[]{:S(2)}, u32[]{:S(2)}) %collective-permute-start.7) | collective-permute-done | bytes 393248 | tf_op jit(solution)/shard_map/ppermute | solution.py:339
  48.0 1.8 %collective-permute-start.9 = (bf16[2,2,384,256]{3,2,1,0:T(8,128)(2,1)S(1)}, bf16[2,2,384,256]{3,2,1,0:T(8,128)(2,1)S(1)}, u32[]{:S(2)}, u32[]{:S(2)}) collective-permute-start(bf16[2,2,384,256]{3,2,1,0:T(8,128)(2,1)S(1)} %near.3.refs_1_.own), channel_id=1, source_target_pairs={{0,2},{1,3},{2,6},{3,7},{4,0},{5,1},{6,4},{7,5},{8,10},{9,11},{10,... | collective-permute-start | bytes 2359304 | tf_op jit(solution)/shard_map/ppermute | solution.py:345
  51.3 1.5 %collective-permute-start.12 = (bf16[2,2,192,256]{3,2,1,0:T(8,128)(2,1)S(1)}, bf16[2,2,192,256]{3,2,1,0:T(8,128)(2,1)S(1)}, u32[]{:S(2)}, u32[]{:S(2)}) collective-permute-start(bf16[2,2,192,256]{3,2,1,0:T(8,128)(2,1)S(1)} %get-tuple-element.67), channel_id=1, source_target_pairs={{0,8},{8,0},{16,24},{24,16},{1,9},{9,1},{17,25},{25,17},{2,10},{10... | collective-permute-start | bytes 1179656 | tf_op jit(solution)/shard_map/ppermute | solution.py:339
  52.8 3.0 %product.4.before = f32[2,384,1024]{2,1,0:T(8,128)S(1)} custom-call(bf16[2,2,384,3072]{3,2,1,0:T(8,128)(2,1)S(1)} %load.1.screened, bf16[2,2,384,256]{3,2,1,0:T(8,128)(2,1)S(1)} %collective-permute-done.10.own, bf16[2,2,384,256]{3,2,1,0:T(8,128)(2,1)S(1)} %collective-permute-done.14.pair, ...), custom_call_target="tpu_custom_call", output_to_operand_aliasing={{}: (3, {})} | custom-call | tf_op jit(solution)/shard_map/product/pallas_call | solution.py:30
  55.8 4.6 %product.5.before = f32[2,384,1024]{2,1,0:T(8,128)S(1)} custom-call(bf16[2,2,384,3072]{3,2,1,0:T(8,128)(2,1)S(1)} %load.1.screened, bf16[2,2,384,256]{3,2,1,0:T(8,128)(2,1)S(1)} %near.3.refs_1_.own, bf16[2,2,2,384,256]{4,3,2,1,0:T(8,128)(2,1)S(1)} %collective-permute-done.13.pairs, f32[2,384,1024]{2,1,0:T(8,128)S(1)} %product.4.before), custom_call_target="tpu_custom_call", output_to_operand_aliasing={{}: (3, {})} | custom-call | tf_op jit(solution)/shard_map/product/pallas_call | solution.py:30
  61.8 3.0 %collective-permute-done.11.rest_0 = bf16[3,2,192,256]{3,2,1,0:T(8,128)(2,1)S(1)} collective-permute-done((bf16[3,2,192,256]{3,2,1,0:T(8,128)(2,1)S(1)}, bf16[3,2,192,256]{3,2,1,0:T(8,128)(2,1)S(1)}, u32[]{:S(2)}, u32[]{:S(2)}) %collective-permute-start.11) | collective-permute-done | bytes 589856 | tf_op jit(solution)/shard_map/ppermute | solution.py:339
  64.8 3.6 %collective-permute-done.9.own = bf16[2,2,384,256]{3,2,1,0:T(8,128)(2,1)S(1)} collective-permute-done((bf16[2,2,384,256]{3,2,1,0:T(8,128)(2,1)S(1)}, bf16[2,2,384,256]{3,2,1,0:T(8,128)(2,1)S(1)}, u32[]{:S(2)}, u32[]{:S(2)}) %collective-permute-start.9) | collective-permute-done | bytes 786464 | tf_op jit(solution)/shard_map/ppermute | solution.py:345
  70.7 2.5 %last.3 = (f32[4,2,2,2,32,256]{5,4,3,2,1,0:T(8,128)S(1)}, bf16[4,2,2,2,32,256]{5,4,3,2,1,0:T(8,128)(2,1)S(1)}) custom-call(bf16[2,2,384,3072]{3,2,1,0:T(8,128)(2,1)S(1)} %load.1.screened, bf16[2,2,384,256]{3,2,1,0:T(8,128)(2,1)S(1)} %collective-permute-done.9.own, bf16[2,2,384,256]{3,2,1,0:T(8,128)(2,1)S(1)} %collective-permute-done.15.pair, ...), custom_call_target="tpu_custom_call" | custom-call | tf_op jit(solution)/shard_map/last/pallas_call | solution.py:30
  73.4 2.5 %last.2 = (f32[4,2,2,2,32,256]{5,4,3,2,1,0:T(8,128)S(1)}, bf16[4,2,2,2,32,256]{5,4,3,2,1,0:T(8,128)(2,1)S(1)}) custom-call(bf16[2,2,384,3072]{3,2,1,0:T(8,128)(2,1)S(1)} %load.1.screened, bf16[2,2,384,256]{3,2,1,0:T(8,128)(2,1)S(1)} %collective-permute-done.9.own, bf16[2,2,384,256]{3,2,1,0:T(8,128)(2,1)S(1)} %collective-permute-done.15.pair, ...), custom_call_target="tpu_custom_call" | custom-call | tf_op jit(solution)/shard_map/last/pallas_call | solution.py:30
  78.0 2.2 %collective-permute-start.17 = (bf16[2,2,2,2,32,256]{5,4,3,2,1,0:T(8,128)(2,1)S(1)}, bf16[2,2,2,2,32,256]{5,4,3,2,1,0:T(8,128)(2,1)S(1)}, u32[]{:S(2)}, u32[]{:S(2)}) collective-permute-start(bf16[2,2,2,2,32,256]{5,4,3,2,1,0:T(8,128)(2,1)S(1)} %get-tuple-element.80), channel_id=1, source_target_pairs={{0,2},{1,3},{2,0},{3,1},{4,6},{5,7},{6,4},{7,5},{8,10},{9,11},{10,... | collective-permute-start | bytes 786440 | tf_op jit(solution)/shard_map/ppermute | solution.py:471
  80.2 11.2 %collective-permute-done.20.came = bf16[2,2,2,2,32,256]{5,4,3,2,1,0:T(8,128)(2,1)S(1)} collective-permute-done((bf16[2,2,2,2,32,256]{5,4,3,2,1,0:T(8,128)(2,1)S(1)}, bf16[2,2,2,2,32,256]{5,4,3,2,1,0:T(8,128)(2,1)S(1)}, u32[]{:S(2)}, u32[]{:S(2)}) %collective-permute-start.20) | collective-permute-done | bytes 262176 | tf_op jit(solution)/shard_map/ppermute | solution.py:471
  91.8 2.4 %collective-permute-start.18 = (bf16[2,2,2,32,256]{4,3,2,1,0:T(8,128)(2,1)S(1)}, bf16[2,2,2,32,256]{4,3,2,1,0:T(8,128)(2,1)S(1)}, u32[]{:S(2)}, u32[]{:S(2)}) collective-permute-start(bf16[2,2,2,32,256]{4,3,2,1,0:T(8,128)(2,1)S(1)} %get-tuple-element.82), channel_id=1, source_target_pairs={{0,4},{1,5},{2,6},{3,7},{4,0},{5,1},{6,2},{7,3},{8,12},{9,13},{10,... | collective-permute-start | bytes 393224 | tf_op jit(solution)/shard_map/ppermute | solution.py:474
  94.2 4.7 %collective-permute-done.21.refs_3_ = bf16[2,2,2,32,256]{4,3,2,1,0:T(8,128)(2,1)S(1)} collective-permute-done((bf16[2,2,2,32,256]{4,3,2,1,0:T(8,128)(2,1)S(1)}, bf16[2,2,2,32,256]{4,3,2,1,0:T(8,128)(2,1)S(1)}, u32[]{:S(2)}, u32[]{:S(2)}) %collective-permute-start.21) | collective-permute-done | bytes 131104 | tf_op jit(solution)/shard_map/ppermute | solution.py:474
  98.9 1.7 %collective-permute-done.18.refs_1_ = bf16[2,2,2,32,256]{4,3,2,1,0:T(8,128)(2,1)S(1)} collective-permute-done((bf16[2,2,2,32,256]{4,3,2,1,0:T(8,128)(2,1)S(1)}, bf16[2,2,2,32,256]{4,3,2,1,0:T(8,128)(2,1)S(1)}, u32[]{:S(2)}, u32[]{:S(2)}) %collective-permute-start.18) | collective-permute-done | bytes 131104 | tf_op jit(solution)/shard_map/ppermute | solution.py:474
  (47 shorter events, 20.1 us)
Async XLA Ops:
  2.5 12.3 %collective-permute-start = (bf16[784,256]{1,0:T(8,128)(2,1)S(1)}, bf16[784,256]{1,0:T(8,128)(2,1)S(1)}, u32[]{:S(2)}, u32[]{:S(2)}) collective-permute-start(bf16[784,256]{1,0:T(8,128)(2,1)S(1)} %get-tuple-element.52.packed_0), channel_id=1, source_target_pairs={{0,8},{8,0},{16,24},{24,16},{1,9},{9,1},{17,25},{25,17},{2,10},{10... | collective-permute-start | bytes 1204232 | tf_op jit(solution)/shard_map/ppermute | solution.py:339
  5.5 21.4 %copy-start.1 = (s32[1,2]{1,0:T(1,128)S(1)}, s32[1,2]{1,0:T(1,128)}, u32[]{:S(2)}) copy-start(s32[1,2]{1,0:T(1,128)} %rows.3) | copy-start | bytes 28
  5.5 10.8 %collective-permute-start.1 = (bf16[784,256]{1,0:T(8,128)(2,1)S(1)}, bf16[784,256]{1,0:T(8,128)(2,1)S(1)}, u32[]{:S(2)}, u32[]{:S(2)}) collective-permute-start(bf16[784,256]{1,0:T(8,128)(2,1)S(1)} %get-tuple-element.53.packed_1), channel_id=1, source_target_pairs={{0,16},{8,24},{16,0},{24,8},{1,17},{9,25},{17,1},{25,9},{2,18},{10... | collective-permute-start | bytes 1204232 | tf_op jit(solution)/shard_map/ppermute | solution.py:339
  7.0 19.8 %collective-permute-start.2 = (bf16[2,2,384,256]{3,2,1,0:T(8,128)(2,1)}, bf16[2,2,384,256]{3,2,1,0:T(8,128)(2,1)S(1)}, u32[]{:S(2)}, u32[]{:S(2)}) collective-permute-start(bf16[2,2,384,256]{3,2,1,0:T(8,128)(2,1)} %densities.1), channel_id=1, source_target_pairs={{0,2},{1,3},{2,6},{3,7},{4,0},{5,1},{6,4},{7,5},{8,10},{9,11},{10,... | collective-permute-start | bytes 2359304 | tf_op jit(solution)/shard_map/ppermute | solution.py:345
  16.8 14.3 %copy-start.2 = (f32[384]{0:T(512)S(1)}, f32[384]{0:T(512)}, u32[]{:S(2)}) copy-start(f32[384]{0:T(512)} %param.6) | copy-start | bytes 4612
  16.8 12.1 %collective-permute-start.5 = (bf16[2,2,192,256]{3,2,1,0:T(8,128)(2,1)S(1)}, bf16[2,2,192,256]{3,2,1,0:T(8,128)(2,1)S(1)}, u32[]{:S(2)}, u32[]{:S(2)}) collective-permute-start(bf16[2,2,192,256]{3,2,1,0:T(8,128)(2,1)S(1)} %get-tuple-element.56), channel_id=1, source_target_pairs={{0,16},{8,24},{16,0},{24,8},{1,17},{9,25},{17,1},{25,9},{2,18},{10... | collective-permute-start | bytes 1179656 | tf_op jit(solution)/shard_map/ppermute | solution.py:339
  18.4 10.5 %collective-permute-start.6 = (bf16[2,2,192,256]{3,2,1,0:T(8,128)(2,1)S(1)}, bf16[2,2,192,256]{3,2,1,0:T(8,128)(2,1)S(1)}, u32[]{:S(2)}, u32[]{:S(2)}) collective-permute-start(bf16[2,2,192,256]{3,2,1,0:T(8,128)(2,1)S(1)} %get-tuple-element.57), channel_id=1, source_target_pairs={{0,8},{8,0},{16,24},{24,16},{1,9},{9,1},{17,25},{25,17},{2,10},{10... | collective-permute-start | bytes 1179656 | tf_op jit(solution)/shard_map/ppermute | solution.py:339
  27.4 9.6 %collective-permute-start.3 = (bf16[784,256]{1,0:T(8,128)(2,1)S(1)}, bf16[784,256]{1,0:T(8,128)(2,1)S(1)}, u32[]{:S(2)}, u32[]{:S(2)}) collective-permute-start(bf16[784,256]{1,0:T(8,128)(2,1)S(1)} %get-tuple-element.50.packed_0), channel_id=1, source_target_pairs={{0,8},{8,0},{16,24},{24,16},{1,9},{9,1},{17,25},{25,17},{2,10},{10... | collective-permute-start | bytes 1204232 | tf_op jit(solution)/shard_map/ppermute | solution.py:339
  28.1 9.3 %collective-permute-start.4 = (bf16[784,256]{1,0:T(8,128)(2,1)S(1)}, bf16[784,256]{1,0:T(8,128)(2,1)S(1)}, u32[]{:S(2)}, u32[]{:S(2)}) collective-permute-start(bf16[784,256]{1,0:T(8,128)(2,1)S(1)} %get-tuple-element.51.packed_1), channel_id=1, source_target_pairs={{0,16},{8,24},{16,0},{24,8},{1,17},{9,25},{17,1},{25,9},{2,18},{10... | collective-permute-start | bytes 1204232 | tf_op jit(solution)/shard_map/ppermute | solution.py:339
  29.3 18.0 %collective-permute-start.10 = (bf16[2,2,384,256]{3,2,1,0:T(8,128)(2,1)S(1)}, bf16[2,2,384,256]{3,2,1,0:T(8,128)(2,1)S(1)}, u32[]{:S(2)}, u32[]{:S(2)}) collective-permute-start(bf16[2,2,384,256]{3,2,1,0:T(8,128)(2,1)S(1)} %near.2.own.refs_0_), channel_id=1, source_target_pairs={{0,4},{1,5},{2,0},{3,1},{4,6},{5,7},{6,2},{7,3},{8,12},{9,13},{10,... | collective-permute-start | bytes 2359304 | tf_op jit(solution)/shard_map/ppermute | solution.py:345
  37.9 8.3 %collective-permute-start.7 = (bf16[2,2,192,256]{3,2,1,0:T(8,128)(2,1)S(1)}, bf16[2,2,192,256]{3,2,1,0:T(8,128)(2,1)S(1)}, u32[]{:S(2)}, u32[]{:S(2)}) collective-permute-start(bf16[2,2,192,256]{3,2,1,0:T(8,128)(2,1)S(1)} %get-tuple-element.64), channel_id=1, source_target_pairs={{0,16},{8,24},{16,0},{24,8},{1,17},{9,25},{17,1},{25,9},{2,18},{10... | collective-permute-start | bytes 1179656 | tf_op jit(solution)/shard_map/ppermute | solution.py:339
  38.7 8.2 %collective-permute-start.8 = (bf16[2,2,192,256]{3,2,1,0:T(8,128)(2,1)S(1)}, bf16[2,2,192,256]{3,2,1,0:T(8,128)(2,1)S(1)}, u32[]{:S(2)}, u32[]{:S(2)}) collective-permute-start(bf16[2,2,192,256]{3,2,1,0:T(8,128)(2,1)S(1)} %get-tuple-element.65), channel_id=1, source_target_pairs={{0,8},{8,0},{16,24},{24,16},{1,9},{9,1},{17,25},{25,17},{2,10},{10... | collective-permute-start | bytes 1179656 | tf_op jit(solution)/shard_map/ppermute | solution.py:339
  47.4 8.4 %collective-permute-start.13 = (bf16[2,2,2,384,256]{4,3,2,1,0:T(8,128)(2,1)S(1)}, bf16[2,2,2,384,256]{4,3,2,1,0:T(8,128)(2,1)S(1)}, u32[]{:S(2)}, u32[]{:S(2)}) collective-permute-start(bf16[2,2,2,384,256]{4,3,2,1,0:T(8,128)(2,1)S(1)} %stack.1), channel_id=1, source_target_pairs={{0,1},{1,0},{2,3},{3,2},{4,5},{5,4},{6,7},{7,6},{8,9},{9,8},{10,11... | collective-permute-start | bytes 4718600 | tf_op jit(solution)/shard_map/ppermute | solution.py:342
  47.5 5.3 %collective-permute-start.14 = (bf16[2,2,384,256]{3,2,1,0:T(8,128)(2,1)S(1)}, bf16[2,2,384,256]{3,2,1,0:T(8,128)(2,1)S(1)}, u32[]{:S(2)}, u32[]{:S(2)}) collective-permute-start(bf16[2,2,384,256]{3,2,1,0:T(8,128)(2,1)S(1)} %collective-permute-done.10.own), channel_id=1, source_target_pairs={{0,1},{1,0},{2,3},{3,2},{4,5},{5,4},{6,7},{7,6},{8,9},{9,8},{10,11... | collective-permute-start | bytes 2359304 | tf_op jit(solution)/shard_map/ppermute | solution.py:342
  48.0 20.4 %collective-permute-start.9 = (bf16[2,2,384,256]{3,2,1,0:T(8,128)(2,1)S(1)}, bf16[2,2,384,256]{3,2,1,0:T(8,128)(2,1)S(1)}, u32[]{:S(2)}, u32[]{:S(2)}) collective-permute-start(bf16[2,2,384,256]{3,2,1,0:T(8,128)(2,1)S(1)} %near.3.refs_1_.own), channel_id=1, source_target_pairs={{0,2},{1,3},{2,6},{3,7},{4,0},{5,1},{6,4},{7,5},{8,10},{9,11},{10,... | collective-permute-start | bytes 2359304 | tf_op jit(solution)/shard_map/ppermute | solution.py:345
  49.7 15.0 %collective-permute-start.11 = (bf16[3,2,192,256]{3,2,1,0:T(8,128)(2,1)S(1)}, bf16[3,2,192,256]{3,2,1,0:T(8,128)(2,1)S(1)}, u32[]{:S(2)}, u32[]{:S(2)}) collective-permute-start(bf16[3,2,192,256]{3,2,1,0:T(8,128)(2,1)S(1)} %get-tuple-element.66), channel_id=1, source_target_pairs={{0,16},{8,24},{16,0},{24,8},{1,17},{9,25},{17,1},{25,9},{2,18},{10... | collective-permute-start | bytes 1769480 | tf_op jit(solution)/shard_map/ppermute | solution.py:339
  51.3 10.5 %collective-permute-start.12 = (bf16[2,2,192,256]{3,2,1,0:T(8,128)(2,1)S(1)}, bf16[2,2,192,256]{3,2,1,0:T(8,128)(2,1)S(1)}, u32[]{:S(2)}, u32[]{:S(2)}) collective-permute-start(bf16[2,2,192,256]{3,2,1,0:T(8,128)(2,1)S(1)} %get-tuple-element.67), channel_id=1, source_target_pairs={{0,8},{8,0},{16,24},{24,16},{1,9},{9,1},{17,25},{25,17},{2,10},{10... | collective-permute-start | bytes 1179656 | tf_op jit(solution)/shard_map/ppermute | solution.py:339
  68.4 2.3 %collective-permute-start.15 = (bf16[2,2,384,256]{3,2,1,0:T(8,128)(2,1)S(1)}, bf16[2,2,384,256]{3,2,1,0:T(8,128)(2,1)S(1)}, u32[]{:S(2)}, u32[]{:S(2)}) collective-permute-start(bf16[2,2,384,256]{3,2,1,0:T(8,128)(2,1)S(1)} %collective-permute-done.9.own), channel_id=1, source_target_pairs={{0,1},{1,0},{2,3},{3,2},{4,5},{5,4},{6,7},{7,6},{8,9},{9,8},{10,11... | collective-permute-start | bytes 2359304 | tf_op jit(solution)/shard_map/ppermute | solution.py:342
  73.2 3.1 %collective-permute-start.19 = (bf16[4,2,2,2,32,256]{5,4,3,2,1,0:T(8,128)(2,1)S(1)}, bf16[4,2,2,2,32,256]{5,4,3,2,1,0:T(8,128)(2,1)S(1)}, u32[]{:S(2)}, u32[]{:S(2)}) collective-permute-start(bf16[4,2,2,2,32,256]{5,4,3,2,1,0:T(8,128)(2,1)S(1)} %get-tuple-element.84), channel_id=1, source_target_pairs={{0,1},{1,0},{2,3},{3,2},{4,5},{5,4},{6,7},{7,6},{8,9},{9,8},{10,11... | collective-permute-start | bytes 1572872 | tf_op jit(solution)/shard_map/ppermute | solution.py:342
  75.9 2.0 %collective-permute-start.16 = (bf16[4,2,2,2,32,256]{5,4,3,2,1,0:T(8,128)(2,1)S(1)}, bf16[4,2,2,2,32,256]{5,4,3,2,1,0:T(8,128)(2,1)S(1)}, u32[]{:S(2)}, u32[]{:S(2)}) collective-permute-start(bf16[4,2,2,2,32,256]{5,4,3,2,1,0:T(8,128)(2,1)S(1)} %get-tuple-element.77), channel_id=1, source_target_pairs={{0,1},{1,0},{2,3},{3,2},{4,5},{5,4},{6,7},{7,6},{8,9},{9,8},{10,11... | collective-permute-start | bytes 1572872 | tf_op jit(solution)/shard_map/ppermute | solution.py:342
  76.4 15.0 %collective-permute-start.20 = (bf16[2,2,2,2,32,256]{5,4,3,2,1,0:T(8,128)(2,1)S(1)}, bf16[2,2,2,2,32,256]{5,4,3,2,1,0:T(8,128)(2,1)S(1)}, u32[]{:S(2)}, u32[]{:S(2)}) collective-permute-start(bf16[2,2,2,2,32,256]{5,4,3,2,1,0:T(8,128)(2,1)S(1)} %get-tuple-element.87), channel_id=1, source_target_pairs={{0,4},{1,5},{2,6},{3,7},{4,0},{5,1},{6,2},{7,3},{8,12},{9,13},{10,... | collective-permute-start | bytes 786440 | tf_op jit(solution)/shard_map/ppermute | solution.py:471
  78.0 13.8 %collective-permute-start.17 = (bf16[2,2,2,2,32,256]{5,4,3,2,1,0:T(8,128)(2,1)S(1)}, bf16[2,2,2,2,32,256]{5,4,3,2,1,0:T(8,128)(2,1)S(1)}, u32[]{:S(2)}, u32[]{:S(2)}) collective-permute-start(bf16[2,2,2,2,32,256]{5,4,3,2,1,0:T(8,128)(2,1)S(1)} %get-tuple-element.80), channel_id=1, source_target_pairs={{0,2},{1,3},{2,0},{3,1},{4,6},{5,7},{6,4},{7,5},{8,10},{9,11},{10,... | collective-permute-start | bytes 786440 | tf_op jit(solution)/shard_map/ppermute | solution.py:471
  91.5 7.4 %collective-permute-start.21 = (bf16[2,2,2,32,256]{4,3,2,1,0:T(8,128)(2,1)S(1)}, bf16[2,2,2,32,256]{4,3,2,1,0:T(8,128)(2,1)S(1)}, u32[]{:S(2)}, u32[]{:S(2)}) collective-permute-start(bf16[2,2,2,32,256]{4,3,2,1,0:T(8,128)(2,1)S(1)} %get-tuple-element.89), channel_id=1, source_target_pairs={{0,2},{1,3},{2,0},{3,1},{4,6},{5,7},{6,4},{7,5},{8,10},{9,11},{10,... | collective-permute-start | bytes 393224 | tf_op jit(solution)/shard_map/ppermute | solution.py:474
  91.8 8.7 %collective-permute-start.18 = (bf16[2,2,2,32,256]{4,3,2,1,0:T(8,128)(2,1)S(1)}, bf16[2,2,2,32,256]{4,3,2,1,0:T(8,128)(2,1)S(1)}, u32[]{:S(2)}, u32[]{:S(2)}) collective-permute-start(bf16[2,2,2,32,256]{4,3,2,1,0:T(8,128)(2,1)S(1)} %get-tuple-element.82), channel_id=1, source_target_pairs={{0,4},{1,5},{2,6},{3,7},{4,0},{5,1},{6,2},{7,3},{8,12},{9,13},{10,... | collective-permute-start | bytes 393224 | tf_op jit(solution)/shard_map/ppermute | solution.py:474
  (1 other events, 0.7 us)

commit v4 on v3

--- a/solution.py
+++ b/solution.py
@@ -455,7 +455,7 @@
         swaps.append((keep, other_core(give)))
     groups = []
     for j, (keep, came_j) in enumerate(swaps):
-        near_z, far_z = ((1, 2), (2, 1))[j % 2]
+        near_z, far_z = ((2, 1), (1, 2))[j % 2]
         own, cross, sends = run(
             functools.partial(split_kernel, near_z, far_z),
             [shape(part, F32), shape(part, F32), shape((2, *part), BF16)],

time: 102 us -> 103 us (level)
  waiting for transfers between devices: 50.2 us -> 53.6 us
  starting transfers between devices: 24.9 us -> 22.5 us
    ppermute x2, waiting for transfers between devices: 11.4 us -> 16.2 us  [quick(): lax.ppermute(sends, 'ga', [(i, i ^ 2 * near_z) for i in range(n_ga)])]
    ppermute x2, starting transfers between devices: 2.46 us -> 0.3 us  [quick(): lax.ppermute(sends, 'ga', [(i, i ^ 2 * far_z) for i in range(n_ga)])]
    ppermute x2, waiting for transfers between devices: 6.35 us -> 4.8 us  [quick(): lax.ppermute(sends, 'ga', [(i, i ^ 2 * far_z) for i in range(n_ga)])]
where the time goes in v4:
time: 103 us; the launch traced here: 102 us
  waiting for transfers between devices  53.6 us (52%)
  Pallas kernels  24.8 us (24%)
  starting transfers between devices  22.5 us (22%)
    pallas_call x20, Pallas kernels, run(): pl.pallas_call(body, in_specs=specs or [VMEM] * len(args), out_specs=[VME...  24.8 us
    ppermute x10, waiting for transfers between devices, across(): return lax.ppermute(x, 'kp', [(i, i ^ bit) for i in range(n_kp)])  19.5 us
    ppermute x2, waiting for transfers between devices, quick(): lax.ppermute(sends, 'ga', [(i, i ^ 2 * near_z) for i in range(n_ga)])  16.2 us
    ppermute x10, starting transfers between devices, across(): return lax.ppermute(x, 'kp', [(i, i ^ bit) for i in range(n_kp)])  12.8 us
    ppermute x3, waiting for transfers between devices, along(): lax.ppermute(x, 'ga', [(i, 2 * chips_on[i // 2] + i % 2) for i in range(n...  11.5 us
    ppermute x3, starting transfers between devices, along(): lax.ppermute(x, 'ga', [(i, 2 * chips_on[i // 2] + i % 2) for i in range(n...  5.13 us
    ppermute x2, waiting for transfers between devices, quick(): lax.ppermute(sends, 'ga', [(i, i ^ 2 * far_z) for i in range(n_ga)])  4.8 us
    ppermute x2, starting transfers between devices, quick(): lax.ppermute(sends, 'ga', [(i, i ^ 2 * near_z) for i in range(n_ga)])  3.09 us
  transfers between devices with their start and end apart: 22, of which 16 were waited for; matrix products, arithmetic and copies ran while one was open for 0% of the time, Pallas kernels for 20%

profile of v4, /device:TPU:0, one launch (start us, length us, event | category | flops | bytes accessed | tf_op | source)
XLA Modules:
  0.0 102.5 jit_solution(12736269689577066503)
XLA Ops:
  2.5 3.0 %collective-permute-start = (bf16[784,256]{1,0:T(8,128)(2,1)S(1)}, bf16[784,256]{1,0:T(8,128)(2,1)S(1)}, u32[]{:S(2)}, u32[]{:S(2)}) collective-permute-start(bf16[784,256]{1,0:T(8,128)(2,1)S(1)} %get-tuple-element.52.packed_0), channel_id=1, source_target_pairs={{0,8},{8,0},{16,24},{24,16},{1,9},{9,1},{17,25},{25,17},{2,10},{10... | collective-permute-start | bytes 1204232 | tf_op jit(solution)/shard_map/ppermute | solution.py:339
  5.5 1.5 %collective-permute-start.1 = (bf16[784,256]{1,0:T(8,128)(2,1)S(1)}, bf16[784,256]{1,0:T(8,128)(2,1)S(1)}, u32[]{:S(2)}, u32[]{:S(2)}) collective-permute-start(bf16[784,256]{1,0:T(8,128)(2,1)S(1)} %get-tuple-element.53.packed_1), channel_id=1, source_target_pairs={{0,16},{8,24},{16,0},{24,8},{1,17},{9,25},{17,1},{25,9},{2,18},{10... | collective-permute-start | bytes 1204232 | tf_op jit(solution)/shard_map/ppermute | solution.py:339
  7.0 1.6 %collective-permute-start.2 = (bf16[2,2,384,256]{3,2,1,0:T(8,128)(2,1)}, bf16[2,2,384,256]{3,2,1,0:T(8,128)(2,1)S(1)}, u32[]{:S(2)}, u32[]{:S(2)}) collective-permute-start(bf16[2,2,384,256]{3,2,1,0:T(8,128)(2,1)} %densities.1), channel_id=1, source_target_pairs={{0,2},{1,3},{2,6},{3,7},{4,0},{5,1},{6,4},{7,5},{8,10},{9,11},{10,... | collective-permute-start | bytes 2359304 | tf_op jit(solution)/shard_map/ppermute | solution.py:345
  8.6 3.8 %load.1.screened = bf16[2,2,384,3072]{3,2,1,0:T(8,128)(2,1)S(1)} custom-call(bf16[2,2,384,3072]{3,2,1,0:T(8,128)(2,1)} %source), custom_call_target="tpu_custom_call" | custom-call | tf_op jit(solution)/shard_map/load/pallas_call | solution.py:30
  12.4 2.4 %collective-permute-done.came_0 = bf16[784,256]{1,0:T(8,128)(2,1)S(1)} collective-permute-done((bf16[784,256]{1,0:T(8,128)(2,1)S(1)}, bf16[784,256]{1,0:T(8,128)(2,1)S(1)}, u32[]{:S(2)}, u32[]{:S(2)}) %collective-permute-start) | collective-permute-done | bytes 401440 | tf_op jit(solution)/shard_map/ppermute | solution.py:339
  16.8 1.6 %collective-permute-start.5 = (bf16[2,2,192,256]{3,2,1,0:T(8,128)(2,1)S(1)}, bf16[2,2,192,256]{3,2,1,0:T(8,128)(2,1)S(1)}, u32[]{:S(2)}, u32[]{:S(2)}) collective-permute-start(bf16[2,2,192,256]{3,2,1,0:T(8,128)(2,1)S(1)} %get-tuple-element.56), channel_id=1, source_target_pairs={{0,16},{8,24},{16,0},{24,8},{1,17},{9,25},{17,1},{25,9},{2,18},{10... | collective-permute-start | bytes 1179656 | tf_op jit(solution)/shard_map/ppermute | solution.py:339
  19.0 7.9 %collective-permute-done.2.densities = bf16[2,2,384,256]{3,2,1,0:T(8,128)(2,1)S(1)} collective-permute-done((bf16[2,2,384,256]{3,2,1,0:T(8,128)(2,1)}, bf16[2,2,384,256]{3,2,1,0:T(8,128)(2,1)S(1)}, u32[]{:S(2)}, u32[]{:S(2)}) %collective-permute-start.2) | collective-permute-done | bytes 786464 | tf_op jit(solution)/shard_map/ppermute | solution.py:345
  29.3 1.8 %collective-permute-start.10 = (bf16[2,2,384,256]{3,2,1,0:T(8,128)(2,1)S(1)}, bf16[2,2,384,256]{3,2,1,0:T(8,128)(2,1)S(1)}, u32[]{:S(2)}, u32[]{:S(2)}) collective-permute-start(bf16[2,2,384,256]{3,2,1,0:T(8,128)(2,1)S(1)} %near.2.own.refs_0_), channel_id=1, source_target_pairs={{0,4},{1,5},{2,0},{3,1},{4,6},{5,7},{6,2},{7,3},{8,12},{9,13},{10,... | collective-permute-start | bytes 2359304 | tf_op jit(solution)/shard_map/ppermute | solution.py:345
  31.1 1.8 %product.3.before = f32[2,384,1024]{2,1,0:T(8,128)S(1)} custom-call(bf16[2,2,384,3072]{3,2,1,0:T(8,128)(2,1)S(1)} %load.1.screened, bf16[2,2,384,256]{3,2,1,0:T(8,128)(2,1)S(1)} %near.2.own.refs_0_, f32[1,384]{1,0:T(1,128)S(1)} %broadcast_in_dim.3.coulomb), custom_call_target="tpu_custom_call" | custom-call | tf_op jit(solution)/shard_map/product/pallas_call | solution.py:30
  32.9 4.2 %collective-permute-done.3.came_0 = bf16[784,256]{1,0:T(8,128)(2,1)S(1)} collective-permute-done((bf16[784,256]{1,0:T(8,128)(2,1)S(1)}, bf16[784,256]{1,0:T(8,128)(2,1)S(1)}, u32[]{:S(2)}, u32[]{:S(2)}) %collective-permute-start.3) | collective-permute-done | bytes 401440 | tf_op jit(solution)/shard_map/ppermute | solution.py:339
  40.0 6.2 %collective-permute-done.7.picked_0 = bf16[2,2,192,256]{3,2,1,0:T(8,128)(2,1)S(1)} collective-permute-done((bf16[2,2,192,256]{3,2,1,0:T(8,128)(2,1)S(1)}, bf16[2,2,192,256]{3,2,1,0:T(8,128)(2,1)S(1)}, u32[]{:S(2)}, u32[]{:S(2)}) %collective-permute-start.7) | collective-permute-done | bytes 393248 | tf_op jit(solution)/shard_map/ppermute | solution.py:339
  48.0 1.8 %collective-permute-start.9 = (bf16[2,2,384,256]{3,2,1,0:T(8,128)(2,1)S(1)}, bf16[2,2,384,256]{3,2,1,0:T(8,128)(2,1)S(1)}, u32[]{:S(2)}, u32[]{:S(2)}) collective-permute-start(bf16[2,2,384,256]{3,2,1,0:T(8,128)(2,1)S(1)} %near.3.refs_1_.own), channel_id=1, source_target_pairs={{0,2},{1,3},{2,6},{3,7},{4,0},{5,1},{6,4},{7,5},{8,10},{9,11},{10,... | collective-permute-start | bytes 2359304 | tf_op jit(solution)/shard_map/ppermute | solution.py:345
  51.3 1.5 %collective-permute-start.12 = (bf16[2,2,192,256]{3,2,1,0:T(8,128)(2,1)S(1)}, bf16[2,2,192,256]{3,2,1,0:T(8,128)(2,1)S(1)}, u32[]{:S(2)}, u32[]{:S(2)}) collective-permute-start(bf16[2,2,192,256]{3,2,1,0:T(8,128)(2,1)S(1)} %get-tuple-element.67), channel_id=1, source_target_pairs={{0,8},{8,0},{16,24},{24,16},{1,9},{9,1},{17,25},{25,17},{2,10},{10... | collective-permute-start | bytes 1179656 | tf_op jit(solution)/shard_map/ppermute | solution.py:339
  52.8 3.0 %product.4.before = f32[2,384,1024]{2,1,0:T(8,128)S(1)} custom-call(bf16[2,2,384,3072]{3,2,1,0:T(8,128)(2,1)S(1)} %load.1.screened, bf16[2,2,384,256]{3,2,1,0:T(8,128)(2,1)S(1)} %collective-permute-done.10.own, bf16[2,2,384,256]{3,2,1,0:T(8,128)(2,1)S(1)} %collective-permute-done.14.pair, ...), custom_call_target="tpu_custom_call", output_to_operand_aliasing={{}: (3, {})} | custom-call | tf_op jit(solution)/shard_map/product/pallas_call | solution.py:30
  55.8 4.6 %product.5.before = f32[2,384,1024]{2,1,0:T(8,128)S(1)} custom-call(bf16[2,2,384,3072]{3,2,1,0:T(8,128)(2,1)S(1)} %load.1.screened, bf16[2,2,384,256]{3,2,1,0:T(8,128)(2,1)S(1)} %near.3.refs_1_.own, bf16[2,2,2,384,256]{4,3,2,1,0:T(8,128)(2,1)S(1)} %collective-permute-done.13.pairs, f32[2,384,1024]{2,1,0:T(8,128)S(1)} %product.4.before), custom_call_target="tpu_custom_call", output_to_operand_aliasing={{}: (3, {})} | custom-call | tf_op jit(solution)/shard_map/product/pallas_call | solution.py:30
  61.8 3.0 %collective-permute-done.11.rest_0 = bf16[3,2,192,256]{3,2,1,0:T(8,128)(2,1)S(1)} collective-permute-done((bf16[3,2,192,256]{3,2,1,0:T(8,128)(2,1)S(1)}, bf16[3,2,192,256]{3,2,1,0:T(8,128)(2,1)S(1)}, u32[]{:S(2)}, u32[]{:S(2)}) %collective-permute-start.11) | collective-permute-done | bytes 589856 | tf_op jit(solution)/shard_map/ppermute | solution.py:339
  64.8 3.6 %collective-permute-done.9.own = bf16[2,2,384,256]{3,2,1,0:T(8,128)(2,1)S(1)} collective-permute-done((bf16[2,2,384,256]{3,2,1,0:T(8,128)(2,1)S(1)}, bf16[2,2,384,256]{3,2,1,0:T(8,128)(2,1)S(1)}, u32[]{:S(2)}, u32[]{:S(2)}) %collective-permute-start.9) | collective-permute-done | bytes 786464 | tf_op jit(solution)/shard_map/ppermute | solution.py:345
  70.7 2.5 %last.3 = (f32[4,2,2,2,32,256]{5,4,3,2,1,0:T(8,128)S(1)}, bf16[4,2,2,2,32,256]{5,4,3,2,1,0:T(8,128)(2,1)S(1)}) custom-call(bf16[2,2,384,3072]{3,2,1,0:T(8,128)(2,1)S(1)} %load.1.screened, bf16[2,2,384,256]{3,2,1,0:T(8,128)(2,1)S(1)} %collective-permute-done.9.own, bf16[2,2,384,256]{3,2,1,0:T(8,128)(2,1)S(1)} %collective-permute-done.15.pair, ...), custom_call_target="tpu_custom_call" | custom-call | tf_op jit(solution)/shard_map/last/pallas_call | solution.py:30
  73.4 2.5 %last.2 = (f32[4,2,2,2,32,256]{5,4,3,2,1,0:T(8,128)S(1)}, bf16[4,2,2,2,32,256]{5,4,3,2,1,0:T(8,128)(2,1)S(1)}) custom-call(bf16[2,2,384,3072]{3,2,1,0:T(8,128)(2,1)S(1)} %load.1.screened, bf16[2,2,384,256]{3,2,1,0:T(8,128)(2,1)S(1)} %collective-permute-done.9.own, bf16[2,2,384,256]{3,2,1,0:T(8,128)(2,1)S(1)} %collective-permute-done.15.pair, ...), custom_call_target="tpu_custom_call" | custom-call | tf_op jit(solution)/shard_map/last/pallas_call | solution.py:30
  78.0 2.2 %collective-permute-start.17 = (bf16[2,2,2,2,32,256]{5,4,3,2,1,0:T(8,128)(2,1)S(1)}, bf16[2,2,2,2,32,256]{5,4,3,2,1,0:T(8,128)(2,1)S(1)}, u32[]{:S(2)}, u32[]{:S(2)}) collective-permute-start(bf16[2,2,2,2,32,256]{5,4,3,2,1,0:T(8,128)(2,1)S(1)} %get-tuple-element.80), channel_id=1, source_target_pairs={{0,4},{1,5},{2,6},{3,7},{4,0},{5,1},{6,2},{7,3},{8,12},{9,13},{10,... | collective-permute-start | bytes 786440 | tf_op jit(solution)/shard_map/ppermute | solution.py:471
  80.2 8.9 %collective-permute-done.20.came = bf16[2,2,2,2,32,256]{5,4,3,2,1,0:T(8,128)(2,1)S(1)} collective-permute-done((bf16[2,2,2,2,32,256]{5,4,3,2,1,0:T(8,128)(2,1)S(1)}, bf16[2,2,2,2,32,256]{5,4,3,2,1,0:T(8,128)(2,1)S(1)}, u32[]{:S(2)}, u32[]{:S(2)}) %collective-permute-start.20) | collective-permute-done | bytes 262176 | tf_op jit(solution)/shard_map/ppermute | solution.py:471
  89.2 7.3 %collective-permute-done.17.came = bf16[2,2,2,2,32,256]{5,4,3,2,1,0:T(8,128)(2,1)S(1)} collective-permute-done((bf16[2,2,2,2,32,256]{5,4,3,2,1,0:T(8,128)(2,1)S(1)}, bf16[2,2,2,2,32,256]{5,4,3,2,1,0:T(8,128)(2,1)S(1)}, u32[]{:S(2)}, u32[]{:S(2)}) %collective-permute-start.17) | collective-permute-done | bytes 262176 | tf_op jit(solution)/shard_map/ppermute | solution.py:471
  96.8 2.0 %collective-permute-done.21.refs_3_ = bf16[2,2,2,32,256]{4,3,2,1,0:T(8,128)(2,1)S(1)} collective-permute-done((bf16[2,2,2,32,256]{4,3,2,1,0:T(8,128)(2,1)S(1)}, bf16[2,2,2,32,256]{4,3,2,1,0:T(8,128)(2,1)S(1)}, u32[]{:S(2)}, u32[]{:S(2)}) %collective-permute-start.21) | collective-permute-done | bytes 131104 | tf_op jit(solution)/shard_map/ppermute | solution.py:474
  98.9 2.8 %collective-permute-done.18.refs_1_ = bf16[2,2,2,32,256]{4,3,2,1,0:T(8,128)(2,1)S(1)} collective-permute-done((bf16[2,2,2,32,256]{4,3,2,1,0:T(8,128)(2,1)S(1)}, bf16[2,2,2,32,256]{4,3,2,1,0:T(8,128)(2,1)S(1)}, u32[]{:S(2)}, u32[]{:S(2)}) %collective-permute-start.18) | collective-permute-done | bytes 131104 | tf_op jit(solution)/shard_map/ppermute | solution.py:474
  (47 shorter events, 20.1 us)
Async XLA Ops:
  2.5 12.3 %collective-permute-start = (bf16[784,256]{1,0:T(8,128)(2,1)S(1)}, bf16[784,256]{1,0:T(8,128)(2,1)S(1)}, u32[]{:S(2)}, u32[]{:S(2)}) collective-permute-start(bf16[784,256]{1,0:T(8,128)(2,1)S(1)} %get-tuple-element.52.packed_0), channel_id=1, source_target_pairs={{0,8},{8,0},{16,24},{24,16},{1,9},{9,1},{17,25},{25,17},{2,10},{10... | collective-permute-start | bytes 1204232 | tf_op jit(solution)/shard_map/ppermute | solution.py:339
  5.5 21.4 %copy-start.1 = (s32[1,2]{1,0:T(1,128)S(1)}, s32[1,2]{1,0:T(1,128)}, u32[]{:S(2)}) copy-start(s32[1,2]{1,0:T(1,128)} %rows.3) | copy-start | bytes 28
  5.5 10.8 %collective-permute-start.1 = (bf16[784,256]{1,0:T(8,128)(2,1)S(1)}, bf16[784,256]{1,0:T(8,128)(2,1)S(1)}, u32[]{:S(2)}, u32[]{:S(2)}) collective-permute-start(bf16[784,256]{1,0:T(8,128)(2,1)S(1)} %get-tuple-element.53.packed_1), channel_id=1, source_target_pairs={{0,16},{8,24},{16,0},{24,8},{1,17},{9,25},{17,1},{25,9},{2,18},{10... | collective-permute-start | bytes 1204232 | tf_op jit(solution)/shard_map/ppermute | solution.py:339
  7.0 19.8 %collective-permute-start.2 = (bf16[2,2,384,256]{3,2,1,0:T(8,128)(2,1)}, bf16[2,2,384,256]{3,2,1,0:T(8,128)(2,1)S(1)}, u32[]{:S(2)}, u32[]{:S(2)}) collective-permute-start(bf16[2,2,384,256]{3,2,1,0:T(8,128)(2,1)} %densities.1), channel_id=1, source_target_pairs={{0,2},{1,3},{2,6},{3,7},{4,0},{5,1},{6,4},{7,5},{8,10},{9,11},{10,... | collective-permute-start | bytes 2359304 | tf_op jit(solution)/shard_map/ppermute | solution.py:345
  16.8 14.3 %copy-start.2 = (f32[384]{0:T(512)S(1)}, f32[384]{0:T(512)}, u32[]{:S(2)}) copy-start(f32[384]{0:T(512)} %param.6) | copy-start | bytes 4612
  16.8 12.1 %collective-permute-start.5 = (bf16[2,2,192,256]{3,2,1,0:T(8,128)(2,1)S(1)}, bf16[2,2,192,256]{3,2,1,0:T(8,128)(2,1)S(1)}, u32[]{:S(2)}, u32[]{:S(2)}) collective-permute-start(bf16[2,2,192,256]{3,2,1,0:T(8,128)(2,1)S(1)} %get-tuple-element.56), channel_id=1, source_target_pairs={{0,16},{8,24},{16,0},{24,8},{1,17},{9,25},{17,1},{25,9},{2,18},{10... | collective-permute-start | bytes 1179656 | tf_op jit(solution)/shard_map/ppermute | solution.py:339
  18.4 10.5 %collective-permute-start.6 = (bf16[2,2,192,256]{3,2,1,0:T(8,128)(2,1)S(1)}, bf16[2,2,192,256]{3,2,1,0:T(8,128)(2,1)S(1)}, u32[]{:S(2)}, u32[]{:S(2)}) collective-permute-start(bf16[2,2,192,256]{3,2,1,0:T(8,128)(2,1)S(1)} %get-tuple-element.57), channel_id=1, source_target_pairs={{0,8},{8,0},{16,24},{24,16},{1,9},{9,1},{17,25},{25,17},{2,10},{10... | collective-permute-start | bytes 1179656 | tf_op jit(solution)/shard_map/ppermute | solution.py:339
  27.4 9.6 %collective-permute-start.3 = (bf16[784,256]{1,0:T(8,128)(2,1)S(1)}, bf16[784,256]{1,0:T(8,128)(2,1)S(1)}, u32[]{:S(2)}, u32[]{:S(2)}) collective-permute-start(bf16[784,256]{1,0:T(8,128)(2,1)S(1)} %get-tuple-element.50.packed_0), channel_id=1, source_target_pairs={{0,8},{8,0},{16,24},{24,16},{1,9},{9,1},{17,25},{25,17},{2,10},{10... | collective-permute-start | bytes 1204232 | tf_op jit(solution)/shard_map/ppermute | solution.py:339
  28.1 9.3 %collective-permute-start.4 = (bf16[784,256]{1,0:T(8,128)(2,1)S(1)}, bf16[784,256]{1,0:T(8,128)(2,1)S(1)}, u32[]{:S(2)}, u32[]{:S(2)}) collective-permute-start(bf16[784,256]{1,0:T(8,128)(2,1)S(1)} %get-tuple-element.51.packed_1), channel_id=1, source_target_pairs={{0,16},{8,24},{16,0},{24,8},{1,17},{9,25},{17,1},{25,9},{2,18},{10... | collective-permute-start | bytes 1204232 | tf_op jit(solution)/shard_map/ppermute | solution.py:339
  29.3 18.0 %collective-permute-start.10 = (bf16[2,2,384,256]{3,2,1,0:T(8,128)(2,1)S(1)}, bf16[2,2,384,256]{3,2,1,0:T(8,128)(2,1)S(1)}, u32[]{:S(2)}, u32[]{:S(2)}) collective-permute-start(bf16[2,2,384,256]{3,2,1,0:T(8,128)(2,1)S(1)} %near.2.own.refs_0_), channel_id=1, source_target_pairs={{0,4},{1,5},{2,0},{3,1},{4,6},{5,7},{6,2},{7,3},{8,12},{9,13},{10,... | collective-permute-start | bytes 2359304 | tf_op jit(solution)/shard_map/ppermute | solution.py:345
  37.9 8.3 %collective-permute-start.7 = (bf16[2,2,192,256]{3,2,1,0:T(8,128)(2,1)S(1)}, bf16[2,2,192,256]{3,2,1,0:T(8,128)(2,1)S(1)}, u32[]{:S(2)}, u32[]{:S(2)}) collective-permute-start(bf16[2,2,192,256]{3,2,1,0:T(8,128)(2,1)S(1)} %get-tuple-element.64), channel_id=1, source_target_pairs={{0,16},{8,24},{16,0},{24,8},{1,17},{9,25},{17,1},{25,9},{2,18},{10... | collective-permute-start | bytes 1179656 | tf_op jit(solution)/shard_map/ppermute | solution.py:339
  38.7 8.2 %collective-permute-start.8 = (bf16[2,2,192,256]{3,2,1,0:T(8,128)(2,1)S(1)}, bf16[2,2,192,256]{3,2,1,0:T(8,128)(2,1)S(1)}, u32[]{:S(2)}, u32[]{:S(2)}) collective-permute-start(bf16[2,2,192,256]{3,2,1,0:T(8,128)(2,1)S(1)} %get-tuple-element.65), channel_id=1, source_target_pairs={{0,8},{8,0},{16,24},{24,16},{1,9},{9,1},{17,25},{25,17},{2,10},{10... | collective-permute-start | bytes 1179656 | tf_op jit(solution)/shard_map/ppermute | solution.py:339
  47.4 8.4 %collective-permute-start.13 = (bf16[2,2,2,384,256]{4,3,2,1,0:T(8,128)(2,1)S(1)}, bf16[2,2,2,384,256]{4,3,2,1,0:T(8,128)(2,1)S(1)}, u32[]{:S(2)}, u32[]{:S(2)}) collective-permute-start(bf16[2,2,2,384,256]{4,3,2,1,0:T(8,128)(2,1)S(1)} %stack.1), channel_id=1, source_target_pairs={{0,1},{1,0},{2,3},{3,2},{4,5},{5,4},{6,7},{7,6},{8,9},{9,8},{10,11... | collective-permute-start | bytes 4718600 | tf_op jit(solution)/shard_map/ppermute | solution.py:342
  47.5 5.3 %collective-permute-start.14 = (bf16[2,2,384,256]{3,2,1,0:T(8,128)(2,1)S(1)}, bf16[2,2,384,256]{3,2,1,0:T(8,128)(2,1)S(1)}, u32[]{:S(2)}, u32[]{:S(2)}) collective-permute-start(bf16[2,2,384,256]{3,2,1,0:T(8,128)(2,1)S(1)} %collective-permute-done.10.own), channel_id=1, source_target_pairs={{0,1},{1,0},{2,3},{3,2},{4,5},{5,4},{6,7},{7,6},{8,9},{9,8},{10,11... | collective-permute-start | bytes 2359304 | tf_op jit(solution)/shard_map/ppermute | solution.py:342
  48.0 20.4 %collective-permute-start.9 = (bf16[2,2,384,256]{3,2,1,0:T(8,128)(2,1)S(1)}, bf16[2,2,384,256]{3,2,1,0:T(8,128)(2,1)S(1)}, u32[]{:S(2)}, u32[]{:S(2)}) collective-permute-start(bf16[2,2,384,256]{3,2,1,0:T(8,128)(2,1)S(1)} %near.3.refs_1_.own), channel_id=1, source_target_pairs={{0,2},{1,3},{2,6},{3,7},{4,0},{5,1},{6,4},{7,5},{8,10},{9,11},{10,... | collective-permute-start | bytes 2359304 | tf_op jit(solution)/shard_map/ppermute | solution.py:345
  49.7 15.0 %collective-permute-start.11 = (bf16[3,2,192,256]{3,2,1,0:T(8,128)(2,1)S(1)}, bf16[3,2,192,256]{3,2,1,0:T(8,128)(2,1)S(1)}, u32[]{:S(2)}, u32[]{:S(2)}) collective-permute-start(bf16[3,2,192,256]{3,2,1,0:T(8,128)(2,1)S(1)} %get-tuple-element.66), channel_id=1, source_target_pairs={{0,16},{8,24},{16,0},{24,8},{1,17},{9,25},{17,1},{25,9},{2,18},{10... | collective-permute-start | bytes 1769480 | tf_op jit(solution)/shard_map/ppermute | solution.py:339
  51.3 10.5 %collective-permute-start.12 = (bf16[2,2,192,256]{3,2,1,0:T(8,128)(2,1)S(1)}, bf16[2,2,192,256]{3,2,1,0:T(8,128)(2,1)S(1)}, u32[]{:S(2)}, u32[]{:S(2)}) collective-permute-start(bf16[2,2,192,256]{3,2,1,0:T(8,128)(2,1)S(1)} %get-tuple-element.67), channel_id=1, source_target_pairs={{0,8},{8,0},{16,24},{24,16},{1,9},{9,1},{17,25},{25,17},{2,10},{10... | collective-permute-start | bytes 1179656 | tf_op jit(solution)/shard_map/ppermute | solution.py:339
  68.4 2.3 %collective-permute-start.15 = (bf16[2,2,384,256]{3,2,1,0:T(8,128)(2,1)S(1)}, bf16[2,2,384,256]{3,2,1,0:T(8,128)(2,1)S(1)}, u32[]{:S(2)}, u32[]{:S(2)}) collective-permute-start(bf16[2,2,384,256]{3,2,1,0:T(8,128)(2,1)S(1)} %collective-permute-done.9.own), channel_id=1, source_target_pairs={{0,1},{1,0},{2,3},{3,2},{4,5},{5,4},{6,7},{7,6},{8,9},{9,8},{10,11... | collective-permute-start | bytes 2359304 | tf_op jit(solution)/shard_map/ppermute | solution.py:342
  73.2 3.1 %collective-permute-start.19 = (bf16[4,2,2,2,32,256]{5,4,3,2,1,0:T(8,128)(2,1)S(1)}, bf16[4,2,2,2,32,256]{5,4,3,2,1,0:T(8,128)(2,1)S(1)}, u32[]{:S(2)}, u32[]{:S(2)}) collective-permute-start(bf16[4,2,2,2,32,256]{5,4,3,2,1,0:T(8,128)(2,1)S(1)} %get-tuple-element.84), channel_id=1, source_target_pairs={{0,1},{1,0},{2,3},{3,2},{4,5},{5,4},{6,7},{7,6},{8,9},{9,8},{10,11... | collective-permute-start | bytes 1572872 | tf_op jit(solution)/shard_map/ppermute | solution.py:342
  75.9 2.0 %collective-permute-start.16 = (bf16[4,2,2,2,32,256]{5,4,3,2,1,0:T(8,128)(2,1)S(1)}, bf16[4,2,2,2,32,256]{5,4,3,2,1,0:T(8,128)(2,1)S(1)}, u32[]{:S(2)}, u32[]{:S(2)}) collective-permute-start(bf16[4,2,2,2,32,256]{5,4,3,2,1,0:T(8,128)(2,1)S(1)} %get-tuple-element.77), channel_id=1, source_target_pairs={{0,1},{1,0},{2,3},{3,2},{4,5},{5,4},{6,7},{7,6},{8,9},{9,8},{10,11... | collective-permute-start | bytes 1572872 | tf_op jit(solution)/shard_map/ppermute | solution.py:342
  76.4 12.6 %collective-permute-start.20 = (bf16[2,2,2,2,32,256]{5,4,3,2,1,0:T(8,128)(2,1)S(1)}, bf16[2,2,2,2,32,256]{5,4,3,2,1,0:T(8,128)(2,1)S(1)}, u32[]{:S(2)}, u32[]{:S(2)}) collective-permute-start(bf16[2,2,2,2,32,256]{5,4,3,2,1,0:T(8,128)(2,1)S(1)} %get-tuple-element.87), channel_id=1, source_target_pairs={{0,2},{1,3},{2,0},{3,1},{4,6},{5,7},{6,4},{7,5},{8,10},{9,11},{10,... | collective-permute-start | bytes 786440 | tf_op jit(solution)/shard_map/ppermute | solution.py:471
  78.0 18.6 %collective-permute-start.17 = (bf16[2,2,2,2,32,256]{5,4,3,2,1,0:T(8,128)(2,1)S(1)}, bf16[2,2,2,2,32,256]{5,4,3,2,1,0:T(8,128)(2,1)S(1)}, u32[]{:S(2)}, u32[]{:S(2)}) collective-permute-start(bf16[2,2,2,2,32,256]{5,4,3,2,1,0:T(8,128)(2,1)S(1)} %get-tuple-element.80), channel_id=1, source_target_pairs={{0,4},{1,5},{2,6},{3,7},{4,0},{5,1},{6,2},{7,3},{8,12},{9,13},{10,... | collective-permute-start | bytes 786440 | tf_op jit(solution)/shard_map/ppermute | solution.py:471
  89.1 9.7 %collective-permute-start.21 = (bf16[2,2,2,32,256]{4,3,2,1,0:T(8,128)(2,1)S(1)}, bf16[2,2,2,32,256]{4,3,2,1,0:T(8,128)(2,1)S(1)}, u32[]{:S(2)}, u32[]{:S(2)}) collective-permute-start(bf16[2,2,2,32,256]{4,3,2,1,0:T(8,128)(2,1)S(1)} %get-tuple-element.89), channel_id=1, source_target_pairs={{0,4},{1,5},{2,6},{3,7},{4,0},{5,1},{6,2},{7,3},{8,12},{9,13},{10,... | collective-permute-start | bytes 393224 | tf_op jit(solution)/shard_map/ppermute | solution.py:474
  96.6 5.0 %collective-permute-start.18 = (bf16[2,2,2,32,256]{4,3,2,1,0:T(8,128)(2,1)S(1)}, bf16[2,2,2,32,256]{4,3,2,1,0:T(8,128)(2,1)S(1)}, u32[]{:S(2)}, u32[]{:S(2)}) collective-permute-start(bf16[2,2,2,32,256]{4,3,2,1,0:T(8,128)(2,1)S(1)} %get-tuple-element.82), channel_id=1, source_target_pairs={{0,2},{1,3},{2,0},{3,1},{4,6},{5,7},{6,4},{7,5},{8,10},{9,11},{10,... | collective-permute-start | bytes 393224 | tf_op jit(solution)/shard_map/ppermute | solution.py:474
  (1 other events, 0.7 us)

commit v5 on v2

--- a/solution.py
+++ b/solution.py
@@ -94,7 +94,7 @@
             copy_if(label_of(came[1 - h], held, half, j), found, sends[h].at[j])
 
 
-def near_kernel(held, packed_0, packed_1, came_0, came_1, picked_0, picked_1, near):
+def near_kernel(held, packed_0, packed_1, came_0, came_1, picked_0, picked_1, near, *each):
     owner = lax.axis_index("kp")
     packed, came, picked = (packed_0, packed_1), (came_0, came_1), (picked_0, picked_1)
     half = picked_0.shape[2]
@@ -109,6 +109,9 @@
             @pl.when(jnp.logical_not(hit))
             def _(h=h, j=j, out=out):
                 out[...] = picked[h][j]
+
+    for j, out in enumerate(each):
+        out[...] = near[j]
 
 
 def stack_kernel(*refs):
@@ -226,14 +229,14 @@
 
 def lay(terms, upper, lower):
     for ref, first in terms:
-        count, _, g_local, t = ref.shape
+        *count, _, g_local, t = ref.shape
         rows = pl.ds(first if isinstance(first, int) else pl.multiple_of(first, 128), g_local)
-        for j in range(count):
+        for j, panel in enumerate([ref.at[j] for j in range(count[0])] if count else [ref]):
             real, imag = slice(2 * j * t, (2 * j + 1) * t), slice((2 * j + 1) * t, (2 * j + 2) * t)
-            upper[rows, real] = ref[j, 0]
-            upper[rows, imag] = ref[j, 1]
-            lower[rows, real] = -ref[j, 1]
-            lower[rows, imag] = ref[j, 0]
+            upper[rows, real] = panel[0]
+            upper[rows, imag] = panel[1]
+            lower[rows, real] = -panel[1]
+            lower[rows, imag] = panel[0]
 
 
 def place():
@@ -280,11 +283,12 @@
         total[s] = value + multiply(screened, s, left, g, upper, lower, 2 * g)
 
 
-def last_kernel(chips, steps, j, screened, own, pair, before, far, keep, give, upper, lower):
+def last_kernel(chips, steps, j, screened, own, pair, before, far, keep, *refs):
     z, core = place()
     g = screened.shape[2]
     t = far.shape[-1]
-    lay([(own.at[j : j + 1], core * g), (pair.at[j : j + 1], (1 - core) * g)], upper, lower)
+    *gives, upper, lower = refs
+    lay([(own, core * g), (pair, (1 - core) * g)], upper, lower)
     span = 2 * chip_at(z, steps) * g
     first = core == 0
     for s in range(screened.shape[0]):
@@ -299,15 +303,23 @@
                 block = parts[which][part]
                 block = block.reshape(chips, 2, t // (2 * chips), t)
                 keep[:, s, which, part] = jnp.where(first, block[:, 0], block[:, 1])
-                give[:, s, which, part] = jnp.where(first, block[:, 1], block[:, 0]).astype(BF16)
-
-
-def split_kernel(keep, came, own, cross, sends):
+                give = jnp.where(first, block[:, 1], block[:, 0])
+                gives[2 * s + which][:, part] = give.astype(BF16)
+
+
+def split_kernel(keep, *refs):
+    *came, own, cross, sends = refs
     z = lax.axis_index("ga") // 2
-    own[...] = keep[z] + came[z].astype(F32)
-    cross[...] = keep[z ^ 2] + came[z ^ 2].astype(F32)
-    for i, at in enumerate((z ^ 1, z ^ 3)):
-        sends[i] = (keep[at] + came[at].astype(F32)).astype(BF16)
+    for s in range(keep.shape[1]):
+        for which in range(2):
+
+            def chip(at):
+                return keep[at, s, which] + came[2 * s + which][at].astype(F32)
+
+            own[s, which] = chip(z)
+            cross[s, which] = chip(z ^ 2)
+            for i, at in enumerate((z ^ 1, z ^ 3)):
+                sends[i, s, which] = chip(at).astype(BF16)
 
 
 def merge_kernel(own, cross, came, total, sends):
@@ -375,9 +387,11 @@
 
     slices = shape((count, 2, g_local, t), BF16)
 
-    def near_of(packed, came, picked):
+    def near_of(packed, came, picked, apart=False):
         kernel = functools.partial(near_kernel, held)
-        return run(kernel, slices, *packed, *came, *picked, name="near")
+        outs = [slices] + [shape(slices.shape[1:], BF16)] * (count if apart else 0)
+        near, *each = run(kernel, outs, *packed, *came, *picked, name="near")
+        return (near, each) if apart else near
 
     before = along(densities, FORTH)
     packed = pack(densities)
@@ -410,8 +424,8 @@
     came_before = [across(packed_before[h], BITS[h][0]) for h in range(2)]
     came_before, total = tie((came_before, total))
     picked_before = pick(packed_before, came_before)
-    near_before = near_of(packed_before, came_before, picked_before)
-    behind = along(near_before, FORTH)
+    near_before, before_each = near_of(packed_before, came_before, picked_before, True)
+    behind = [along(x, FORTH) for x in before_each]
 
     rest_sends, ahead, _ = tie((rest_sends, ahead, near_before))
     rest = [across(rest_sends[h], BITS[h][1]) for h in range(2)]
@@ -424,7 +438,8 @@
     total = product(
         functools.partial(second_kernel, -1), 3, near_before, other_core(both), total
     )
-    behind, rest, total = tie((behind, rest, total))
+    behind[0], _ = tie((behind[0], total))
+    rest, total = tie((rest, total))
     far = run(
         functools.partial(far_kernel, held),
         shape((count, transfers, 2, g_local, t), BF16),
@@ -437,38 +452,39 @@
 
     parts = shape((chips, transfers, 2, 2, t // n_ga, t), F32)
     part = parts.shape[1:]
-    pair = other_core(behind)
-    swaps = []
+    behind[1:], _ = tie((behind[1:], far))
+    stages = []
+    done = total
     for j in range(count):
-        keep, give = run(
+        total, _ = tie((total, done))
+        keep, *gives = run(
             functools.partial(last_kernel, chips, -2, j),
-            [parts, shape(parts.shape, BF16)],
+            [parts] + [shape((chips, 2, t // n_ga, t), BF16)] * (2 * transfers),
             screened,
-            behind,
-            pair,
+            behind[j],
+            other_core(behind[j]),
             total,
             far,
             scratch=[pltpu.VMEM((2 * g_local, 2 * t), BF16)] * 2,
             name="last",
             mib=24,
         )
-        swaps.append((keep, other_core(give)))
-    groups = []
-    for keep, came_j in swaps:
         own, cross, sends = run(
             split_kernel,
             [shape(part, F32), shape(part, F32), shape((2, *part), BF16)],
             keep,
-            came_j,
+            *[other_core(x) for x in gives],
             name="split",
         )
+        if stages:
+            sends, _ = tie((sends, stages[-1][2]))
+        done = own
+        came_j = lax.ppermute(sends, "ga", [(i, i ^ 2) for i in range(n_ga)])
+        stages.append((own, cross, came_j))
+    groups = []
+    for own, cross, came_j in stages:
         own, sends = run(
-            merge_kernel,
-            [shape(part, F32), shape(part, BF16)],
-            own,
-            cross,
-            lax.ppermute(sends, "ga", [(i, i ^ 2) for i in range(n_ga)]),
-            name="merge",
+            merge_kernel, [shape(part, F32), shape(part, BF16)], own, cross, came_j, name="merge"
         )
         groups += [own, lax.ppermute(sends, "ga", [(i, i ^ 4) for i in range(n_ga)])]
     result = shape((count, transfers, 2, t // n_ga, t), F32)

time: 102 us -> 101 us (level)
  waiting for transfers between devices: 53.1 us -> 46.1 us
  starting transfers between devices: 22.6 us -> 28.4 us
    ppermute x2, waiting for transfers between devices: 12.8 us -> 9.57 us  [quick(): came_j = lax.ppermute(sends, 'ga', [(i, i ^ 2) for i in range(n_ga)])]
    ppermute x2, starting transfers between devices: 1.71 us -> 4.11 us  [quick(): lax.ppermute(sends, 'ga', [(i, i ^ 4) for i in range(n_ga)])]
    ppermute x10, waiting for transfers between devices: 19.5 us -> 17.5 us  [across(): return lax.ppermute(x, 'kp', [(i, i ^ bit) for i in range(n_kp)])]
    ppermute x3 -> x4, starting transfers between devices: 5.13 us -> 6.95 us  [along(): lax.ppermute(x, 'ga', [(i, 2 * chips_on[i // 2] + i % 2) for i in range(n...]
    ppermute x5 -> x12, starting transfers between devices: 1.22 us -> 2.88 us  [other_core(): return lax.ppermute(x, 'ga', [(i, i ^ 1) for i in range(n_ga)])]
    ppermute x2, waiting for transfers between devices: 7.69 us -> 6.42 us  [quick(): lax.ppermute(sends, 'ga', [(i, i ^ 4) for i in range(n_ga)])]
    ppermute x3 -> x4, waiting for transfers between devices: 11.5 us -> 10.3 us  [along(): lax.ppermute(x, 'ga', [(i, 2 * chips_on[i // 2] + i % 2) for i in range(n...]
    ppermute x5 -> x12, waiting for transfers between devices: 1.57 us -> 2.3 us  [other_core(): return lax.ppermute(x, 'ga', [(i, i ^ 1) for i in range(n_ga)])]
  transfers between devices with their start and end apart: 22 -> 30, of which waited for: 15 -> 20; matrix products, arithmetic and copies ran while one was open for 0% -> 0% of each run, Pallas kernels for 20% -> 23%
where the time goes in v5:
time: 101 us
  waiting for transfers between devices  46.1 us (46%)
  starting transfers between devices  28.4 us (28%)
  Pallas kernels  24.9 us (25%)
    pallas_call x20, Pallas kernels, run(): pl.pallas_call(body, in_specs=specs or [VMEM] * len(args), out_specs=[VME...  24.9 us
    ppermute x10, waiting for transfers between devices, across(): return lax.ppermute(x, 'kp', [(i, i ^ bit) for i in range(n_kp)])  17.5 us
    ppermute x10, starting transfers between devices, across(): return lax.ppermute(x, 'kp', [(i, i ^ bit) for i in range(n_kp)])  12.8 us
    ppermute x4, waiting for transfers between devices, along(): lax.ppermute(x, 'ga', [(i, 2 * chips_on[i // 2] + i % 2) for i in range(n...  10.3 us
    ppermute x2, waiting for transfers between devices, quick(): came_j = lax.ppermute(sends, 'ga', [(i, i ^ 2) for i in range(n_ga)])  9.57 us
    ppermute x4, starting transfers between devices, along(): lax.ppermute(x, 'ga', [(i, 2 * chips_on[i // 2] + i % 2) for i in range(n...  6.95 us
    ppermute x2, waiting for transfers between devices, quick(): lax.ppermute(sends, 'ga', [(i, i ^ 4) for i in range(n_ga)])  6.42 us
    ppermute x2, starting transfers between devices, quick(): lax.ppermute(sends, 'ga', [(i, i ^ 4) for i in range(n_ga)])  4.11 us
  transfers between devices with their start and end apart: 30, of which 20 were waited for; matrix products, arithmetic and copies ran while one was open for 0% of the time, Pallas kernels for 23%

profile of v5, /device:TPU:0, one launch (start us, length us, event | category | flops | bytes accessed | tf_op | source)
XLA Modules:
  0.0 100.8 jit_solution(3965169852910892060)
XLA Ops:
  2.5 3.0 %collective-permute-start = (bf16[784,256]{1,0:T(8,128)(2,1)S(1)}, bf16[784,256]{1,0:T(8,128)(2,1)S(1)}, u32[]{:S(2)}, u32[]{:S(2)}) collective-permute-start(bf16[784,256]{1,0:T(8,128)(2,1)S(1)} %get-tuple-element.64.packed_0), channel_id=1, source_target_pairs={{0,8},{8,0},{16,24},{24,16},{1,9},{9,1},{17,25},{25,17},{2,10},{10... | collective-permute-start | bytes 1204232 | tf_op jit(solution)/shard_map/ppermute | solution.py:351
  5.5 1.5 %collective-permute-start.1 = (bf16[784,256]{1,0:T(8,128)(2,1)S(1)}, bf16[784,256]{1,0:T(8,128)(2,1)S(1)}, u32[]{:S(2)}, u32[]{:S(2)}) collective-permute-start(bf16[784,256]{1,0:T(8,128)(2,1)S(1)} %get-tuple-element.65.packed_1), channel_id=1, source_target_pairs={{0,16},{8,24},{16,0},{24,8},{1,17},{9,25},{17,1},{25,9},{2,18},{10... | collective-permute-start | bytes 1204232 | tf_op jit(solution)/shard_map/ppermute | solution.py:351
  7.0 1.6 %collective-permute-start.2 = (bf16[2,2,384,256]{3,2,1,0:T(8,128)(2,1)}, bf16[2,2,384,256]{3,2,1,0:T(8,128)(2,1)S(1)}, u32[]{:S(2)}, u32[]{:S(2)}) collective-permute-start(bf16[2,2,384,256]{3,2,1,0:T(8,128)(2,1)} %densities.1), channel_id=1, source_target_pairs={{0,2},{1,3},{2,6},{3,7},{4,0},{5,1},{6,4},{7,5},{8,10},{9,11},{10,... | collective-permute-start | bytes 2359304 | tf_op jit(solution)/shard_map/ppermute | solution.py:357
  8.6 3.8 %load.1.screened = bf16[2,2,384,3072]{3,2,1,0:T(8,128)(2,1)S(1)} custom-call(bf16[2,2,384,3072]{3,2,1,0:T(8,128)(2,1)} %source), custom_call_target="tpu_custom_call" | custom-call | tf_op jit(solution)/shard_map/load/pallas_call | solution.py:30
  12.4 2.4 %collective-permute-done.came_0 = bf16[784,256]{1,0:T(8,128)(2,1)S(1)} collective-permute-done((bf16[784,256]{1,0:T(8,128)(2,1)S(1)}, bf16[784,256]{1,0:T(8,128)(2,1)S(1)}, u32[]{:S(2)}, u32[]{:S(2)}) %collective-permute-start) | collective-permute-done | bytes 401440 | tf_op jit(solution)/shard_map/ppermute | solution.py:351
  16.8 1.6 %collective-permute-start.5 = (bf16[2,2,192,256]{3,2,1,0:T(8,128)(2,1)S(1)}, bf16[2,2,192,256]{3,2,1,0:T(8,128)(2,1)S(1)}, u32[]{:S(2)}, u32[]{:S(2)}) collective-permute-start(bf16[2,2,192,256]{3,2,1,0:T(8,128)(2,1)S(1)} %get-tuple-element.68), channel_id=1, source_target_pairs={{0,16},{8,24},{16,0},{24,8},{1,17},{9,25},{17,1},{25,9},{2,18},{10... | collective-permute-start | bytes 1179656 | tf_op jit(solution)/shard_map/ppermute | solution.py:351
  19.0 7.9 %collective-permute-done.2.densities = bf16[2,2,384,256]{3,2,1,0:T(8,128)(2,1)S(1)} collective-permute-done((bf16[2,2,384,256]{3,2,1,0:T(8,128)(2,1)}, bf16[2,2,384,256]{3,2,1,0:T(8,128)(2,1)S(1)}, u32[]{:S(2)}, u32[]{:S(2)}) %collective-permute-start.2) | collective-permute-done | bytes 786464 | tf_op jit(solution)/shard_map/ppermute | solution.py:357
  29.3 1.8 %collective-permute-start.10 = (bf16[2,2,384,256]{3,2,1,0:T(8,128)(2,1)S(1)}, bf16[2,2,384,256]{3,2,1,0:T(8,128)(2,1)S(1)}, u32[]{:S(2)}, u32[]{:S(2)}) collective-permute-start(bf16[2,2,384,256]{3,2,1,0:T(8,128)(2,1)S(1)} %near.2.own.refs_0_), channel_id=1, source_target_pairs={{0,4},{1,5},{2,0},{3,1},{4,6},{5,7},{6,2},{7,3},{8,12},{9,13},{10,... | collective-permute-start | bytes 2359304 | tf_op jit(solution)/shard_map/ppermute | solution.py:357
  31.1 1.8 %product.3.before = f32[2,384,1024]{2,1,0:T(8,128)S(1)} custom-call(bf16[2,2,384,3072]{3,2,1,0:T(8,128)(2,1)S(1)} %load.1.screened, bf16[2,2,384,256]{3,2,1,0:T(8,128)(2,1)S(1)} %near.2.own.refs_0_, f32[1,384]{1,0:T(1,128)S(1)} %broadcast_in_dim.3.coulomb), custom_call_target="tpu_custom_call" | custom-call | tf_op jit(solution)/shard_map/product/pallas_call | solution.py:30
  32.9 4.2 %collective-permute-done.3.came_0 = bf16[784,256]{1,0:T(8,128)(2,1)S(1)} collective-permute-done((bf16[784,256]{1,0:T(8,128)(2,1)S(1)}, bf16[784,256]{1,0:T(8,128)(2,1)S(1)}, u32[]{:S(2)}, u32[]{:S(2)}) %collective-permute-start.3) | collective-permute-done | bytes 401440 | tf_op jit(solution)/shard_map/ppermute | solution.py:351
  40.0 6.2 %collective-permute-done.7.picked_0 = bf16[2,2,192,256]{3,2,1,0:T(8,128)(2,1)S(1)} collective-permute-done((bf16[2,2,192,256]{3,2,1,0:T(8,128)(2,1)S(1)}, bf16[2,2,192,256]{3,2,1,0:T(8,128)(2,1)S(1)}, u32[]{:S(2)}, u32[]{:S(2)}) %collective-permute-start.7) | collective-permute-done | bytes 393248 | tf_op jit(solution)/shard_map/ppermute | solution.py:351
  48.0 1.7 %collective-permute-start.9 = (bf16[2,384,256]{2,1,0:T(8,128)(2,1)S(1)}, bf16[2,384,256]{2,1,0:T(8,128)(2,1)S(1)}, u32[]{:S(2)}, u32[]{:S(2)}) collective-permute-start(bf16[2,384,256]{2,1,0:T(8,128)(2,1)S(1)} %get-tuple-element.78), channel_id=1, source_target_pairs={{0,2},{1,3},{2,6},{3,7},{4,0},{5,1},{6,4},{7,5},{8,10},{9,11},{10,... | collective-permute-start | bytes 1179656 | tf_op jit(solution)/shard_map/ppermute | solution.py:357
  49.7 1.5 %collective-permute-start.14 = (bf16[3,2,192,256]{3,2,1,0:T(8,128)(2,1)S(1)}, bf16[3,2,192,256]{3,2,1,0:T(8,128)(2,1)S(1)}, u32[]{:S(2)}, u32[]{:S(2)}) collective-permute-start(bf16[3,2,192,256]{3,2,1,0:T(8,128)(2,1)S(1)} %get-tuple-element.85), channel_id=1, source_target_pairs={{0,16},{8,24},{16,0},{24,8},{1,17},{9,25},{17,1},{25,9},{2,18},{10... | collective-permute-start | bytes 1769480 | tf_op jit(solution)/shard_map/ppermute | solution.py:351
  52.8 1.9 %collective-permute-start.22 = (bf16[2,384,256]{2,1,0:T(8,128)(2,1)S(1)}, bf16[2,384,256]{2,1,0:T(8,128)(2,1)S(1)}, u32[]{:S(2)}, u32[]{:S(2)}) collective-permute-start(bf16[2,384,256]{2,1,0:T(8,128)(2,1)S(1)} %get-tuple-element.100), channel_id=1, source_target_pairs={{0,2},{1,3},{2,6},{3,7},{4,0},{5,1},{6,4},{7,5},{8,10},{9,11},{10,... | collective-permute-start | bytes 1179656 | tf_op jit(solution)/shard_map/ppermute | solution.py:357
  54.7 3.0 %product.4.before = f32[2,384,1024]{2,1,0:T(8,128)S(1)} custom-call(bf16[2,2,384,3072]{3,2,1,0:T(8,128)(2,1)S(1)} %load.1.screened, bf16[2,2,384,256]{3,2,1,0:T(8,128)(2,1)S(1)} %collective-permute-done.10.own, bf16[2,2,384,256]{3,2,1,0:T(8,128)(2,1)S(1)} %collective-permute-done.12.pair, ...), custom_call_target="tpu_custom_call", output_to_operand_aliasing={{}: (3, {})} | custom-call | tf_op jit(solution)/shard_map/product/pallas_call | solution.py:30
  57.7 4.6 %product.5.before = f32[2,384,1024]{2,1,0:T(8,128)S(1)} custom-call(bf16[2,2,384,3072]{3,2,1,0:T(8,128)(2,1)S(1)} %load.1.screened, bf16[2,2,384,256]{3,2,1,0:T(8,128)(2,1)S(1)} %get-tuple-element.82.refs_1_.own, bf16[2,2,2,384,256]{4,3,2,1,0:T(8,128)(2,1)S(1)} %collective-permute-done.11.pairs, ...), custom_call_target="tpu_custom_call", output_to_operand_aliasing={{}: (3, {})} | custom-call | tf_op jit(solution)/shard_map/product/pallas_call | solution.py:30
  62.5 2.3 %collective-permute-done.14.rest_0 = bf16[3,2,192,256]{3,2,1,0:T(8,128)(2,1)S(1)} collective-permute-done((bf16[3,2,192,256]{3,2,1,0:T(8,128)(2,1)S(1)}, bf16[3,2,192,256]{3,2,1,0:T(8,128)(2,1)S(1)}, u32[]{:S(2)}, u32[]{:S(2)}) %collective-permute-start.14) | collective-permute-done | bytes 589856 | tf_op jit(solution)/shard_map/ppermute | solution.py:351
  66.1 2.4 %collective-permute-done.22.own = bf16[2,384,256]{2,1,0:T(8,128)(2,1)S(1)} collective-permute-done((bf16[2,384,256]{2,1,0:T(8,128)(2,1)S(1)}, bf16[2,384,256]{2,1,0:T(8,128)(2,1)S(1)}, u32[]{:S(2)}, u32[]{:S(2)}) %collective-permute-start.22) | collective-permute-done | bytes 393248 | tf_op jit(solution)/shard_map/ppermute | solution.py:357
  68.5 2.5 %last.2 = (f32[4,2,2,2,32,256]{5,4,3,2,1,0:T(8,128)S(1)}, bf16[4,2,32,256]{3,2,1,0:T(8,128)(2,1)S(1)}, bf16[4,2,32,256]{3,2,1,0:T(8,128)(2,1)S(1)}, bf16[4,2,32,...) custom-call(bf16[2,2,384,3072]{3,2,1,0:T(8,128)(2,1)S(1)} %load.1.screened, ...), custom_call_target="tpu_custom_call" | custom-call | tf_op jit(solution)/shard_map/last/pallas_call | solution.py:30
  74.3 2.5 %last.3 = (f32[4,2,2,2,32,256]{5,4,3,2,1,0:T(8,128)S(1)}, bf16[4,2,32,256]{3,2,1,0:T(8,128)(2,1)S(1)}, bf16[4,2,32,256]{3,2,1,0:T(8,128)(2,1)S(1)}, bf16[4,2,32,...) custom-call(bf16[2,2,384,3072]{3,2,1,0:T(8,128)(2,1)S(1)} %load.1.screened, ...), custom_call_target="tpu_custom_call" | custom-call | tf_op jit(solution)/shard_map/last/pallas_call | solution.py:30
  79.0 2.9 %collective-permute-done.20.came = bf16[2,2,2,2,32,256]{5,4,3,2,1,0:T(8,128)(2,1)S(1)} collective-permute-done((bf16[2,2,2,2,32,256]{5,4,3,2,1,0:T(8,128)(2,1)S(1)}, bf16[2,2,2,2,32,256]{5,4,3,2,1,0:T(8,128)(2,1)S(1)}, u32[]{:S(2)}, u32[]{:S(2)}) %collective-permute-start.20) | collective-permute-done | bytes 262176 | tf_op jit(solution)/shard_map/ppermute | solution.py:482
  82.8 2.9 %collective-permute-start.21 = (bf16[2,2,2,32,256]{4,3,2,1,0:T(8,128)(2,1)S(1)}, bf16[2,2,2,32,256]{4,3,2,1,0:T(8,128)(2,1)S(1)}, u32[]{:S(2)}, u32[]{:S(2)}) collective-permute-start(bf16[2,2,2,32,256]{4,3,2,1,0:T(8,128)(2,1)S(1)} %get-tuple-element.99), channel_id=1, source_target_pairs={{0,4},{1,5},{2,6},{3,7},{4,0},{5,1},{6,2},{7,3},{8,12},{9,13},{10,... | collective-permute-start | bytes 393224 | tf_op jit(solution)/shard_map/ppermute | solution.py:489
  85.7 6.6 %collective-permute-done.28.came = bf16[2,2,2,2,32,256]{5,4,3,2,1,0:T(8,128)(2,1)S(1)} collective-permute-done((bf16[2,2,2,2,32,256]{5,4,3,2,1,0:T(8,128)(2,1)S(1)}, bf16[2,2,2,2,32,256]{5,4,3,2,1,0:T(8,128)(2,1)S(1)}, u32[]{:S(2)}, u32[]{:S(2)}) %collective-permute-start.28) | collective-permute-done | bytes 262176 | tf_op jit(solution)/shard_map/ppermute | solution.py:482
  93.6 6.4 %collective-permute-done.29.refs_3_ = bf16[2,2,2,32,256]{4,3,2,1,0:T(8,128)(2,1)S(1)} collective-permute-done((bf16[2,2,2,32,256]{4,3,2,1,0:T(8,128)(2,1)S(1)}, bf16[2,2,2,32,256]{4,3,2,1,0:T(8,128)(2,1)S(1)}, u32[]{:S(2)}, u32[]{:S(2)}) %collective-permute-start.29) | collective-permute-done | bytes 131104 | tf_op jit(solution)/shard_map/ppermute | solution.py:489
  (63 shorter events, 22.9 us)
Async XLA Ops:
  2.5 12.3 %collective-permute-start = (bf16[784,256]{1,0:T(8,128)(2,1)S(1)}, bf16[784,256]{1,0:T(8,128)(2,1)S(1)}, u32[]{:S(2)}, u32[]{:S(2)}) collective-permute-start(bf16[784,256]{1,0:T(8,128)(2,1)S(1)} %get-tuple-element.64.packed_0), channel_id=1, source_target_pairs={{0,8},{8,0},{16,24},{24,16},{1,9},{9,1},{17,25},{25,17},{2,10},{10... | collective-permute-start | bytes 1204232 | tf_op jit(solution)/shard_map/ppermute | solution.py:351
  5.5 10.8 %collective-permute-start.1 = (bf16[784,256]{1,0:T(8,128)(2,1)S(1)}, bf16[784,256]{1,0:T(8,128)(2,1)S(1)}, u32[]{:S(2)}, u32[]{:S(2)}) collective-permute-start(bf16[784,256]{1,0:T(8,128)(2,1)S(1)} %get-tuple-element.65.packed_1), channel_id=1, source_target_pairs={{0,16},{8,24},{16,0},{24,8},{1,17},{9,25},{17,1},{25,9},{2,18},{10... | collective-permute-start | bytes 1204232 | tf_op jit(solution)/shard_map/ppermute | solution.py:351
  7.0 19.8 %collective-permute-start.2 = (bf16[2,2,384,256]{3,2,1,0:T(8,128)(2,1)}, bf16[2,2,384,256]{3,2,1,0:T(8,128)(2,1)S(1)}, u32[]{:S(2)}, u32[]{:S(2)}) collective-permute-start(bf16[2,2,384,256]{3,2,1,0:T(8,128)(2,1)} %densities.1), channel_id=1, source_target_pairs={{0,2},{1,3},{2,6},{3,7},{4,0},{5,1},{6,4},{7,5},{8,10},{9,11},{10,... | collective-permute-start | bytes 2359304 | tf_op jit(solution)/shard_map/ppermute | solution.py:357
  16.8 12.0 %collective-permute-start.5 = (bf16[2,2,192,256]{3,2,1,0:T(8,128)(2,1)S(1)}, bf16[2,2,192,256]{3,2,1,0:T(8,128)(2,1)S(1)}, u32[]{:S(2)}, u32[]{:S(2)}) collective-permute-start(bf16[2,2,192,256]{3,2,1,0:T(8,128)(2,1)S(1)} %get-tuple-element.68), channel_id=1, source_target_pairs={{0,16},{8,24},{16,0},{24,8},{1,17},{9,25},{17,1},{25,9},{2,18},{10... | collective-permute-start | bytes 1179656 | tf_op jit(solution)/shard_map/ppermute | solution.py:351
  18.4 10.5 %collective-permute-start.6 = (bf16[2,2,192,256]{3,2,1,0:T(8,128)(2,1)S(1)}, bf16[2,2,192,256]{3,2,1,0:T(8,128)(2,1)S(1)}, u32[]{:S(2)}, u32[]{:S(2)}) collective-permute-start(bf16[2,2,192,256]{3,2,1,0:T(8,128)(2,1)S(1)} %get-tuple-element.69), channel_id=1, source_target_pairs={{0,8},{8,0},{16,24},{24,16},{1,9},{9,1},{17,25},{25,17},{2,10},{10... | collective-permute-start | bytes 1179656 | tf_op jit(solution)/shard_map/ppermute | solution.py:351
  27.4 9.6 %collective-permute-start.3 = (bf16[784,256]{1,0:T(8,128)(2,1)S(1)}, bf16[784,256]{1,0:T(8,128)(2,1)S(1)}, u32[]{:S(2)}, u32[]{:S(2)}) collective-permute-start(bf16[784,256]{1,0:T(8,128)(2,1)S(1)} %get-tuple-element.62.packed_0), channel_id=1, source_target_pairs={{0,8},{8,0},{16,24},{24,16},{1,9},{9,1},{17,25},{25,17},{2,10},{10... | collective-permute-start | bytes 1204232 | tf_op jit(solution)/shard_map/ppermute | solution.py:351
  28.1 9.3 %collective-permute-start.4 = (bf16[784,256]{1,0:T(8,128)(2,1)S(1)}, bf16[784,256]{1,0:T(8,128)(2,1)S(1)}, u32[]{:S(2)}, u32[]{:S(2)}) collective-permute-start(bf16[784,256]{1,0:T(8,128)(2,1)S(1)} %get-tuple-element.63.packed_1), channel_id=1, source_target_pairs={{0,16},{8,24},{16,0},{24,8},{1,17},{9,25},{17,1},{25,9},{2,18},{10... | collective-permute-start | bytes 1204232 | tf_op jit(solution)/shard_map/ppermute | solution.py:351
  29.3 18.1 %collective-permute-start.10 = (bf16[2,2,384,256]{3,2,1,0:T(8,128)(2,1)S(1)}, bf16[2,2,384,256]{3,2,1,0:T(8,128)(2,1)S(1)}, u32[]{:S(2)}, u32[]{:S(2)}) collective-permute-start(bf16[2,2,384,256]{3,2,1,0:T(8,128)(2,1)S(1)} %near.2.own.refs_0_), channel_id=1, source_target_pairs={{0,4},{1,5},{2,0},{3,1},{4,6},{5,7},{6,2},{7,3},{8,12},{9,13},{10,... | collective-permute-start | bytes 2359304 | tf_op jit(solution)/shard_map/ppermute | solution.py:357
  37.9 8.3 %collective-permute-start.7 = (bf16[2,2,192,256]{3,2,1,0:T(8,128)(2,1)S(1)}, bf16[2,2,192,256]{3,2,1,0:T(8,128)(2,1)S(1)}, u32[]{:S(2)}, u32[]{:S(2)}) collective-permute-start(bf16[2,2,192,256]{3,2,1,0:T(8,128)(2,1)S(1)} %get-tuple-element.76), channel_id=1, source_target_pairs={{0,16},{8,24},{16,0},{24,8},{1,17},{9,25},{17,1},{25,9},{2,18},{10... | collective-permute-start | bytes 1179656 | tf_op jit(solution)/shard_map/ppermute | solution.py:351
  38.7 8.2 %collective-permute-start.8 = (bf16[2,2,192,256]{3,2,1,0:T(8,128)(2,1)S(1)}, bf16[2,2,192,256]{3,2,1,0:T(8,128)(2,1)S(1)}, u32[]{:S(2)}, u32[]{:S(2)}) collective-permute-start(bf16[2,2,192,256]{3,2,1,0:T(8,128)(2,1)S(1)} %get-tuple-element.77), channel_id=1, source_target_pairs={{0,8},{8,0},{16,24},{24,16},{1,9},{9,1},{17,25},{25,17},{2,10},{10... | collective-permute-start | bytes 1179656 | tf_op jit(solution)/shard_map/ppermute | solution.py:351
  47.5 10.3 %collective-permute-start.11 = (bf16[2,2,2,384,256]{4,3,2,1,0:T(8,128)(2,1)S(1)}, bf16[2,2,2,384,256]{4,3,2,1,0:T(8,128)(2,1)S(1)}, u32[]{:S(2)}, u32[]{:S(2)}) collective-permute-start(bf16[2,2,2,384,256]{4,3,2,1,0:T(8,128)(2,1)S(1)} %stack.1), channel_id=1, source_target_pairs={{0,1},{1,0},{2,3},{3,2},{4,5},{5,4},{6,7},{7,6},{8,9},{9,8},{10,11... | collective-permute-start | bytes 4718600 | tf_op jit(solution)/shard_map/ppermute | solution.py:354
  47.5 5.2 %collective-permute-start.12 = (bf16[2,2,384,256]{3,2,1,0:T(8,128)(2,1)S(1)}, bf16[2,2,384,256]{3,2,1,0:T(8,128)(2,1)S(1)}, u32[]{:S(2)}, u32[]{:S(2)}) collective-permute-start(bf16[2,2,384,256]{3,2,1,0:T(8,128)(2,1)S(1)} %collective-permute-done.10.own), channel_id=1, source_target_pairs={{0,1},{1,0},{2,3},{3,2},{4,5},{5,4},{6,7},{7,6},{8,9},{9,8},{10,11... | collective-permute-start | bytes 2359304 | tf_op jit(solution)/shard_map/ppermute | solution.py:354
  48.0 14.3 %collective-permute-start.9 = (bf16[2,384,256]{2,1,0:T(8,128)(2,1)S(1)}, bf16[2,384,256]{2,1,0:T(8,128)(2,1)S(1)}, u32[]{:S(2)}, u32[]{:S(2)}) collective-permute-start(bf16[2,384,256]{2,1,0:T(8,128)(2,1)S(1)} %get-tuple-element.78), channel_id=1, source_target_pairs={{0,2},{1,3},{2,6},{3,7},{4,0},{5,1},{6,4},{7,5},{8,10},{9,11},{10,... | collective-permute-start | bytes 1179656 | tf_op jit(solution)/shard_map/ppermute | solution.py:357
  49.7 15.0 %collective-permute-start.14 = (bf16[3,2,192,256]{3,2,1,0:T(8,128)(2,1)S(1)}, bf16[3,2,192,256]{3,2,1,0:T(8,128)(2,1)S(1)}, u32[]{:S(2)}, u32[]{:S(2)}) collective-permute-start(bf16[3,2,192,256]{3,2,1,0:T(8,128)(2,1)S(1)} %get-tuple-element.85), channel_id=1, source_target_pairs={{0,16},{8,24},{16,0},{24,8},{1,17},{9,25},{17,1},{25,9},{2,18},{10... | collective-permute-start | bytes 1769480 | tf_op jit(solution)/shard_map/ppermute | solution.py:351
  51.3 11.2 %collective-permute-start.15 = (bf16[2,2,192,256]{3,2,1,0:T(8,128)(2,1)S(1)}, bf16[2,2,192,256]{3,2,1,0:T(8,128)(2,1)S(1)}, u32[]{:S(2)}, u32[]{:S(2)}) collective-permute-start(bf16[2,2,192,256]{3,2,1,0:T(8,128)(2,1)S(1)} %get-tuple-element.86), channel_id=1, source_target_pairs={{0,8},{8,0},{16,24},{24,16},{1,9},{9,1},{17,25},{25,17},{2,10},{10... | collective-permute-start | bytes 1179656 | tf_op jit(solution)/shard_map/ppermute | solution.py:351
  52.8 15.7 %collective-permute-start.22 = (bf16[2,384,256]{2,1,0:T(8,128)(2,1)S(1)}, bf16[2,384,256]{2,1,0:T(8,128)(2,1)S(1)}, u32[]{:S(2)}, u32[]{:S(2)}) collective-permute-start(bf16[2,384,256]{2,1,0:T(8,128)(2,1)S(1)} %get-tuple-element.100), channel_id=1, source_target_pairs={{0,2},{1,3},{2,6},{3,7},{4,0},{5,1},{6,4},{7,5},{8,10},{9,11},{10,... | collective-permute-start | bytes 1179656 | tf_op jit(solution)/shard_map/ppermute | solution.py:357
  62.4 6.1 %collective-permute-start.13 = (bf16[2,384,256]{2,1,0:T(8,128)(2,1)S(1)}, bf16[2,384,256]{2,1,0:T(8,128)(2,1)S(1)}, u32[]{:S(2)}, u32[]{:S(2)}) collective-permute-start(bf16[2,384,256]{2,1,0:T(8,128)(2,1)S(1)} %collective-permute-done.9.own), channel_id=1, source_target_pairs={{0,1},{1,0},{2,3},{3,2},{4,5},{5,4},{6,7},{7,6},{8,9},{9,8},{10,11... | collective-permute-start | bytes 1179656 | tf_op jit(solution)/shard_map/ppermute | solution.py:354
  68.5 5.9 %collective-permute-start.23 = (bf16[2,384,256]{2,1,0:T(8,128)(2,1)S(1)}, bf16[2,384,256]{2,1,0:T(8,128)(2,1)S(1)}, u32[]{:S(2)}, u32[]{:S(2)}) collective-permute-start(bf16[2,384,256]{2,1,0:T(8,128)(2,1)S(1)} %collective-permute-done.22.own), channel_id=1, source_target_pairs={{0,1},{1,0},{2,3},{3,2},{4,5},{5,4},{6,7},{7,6},{8,9},{9,8},{10,11... | collective-permute-start | bytes 1179656 | tf_op jit(solution)/shard_map/ppermute | solution.py:354
  71.0 1.6 %collective-permute-start.16 = (bf16[4,2,32,256]{3,2,1,0:T(8,128)(2,1)S(1)}, bf16[4,2,32,256]{3,2,1,0:T(8,128)(2,1)S(1)}, u32[]{:S(2)}, u32[]{:S(2)}) collective-permute-start(bf16[4,2,32,256]{3,2,1,0:T(8,128)(2,1)S(1)} %get-tuple-element.91), channel_id=1, source_target_pairs={{0,1},{1,0},{2,3},{3,2},{4,5},{5,4},{6,7},{7,6},{8,9},{9,8},{10,11... | collective-permute-start | bytes 393224 | tf_op jit(solution)/shard_map/ppermute | solution.py:354
  73.5 8.5 %collective-permute-start.20 = (bf16[2,2,2,2,32,256]{5,4,3,2,1,0:T(8,128)(2,1)S(1)}, bf16[2,2,2,2,32,256]{5,4,3,2,1,0:T(8,128)(2,1)S(1)}, u32[]{:S(2)}, u32[]{:S(2)}) collective-permute-start(bf16[2,2,2,2,32,256]{5,4,3,2,1,0:T(8,128)(2,1)S(1)} %get-tuple-element.97), channel_id=1, source_target_pairs={{0,2},{1,3},{2,0},{3,1},{4,6},{5,7},{6,4},{7,5},{8,10},{9,11},{10,... | collective-permute-start | bytes 786440 | tf_op jit(solution)/shard_map/ppermute | solution.py:482
  76.9 1.5 %collective-permute-start.25 = (bf16[4,2,32,256]{3,2,1,0:T(8,128)(2,1)S(1)}, bf16[4,2,32,256]{3,2,1,0:T(8,128)(2,1)S(1)}, u32[]{:S(2)}, u32[]{:S(2)}) collective-permute-start(bf16[4,2,32,256]{3,2,1,0:T(8,128)(2,1)S(1)} %get-tuple-element.105), channel_id=1, source_target_pairs={{0,1},{1,0},{2,3},{3,2},{4,5},{5,4},{6,7},{7,6},{8,9},{9,8},{10,11... | collective-permute-start | bytes 393224 | tf_op jit(solution)/shard_map/ppermute | solution.py:354
  82.0 10.4 %collective-permute-start.28 = (bf16[2,2,2,2,32,256]{5,4,3,2,1,0:T(8,128)(2,1)S(1)}, bf16[2,2,2,2,32,256]{5,4,3,2,1,0:T(8,128)(2,1)S(1)}, u32[]{:S(2)}, u32[]{:S(2)}) collective-permute-start(bf16[2,2,2,2,32,256]{5,4,3,2,1,0:T(8,128)(2,1)S(1)} %get-tuple-element.111), channel_id=1, source_target_pairs={{0,2},{1,3},{2,0},{3,1},{4,6},{5,7},{6,4},{7,5},{8,10},{9,11},{10,... | collective-permute-start | bytes 786440 | tf_op jit(solution)/shard_map/ppermute | solution.py:482
  82.8 10.8 %collective-permute-start.21 = (bf16[2,2,2,32,256]{4,3,2,1,0:T(8,128)(2,1)S(1)}, bf16[2,2,2,32,256]{4,3,2,1,0:T(8,128)(2,1)S(1)}, u32[]{:S(2)}, u32[]{:S(2)}) collective-permute-start(bf16[2,2,2,32,256]{4,3,2,1,0:T(8,128)(2,1)S(1)} %get-tuple-element.99), channel_id=1, source_target_pairs={{0,4},{1,5},{2,6},{3,7},{4,0},{5,1},{6,2},{7,3},{8,12},{9,13},{10,... | collective-permute-start | bytes 393224 | tf_op jit(solution)/shard_map/ppermute | solution.py:489
  92.4 7.6 %collective-permute-start.29 = (bf16[2,2,2,32,256]{4,3,2,1,0:T(8,128)(2,1)S(1)}, bf16[2,2,2,32,256]{4,3,2,1,0:T(8,128)(2,1)S(1)}, u32[]{:S(2)}, u32[]{:S(2)}) collective-permute-start(bf16[2,2,2,32,256]{4,3,2,1,0:T(8,128)(2,1)S(1)} %get-tuple-element.113), channel_id=1, source_target_pairs={{0,4},{1,5},{2,6},{3,7},{4,0},{5,1},{6,2},{7,3},{8,12},{9,13},{10,... | collective-permute-start | bytes 393224 | tf_op jit(solution)/shard_map/ppermute | solution.py:489
  (9 other events, 44.6 us)

commit v6 on v5

--- a/solution.py
+++ b/solution.py
@@ -283,12 +283,17 @@
         total[s] = value + multiply(screened, s, left, g, upper, lower, 2 * g)
 
 
-def last_kernel(chips, steps, j, screened, own, pair, before, far, keep, *refs):
+def last_kernel(chips, steps, j, screened, own, pair_real, pair_imag, before, far, keep, *refs):
     z, core = place()
     g = screened.shape[2]
     t = far.shape[-1]
     *gives, upper, lower = refs
-    lay([(own, core * g), (pair, (1 - core) * g)], upper, lower)
+    lay([(own, core * g)], upper, lower)
+    rows = pl.ds(pl.multiple_of((1 - core) * g, 128), g)
+    upper[rows, :t] = pair_real[...]
+    upper[rows, t:] = pair_imag[...]
+    lower[rows, :t] = -pair_imag[...]
+    lower[rows, t:] = pair_real[...]
     span = 2 * chip_at(z, steps) * g
     first = core == 0
     for s in range(screened.shape[0]):
@@ -452,7 +457,6 @@
 
     parts = shape((chips, transfers, 2, 2, t // n_ga, t), F32)
     part = parts.shape[1:]
-    behind[1:], _ = tie((behind[1:], far))
     stages = []
     done = total
     for j in range(count):
@@ -462,7 +466,7 @@
             [parts] + [shape((chips, 2, t // n_ga, t), BF16)] * (2 * transfers),
             screened,
             behind[j],
-            other_core(behind[j]),
+            *[other_core(behind[j][part]) for part in range(2)],
             total,
             far,
             scratch=[pltpu.VMEM((2 * g_local, 2 * t), BF16)] * 2,
@@ -476,6 +480,8 @@
             *[other_core(x) for x in gives],
             name="split",
         )
+        if j + 1 < count:
+            behind[j + 1], _ = tie((behind[j + 1], keep))
         if stages:
             sends, _ = tie((sends, stages[-1][2]))
         done = own

time: 101 us -> 98.3 us (0.973)
  waiting for transfers between devices: 46.1 us -> 44.1 us
    ppermute x2, starting transfers between devices: 4.11 us -> 0.41 us  [quick(): lax.ppermute(sends, 'ga', [(i, i ^ 4) for i in range(n_ga)])]
    ppermute x4, waiting for transfers between devices: 10.3 us -> 7.91 us  [along(): lax.ppermute(x, 'ga', [(i, 2 * chips_on[i // 2] + i % 2) for i in range(n...]
    ppermute x2, starting transfers between devices: 1.62 us -> 3.74 us  [quick(): came_j = lax.ppermute(sends, 'ga', [(i, i ^ 2) for i in range(n_ga)])]
    ppermute x2, waiting for transfers between devices: 9.57 us -> 10.7 us  [quick(): came_j = lax.ppermute(sends, 'ga', [(i, i ^ 2) for i in range(n_ga)])]
    ppermute x12 -> x14, starting transfers between devices: 2.88 us -> 3.73 us  [other_core(): return lax.ppermute(x, 'ga', [(i, i ^ 1) for i in range(n_ga)])]
    ppermute x12 -> x14, waiting for transfers between devices: 2.3 us -> 1.6 us  [other_core(): return lax.ppermute(x, 'ga', [(i, i ^ 1) for i in range(n_ga)])]
  transfers between devices with their start and end apart: 30 -> 32, of which waited for: 20 -> 18; matrix products, arithmetic and copies ran while one was open for 0% -> 0% of each run, Pallas kernels for 23% -> 23%
where the time goes in v6:
time: 98.3 us; the launch traced here: 98.1 us
  waiting for transfers between devices  44.1 us (45%)
  starting transfers between devices  27.6 us (28%)
  Pallas kernels  24.9 us (25%)
    pallas_call x20, Pallas kernels, run(): pl.pallas_call(body, in_specs=specs or [VMEM] * len(args), out_specs=[VME...  24.9 us
    ppermute x10, waiting for transfers between devices, across(): return lax.ppermute(x, 'kp', [(i, i ^ bit) for i in range(n_kp)])  17 us
    ppermute x10, starting transfers between devices, across(): return lax.ppermute(x, 'kp', [(i, i ^ bit) for i in range(n_kp)])  12.7 us
    ppermute x2, waiting for transfers between devices, quick(): came_j = lax.ppermute(sends, 'ga', [(i, i ^ 2) for i in range(n_ga)])  10.7 us
    ppermute x4, waiting for transfers between devices, along(): lax.ppermute(x, 'ga', [(i, 2 * chips_on[i // 2] + i % 2) for i in range(n...  7.91 us
    ppermute x4, starting transfers between devices, along(): lax.ppermute(x, 'ga', [(i, 2 * chips_on[i // 2] + i % 2) for i in range(n...  6.98 us
    ppermute x2, waiting for transfers between devices, quick(): lax.ppermute(sends, 'ga', [(i, i ^ 4) for i in range(n_ga)])  6.8 us
    ppermute x2, starting transfers between devices, quick(): came_j = lax.ppermute(sends, 'ga', [(i, i ^ 2) for i in range(n_ga)])  3.74 us
  transfers between devices with their start and end apart: 32, of which 18 were waited for; matrix products, arithmetic and copies ran while one was open for 0% of the time, Pallas kernels for 23%

profile of v6, /device:TPU:0, one launch (start us, length us, event | category | flops | bytes accessed | tf_op | source)
XLA Modules:
  0.0 98.1 jit_solution(7285854948568102548)
XLA Ops:
  2.5 3.0 %collective-permute-start = (bf16[784,256]{1,0:T(8,128)(2,1)S(1)}, bf16[784,256]{1,0:T(8,128)(2,1)S(1)}, u32[]{:S(2)}, u32[]{:S(2)}) collective-permute-start(bf16[784,256]{1,0:T(8,128)(2,1)S(1)} %get-tuple-element.64.packed_0), channel_id=1, source_target_pairs={{0,8},{8,0},{16,24},{24,16},{1,9},{9,1},{17,25},{25,17},{2,10},{10... | collective-permute-start | bytes 1204232 | tf_op jit(solution)/shard_map/ppermute | solution.py:356
  5.5 1.5 %collective-permute-start.1 = (bf16[784,256]{1,0:T(8,128)(2,1)S(1)}, bf16[784,256]{1,0:T(8,128)(2,1)S(1)}, u32[]{:S(2)}, u32[]{:S(2)}) collective-permute-start(bf16[784,256]{1,0:T(8,128)(2,1)S(1)} %get-tuple-element.65.packed_1), channel_id=1, source_target_pairs={{0,16},{8,24},{16,0},{24,8},{1,17},{9,25},{17,1},{25,9},{2,18},{10... | collective-permute-start | bytes 1204232 | tf_op jit(solution)/shard_map/ppermute | solution.py:356
  7.0 1.6 %collective-permute-start.2 = (bf16[2,2,384,256]{3,2,1,0:T(8,128)(2,1)}, bf16[2,2,384,256]{3,2,1,0:T(8,128)(2,1)S(1)}, u32[]{:S(2)}, u32[]{:S(2)}) collective-permute-start(bf16[2,2,384,256]{3,2,1,0:T(8,128)(2,1)} %densities.1), channel_id=1, source_target_pairs={{0,2},{1,3},{2,6},{3,7},{4,0},{5,1},{6,4},{7,5},{8,10},{9,11},{10,... | collective-permute-start | bytes 2359304 | tf_op jit(solution)/shard_map/ppermute | solution.py:362
  8.6 3.8 %load.1.screened = bf16[2,2,384,3072]{3,2,1,0:T(8,128)(2,1)S(1)} custom-call(bf16[2,2,384,3072]{3,2,1,0:T(8,128)(2,1)} %source), custom_call_target="tpu_custom_call" | custom-call | tf_op jit(solution)/shard_map/load/pallas_call | solution.py:30
  12.4 2.4 %collective-permute-done.came_0 = bf16[784,256]{1,0:T(8,128)(2,1)S(1)} collective-permute-done((bf16[784,256]{1,0:T(8,128)(2,1)S(1)}, bf16[784,256]{1,0:T(8,128)(2,1)S(1)}, u32[]{:S(2)}, u32[]{:S(2)}) %collective-permute-start) | collective-permute-done | bytes 401440 | tf_op jit(solution)/shard_map/ppermute | solution.py:356
  16.9 1.6 %collective-permute-start.5 = (bf16[2,2,192,256]{3,2,1,0:T(8,128)(2,1)S(1)}, bf16[2,2,192,256]{3,2,1,0:T(8,128)(2,1)S(1)}, u32[]{:S(2)}, u32[]{:S(2)}) collective-permute-start(bf16[2,2,192,256]{3,2,1,0:T(8,128)(2,1)S(1)} %get-tuple-element.68), channel_id=1, source_target_pairs={{0,16},{8,24},{16,0},{24,8},{1,17},{9,25},{17,1},{25,9},{2,18},{10... | collective-permute-start | bytes 1179656 | tf_op jit(solution)/shard_map/ppermute | solution.py:356
  18.9 7.9 %collective-permute-done.2.densities = bf16[2,2,384,256]{3,2,1,0:T(8,128)(2,1)S(1)} collective-permute-done((bf16[2,2,384,256]{3,2,1,0:T(8,128)(2,1)}, bf16[2,2,384,256]{3,2,1,0:T(8,128)(2,1)S(1)}, u32[]{:S(2)}, u32[]{:S(2)}) %collective-permute-start.2) | collective-permute-done | bytes 786464 | tf_op jit(solution)/shard_map/ppermute | solution.py:362
  29.3 1.8 %collective-permute-start.10 = (bf16[2,2,384,256]{3,2,1,0:T(8,128)(2,1)S(1)}, bf16[2,2,384,256]{3,2,1,0:T(8,128)(2,1)S(1)}, u32[]{:S(2)}, u32[]{:S(2)}) collective-permute-start(bf16[2,2,384,256]{3,2,1,0:T(8,128)(2,1)S(1)} %near.2.own.refs_0_), channel_id=1, source_target_pairs={{0,4},{1,5},{2,0},{3,1},{4,6},{5,7},{6,2},{7,3},{8,12},{9,13},{10,... | collective-permute-start | bytes 2359304 | tf_op jit(solution)/shard_map/ppermute | solution.py:362
  31.1 1.8 %product.3.before = f32[2,384,1024]{2,1,0:T(8,128)S(1)} custom-call(bf16[2,2,384,3072]{3,2,1,0:T(8,128)(2,1)S(1)} %load.1.screened, bf16[2,2,384,256]{3,2,1,0:T(8,128)(2,1)S(1)} %near.2.own.refs_0_, f32[1,384]{1,0:T(1,128)S(1)} %broadcast_in_dim.3.coulomb), custom_call_target="tpu_custom_call" | custom-call | tf_op jit(solution)/shard_map/product/pallas_call | solution.py:30
  32.9 4.2 %collective-permute-done.3.came_0 = bf16[784,256]{1,0:T(8,128)(2,1)S(1)} collective-permute-done((bf16[784,256]{1,0:T(8,128)(2,1)S(1)}, bf16[784,256]{1,0:T(8,128)(2,1)S(1)}, u32[]{:S(2)}, u32[]{:S(2)}) %collective-permute-start.3) | collective-permute-done | bytes 401440 | tf_op jit(solution)/shard_map/ppermute | solution.py:356
  39.9 6.2 %collective-permute-done.7.picked_0 = bf16[2,2,192,256]{3,2,1,0:T(8,128)(2,1)S(1)} collective-permute-done((bf16[2,2,192,256]{3,2,1,0:T(8,128)(2,1)S(1)}, bf16[2,2,192,256]{3,2,1,0:T(8,128)(2,1)S(1)}, u32[]{:S(2)}, u32[]{:S(2)}) %collective-permute-start.7) | collective-permute-done | bytes 393248 | tf_op jit(solution)/shard_map/ppermute | solution.py:356
  48.0 1.7 %collective-permute-start.9 = (bf16[2,384,256]{2,1,0:T(8,128)(2,1)S(1)}, bf16[2,384,256]{2,1,0:T(8,128)(2,1)S(1)}, u32[]{:S(2)}, u32[]{:S(2)}) collective-permute-start(bf16[2,384,256]{2,1,0:T(8,128)(2,1)S(1)} %get-tuple-element.78), channel_id=1, source_target_pairs={{0,2},{1,3},{2,6},{3,7},{4,0},{5,1},{6,4},{7,5},{8,10},{9,11},{10,... | collective-permute-start | bytes 1179656 | tf_op jit(solution)/shard_map/ppermute | solution.py:362
  49.7 1.5 %collective-permute-start.15 = (bf16[3,2,192,256]{3,2,1,0:T(8,128)(2,1)S(1)}, bf16[3,2,192,256]{3,2,1,0:T(8,128)(2,1)S(1)}, u32[]{:S(2)}, u32[]{:S(2)}) collective-permute-start(bf16[3,2,192,256]{3,2,1,0:T(8,128)(2,1)S(1)} %get-tuple-element.85), channel_id=1, source_target_pairs={{0,16},{8,24},{16,0},{24,8},{1,17},{9,25},{17,1},{25,9},{2,18},{10... | collective-permute-start | bytes 1769480 | tf_op jit(solution)/shard_map/ppermute | solution.py:356
  52.8 1.9 %collective-permute-start.23 = (bf16[2,384,256]{2,1,0:T(8,128)(2,1)S(1)}, bf16[2,384,256]{2,1,0:T(8,128)(2,1)S(1)}, u32[]{:S(2)}, u32[]{:S(2)}) collective-permute-start(bf16[2,384,256]{2,1,0:T(8,128)(2,1)S(1)} %get-tuple-element.100), channel_id=1, source_target_pairs={{0,2},{1,3},{2,6},{3,7},{4,0},{5,1},{6,4},{7,5},{8,10},{9,11},{10,... | collective-permute-start | bytes 1179656 | tf_op jit(solution)/shard_map/ppermute | solution.py:362
  54.7 3.0 %product.4.before = f32[2,384,1024]{2,1,0:T(8,128)S(1)} custom-call(bf16[2,2,384,3072]{3,2,1,0:T(8,128)(2,1)S(1)} %load.1.screened, bf16[2,2,384,256]{3,2,1,0:T(8,128)(2,1)S(1)} %collective-permute-done.10.own, bf16[2,2,384,256]{3,2,1,0:T(8,128)(2,1)S(1)} %collective-permute-done.12.pair, ...), custom_call_target="tpu_custom_call", output_to_operand_aliasing={{}: (3, {})} | custom-call | tf_op jit(solution)/shard_map/product/pallas_call | solution.py:30
  57.7 4.6 %product.5.before = f32[2,384,1024]{2,1,0:T(8,128)S(1)} custom-call(bf16[2,2,384,3072]{3,2,1,0:T(8,128)(2,1)S(1)} %load.1.screened, bf16[2,2,384,256]{3,2,1,0:T(8,128)(2,1)S(1)} %get-tuple-element.82.refs_1_.own, bf16[2,2,2,384,256]{4,3,2,1,0:T(8,128)(2,1)S(1)} %collective-permute-done.11.pairs, ...), custom_call_target="tpu_custom_call", output_to_operand_aliasing={{}: (3, {})} | custom-call | tf_op jit(solution)/shard_map/product/pallas_call | solution.py:30
  63.0 1.8 %collective-permute-done.15.rest_0 = bf16[3,2,192,256]{3,2,1,0:T(8,128)(2,1)S(1)} collective-permute-done((bf16[3,2,192,256]{3,2,1,0:T(8,128)(2,1)S(1)}, bf16[3,2,192,256]{3,2,1,0:T(8,128)(2,1)S(1)}, u32[]{:S(2)}, u32[]{:S(2)}) %collective-permute-start.15) | collective-permute-done | bytes 589856 | tf_op jit(solution)/shard_map/ppermute | solution.py:356
  66.1 2.5 %last.2 = (f32[4,2,2,2,32,256]{5,4,3,2,1,0:T(8,128)S(1)}, bf16[4,2,32,256]{3,2,1,0:T(8,128)(2,1)S(1)}, bf16[4,2,32,256]{3,2,1,0:T(8,128)(2,1)S(1)}, bf16[4,2,32,...) custom-call(bf16[2,2,384,3072]{3,2,1,0:T(8,128)(2,1)S(1)} %load.1.screened, ...), custom_call_target="tpu_custom_call" | custom-call | tf_op jit(solution)/shard_map/last/pallas_call | solution.py:30
  70.8 2.0 %collective-permute-start.21 = (bf16[2,2,2,2,32,256]{5,4,3,2,1,0:T(8,128)(2,1)S(1)}, bf16[2,2,2,2,32,256]{5,4,3,2,1,0:T(8,128)(2,1)S(1)}, u32[]{:S(2)}, u32[]{:S(2)}) collective-permute-start(bf16[2,2,2,2,32,256]{5,4,3,2,1,0:T(8,128)(2,1)S(1)} %get-tuple-element.97), channel_id=1, source_target_pairs={{0,2},{1,3},{2,0},{3,1},{4,6},{5,7},{6,4},{7,5},{8,10},{9,11},{10,... | collective-permute-start | bytes 786440 | tf_op jit(solution)/shard_map/ppermute | solution.py:488
  72.8 2.5 %last.3 = (f32[4,2,2,2,32,256]{5,4,3,2,1,0:T(8,128)S(1)}, bf16[4,2,32,256]{3,2,1,0:T(8,128)(2,1)S(1)}, bf16[4,2,32,256]{3,2,1,0:T(8,128)(2,1)S(1)}, bf16[4,2,32,...) custom-call(bf16[2,2,384,3072]{3,2,1,0:T(8,128)(2,1)S(1)} %load.1.screened, ...), custom_call_target="tpu_custom_call" | custom-call | tf_op jit(solution)/shard_map/last/pallas_call | solution.py:30
  77.5 2.1 %collective-permute-done.21.came = bf16[2,2,2,2,32,256]{5,4,3,2,1,0:T(8,128)(2,1)S(1)} collective-permute-done((bf16[2,2,2,2,32,256]{5,4,3,2,1,0:T(8,128)(2,1)S(1)}, bf16[2,2,2,2,32,256]{5,4,3,2,1,0:T(8,128)(2,1)S(1)}, u32[]{:S(2)}, u32[]{:S(2)}) %collective-permute-start.21) | collective-permute-done | bytes 262176 | tf_op jit(solution)/shard_map/ppermute | solution.py:488
  79.6 1.7 %collective-permute-start.30 = (bf16[2,2,2,2,32,256]{5,4,3,2,1,0:T(8,128)(2,1)S(1)}, bf16[2,2,2,2,32,256]{5,4,3,2,1,0:T(8,128)(2,1)S(1)}, u32[]{:S(2)}, u32[]{:S(2)}) collective-permute-start(bf16[2,2,2,2,32,256]{5,4,3,2,1,0:T(8,128)(2,1)S(1)} %get-tuple-element.111), channel_id=1, source_target_pairs={{0,2},{1,3},{2,0},{3,1},{4,6},{5,7},{6,4},{7,5},{8,10},{9,11},{10,... | collective-permute-start | bytes 786440 | tf_op jit(solution)/shard_map/ppermute | solution.py:488
  81.7 8.6 %collective-permute-done.30.came = bf16[2,2,2,2,32,256]{5,4,3,2,1,0:T(8,128)(2,1)S(1)} collective-permute-done((bf16[2,2,2,2,32,256]{5,4,3,2,1,0:T(8,128)(2,1)S(1)}, bf16[2,2,2,2,32,256]{5,4,3,2,1,0:T(8,128)(2,1)S(1)}, u32[]{:S(2)}, u32[]{:S(2)}) %collective-permute-start.30) | collective-permute-done | bytes 262176 | tf_op jit(solution)/shard_map/ppermute | solution.py:488
  90.5 6.8 %collective-permute-done.31.refs_3_ = bf16[2,2,2,32,256]{4,3,2,1,0:T(8,128)(2,1)S(1)} collective-permute-done((bf16[2,2,2,32,256]{4,3,2,1,0:T(8,128)(2,1)S(1)}, bf16[2,2,2,32,256]{4,3,2,1,0:T(8,128)(2,1)S(1)}, u32[]{:S(2)}, u32[]{:S(2)}) %collective-permute-start.31) | collective-permute-done | bytes 131104 | tf_op jit(solution)/shard_map/ppermute | solution.py:495
  (69 shorter events, 20.6 us)
Async XLA Ops:
  2.5 12.3 %collective-permute-start = (bf16[784,256]{1,0:T(8,128)(2,1)S(1)}, bf16[784,256]{1,0:T(8,128)(2,1)S(1)}, u32[]{:S(2)}, u32[]{:S(2)}) collective-permute-start(bf16[784,256]{1,0:T(8,128)(2,1)S(1)} %get-tuple-element.64.packed_0), channel_id=1, source_target_pairs={{0,8},{8,0},{16,24},{24,16},{1,9},{9,1},{17,25},{25,17},{2,10},{10... | collective-permute-start | bytes 1204232 | tf_op jit(solution)/shard_map/ppermute | solution.py:356
  5.5 10.8 %collective-permute-start.1 = (bf16[784,256]{1,0:T(8,128)(2,1)S(1)}, bf16[784,256]{1,0:T(8,128)(2,1)S(1)}, u32[]{:S(2)}, u32[]{:S(2)}) collective-permute-start(bf16[784,256]{1,0:T(8,128)(2,1)S(1)} %get-tuple-element.65.packed_1), channel_id=1, source_target_pairs={{0,16},{8,24},{16,0},{24,8},{1,17},{9,25},{17,1},{25,9},{2,18},{10... | collective-permute-start | bytes 1204232 | tf_op jit(solution)/shard_map/ppermute | solution.py:356
  7.0 19.8 %collective-permute-start.2 = (bf16[2,2,384,256]{3,2,1,0:T(8,128)(2,1)}, bf16[2,2,384,256]{3,2,1,0:T(8,128)(2,1)S(1)}, u32[]{:S(2)}, u32[]{:S(2)}) collective-permute-start(bf16[2,2,384,256]{3,2,1,0:T(8,128)(2,1)} %densities.1), channel_id=1, source_target_pairs={{0,2},{1,3},{2,6},{3,7},{4,0},{5,1},{6,4},{7,5},{8,10},{9,11},{10,... | collective-permute-start | bytes 2359304 | tf_op jit(solution)/shard_map/ppermute | solution.py:362
  16.9 12.0 %collective-permute-start.5 = (bf16[2,2,192,256]{3,2,1,0:T(8,128)(2,1)S(1)}, bf16[2,2,192,256]{3,2,1,0:T(8,128)(2,1)S(1)}, u32[]{:S(2)}, u32[]{:S(2)}) collective-permute-start(bf16[2,2,192,256]{3,2,1,0:T(8,128)(2,1)S(1)} %get-tuple-element.68), channel_id=1, source_target_pairs={{0,16},{8,24},{16,0},{24,8},{1,17},{9,25},{17,1},{25,9},{2,18},{10... | collective-permute-start | bytes 1179656 | tf_op jit(solution)/shard_map/ppermute | solution.py:356
  18.4 10.5 %collective-permute-start.6 = (bf16[2,2,192,256]{3,2,1,0:T(8,128)(2,1)S(1)}, bf16[2,2,192,256]{3,2,1,0:T(8,128)(2,1)S(1)}, u32[]{:S(2)}, u32[]{:S(2)}) collective-permute-start(bf16[2,2,192,256]{3,2,1,0:T(8,128)(2,1)S(1)} %get-tuple-element.69), channel_id=1, source_target_pairs={{0,8},{8,0},{16,24},{24,16},{1,9},{9,1},{17,25},{25,17},{2,10},{10... | collective-permute-start | bytes 1179656 | tf_op jit(solution)/shard_map/ppermute | solution.py:356
  27.4 9.6 %collective-permute-start.3 = (bf16[784,256]{1,0:T(8,128)(2,1)S(1)}, bf16[784,256]{1,0:T(8,128)(2,1)S(1)}, u32[]{:S(2)}, u32[]{:S(2)}) collective-permute-start(bf16[784,256]{1,0:T(8,128)(2,1)S(1)} %get-tuple-element.62.packed_0), channel_id=1, source_target_pairs={{0,8},{8,0},{16,24},{24,16},{1,9},{9,1},{17,25},{25,17},{2,10},{10... | collective-permute-start | bytes 1204232 | tf_op jit(solution)/shard_map/ppermute | solution.py:356
  28.1 9.3 %collective-permute-start.4 = (bf16[784,256]{1,0:T(8,128)(2,1)S(1)}, bf16[784,256]{1,0:T(8,128)(2,1)S(1)}, u32[]{:S(2)}, u32[]{:S(2)}) collective-permute-start(bf16[784,256]{1,0:T(8,128)(2,1)S(1)} %get-tuple-element.63.packed_1), channel_id=1, source_target_pairs={{0,16},{8,24},{16,0},{24,8},{1,17},{9,25},{17,1},{25,9},{2,18},{10... | collective-permute-start | bytes 1204232 | tf_op jit(solution)/shard_map/ppermute | solution.py:356
  29.3 18.1 %collective-permute-start.10 = (bf16[2,2,384,256]{3,2,1,0:T(8,128)(2,1)S(1)}, bf16[2,2,384,256]{3,2,1,0:T(8,128)(2,1)S(1)}, u32[]{:S(2)}, u32[]{:S(2)}) collective-permute-start(bf16[2,2,384,256]{3,2,1,0:T(8,128)(2,1)S(1)} %near.2.own.refs_0_), channel_id=1, source_target_pairs={{0,4},{1,5},{2,0},{3,1},{4,6},{5,7},{6,2},{7,3},{8,12},{9,13},{10,... | collective-permute-start | bytes 2359304 | tf_op jit(solution)/shard_map/ppermute | solution.py:362
  37.9 8.3 %collective-permute-start.7 = (bf16[2,2,192,256]{3,2,1,0:T(8,128)(2,1)S(1)}, bf16[2,2,192,256]{3,2,1,0:T(8,128)(2,1)S(1)}, u32[]{:S(2)}, u32[]{:S(2)}) collective-permute-start(bf16[2,2,192,256]{3,2,1,0:T(8,128)(2,1)S(1)} %get-tuple-element.76), channel_id=1, source_target_pairs={{0,16},{8,24},{16,0},{24,8},{1,17},{9,25},{17,1},{25,9},{2,18},{10... | collective-permute-start | bytes 1179656 | tf_op jit(solution)/shard_map/ppermute | solution.py:356
  38.7 8.2 %collective-permute-start.8 = (bf16[2,2,192,256]{3,2,1,0:T(8,128)(2,1)S(1)}, bf16[2,2,192,256]{3,2,1,0:T(8,128)(2,1)S(1)}, u32[]{:S(2)}, u32[]{:S(2)}) collective-permute-start(bf16[2,2,192,256]{3,2,1,0:T(8,128)(2,1)S(1)} %get-tuple-element.77), channel_id=1, source_target_pairs={{0,8},{8,0},{16,24},{24,16},{1,9},{9,1},{17,25},{25,17},{2,10},{10... | collective-permute-start | bytes 1179656 | tf_op jit(solution)/shard_map/ppermute | solution.py:356
  47.5 10.3 %collective-permute-start.11 = (bf16[2,2,2,384,256]{4,3,2,1,0:T(8,128)(2,1)S(1)}, bf16[2,2,2,384,256]{4,3,2,1,0:T(8,128)(2,1)S(1)}, u32[]{:S(2)}, u32[]{:S(2)}) collective-permute-start(bf16[2,2,2,384,256]{4,3,2,1,0:T(8,128)(2,1)S(1)} %stack.1), channel_id=1, source_target_pairs={{0,1},{1,0},{2,3},{3,2},{4,5},{5,4},{6,7},{7,6},{8,9},{9,8},{10,11... | collective-permute-start | bytes 4718600 | tf_op jit(solution)/shard_map/ppermute | solution.py:359
  47.5 5.2 %collective-permute-start.12 = (bf16[2,2,384,256]{3,2,1,0:T(8,128)(2,1)S(1)}, bf16[2,2,384,256]{3,2,1,0:T(8,128)(2,1)S(1)}, u32[]{:S(2)}, u32[]{:S(2)}) collective-permute-start(bf16[2,2,384,256]{3,2,1,0:T(8,128)(2,1)S(1)} %collective-permute-done.10.own), channel_id=1, source_target_pairs={{0,1},{1,0},{2,3},{3,2},{4,5},{5,4},{6,7},{7,6},{8,9},{9,8},{10,11... | collective-permute-start | bytes 2359304 | tf_op jit(solution)/shard_map/ppermute | solution.py:359
  48.0 14.3 %collective-permute-start.9 = (bf16[2,384,256]{2,1,0:T(8,128)(2,1)S(1)}, bf16[2,384,256]{2,1,0:T(8,128)(2,1)S(1)}, u32[]{:S(2)}, u32[]{:S(2)}) collective-permute-start(bf16[2,384,256]{2,1,0:T(8,128)(2,1)S(1)} %get-tuple-element.78), channel_id=1, source_target_pairs={{0,2},{1,3},{2,6},{3,7},{4,0},{5,1},{6,4},{7,5},{8,10},{9,11},{10,... | collective-permute-start | bytes 1179656 | tf_op jit(solution)/shard_map/ppermute | solution.py:362
  49.7 15.0 %collective-permute-start.15 = (bf16[3,2,192,256]{3,2,1,0:T(8,128)(2,1)S(1)}, bf16[3,2,192,256]{3,2,1,0:T(8,128)(2,1)S(1)}, u32[]{:S(2)}, u32[]{:S(2)}) collective-permute-start(bf16[3,2,192,256]{3,2,1,0:T(8,128)(2,1)S(1)} %get-tuple-element.85), channel_id=1, source_target_pairs={{0,16},{8,24},{16,0},{24,8},{1,17},{9,25},{17,1},{25,9},{2,18},{10... | collective-permute-start | bytes 1769480 | tf_op jit(solution)/shard_map/ppermute | solution.py:356
  51.3 11.7 %collective-permute-start.16 = (bf16[2,2,192,256]{3,2,1,0:T(8,128)(2,1)S(1)}, bf16[2,2,192,256]{3,2,1,0:T(8,128)(2,1)S(1)}, u32[]{:S(2)}, u32[]{:S(2)}) collective-permute-start(bf16[2,2,192,256]{3,2,1,0:T(8,128)(2,1)S(1)} %get-tuple-element.86), channel_id=1, source_target_pairs={{0,8},{8,0},{16,24},{24,16},{1,9},{9,1},{17,25},{25,17},{2,10},{10... | collective-permute-start | bytes 1179656 | tf_op jit(solution)/shard_map/ppermute | solution.py:356
  52.8 16.9 %collective-permute-start.23 = (bf16[2,384,256]{2,1,0:T(8,128)(2,1)S(1)}, bf16[2,384,256]{2,1,0:T(8,128)(2,1)S(1)}, u32[]{:S(2)}, u32[]{:S(2)}) collective-permute-start(bf16[2,384,256]{2,1,0:T(8,128)(2,1)S(1)} %get-tuple-element.100), channel_id=1, source_target_pairs={{0,2},{1,3},{2,6},{3,7},{4,0},{5,1},{6,4},{7,5},{8,10},{9,11},{10,... | collective-permute-start | bytes 1179656 | tf_op jit(solution)/shard_map/ppermute | solution.py:362
  62.4 3.7 %collective-permute-start.13 = (bf16[384,256]{1,0:T(8,128)(2,1)S(1)}, bf16[384,256]{1,0:T(8,128)(2,1)S(1)}, u32[]{:S(2)}, u32[]{:S(2)}) collective-permute-start(bf16[384,256]{1,0:T(8,128)(2,1)S(1)} %get-tuple-element.117), channel_id=1, source_target_pairs={{0,1},{1,0},{2,3},{3,2},{4,5},{5,4},{6,7},{7,6},{8,9},{9,8},{10,11... | collective-permute-start | bytes 589832 | tf_op jit(solution)/shard_map/ppermute | solution.py:359
  62.5 3.6 %collective-permute-start.14 = (bf16[384,256]{1,0:T(8,128)(2,1)S(1)}, bf16[384,256]{1,0:T(8,128)(2,1)S(1)}, u32[]{:S(2)}, u32[]{:S(2)}) collective-permute-start(bf16[384,256]{1,0:T(8,128)(2,1)S(1)} %get-tuple-element.116), channel_id=1, source_target_pairs={{0,1},{1,0},{2,3},{3,2},{4,5},{5,4},{6,7},{7,6},{8,9},{9,8},{10,11... | collective-permute-start | bytes 589832 | tf_op jit(solution)/shard_map/ppermute | solution.py:359
  69.7 3.1 %collective-permute-start.24 = (bf16[384,256]{1,0:T(8,128)(2,1)S(1)}, bf16[384,256]{1,0:T(8,128)(2,1)S(1)}, u32[]{:S(2)}, u32[]{:S(2)}) collective-permute-start(bf16[384,256]{1,0:T(8,128)(2,1)S(1)} %get-tuple-element.115), channel_id=1, source_target_pairs={{0,1},{1,0},{2,3},{3,2},{4,5},{5,4},{6,7},{7,6},{8,9},{9,8},{10,11... | collective-permute-start | bytes 589832 | tf_op jit(solution)/shard_map/ppermute | solution.py:359
  70.0 2.8 %collective-permute-start.25 = (bf16[384,256]{1,0:T(8,128)(2,1)S(1)}, bf16[384,256]{1,0:T(8,128)(2,1)S(1)}, u32[]{:S(2)}, u32[]{:S(2)}) collective-permute-start(bf16[384,256]{1,0:T(8,128)(2,1)S(1)} %get-tuple-element.114), channel_id=1, source_target_pairs={{0,1},{1,0},{2,3},{3,2},{4,5},{5,4},{6,7},{7,6},{8,9},{9,8},{10,11... | collective-permute-start | bytes 589832 | tf_op jit(solution)/shard_map/ppermute | solution.py:359
  70.8 8.8 %collective-permute-start.21 = (bf16[2,2,2,2,32,256]{5,4,3,2,1,0:T(8,128)(2,1)S(1)}, bf16[2,2,2,2,32,256]{5,4,3,2,1,0:T(8,128)(2,1)S(1)}, u32[]{:S(2)}, u32[]{:S(2)}) collective-permute-start(bf16[2,2,2,2,32,256]{5,4,3,2,1,0:T(8,128)(2,1)S(1)} %get-tuple-element.97), channel_id=1, source_target_pairs={{0,2},{1,3},{2,0},{3,1},{4,6},{5,7},{6,4},{7,5},{8,10},{9,11},{10,... | collective-permute-start | bytes 786440 | tf_op jit(solution)/shard_map/ppermute | solution.py:488
  79.6 10.8 %collective-permute-start.30 = (bf16[2,2,2,2,32,256]{5,4,3,2,1,0:T(8,128)(2,1)S(1)}, bf16[2,2,2,2,32,256]{5,4,3,2,1,0:T(8,128)(2,1)S(1)}, u32[]{:S(2)}, u32[]{:S(2)}) collective-permute-start(bf16[2,2,2,2,32,256]{5,4,3,2,1,0:T(8,128)(2,1)S(1)} %get-tuple-element.111), channel_id=1, source_target_pairs={{0,2},{1,3},{2,0},{3,1},{4,6},{5,7},{6,4},{7,5},{8,10},{9,11},{10,... | collective-permute-start | bytes 786440 | tf_op jit(solution)/shard_map/ppermute | solution.py:488
  81.4 9.1 %collective-permute-start.22 = (bf16[2,2,2,32,256]{4,3,2,1,0:T(8,128)(2,1)S(1)}, bf16[2,2,2,32,256]{4,3,2,1,0:T(8,128)(2,1)S(1)}, u32[]{:S(2)}, u32[]{:S(2)}) collective-permute-start(bf16[2,2,2,32,256]{4,3,2,1,0:T(8,128)(2,1)S(1)} %get-tuple-element.99), channel_id=1, source_target_pairs={{0,4},{1,5},{2,6},{3,7},{4,0},{5,1},{6,2},{7,3},{8,12},{9,13},{10,... | collective-permute-start | bytes 393224 | tf_op jit(solution)/shard_map/ppermute | solution.py:495
  90.4 6.9 %collective-permute-start.31 = (bf16[2,2,2,32,256]{4,3,2,1,0:T(8,128)(2,1)S(1)}, bf16[2,2,2,32,256]{4,3,2,1,0:T(8,128)(2,1)S(1)}, u32[]{:S(2)}, u32[]{:S(2)}) collective-permute-start(bf16[2,2,2,32,256]{4,3,2,1,0:T(8,128)(2,1)S(1)} %get-tuple-element.113), channel_id=1, source_target_pairs={{0,4},{1,5},{2,6},{3,7},{4,0},{5,1},{6,2},{7,3},{8,12},{9,13},{10,... | collective-permute-start | bytes 393224 | tf_op jit(solution)/shard_map/ppermute | solution.py:495
  (11 other events, 47.8 us)

commit v7 on v6

--- a/solution.py
+++ b/solution.py
@@ -167,12 +167,12 @@
 
 
 def far_kernel(
-    held, packed_0, packed_1, came_0, came_1, picked_0, picked_1, rest_0, rest_1, far
+    held, j, count, packed_0, packed_1, came_0, came_1, picked_0, picked_1, rest_0, rest_1, far
 ):
     owner = lax.axis_index("kp")
     packed, came = (packed_0, packed_1), (came_0, came_1)
     picked, rest = (picked_0, picked_1), (rest_0, rest_1)
-    count, transfers, _, g_local, _ = far.shape
+    transfers, _, g_local, _ = far.shape
     half = g_local // 2
     rows = [label_of(packed_0, held, half, j) for j in range(count)]
     for h in range(2):
@@ -183,25 +183,24 @@
             who * held + k for who in (owner ^ second, owner ^ second ^ first) for k in range(held)
         ]
         places = slots(side, rows, owner, transfers)
-        for j in range(count):
-            for s in range(transfers):
-                label = rows[j] + owner * transfers + s
-                out = far.at[j, s, :, h * half : (h + 1) * half]
-                hit = copy_if(label, found, out)
-                for i in range(count):
-                    match = (label == rows[i]) & jnp.logical_not(hit)
-                    hit = hit | match
-
-                    @pl.when(match)
+        for s in range(transfers):
+            label = rows[j] + owner * transfers + s
+            out = far.at[s, :, h * half : (h + 1) * half]
+            hit = copy_if(label, found, out)
+            for i in range(count):
+                match = (label == rows[i]) & jnp.logical_not(hit)
+                hit = hit | match
+
+                @pl.when(match)
+                def _(h=h, i=i, out=out):
+                    out[...] = picked[h][i]
+
+            for name, (need, place) in zip(side, places):
+                for i in range(rest[h].shape[0]):
+
+                    @pl.when((label == name) & need & (place == i))
                     def _(h=h, i=i, out=out):
-                        out[...] = picked[h][i]
-
-                for name, (need, place) in zip(side, places):
-                    for i in range(rest[h].shape[0]):
-
-                        @pl.when((label == name) & need & (place == i))
-                        def _(h=h, i=i, out=out):
-                            out[...] = rest[h][i]
+                        out[...] = rest[h][i]
 
 
 def load_kernel(source, panels, sems):
@@ -283,11 +282,10 @@
         total[s] = value + multiply(screened, s, left, g, upper, lower, 2 * g)
 
 
-def last_kernel(chips, steps, j, screened, own, pair_real, pair_imag, before, far, keep, *refs):
+def image_kernel(steps, j, screened, own, pair_real, pair_imag, before, image, upper, lower):
     z, core = place()
     g = screened.shape[2]
-    t = far.shape[-1]
-    *gives, upper, lower = refs
+    t = own.shape[2]
     lay([(own, core * g)], upper, lower)
     rows = pl.ds(pl.multiple_of((1 - core) * g, 128), g)
     upper[rows, :t] = pair_real[...]
@@ -295,11 +293,16 @@
     lower[rows, :t] = -pair_imag[...]
     lower[rows, t:] = pair_real[...]
     span = 2 * chip_at(z, steps) * g
-    first = core == 0
     for s in range(screened.shape[0]):
         value = before[s, :, 2 * j * t : 2 * (j + 1) * t]
-        image = (value + multiply(screened, s, span, 2 * g, upper, lower)).astype(BF16)
-        by_real, by_imag = tdot(far[j, s, 0], image), tdot(far[j, s, 1], image)
+        image[s] = (value + multiply(screened, s, span, 2 * g, upper, lower)).astype(BF16)
+
+
+def mirror_kernel(chips, image, far, keep, *gives):
+    first = lax.rem(lax.axis_index("ga"), 2) == 0
+    t = far.shape[-1]
+    for s in range(image.shape[0]):
+        by_real, by_imag = tdot(far[s, 0], image[s]), tdot(far[s, 1], image[s])
         real = by_real[:, :t] + by_imag[:, t:]
         imag = by_real[:, t:] - by_imag[:, :t]
         parts = ((real, imag), (real.T, -imag.T))
@@ -444,33 +447,39 @@
         functools.partial(second_kernel, -1), 3, near_before, other_core(both), total
     )
     behind[0], _ = tie((behind[0], total))
-    rest, total = tie((rest, total))
-    far = run(
-        functools.partial(far_kernel, held),
-        shape((count, transfers, 2, g_local, t), BF16),
-        *packed,
-        *came,
-        *picked,
-        *rest,
-        name="far",
-    )
-
     parts = shape((chips, transfers, 2, 2, t // n_ga, t), F32)
     part = parts.shape[1:]
     stages = []
     done = total
     for j in range(count):
         total, _ = tie((total, done))
-        keep, *gives = run(
-            functools.partial(last_kernel, chips, -2, j),
-            [parts] + [shape((chips, 2, t // n_ga, t), BF16)] * (2 * transfers),
+        image = run(
+            functools.partial(image_kernel, -2, j),
+            shape((transfers, g_local, 2 * t), BF16),
             screened,
             behind[j],
             *[other_core(behind[j][part]) for part in range(2)],
             total,
+            scratch=[pltpu.VMEM((2 * g_local, 2 * t), BF16)] * 2,
+            name="image",
+            mib=24,
+        )
+        rest, _ = tie((rest, image if j == 0 else done))
+        far = run(
+            functools.partial(far_kernel, held, j, count),
+            shape((transfers, 2, g_local, t), BF16),
+            *packed,
+            *came,
+            *picked,
+            *rest,
+            name="far",
+        )
+        keep, *gives = run(
+            functools.partial(mirror_kernel, chips),
+            [parts] + [shape((chips, 2, t // n_ga, t), BF16)] * (2 * transfers),
+            image,
             far,
-            scratch=[pltpu.VMEM((2 * g_local, 2 * t), BF16)] * 2,
-            name="last",
+            name="mirror",
             mib=24,
         )
         own, cross, sends = run(

time: 98.3 us -> 97.1 us (0.988)
  waiting for transfers between devices: 44.1 us -> 42.5 us
    ppermute x2, starting transfers between devices: 0.41 us -> 2.5 us  [quick(): lax.ppermute(sends, 'ga', [(i, i ^ 4) for i in range(n_ga)])]
    ppermute x10, waiting for transfers between devices: 17 us -> 15.2 us  [across(): return lax.ppermute(x, 'kp', [(i, i ^ bit) for i in range(n_kp)])]
    ppermute x2, starting transfers between devices: 3.74 us -> 2.04 us  [quick(): came_j = lax.ppermute(sends, 'ga', [(i, i ^ 2) for i in range(n_ga)])]
    ppermute x14, waiting for transfers between devices: 1.6 us -> 2.71 us  [other_core(): return lax.ppermute(x, 'ga', [(i, i ^ 1) for i in range(n_ga)])]
    ppermute x2, waiting for transfers between devices: 10.7 us -> 9.65 us  [quick(): came_j = lax.ppermute(sends, 'ga', [(i, i ^ 2) for i in range(n_ga)])]
    pallas_call x20 -> x23, Pallas kernels: 24.9 us -> 24.6 us  [run(): pl.pallas_call(body, in_specs=specs or [VMEM] * len(args), out_specs=[VME...]
where the time goes in v7:
time: 97.1 us; the launch traced here: 96.9 us
  waiting for transfers between devices  42.5 us (44%)
  starting transfers between devices  28.1 us (29%)
  Pallas kernels  24.6 us (25%)
    pallas_call x23, Pallas kernels, run(): pl.pallas_call(body, in_specs=specs or [VMEM] * len(args), out_specs=[VME...  24.6 us
    ppermute x10, waiting for transfers between devices, across(): return lax.ppermute(x, 'kp', [(i, i ^ bit) for i in range(n_kp)])  15.2 us
    ppermute x10, starting transfers between devices, across(): return lax.ppermute(x, 'kp', [(i, i ^ bit) for i in range(n_kp)])  12.7 us
    ppermute x2, waiting for transfers between devices, quick(): came_j = lax.ppermute(sends, 'ga', [(i, i ^ 2) for i in range(n_ga)])  9.65 us
    ppermute x4, waiting for transfers between devices, along(): lax.ppermute(x, 'ga', [(i, 2 * chips_on[i // 2] + i % 2) for i in range(n...  7.9 us
    ppermute x2, waiting for transfers between devices, quick(): lax.ppermute(sends, 'ga', [(i, i ^ 4) for i in range(n_ga)])  6.99 us
    ppermute x4, starting transfers between devices, along(): lax.ppermute(x, 'ga', [(i, 2 * chips_on[i // 2] + i % 2) for i in range(n...  6.99 us
    ppermute x14, starting transfers between devices, other_core(): return lax.ppermute(x, 'ga', [(i, i ^ 1) for i in range(n_ga)])  3.88 us
  transfers between devices with their start and end apart: 32, of which 18 were waited for; matrix products, arithmetic and copies ran while one was open for 0% of the time, Pallas kernels for 23%

profile of v7, /device:TPU:0, one launch (start us, length us, event | category | flops | bytes accessed | tf_op | source)
XLA Modules:
  0.0 96.9 jit_solution(6597471953587041472)
XLA Ops:
  2.5 3.0 %collective-permute-start = (bf16[784,256]{1,0:T(8,128)(2,1)S(1)}, bf16[784,256]{1,0:T(8,128)(2,1)S(1)}, u32[]{:S(2)}, u32[]{:S(2)}) collective-permute-start(bf16[784,256]{1,0:T(8,128)(2,1)S(1)} %get-tuple-element.66.packed_0), channel_id=1, source_target_pairs={{0,8},{8,0},{16,24},{24,16},{1,9},{9,1},{17,25},{25,17},{2,10},{10... | collective-permute-start | bytes 1204232 | tf_op jit(solution)/shard_map/ppermute | solution.py:359
  5.5 1.5 %collective-permute-start.1 = (bf16[784,256]{1,0:T(8,128)(2,1)S(1)}, bf16[784,256]{1,0:T(8,128)(2,1)S(1)}, u32[]{:S(2)}, u32[]{:S(2)}) collective-permute-start(bf16[784,256]{1,0:T(8,128)(2,1)S(1)} %get-tuple-element.67.packed_1), channel_id=1, source_target_pairs={{0,16},{8,24},{16,0},{24,8},{1,17},{9,25},{17,1},{25,9},{2,18},{10... | collective-permute-start | bytes 1204232 | tf_op jit(solution)/shard_map/ppermute | solution.py:359
  7.0 1.6 %collective-permute-start.2 = (bf16[2,2,384,256]{3,2,1,0:T(8,128)(2,1)}, bf16[2,2,384,256]{3,2,1,0:T(8,128)(2,1)S(1)}, u32[]{:S(2)}, u32[]{:S(2)}) collective-permute-start(bf16[2,2,384,256]{3,2,1,0:T(8,128)(2,1)} %densities.1), channel_id=1, source_target_pairs={{0,2},{1,3},{2,6},{3,7},{4,0},{5,1},{6,4},{7,5},{8,10},{9,11},{10,... | collective-permute-start | bytes 2359304 | tf_op jit(solution)/shard_map/ppermute | solution.py:365
  8.6 3.8 %load.1.screened = bf16[2,2,384,3072]{3,2,1,0:T(8,128)(2,1)S(1)} custom-call(bf16[2,2,384,3072]{3,2,1,0:T(8,128)(2,1)} %source), custom_call_target="tpu_custom_call" | custom-call | tf_op jit(solution)/shard_map/load/pallas_call | solution.py:30
  12.4 2.4 %collective-permute-done.came_0 = bf16[784,256]{1,0:T(8,128)(2,1)S(1)} collective-permute-done((bf16[784,256]{1,0:T(8,128)(2,1)S(1)}, bf16[784,256]{1,0:T(8,128)(2,1)S(1)}, u32[]{:S(2)}, u32[]{:S(2)}) %collective-permute-start) | collective-permute-done | bytes 401440 | tf_op jit(solution)/shard_map/ppermute | solution.py:359
  14.8 1.5 %collective-permute-done.1.came_1 = bf16[784,256]{1,0:T(8,128)(2,1)S(1)} collective-permute-done((bf16[784,256]{1,0:T(8,128)(2,1)S(1)}, bf16[784,256]{1,0:T(8,128)(2,1)S(1)}, u32[]{:S(2)}, u32[]{:S(2)}) %collective-permute-start.1) | collective-permute-done | bytes 401440 | tf_op jit(solution)/shard_map/ppermute | solution.py:359
  16.9 1.6 %collective-permute-start.5 = (bf16[2,2,192,256]{3,2,1,0:T(8,128)(2,1)S(1)}, bf16[2,2,192,256]{3,2,1,0:T(8,128)(2,1)S(1)}, u32[]{:S(2)}, u32[]{:S(2)}) collective-permute-start(bf16[2,2,192,256]{3,2,1,0:T(8,128)(2,1)S(1)} %get-tuple-element.70), channel_id=1, source_target_pairs={{0,16},{8,24},{16,0},{24,8},{1,17},{9,25},{17,1},{25,9},{2,18},{10... | collective-permute-start | bytes 1179656 | tf_op jit(solution)/shard_map/ppermute | solution.py:359
  19.0 7.9 %collective-permute-done.2.densities = bf16[2,2,384,256]{3,2,1,0:T(8,128)(2,1)S(1)} collective-permute-done((bf16[2,2,384,256]{3,2,1,0:T(8,128)(2,1)}, bf16[2,2,384,256]{3,2,1,0:T(8,128)(2,1)S(1)}, u32[]{:S(2)}, u32[]{:S(2)}) %collective-permute-start.2) | collective-permute-done | bytes 786464 | tf_op jit(solution)/shard_map/ppermute | solution.py:365
  29.3 1.8 %collective-permute-start.10 = (bf16[2,2,384,256]{3,2,1,0:T(8,128)(2,1)S(1)}, bf16[2,2,384,256]{3,2,1,0:T(8,128)(2,1)S(1)}, u32[]{:S(2)}, u32[]{:S(2)}) collective-permute-start(bf16[2,2,384,256]{3,2,1,0:T(8,128)(2,1)S(1)} %near.2.own.refs_0_), channel_id=1, source_target_pairs={{0,4},{1,5},{2,0},{3,1},{4,6},{5,7},{6,2},{7,3},{8,12},{9,13},{10,... | collective-permute-start | bytes 2359304 | tf_op jit(solution)/shard_map/ppermute | solution.py:365
  31.1 1.8 %product.3.before = f32[2,384,1024]{2,1,0:T(8,128)S(1)} custom-call(bf16[2,2,384,3072]{3,2,1,0:T(8,128)(2,1)S(1)} %load.1.screened, bf16[2,2,384,256]{3,2,1,0:T(8,128)(2,1)S(1)} %near.2.own.refs_0_, f32[1,384]{1,0:T(1,128)S(1)} %broadcast_in_dim.3.coulomb), custom_call_target="tpu_custom_call" | custom-call | tf_op jit(solution)/shard_map/product/pallas_call | solution.py:30
  32.9 4.2 %collective-permute-done.3.came_0 = bf16[784,256]{1,0:T(8,128)(2,1)S(1)} collective-permute-done((bf16[784,256]{1,0:T(8,128)(2,1)S(1)}, bf16[784,256]{1,0:T(8,128)(2,1)S(1)}, u32[]{:S(2)}, u32[]{:S(2)}) %collective-permute-start.3) | collective-permute-done | bytes 401440 | tf_op jit(solution)/shard_map/ppermute | solution.py:359
  40.0 6.2 %collective-permute-done.7.picked_0 = bf16[2,2,192,256]{3,2,1,0:T(8,128)(2,1)S(1)} collective-permute-done((bf16[2,2,192,256]{3,2,1,0:T(8,128)(2,1)S(1)}, bf16[2,2,192,256]{3,2,1,0:T(8,128)(2,1)S(1)}, u32[]{:S(2)}, u32[]{:S(2)}) %collective-permute-start.7) | collective-permute-done | bytes 393248 | tf_op jit(solution)/shard_map/ppermute | solution.py:359
  48.0 1.7 %collective-permute-start.9 = (bf16[2,384,256]{2,1,0:T(8,128)(2,1)S(1)}, bf16[2,384,256]{2,1,0:T(8,128)(2,1)S(1)}, u32[]{:S(2)}, u32[]{:S(2)}) collective-permute-start(bf16[2,384,256]{2,1,0:T(8,128)(2,1)S(1)} %get-tuple-element.80), channel_id=1, source_target_pairs={{0,2},{1,3},{2,6},{3,7},{4,0},{5,1},{6,4},{7,5},{8,10},{9,11},{10,... | collective-permute-start | bytes 1179656 | tf_op jit(solution)/shard_map/ppermute | solution.py:365
  49.7 1.5 %collective-permute-start.15 = (bf16[3,2,192,256]{3,2,1,0:T(8,128)(2,1)S(1)}, bf16[3,2,192,256]{3,2,1,0:T(8,128)(2,1)S(1)}, u32[]{:S(2)}, u32[]{:S(2)}) collective-permute-start(bf16[3,2,192,256]{3,2,1,0:T(8,128)(2,1)S(1)} %get-tuple-element.88), channel_id=1, source_target_pairs={{0,16},{8,24},{16,0},{24,8},{1,17},{9,25},{17,1},{25,9},{2,18},{10... | collective-permute-start | bytes 1769480 | tf_op jit(solution)/shard_map/ppermute | solution.py:359
  51.3 1.5 %collective-permute-start.16 = (bf16[2,2,192,256]{3,2,1,0:T(8,128)(2,1)S(1)}, bf16[2,2,192,256]{3,2,1,0:T(8,128)(2,1)S(1)}, u32[]{:S(2)}, u32[]{:S(2)}) collective-permute-start(bf16[2,2,192,256]{3,2,1,0:T(8,128)(2,1)S(1)} %get-tuple-element.89), channel_id=1, source_target_pairs={{0,8},{8,0},{16,24},{24,16},{1,9},{9,1},{17,25},{25,17},{2,10},{10... | collective-permute-start | bytes 1179656 | tf_op jit(solution)/shard_map/ppermute | solution.py:359
  52.8 1.9 %collective-permute-start.23 = (bf16[2,384,256]{2,1,0:T(8,128)(2,1)S(1)}, bf16[2,384,256]{2,1,0:T(8,128)(2,1)S(1)}, u32[]{:S(2)}, u32[]{:S(2)}) collective-permute-start(bf16[2,384,256]{2,1,0:T(8,128)(2,1)S(1)} %get-tuple-element.102), channel_id=1, source_target_pairs={{0,2},{1,3},{2,6},{3,7},{4,0},{5,1},{6,4},{7,5},{8,10},{9,11},{10,... | collective-permute-start | bytes 1179656 | tf_op jit(solution)/shard_map/ppermute | solution.py:365
  54.7 3.0 %product.4.before = f32[2,384,1024]{2,1,0:T(8,128)S(1)} custom-call(bf16[2,2,384,3072]{3,2,1,0:T(8,128)(2,1)S(1)} %load.1.screened, bf16[2,2,384,256]{3,2,1,0:T(8,128)(2,1)S(1)} %collective-permute-done.10.own, bf16[2,2,384,256]{3,2,1,0:T(8,128)(2,1)S(1)} %collective-permute-done.12.pair, ...), custom_call_target="tpu_custom_call", output_to_operand_aliasing={{}: (3, {})} | custom-call | tf_op jit(solution)/shard_map/product/pallas_call | solution.py:30
  57.7 4.6 %product.5.before = f32[2,384,1024]{2,1,0:T(8,128)S(1)} custom-call(bf16[2,2,384,3072]{3,2,1,0:T(8,128)(2,1)S(1)} %load.1.screened, bf16[2,2,384,256]{3,2,1,0:T(8,128)(2,1)S(1)} %get-tuple-element.84.refs_1_.own, bf16[2,2,2,384,256]{4,3,2,1,0:T(8,128)(2,1)S(1)} %collective-permute-done.11.pairs, ...), custom_call_target="tpu_custom_call", output_to_operand_aliasing={{}: (3, {})} | custom-call | tf_op jit(solution)/shard_map/product/pallas_call | solution.py:30
  64.2 1.5 %image.2 = bf16[2,384,512]{2,1,0:T(8,128)(2,1)S(1)} custom-call(bf16[2,2,384,3072]{3,2,1,0:T(8,128)(2,1)S(1)} %load.1.screened, bf16[2,384,256]{2,1,0:T(8,128)(2,1)S(1)} %collective-permute-done.9.own, bf16[384,256]{1,0:T(8,128)(2,1)S(1)} %collective-permute-done.13.pair_real, bf16[384,256]{1,0:T(8,128)(2,1)S(1)} %collective-permute-done.14.pair_imag, ...), custom_call_target="tpu_custom_call" | custom-call | tf_op jit(solution)/shard_map/image/pallas_call | solution.py:30
  71.3 1.5 %image.3 = bf16[2,384,512]{2,1,0:T(8,128)(2,1)S(1)} custom-call(bf16[2,2,384,3072]{3,2,1,0:T(8,128)(2,1)S(1)} %load.1.screened, bf16[2,384,256]{2,1,0:T(8,128)(2,1)S(1)} %collective-permute-done.23.own, bf16[384,256]{1,0:T(8,128)(2,1)S(1)} %collective-permute-done.24.pair_real, bf16[384,256]{1,0:T(8,128)(2,1)S(1)} %collective-permute-done.25.pair_imag, ...), custom_call_target="tpu_custom_call" | custom-call | tf_op jit(solution)/shard_map/image/pallas_call | solution.py:30
  75.8 2.3 %collective-permute-done.21.came = bf16[2,2,2,2,32,256]{5,4,3,2,1,0:T(8,128)(2,1)S(1)} collective-permute-done((bf16[2,2,2,2,32,256]{5,4,3,2,1,0:T(8,128)(2,1)S(1)}, bf16[2,2,2,2,32,256]{5,4,3,2,1,0:T(8,128)(2,1)S(1)}, u32[]{:S(2)}, u32[]{:S(2)}) %collective-permute-start.21) | collective-permute-done | bytes 262176 | tf_op jit(solution)/shard_map/ppermute | solution.py:497
  79.2 2.1 %collective-permute-start.22 = (bf16[2,2,2,32,256]{4,3,2,1,0:T(8,128)(2,1)S(1)}, bf16[2,2,2,32,256]{4,3,2,1,0:T(8,128)(2,1)S(1)}, u32[]{:S(2)}, u32[]{:S(2)}) collective-permute-start(bf16[2,2,2,32,256]{4,3,2,1,0:T(8,128)(2,1)S(1)} %get-tuple-element.101), channel_id=1, source_target_pairs={{0,4},{1,5},{2,6},{3,7},{4,0},{5,1},{6,2},{7,3},{8,12},{9,13},{10,... | collective-permute-start | bytes 393224 | tf_op jit(solution)/shard_map/ppermute | solution.py:504
  81.3 7.3 %collective-permute-done.30.came = bf16[2,2,2,2,32,256]{5,4,3,2,1,0:T(8,128)(2,1)S(1)} collective-permute-done((bf16[2,2,2,2,32,256]{5,4,3,2,1,0:T(8,128)(2,1)S(1)}, bf16[2,2,2,2,32,256]{5,4,3,2,1,0:T(8,128)(2,1)S(1)}, u32[]{:S(2)}, u32[]{:S(2)}) %collective-permute-start.30) | collective-permute-done | bytes 262176 | tf_op jit(solution)/shard_map/ppermute | solution.py:497
  89.1 7.0 %collective-permute-done.31.refs_3_ = bf16[2,2,2,32,256]{4,3,2,1,0:T(8,128)(2,1)S(1)} collective-permute-done((bf16[2,2,2,32,256]{4,3,2,1,0:T(8,128)(2,1)S(1)}, bf16[2,2,2,32,256]{4,3,2,1,0:T(8,128)(2,1)S(1)}, u32[]{:S(2)}, u32[]{:S(2)}) %collective-permute-start.31) | collective-permute-done | bytes 131104 | tf_op jit(solution)/shard_map/ppermute | solution.py:504
  (72 shorter events, 22.8 us)
Async XLA Ops:
  2.5 12.3 %collective-permute-start = (bf16[784,256]{1,0:T(8,128)(2,1)S(1)}, bf16[784,256]{1,0:T(8,128)(2,1)S(1)}, u32[]{:S(2)}, u32[]{:S(2)}) collective-permute-start(bf16[784,256]{1,0:T(8,128)(2,1)S(1)} %get-tuple-element.66.packed_0), channel_id=1, source_target_pairs={{0,8},{8,0},{16,24},{24,16},{1,9},{9,1},{17,25},{25,17},{2,10},{10... | collective-permute-start | bytes 1204232 | tf_op jit(solution)/shard_map/ppermute | solution.py:359
  5.5 10.8 %collective-permute-start.1 = (bf16[784,256]{1,0:T(8,128)(2,1)S(1)}, bf16[784,256]{1,0:T(8,128)(2,1)S(1)}, u32[]{:S(2)}, u32[]{:S(2)}) collective-permute-start(bf16[784,256]{1,0:T(8,128)(2,1)S(1)} %get-tuple-element.67.packed_1), channel_id=1, source_target_pairs={{0,16},{8,24},{16,0},{24,8},{1,17},{9,25},{17,1},{25,9},{2,18},{10... | collective-permute-start | bytes 1204232 | tf_op jit(solution)/shard_map/ppermute | solution.py:359
  7.0 19.8 %collective-permute-start.2 = (bf16[2,2,384,256]{3,2,1,0:T(8,128)(2,1)}, bf16[2,2,384,256]{3,2,1,0:T(8,128)(2,1)S(1)}, u32[]{:S(2)}, u32[]{:S(2)}) collective-permute-start(bf16[2,2,384,256]{3,2,1,0:T(8,128)(2,1)} %densities.1), channel_id=1, source_target_pairs={{0,2},{1,3},{2,6},{3,7},{4,0},{5,1},{6,4},{7,5},{8,10},{9,11},{10,... | collective-permute-start | bytes 2359304 | tf_op jit(solution)/shard_map/ppermute | solution.py:365
  16.9 12.0 %collective-permute-start.5 = (bf16[2,2,192,256]{3,2,1,0:T(8,128)(2,1)S(1)}, bf16[2,2,192,256]{3,2,1,0:T(8,128)(2,1)S(1)}, u32[]{:S(2)}, u32[]{:S(2)}) collective-permute-start(bf16[2,2,192,256]{3,2,1,0:T(8,128)(2,1)S(1)} %get-tuple-element.70), channel_id=1, source_target_pairs={{0,16},{8,24},{16,0},{24,8},{1,17},{9,25},{17,1},{25,9},{2,18},{10... | collective-permute-start | bytes 1179656 | tf_op jit(solution)/shard_map/ppermute | solution.py:359
  18.4 10.5 %collective-permute-start.6 = (bf16[2,2,192,256]{3,2,1,0:T(8,128)(2,1)S(1)}, bf16[2,2,192,256]{3,2,1,0:T(8,128)(2,1)S(1)}, u32[]{:S(2)}, u32[]{:S(2)}) collective-permute-start(bf16[2,2,192,256]{3,2,1,0:T(8,128)(2,1)S(1)} %get-tuple-element.71), channel_id=1, source_target_pairs={{0,8},{8,0},{16,24},{24,16},{1,9},{9,1},{17,25},{25,17},{2,10},{10... | collective-permute-start | bytes 1179656 | tf_op jit(solution)/shard_map/ppermute | solution.py:359
  27.4 9.6 %collective-permute-start.3 = (bf16[784,256]{1,0:T(8,128)(2,1)S(1)}, bf16[784,256]{1,0:T(8,128)(2,1)S(1)}, u32[]{:S(2)}, u32[]{:S(2)}) collective-permute-start(bf16[784,256]{1,0:T(8,128)(2,1)S(1)} %get-tuple-element.64.packed_0), channel_id=1, source_target_pairs={{0,8},{8,0},{16,24},{24,16},{1,9},{9,1},{17,25},{25,17},{2,10},{10... | collective-permute-start | bytes 1204232 | tf_op jit(solution)/shard_map/ppermute | solution.py:359
  28.1 9.3 %collective-permute-start.4 = (bf16[784,256]{1,0:T(8,128)(2,1)S(1)}, bf16[784,256]{1,0:T(8,128)(2,1)S(1)}, u32[]{:S(2)}, u32[]{:S(2)}) collective-permute-start(bf16[784,256]{1,0:T(8,128)(2,1)S(1)} %get-tuple-element.65.packed_1), channel_id=1, source_target_pairs={{0,16},{8,24},{16,0},{24,8},{1,17},{9,25},{17,1},{25,9},{2,18},{10... | collective-permute-start | bytes 1204232 | tf_op jit(solution)/shard_map/ppermute | solution.py:359
  29.3 18.1 %collective-permute-start.10 = (bf16[2,2,384,256]{3,2,1,0:T(8,128)(2,1)S(1)}, bf16[2,2,384,256]{3,2,1,0:T(8,128)(2,1)S(1)}, u32[]{:S(2)}, u32[]{:S(2)}) collective-permute-start(bf16[2,2,384,256]{3,2,1,0:T(8,128)(2,1)S(1)} %near.2.own.refs_0_), channel_id=1, source_target_pairs={{0,4},{1,5},{2,0},{3,1},{4,6},{5,7},{6,2},{7,3},{8,12},{9,13},{10,... | collective-permute-start | bytes 2359304 | tf_op jit(solution)/shard_map/ppermute | solution.py:365
  37.9 8.3 %collective-permute-start.7 = (bf16[2,2,192,256]{3,2,1,0:T(8,128)(2,1)S(1)}, bf16[2,2,192,256]{3,2,1,0:T(8,128)(2,1)S(1)}, u32[]{:S(2)}, u32[]{:S(2)}) collective-permute-start(bf16[2,2,192,256]{3,2,1,0:T(8,128)(2,1)S(1)} %get-tuple-element.78), channel_id=1, source_target_pairs={{0,16},{8,24},{16,0},{24,8},{1,17},{9,25},{17,1},{25,9},{2,18},{10... | collective-permute-start | bytes 1179656 | tf_op jit(solution)/shard_map/ppermute | solution.py:359
  38.7 8.2 %collective-permute-start.8 = (bf16[2,2,192,256]{3,2,1,0:T(8,128)(2,1)S(1)}, bf16[2,2,192,256]{3,2,1,0:T(8,128)(2,1)S(1)}, u32[]{:S(2)}, u32[]{:S(2)}) collective-permute-start(bf16[2,2,192,256]{3,2,1,0:T(8,128)(2,1)S(1)} %get-tuple-element.79), channel_id=1, source_target_pairs={{0,8},{8,0},{16,24},{24,16},{1,9},{9,1},{17,25},{25,17},{2,10},{10... | collective-permute-start | bytes 1179656 | tf_op jit(solution)/shard_map/ppermute | solution.py:359
  47.5 10.3 %collective-permute-start.11 = (bf16[2,2,2,384,256]{4,3,2,1,0:T(8,128)(2,1)S(1)}, bf16[2,2,2,384,256]{4,3,2,1,0:T(8,128)(2,1)S(1)}, u32[]{:S(2)}, u32[]{:S(2)}) collective-permute-start(bf16[2,2,2,384,256]{4,3,2,1,0:T(8,128)(2,1)S(1)} %stack.1), channel_id=1, source_target_pairs={{0,1},{1,0},{2,3},{3,2},{4,5},{5,4},{6,7},{7,6},{8,9},{9,8},{10,11... | collective-permute-start | bytes 4718600 | tf_op jit(solution)/shard_map/ppermute | solution.py:362
  47.5 5.2 %collective-permute-start.12 = (bf16[2,2,384,256]{3,2,1,0:T(8,128)(2,1)S(1)}, bf16[2,2,384,256]{3,2,1,0:T(8,128)(2,1)S(1)}, u32[]{:S(2)}, u32[]{:S(2)}) collective-permute-start(bf16[2,2,384,256]{3,2,1,0:T(8,128)(2,1)S(1)} %collective-permute-done.10.own), channel_id=1, source_target_pairs={{0,1},{1,0},{2,3},{3,2},{4,5},{5,4},{6,7},{7,6},{8,9},{9,8},{10,11... | collective-permute-start | bytes 2359304 | tf_op jit(solution)/shard_map/ppermute | solution.py:362
  48.0 14.3 %collective-permute-start.9 = (bf16[2,384,256]{2,1,0:T(8,128)(2,1)S(1)}, bf16[2,384,256]{2,1,0:T(8,128)(2,1)S(1)}, u32[]{:S(2)}, u32[]{:S(2)}) collective-permute-start(bf16[2,384,256]{2,1,0:T(8,128)(2,1)S(1)} %get-tuple-element.80), channel_id=1, source_target_pairs={{0,2},{1,3},{2,6},{3,7},{4,0},{5,1},{6,4},{7,5},{8,10},{9,11},{10,... | collective-permute-start | bytes 1179656 | tf_op jit(solution)/shard_map/ppermute | solution.py:365
  49.7 16.0 %collective-permute-start.15 = (bf16[3,2,192,256]{3,2,1,0:T(8,128)(2,1)S(1)}, bf16[3,2,192,256]{3,2,1,0:T(8,128)(2,1)S(1)}, u32[]{:S(2)}, u32[]{:S(2)}) collective-permute-start(bf16[3,2,192,256]{3,2,1,0:T(8,128)(2,1)S(1)} %get-tuple-element.88), channel_id=1, source_target_pairs={{0,16},{8,24},{16,0},{24,8},{1,17},{9,25},{17,1},{25,9},{2,18},{10... | collective-permute-start | bytes 1769480 | tf_op jit(solution)/shard_map/ppermute | solution.py:359
  51.3 14.4 %collective-permute-start.16 = (bf16[2,2,192,256]{3,2,1,0:T(8,128)(2,1)S(1)}, bf16[2,2,192,256]{3,2,1,0:T(8,128)(2,1)S(1)}, u32[]{:S(2)}, u32[]{:S(2)}) collective-permute-start(bf16[2,2,192,256]{3,2,1,0:T(8,128)(2,1)S(1)} %get-tuple-element.89), channel_id=1, source_target_pairs={{0,8},{8,0},{16,24},{24,16},{1,9},{9,1},{17,25},{25,17},{2,10},{10... | collective-permute-start | bytes 1179656 | tf_op jit(solution)/shard_map/ppermute | solution.py:359
  52.8 15.7 %collective-permute-start.23 = (bf16[2,384,256]{2,1,0:T(8,128)(2,1)S(1)}, bf16[2,384,256]{2,1,0:T(8,128)(2,1)S(1)}, u32[]{:S(2)}, u32[]{:S(2)}) collective-permute-start(bf16[2,384,256]{2,1,0:T(8,128)(2,1)S(1)} %get-tuple-element.102), channel_id=1, source_target_pairs={{0,2},{1,3},{2,6},{3,7},{4,0},{5,1},{6,4},{7,5},{8,10},{9,11},{10,... | collective-permute-start | bytes 1179656 | tf_op jit(solution)/shard_map/ppermute | solution.py:365
  62.4 1.5 %collective-permute-start.13 = (bf16[384,256]{1,0:T(8,128)(2,1)S(1)}, bf16[384,256]{1,0:T(8,128)(2,1)S(1)}, u32[]{:S(2)}, u32[]{:S(2)}) collective-permute-start(bf16[384,256]{1,0:T(8,128)(2,1)S(1)} %get-tuple-element.121), channel_id=1, source_target_pairs={{0,1},{1,0},{2,3},{3,2},{4,5},{5,4},{6,7},{7,6},{8,9},{9,8},{10,11... | collective-permute-start | bytes 589832 | tf_op jit(solution)/shard_map/ppermute | solution.py:362
  62.5 1.7 %collective-permute-start.14 = (bf16[384,256]{1,0:T(8,128)(2,1)S(1)}, bf16[384,256]{1,0:T(8,128)(2,1)S(1)}, u32[]{:S(2)}, u32[]{:S(2)}) collective-permute-start(bf16[384,256]{1,0:T(8,128)(2,1)S(1)} %get-tuple-element.120), channel_id=1, source_target_pairs={{0,1},{1,0},{2,3},{3,2},{4,5},{5,4},{6,7},{7,6},{8,9},{9,8},{10,11... | collective-permute-start | bytes 589832 | tf_op jit(solution)/shard_map/ppermute | solution.py:362
  68.5 2.8 %collective-permute-start.24 = (bf16[384,256]{1,0:T(8,128)(2,1)S(1)}, bf16[384,256]{1,0:T(8,128)(2,1)S(1)}, u32[]{:S(2)}, u32[]{:S(2)}) collective-permute-start(bf16[384,256]{1,0:T(8,128)(2,1)S(1)} %get-tuple-element.119), channel_id=1, source_target_pairs={{0,1},{1,0},{2,3},{3,2},{4,5},{5,4},{6,7},{7,6},{8,9},{9,8},{10,11... | collective-permute-start | bytes 589832 | tf_op jit(solution)/shard_map/ppermute | solution.py:362
  68.8 2.5 %collective-permute-start.25 = (bf16[384,256]{1,0:T(8,128)(2,1)S(1)}, bf16[384,256]{1,0:T(8,128)(2,1)S(1)}, u32[]{:S(2)}, u32[]{:S(2)}) collective-permute-start(bf16[384,256]{1,0:T(8,128)(2,1)S(1)} %get-tuple-element.118), channel_id=1, source_target_pairs={{0,1},{1,0},{2,3},{3,2},{4,5},{5,4},{6,7},{7,6},{8,9},{9,8},{10,11... | collective-permute-start | bytes 589832 | tf_op jit(solution)/shard_map/ppermute | solution.py:362
  69.6 8.5 %collective-permute-start.21 = (bf16[2,2,2,2,32,256]{5,4,3,2,1,0:T(8,128)(2,1)S(1)}, bf16[2,2,2,2,32,256]{5,4,3,2,1,0:T(8,128)(2,1)S(1)}, u32[]{:S(2)}, u32[]{:S(2)}) collective-permute-start(bf16[2,2,2,2,32,256]{5,4,3,2,1,0:T(8,128)(2,1)S(1)} %get-tuple-element.99), channel_id=1, source_target_pairs={{0,2},{1,3},{2,0},{3,1},{4,6},{5,7},{6,4},{7,5},{8,10},{9,11},{10,... | collective-permute-start | bytes 786440 | tf_op jit(solution)/shard_map/ppermute | solution.py:497
  78.2 10.5 %collective-permute-start.30 = (bf16[2,2,2,2,32,256]{5,4,3,2,1,0:T(8,128)(2,1)S(1)}, bf16[2,2,2,2,32,256]{5,4,3,2,1,0:T(8,128)(2,1)S(1)}, u32[]{:S(2)}, u32[]{:S(2)}) collective-permute-start(bf16[2,2,2,2,32,256]{5,4,3,2,1,0:T(8,128)(2,1)S(1)} %get-tuple-element.115), channel_id=1, source_target_pairs={{0,2},{1,3},{2,0},{3,1},{4,6},{5,7},{6,4},{7,5},{8,10},{9,11},{10,... | collective-permute-start | bytes 786440 | tf_op jit(solution)/shard_map/ppermute | solution.py:497
  79.2 9.9 %collective-permute-start.22 = (bf16[2,2,2,32,256]{4,3,2,1,0:T(8,128)(2,1)S(1)}, bf16[2,2,2,32,256]{4,3,2,1,0:T(8,128)(2,1)S(1)}, u32[]{:S(2)}, u32[]{:S(2)}) collective-permute-start(bf16[2,2,2,32,256]{4,3,2,1,0:T(8,128)(2,1)S(1)} %get-tuple-element.101), channel_id=1, source_target_pairs={{0,4},{1,5},{2,6},{3,7},{4,0},{5,1},{6,2},{7,3},{8,12},{9,13},{10,... | collective-permute-start | bytes 393224 | tf_op jit(solution)/shard_map/ppermute | solution.py:504
  88.7 7.4 %collective-permute-start.31 = (bf16[2,2,2,32,256]{4,3,2,1,0:T(8,128)(2,1)S(1)}, bf16[2,2,2,32,256]{4,3,2,1,0:T(8,128)(2,1)S(1)}, u32[]{:S(2)}, u32[]{:S(2)}) collective-permute-start(bf16[2,2,2,32,256]{4,3,2,1,0:T(8,128)(2,1)S(1)} %get-tuple-element.117), channel_id=1, source_target_pairs={{0,4},{1,5},{2,6},{3,7},{4,0},{5,1},{6,2},{7,3},{8,12},{9,13},{10,... | collective-permute-start | bytes 393224 | tf_op jit(solution)/shard_map/ppermute | solution.py:504
  (11 other events, 47.5 us)

commit v8 on v7

--- a/solution.py
+++ b/solution.py
@@ -366,9 +366,6 @@
 
     message = shape((2 * held * half + LABELS, t), BF16)
 
-    def pack(panels):
-        return run(pack_kernel, [message] * 2, block_rows, panels, specs=[SMEM, VMEM], name="pack")
-
     sums = shape((transfers, g_local, 2 * count * t), F32)
 
     def product(body, terms, *args):
@@ -401,8 +398,10 @@
         near, *each = run(kernel, outs, *packed, *came, *picked, name="near")
         return (near, each) if apart else near
 
-    before = along(densities, FORTH)
-    packed = pack(densities)
+    packed = run(
+        pack_kernel, [message] * 2, block_rows, densities, specs=[SMEM, VMEM], name="pack", mib=53
+    )
+    packed_before = [along(x, FORTH) for x in packed]
     came = [across(packed[h], BITS[h][0]) for h in range(2)]
     source, packed = tie((screened, packed))
     screened = run(
@@ -416,7 +415,6 @@
     )
     came, screened = tie((came, screened))
     picked = pick(packed, came)
-    packed_before = pack(before)
     rest_sends = run(
         functools.partial(rest_kernel, held, transfers, count),
         [shape((room, 2, half, t), BF16) for room in left_over(n_kp, held, transfers, count)],

time: 97.1 us -> 96.3 us (level)
  waiting for transfers between devices: 42.5 us -> 37.8 us
  starting transfers between devices: 28.1 us -> 32.6 us
    ppermute x4 -> x5, starting transfers between devices: 6.99 us -> 11 us  [along(): lax.ppermute(x, 'ga', [(i, 2 * chips_on[i // 2] + i % 2) for i in range(n...]
    ppermute x10, waiting for transfers between devices: 15.2 us -> 12.5 us  [across(): return lax.ppermute(x, 'kp', [(i, i ^ bit) for i in range(n_kp)])]
    ppermute x10, starting transfers between devices: 12.7 us -> 11 us  [across(): return lax.ppermute(x, 'kp', [(i, i ^ bit) for i in range(n_kp)])]
    ppermute x2, starting transfers between devices: 2.04 us -> 3.53 us  [quick(): came_j = lax.ppermute(sends, 'ga', [(i, i ^ 2) for i in range(n_ga)])]
    ppermute x2, waiting for transfers between devices: 9.65 us -> 8.25 us  [quick(): came_j = lax.ppermute(sends, 'ga', [(i, i ^ 2) for i in range(n_ga)])]
    pallas_call x23 -> x22, Pallas kernels: 24.6 us -> 24.1 us  [run(): pl.pallas_call(body, in_specs=specs or [VMEM] * len(args), out_specs=[VME...]
    ppermute x4 -> x5, waiting for transfers between devices: 7.9 us -> 8.12 us  [along(): lax.ppermute(x, 'ga', [(i, 2 * chips_on[i // 2] + i % 2) for i in range(n...]
  transfers between devices with their start and end apart: 32 -> 33, of which waited for: 18 -> 18; matrix products, arithmetic and copies ran while one was open for 0% -> 0% of each run, Pallas kernels for 23% -> 23%
where the time goes in v8:
time: 96.3 us; the launch traced here: 96.1 us
  waiting for transfers between devices  37.8 us (39%)
  starting transfers between devices  32.6 us (34%)
  Pallas kernels  24.1 us (25%)
    pallas_call x22, Pallas kernels, run(): pl.pallas_call(body, in_specs=specs or [VMEM] * len(args), out_specs=[VME...  24.1 us
    ppermute x10, waiting for transfers between devices, across(): return lax.ppermute(x, 'kp', [(i, i ^ bit) for i in range(n_kp)])  12.5 us
    ppermute x10, starting transfers between devices, across(): return lax.ppermute(x, 'kp', [(i, i ^ bit) for i in range(n_kp)])  11 us
    ppermute x5, starting transfers between devices, along(): lax.ppermute(x, 'ga', [(i, 2 * chips_on[i // 2] + i % 2) for i in range(n...  11 us
    ppermute x2, waiting for transfers between devices, quick(): came_j = lax.ppermute(sends, 'ga', [(i, i ^ 2) for i in range(n_ga)])  8.25 us
    ppermute x5, waiting for transfers between devices, along(): lax.ppermute(x, 'ga', [(i, 2 * chips_on[i // 2] + i % 2) for i in range(n...  8.12 us
    ppermute x2, waiting for transfers between devices, quick(): lax.ppermute(sends, 'ga', [(i, i ^ 4) for i in range(n_ga)])  6.69 us
    ppermute x14, starting transfers between devices, other_core(): return lax.ppermute(x, 'ga', [(i, i ^ 1) for i in range(n_ga)])  3.87 us
  transfers between devices with their start and end apart: 33, of which 18 were waited for; matrix products, arithmetic and copies ran while one was open for 0% of the time, Pallas kernels for 23%

profile of v8, /device:TPU:0, one launch (start us, length us, event | category | flops | bytes accessed | tf_op | source)
XLA Modules:
  0.0 96.1 jit_solution(13129502780743597935)
XLA Ops:
  2.5 3.0 %collective-permute-start = (bf16[784,256]{1,0:T(8,128)(2,1)S(1)}, bf16[784,256]{1,0:T(8,128)(2,1)S(1)}, u32[]{:S(2)}, u32[]{:S(2)}) collective-permute-start(bf16[784,256]{1,0:T(8,128)(2,1)S(1)} %get-tuple-element.62.packed_0), channel_id=1, source_target_pairs={{0,8},{8,0},{16,24},{24,16},{1,9},{9,1},{17,25},{25,17},{2,10},{10... | collective-permute-start | bytes 1204232 | tf_op jit(solution)/shard_map/ppermute | solution.py:359
  5.5 1.5 %collective-permute-start.1 = (bf16[784,256]{1,0:T(8,128)(2,1)S(1)}, bf16[784,256]{1,0:T(8,128)(2,1)S(1)}, u32[]{:S(2)}, u32[]{:S(2)}) collective-permute-start(bf16[784,256]{1,0:T(8,128)(2,1)S(1)} %get-tuple-element.63.packed_1), channel_id=1, source_target_pairs={{0,16},{8,24},{16,0},{24,8},{1,17},{9,25},{17,1},{25,9},{2,18},{10... | collective-permute-start | bytes 1204232 | tf_op jit(solution)/shard_map/ppermute | solution.py:359
  7.0 1.6 %collective-permute-start.2 = (bf16[784,256]{1,0:T(8,128)(2,1)S(1)}, bf16[784,256]{1,0:T(8,128)(2,1)S(1)}, u32[]{:S(2)}, u32[]{:S(2)}) collective-permute-start(bf16[784,256]{1,0:T(8,128)(2,1)S(1)} %get-tuple-element.62.packed_0), channel_id=1, source_target_pairs={{0,2},{1,3},{2,6},{3,7},{4,0},{5,1},{6,4},{7,5},{8,10},{9,11},{10,... | collective-permute-start | bytes 1204232 | tf_op jit(solution)/shard_map/ppermute | solution.py:365
  8.6 2.6 %collective-permute-start.3 = (bf16[784,256]{1,0:T(8,128)(2,1)S(1)}, bf16[784,256]{1,0:T(8,128)(2,1)S(1)}, u32[]{:S(2)}, u32[]{:S(2)}) collective-permute-start(bf16[784,256]{1,0:T(8,128)(2,1)S(1)} %get-tuple-element.63.packed_1), channel_id=1, source_target_pairs={{0,2},{1,3},{2,6},{3,7},{4,0},{5,1},{6,4},{7,5},{8,10},{9,11},{10,... | collective-permute-start | bytes 1204232 | tf_op jit(solution)/shard_map/ppermute | solution.py:365
  11.2 3.8 %load.1.screened = bf16[2,2,384,3072]{3,2,1,0:T(8,128)(2,1)S(1)} custom-call(bf16[2,2,384,3072]{3,2,1,0:T(8,128)(2,1)} %source), custom_call_target="tpu_custom_call" | custom-call | tf_op jit(solution)/shard_map/load/pallas_call | solution.py:30
  16.8 1.6 %collective-permute-start.6 = (bf16[2,2,192,256]{3,2,1,0:T(8,128)(2,1)S(1)}, bf16[2,2,192,256]{3,2,1,0:T(8,128)(2,1)S(1)}, u32[]{:S(2)}, u32[]{:S(2)}) collective-permute-start(bf16[2,2,192,256]{3,2,1,0:T(8,128)(2,1)S(1)} %get-tuple-element.66), channel_id=1, source_target_pairs={{0,16},{8,24},{16,0},{24,8},{1,17},{9,25},{17,1},{25,9},{2,18},{10... | collective-permute-start | bytes 1179656 | tf_op jit(solution)/shard_map/ppermute | solution.py:359
  20.7 6.3 %collective-permute-done.3.packed_1 = bf16[784,256]{1,0:T(8,128)(2,1)S(1)} collective-permute-done((bf16[784,256]{1,0:T(8,128)(2,1)S(1)}, bf16[784,256]{1,0:T(8,128)(2,1)S(1)}, u32[]{:S(2)}, u32[]{:S(2)}) %collective-permute-start.3) | collective-permute-done | bytes 401440 | tf_op jit(solution)/shard_map/ppermute | solution.py:365
  27.9 2.6 %collective-permute-done.7.picked_1 = bf16[2,2,192,256]{3,2,1,0:T(8,128)(2,1)S(1)} collective-permute-done((bf16[2,2,192,256]{3,2,1,0:T(8,128)(2,1)S(1)}, bf16[2,2,192,256]{3,2,1,0:T(8,128)(2,1)S(1)}, u32[]{:S(2)}, u32[]{:S(2)}) %collective-permute-start.7) | collective-permute-done | bytes 393248 | tf_op jit(solution)/shard_map/ppermute | solution.py:359
  30.9 2.6 %collective-permute-start.11 = (bf16[2,2,384,256]{3,2,1,0:T(8,128)(2,1)S(1)}, bf16[2,2,384,256]{3,2,1,0:T(8,128)(2,1)S(1)}, u32[]{:S(2)}, u32[]{:S(2)}) collective-permute-start(bf16[2,2,384,256]{3,2,1,0:T(8,128)(2,1)S(1)} %near.2.own.refs_0_), channel_id=1, source_target_pairs={{0,4},{1,5},{2,0},{3,1},{4,6},{5,7},{6,2},{7,3},{8,12},{9,13},{10,... | collective-permute-start | bytes 2359304 | tf_op jit(solution)/shard_map/ppermute | solution.py:365
  33.5 1.8 %product.3.before = f32[2,384,1024]{2,1,0:T(8,128)S(1)} custom-call(bf16[2,2,384,3072]{3,2,1,0:T(8,128)(2,1)S(1)} %load.1.screened, bf16[2,2,384,256]{3,2,1,0:T(8,128)(2,1)S(1)} %near.2.own.refs_0_, f32[1,384]{1,0:T(1,128)S(1)} %broadcast_in_dim.3.coulomb), custom_call_target="tpu_custom_call" | custom-call | tf_op jit(solution)/shard_map/product/pallas_call | solution.py:30
  38.4 7.2 %collective-permute-done.8.picked_0 = bf16[2,2,192,256]{3,2,1,0:T(8,128)(2,1)S(1)} collective-permute-done((bf16[2,2,192,256]{3,2,1,0:T(8,128)(2,1)S(1)}, bf16[2,2,192,256]{3,2,1,0:T(8,128)(2,1)S(1)}, u32[]{:S(2)}, u32[]{:S(2)}) %collective-permute-start.8) | collective-permute-done | bytes 393248 | tf_op jit(solution)/shard_map/ppermute | solution.py:359
  47.0 2.0 %collective-permute-start.10 = (bf16[2,384,256]{2,1,0:T(8,128)(2,1)S(1)}, bf16[2,384,256]{2,1,0:T(8,128)(2,1)S(1)}, u32[]{:S(2)}, u32[]{:S(2)}) collective-permute-start(bf16[2,384,256]{2,1,0:T(8,128)(2,1)S(1)} %get-tuple-element.76), channel_id=1, source_target_pairs={{0,2},{1,3},{2,6},{3,7},{4,0},{5,1},{6,4},{7,5},{8,10},{9,11},{10,... | collective-permute-start | bytes 1179656 | tf_op jit(solution)/shard_map/ppermute | solution.py:365
  49.0 1.5 %collective-permute-start.16 = (bf16[3,2,192,256]{3,2,1,0:T(8,128)(2,1)S(1)}, bf16[3,2,192,256]{3,2,1,0:T(8,128)(2,1)S(1)}, u32[]{:S(2)}, u32[]{:S(2)}) collective-permute-start(bf16[3,2,192,256]{3,2,1,0:T(8,128)(2,1)S(1)} %get-tuple-element.84), channel_id=1, source_target_pairs={{0,16},{8,24},{16,0},{24,8},{1,17},{9,25},{17,1},{25,9},{2,18},{10... | collective-permute-start | bytes 1769480 | tf_op jit(solution)/shard_map/ppermute | solution.py:359
  50.5 2.2 %collective-permute-start.24 = (bf16[2,384,256]{2,1,0:T(8,128)(2,1)S(1)}, bf16[2,384,256]{2,1,0:T(8,128)(2,1)S(1)}, u32[]{:S(2)}, u32[]{:S(2)}) collective-permute-start(bf16[2,384,256]{2,1,0:T(8,128)(2,1)S(1)} %get-tuple-element.98), channel_id=1, source_target_pairs={{0,2},{1,3},{2,6},{3,7},{4,0},{5,1},{6,4},{7,5},{8,10},{9,11},{10,... | collective-permute-start | bytes 1179656 | tf_op jit(solution)/shard_map/ppermute | solution.py:365
  53.2 3.0 %product.4.before = f32[2,384,1024]{2,1,0:T(8,128)S(1)} custom-call(bf16[2,2,384,3072]{3,2,1,0:T(8,128)(2,1)S(1)} %load.1.screened, bf16[2,2,384,256]{3,2,1,0:T(8,128)(2,1)S(1)} %collective-permute-done.11.own, bf16[2,2,384,256]{3,2,1,0:T(8,128)(2,1)S(1)} %collective-permute-done.13.pair, ...), custom_call_target="tpu_custom_call", output_to_operand_aliasing={{}: (3, {})} | custom-call | tf_op jit(solution)/shard_map/product/pallas_call | solution.py:30
  56.3 4.6 %product.5.before = f32[2,384,1024]{2,1,0:T(8,128)S(1)} custom-call(bf16[2,2,384,3072]{3,2,1,0:T(8,128)(2,1)S(1)} %load.1.screened, bf16[2,2,384,256]{3,2,1,0:T(8,128)(2,1)S(1)} %get-tuple-element.80.refs_1_.own, bf16[2,2,2,384,256]{4,3,2,1,0:T(8,128)(2,1)S(1)} %collective-permute-done.12.pairs, ...), custom_call_target="tpu_custom_call", output_to_operand_aliasing={{}: (3, {})} | custom-call | tf_op jit(solution)/shard_map/product/pallas_call | solution.py:30
  62.7 1.5 %image.2 = bf16[2,384,512]{2,1,0:T(8,128)(2,1)S(1)} custom-call(bf16[2,2,384,3072]{3,2,1,0:T(8,128)(2,1)S(1)} %load.1.screened, bf16[2,384,256]{2,1,0:T(8,128)(2,1)S(1)} %collective-permute-done.10.own, bf16[384,256]{1,0:T(8,128)(2,1)S(1)} %collective-permute-done.14.pair_real, bf16[384,256]{1,0:T(8,128)(2,1)S(1)} %collective-permute-done.15.pair_imag, ...), custom_call_target="tpu_custom_call" | custom-call | tf_op jit(solution)/shard_map/image/pallas_call | solution.py:30
  68.3 1.8 %collective-permute-start.22 = (bf16[2,2,2,2,32,256]{5,4,3,2,1,0:T(8,128)(2,1)S(1)}, bf16[2,2,2,2,32,256]{5,4,3,2,1,0:T(8,128)(2,1)S(1)}, u32[]{:S(2)}, u32[]{:S(2)}) collective-permute-start(bf16[2,2,2,2,32,256]{5,4,3,2,1,0:T(8,128)(2,1)S(1)} %get-tuple-element.95), channel_id=1, source_target_pairs={{0,2},{1,3},{2,0},{3,1},{4,6},{5,7},{6,4},{7,5},{8,10},{9,11},{10,... | collective-permute-start | bytes 786440 | tf_op jit(solution)/shard_map/ppermute | solution.py:495
  70.7 1.5 %image.3 = bf16[2,384,512]{2,1,0:T(8,128)(2,1)S(1)} custom-call(bf16[2,2,384,3072]{3,2,1,0:T(8,128)(2,1)S(1)} %load.1.screened, bf16[2,384,256]{2,1,0:T(8,128)(2,1)S(1)} %collective-permute-done.24.own, bf16[384,256]{1,0:T(8,128)(2,1)S(1)} %collective-permute-done.25.pair_real, bf16[384,256]{1,0:T(8,128)(2,1)S(1)} %collective-permute-done.26.pair_imag, ...), custom_call_target="tpu_custom_call" | custom-call | tf_op jit(solution)/shard_map/image/pallas_call | solution.py:30
  75.3 1.6 %collective-permute-done.22.came = bf16[2,2,2,2,32,256]{5,4,3,2,1,0:T(8,128)(2,1)S(1)} collective-permute-done((bf16[2,2,2,2,32,256]{5,4,3,2,1,0:T(8,128)(2,1)S(1)}, bf16[2,2,2,2,32,256]{5,4,3,2,1,0:T(8,128)(2,1)S(1)}, u32[]{:S(2)}, u32[]{:S(2)}) %collective-permute-start.22) | collective-permute-done | bytes 262176 | tf_op jit(solution)/shard_map/ppermute | solution.py:495
  76.9 1.7 %collective-permute-start.31 = (bf16[2,2,2,2,32,256]{5,4,3,2,1,0:T(8,128)(2,1)S(1)}, bf16[2,2,2,2,32,256]{5,4,3,2,1,0:T(8,128)(2,1)S(1)}, u32[]{:S(2)}, u32[]{:S(2)}) collective-permute-start(bf16[2,2,2,2,32,256]{5,4,3,2,1,0:T(8,128)(2,1)S(1)} %get-tuple-element.111), channel_id=1, source_target_pairs={{0,2},{1,3},{2,0},{3,1},{4,6},{5,7},{6,4},{7,5},{8,10},{9,11},{10,... | collective-permute-start | bytes 786440 | tf_op jit(solution)/shard_map/ppermute | solution.py:495
  78.7 2.1 %collective-permute-start.23 = (bf16[2,2,2,32,256]{4,3,2,1,0:T(8,128)(2,1)S(1)}, bf16[2,2,2,32,256]{4,3,2,1,0:T(8,128)(2,1)S(1)}, u32[]{:S(2)}, u32[]{:S(2)}) collective-permute-start(bf16[2,2,2,32,256]{4,3,2,1,0:T(8,128)(2,1)S(1)} %get-tuple-element.97), channel_id=1, source_target_pairs={{0,4},{1,5},{2,6},{3,7},{4,0},{5,1},{6,2},{7,3},{8,12},{9,13},{10,... | collective-permute-start | bytes 393224 | tf_op jit(solution)/shard_map/ppermute | solution.py:502
  80.8 6.6 %collective-permute-done.31.came = bf16[2,2,2,2,32,256]{5,4,3,2,1,0:T(8,128)(2,1)S(1)} collective-permute-done((bf16[2,2,2,2,32,256]{5,4,3,2,1,0:T(8,128)(2,1)S(1)}, bf16[2,2,2,2,32,256]{5,4,3,2,1,0:T(8,128)(2,1)S(1)}, u32[]{:S(2)}, u32[]{:S(2)}) %collective-permute-start.31) | collective-permute-done | bytes 262176 | tf_op jit(solution)/shard_map/ppermute | solution.py:495
  88.6 6.7 %collective-permute-done.32.refs_3_ = bf16[2,2,2,32,256]{4,3,2,1,0:T(8,128)(2,1)S(1)} collective-permute-done((bf16[2,2,2,32,256]{4,3,2,1,0:T(8,128)(2,1)S(1)}, bf16[2,2,2,32,256]{4,3,2,1,0:T(8,128)(2,1)S(1)}, u32[]{:S(2)}, u32[]{:S(2)}) %collective-permute-start.32) | collective-permute-done | bytes 131104 | tf_op jit(solution)/shard_map/ppermute | solution.py:502
  (71 shorter events, 23.7 us)
Async XLA Ops:
  2.5 12.5 %collective-permute-start = (bf16[784,256]{1,0:T(8,128)(2,1)S(1)}, bf16[784,256]{1,0:T(8,128)(2,1)S(1)}, u32[]{:S(2)}, u32[]{:S(2)}) collective-permute-start(bf16[784,256]{1,0:T(8,128)(2,1)S(1)} %get-tuple-element.62.packed_0), channel_id=1, source_target_pairs={{0,8},{8,0},{16,24},{24,16},{1,9},{9,1},{17,25},{25,17},{2,10},{10... | collective-permute-start | bytes 1204232 | tf_op jit(solution)/shard_map/ppermute | solution.py:359
  5.5 10.8 %collective-permute-start.1 = (bf16[784,256]{1,0:T(8,128)(2,1)S(1)}, bf16[784,256]{1,0:T(8,128)(2,1)S(1)}, u32[]{:S(2)}, u32[]{:S(2)}) collective-permute-start(bf16[784,256]{1,0:T(8,128)(2,1)S(1)} %get-tuple-element.63.packed_1), channel_id=1, source_target_pairs={{0,16},{8,24},{16,0},{24,8},{1,17},{9,25},{17,1},{25,9},{2,18},{10... | collective-permute-start | bytes 1204232 | tf_op jit(solution)/shard_map/ppermute | solution.py:359
  7.0 13.1 %collective-permute-start.2 = (bf16[784,256]{1,0:T(8,128)(2,1)S(1)}, bf16[784,256]{1,0:T(8,128)(2,1)S(1)}, u32[]{:S(2)}, u32[]{:S(2)}) collective-permute-start(bf16[784,256]{1,0:T(8,128)(2,1)S(1)} %get-tuple-element.62.packed_0), channel_id=1, source_target_pairs={{0,2},{1,3},{2,6},{3,7},{4,0},{5,1},{6,4},{7,5},{8,10},{9,11},{10,... | collective-permute-start | bytes 1204232 | tf_op jit(solution)/shard_map/ppermute | solution.py:365
  8.6 18.4 %collective-permute-start.3 = (bf16[784,256]{1,0:T(8,128)(2,1)S(1)}, bf16[784,256]{1,0:T(8,128)(2,1)S(1)}, u32[]{:S(2)}, u32[]{:S(2)}) collective-permute-start(bf16[784,256]{1,0:T(8,128)(2,1)S(1)} %get-tuple-element.63.packed_1), channel_id=1, source_target_pairs={{0,2},{1,3},{2,6},{3,7},{4,0},{5,1},{6,4},{7,5},{8,10},{9,11},{10,... | collective-permute-start | bytes 1204232 | tf_op jit(solution)/shard_map/ppermute | solution.py:365
  16.8 11.0 %collective-permute-start.6 = (bf16[2,2,192,256]{3,2,1,0:T(8,128)(2,1)S(1)}, bf16[2,2,192,256]{3,2,1,0:T(8,128)(2,1)S(1)}, u32[]{:S(2)}, u32[]{:S(2)}) collective-permute-start(bf16[2,2,192,256]{3,2,1,0:T(8,128)(2,1)S(1)} %get-tuple-element.66), channel_id=1, source_target_pairs={{0,16},{8,24},{16,0},{24,8},{1,17},{9,25},{17,1},{25,9},{2,18},{10... | collective-permute-start | bytes 1179656 | tf_op jit(solution)/shard_map/ppermute | solution.py:359
  18.4 12.1 %collective-permute-start.7 = (bf16[2,2,192,256]{3,2,1,0:T(8,128)(2,1)S(1)}, bf16[2,2,192,256]{3,2,1,0:T(8,128)(2,1)S(1)}, u32[]{:S(2)}, u32[]{:S(2)}) collective-permute-start(bf16[2,2,192,256]{3,2,1,0:T(8,128)(2,1)S(1)} %get-tuple-element.67), channel_id=1, source_target_pairs={{0,8},{8,0},{16,24},{24,16},{1,9},{9,1},{17,25},{25,17},{2,10},{10... | collective-permute-start | bytes 1179656 | tf_op jit(solution)/shard_map/ppermute | solution.py:359
  20.1 16.3 %collective-permute-start.4 = (bf16[784,256]{1,0:T(8,128)(2,1)S(1)}, bf16[784,256]{1,0:T(8,128)(2,1)S(1)}, u32[]{:S(2)}, u32[]{:S(2)}) collective-permute-start(bf16[784,256]{1,0:T(8,128)(2,1)S(1)} %collective-permute-done.2.packed_0), channel_id=1, source_target_pairs={{0,8},{8,0},{16,24},{24,16},{1,9},{9,1},{17,25},{25,17},{2,10},{10... | collective-permute-start | bytes 1204232 | tf_op jit(solution)/shard_map/ppermute | solution.py:359
  27.0 9.5 %collective-permute-start.5 = (bf16[784,256]{1,0:T(8,128)(2,1)S(1)}, bf16[784,256]{1,0:T(8,128)(2,1)S(1)}, u32[]{:S(2)}, u32[]{:S(2)}) collective-permute-start(bf16[784,256]{1,0:T(8,128)(2,1)S(1)} %collective-permute-done.3.packed_1), channel_id=1, source_target_pairs={{0,16},{8,24},{16,0},{24,8},{1,17},{9,25},{17,1},{25,9},{2,18},{10... | collective-permute-start | bytes 1204232 | tf_op jit(solution)/shard_map/ppermute | solution.py:359
  30.9 15.4 %collective-permute-start.11 = (bf16[2,2,384,256]{3,2,1,0:T(8,128)(2,1)S(1)}, bf16[2,2,384,256]{3,2,1,0:T(8,128)(2,1)S(1)}, u32[]{:S(2)}, u32[]{:S(2)}) collective-permute-start(bf16[2,2,384,256]{3,2,1,0:T(8,128)(2,1)S(1)} %near.2.own.refs_0_), channel_id=1, source_target_pairs={{0,4},{1,5},{2,0},{3,1},{4,6},{5,7},{6,2},{7,3},{8,12},{9,13},{10,... | collective-permute-start | bytes 2359304 | tf_op jit(solution)/shard_map/ppermute | solution.py:365
  37.1 8.5 %collective-permute-start.8 = (bf16[2,2,192,256]{3,2,1,0:T(8,128)(2,1)S(1)}, bf16[2,2,192,256]{3,2,1,0:T(8,128)(2,1)S(1)}, u32[]{:S(2)}, u32[]{:S(2)}) collective-permute-start(bf16[2,2,192,256]{3,2,1,0:T(8,128)(2,1)S(1)} %get-tuple-element.74), channel_id=1, source_target_pairs={{0,16},{8,24},{16,0},{24,8},{1,17},{9,25},{17,1},{25,9},{2,18},{10... | collective-permute-start | bytes 1179656 | tf_op jit(solution)/shard_map/ppermute | solution.py:359
  37.7 8.2 %collective-permute-start.9 = (bf16[2,2,192,256]{3,2,1,0:T(8,128)(2,1)S(1)}, bf16[2,2,192,256]{3,2,1,0:T(8,128)(2,1)S(1)}, u32[]{:S(2)}, u32[]{:S(2)}) collective-permute-start(bf16[2,2,192,256]{3,2,1,0:T(8,128)(2,1)S(1)} %get-tuple-element.75), channel_id=1, source_target_pairs={{0,8},{8,0},{16,24},{24,16},{1,9},{9,1},{17,25},{25,17},{2,10},{10... | collective-permute-start | bytes 1179656 | tf_op jit(solution)/shard_map/ppermute | solution.py:359
  46.4 9.8 %collective-permute-start.12 = (bf16[2,2,2,384,256]{4,3,2,1,0:T(8,128)(2,1)S(1)}, bf16[2,2,2,384,256]{4,3,2,1,0:T(8,128)(2,1)S(1)}, u32[]{:S(2)}, u32[]{:S(2)}) collective-permute-start(bf16[2,2,2,384,256]{4,3,2,1,0:T(8,128)(2,1)S(1)} %stack.1), channel_id=1, source_target_pairs={{0,1},{1,0},{2,3},{3,2},{4,5},{5,4},{6,7},{7,6},{8,9},{9,8},{10,11... | collective-permute-start | bytes 4718600 | tf_op jit(solution)/shard_map/ppermute | solution.py:362
  46.5 6.2 %collective-permute-start.13 = (bf16[2,2,384,256]{3,2,1,0:T(8,128)(2,1)S(1)}, bf16[2,2,384,256]{3,2,1,0:T(8,128)(2,1)S(1)}, u32[]{:S(2)}, u32[]{:S(2)}) collective-permute-start(bf16[2,2,384,256]{3,2,1,0:T(8,128)(2,1)S(1)} %collective-permute-done.11.own), channel_id=1, source_target_pairs={{0,1},{1,0},{2,3},{3,2},{4,5},{5,4},{6,7},{7,6},{8,9},{9,8},{10,11... | collective-permute-start | bytes 2359304 | tf_op jit(solution)/shard_map/ppermute | solution.py:362
  47.0 13.9 %collective-permute-start.10 = (bf16[2,384,256]{2,1,0:T(8,128)(2,1)S(1)}, bf16[2,384,256]{2,1,0:T(8,128)(2,1)S(1)}, u32[]{:S(2)}, u32[]{:S(2)}) collective-permute-start(bf16[2,384,256]{2,1,0:T(8,128)(2,1)S(1)} %get-tuple-element.76), channel_id=1, source_target_pairs={{0,2},{1,3},{2,6},{3,7},{4,0},{5,1},{6,4},{7,5},{8,10},{9,11},{10,... | collective-permute-start | bytes 1179656 | tf_op jit(solution)/shard_map/ppermute | solution.py:365
  49.0 15.3 %collective-permute-start.16 = (bf16[3,2,192,256]{3,2,1,0:T(8,128)(2,1)S(1)}, bf16[3,2,192,256]{3,2,1,0:T(8,128)(2,1)S(1)}, u32[]{:S(2)}, u32[]{:S(2)}) collective-permute-start(bf16[3,2,192,256]{3,2,1,0:T(8,128)(2,1)S(1)} %get-tuple-element.84), channel_id=1, source_target_pairs={{0,16},{8,24},{16,0},{24,8},{1,17},{9,25},{17,1},{25,9},{2,18},{10... | collective-permute-start | bytes 1769480 | tf_op jit(solution)/shard_map/ppermute | solution.py:359
  50.5 17.1 %collective-permute-start.24 = (bf16[2,384,256]{2,1,0:T(8,128)(2,1)S(1)}, bf16[2,384,256]{2,1,0:T(8,128)(2,1)S(1)}, u32[]{:S(2)}, u32[]{:S(2)}) collective-permute-start(bf16[2,384,256]{2,1,0:T(8,128)(2,1)S(1)} %get-tuple-element.98), channel_id=1, source_target_pairs={{0,2},{1,3},{2,6},{3,7},{4,0},{5,1},{6,4},{7,5},{8,10},{9,11},{10,... | collective-permute-start | bytes 1179656 | tf_op jit(solution)/shard_map/ppermute | solution.py:365
  52.7 11.5 %collective-permute-start.17 = (bf16[2,2,192,256]{3,2,1,0:T(8,128)(2,1)S(1)}, bf16[2,2,192,256]{3,2,1,0:T(8,128)(2,1)S(1)}, u32[]{:S(2)}, u32[]{:S(2)}) collective-permute-start(bf16[2,2,192,256]{3,2,1,0:T(8,128)(2,1)S(1)} %get-tuple-element.85), channel_id=1, source_target_pairs={{0,8},{8,0},{16,24},{24,16},{1,9},{9,1},{17,25},{25,17},{2,10},{10... | collective-permute-start | bytes 1179656 | tf_op jit(solution)/shard_map/ppermute | solution.py:359
  66.2 2.0 %collective-permute-start.19 = (bf16[4,2,32,256]{3,2,1,0:T(8,128)(2,1)S(1)}, bf16[4,2,32,256]{3,2,1,0:T(8,128)(2,1)S(1)}, u32[]{:S(2)}, u32[]{:S(2)}) collective-permute-start(bf16[4,2,32,256]{3,2,1,0:T(8,128)(2,1)S(1)} %get-tuple-element.90), channel_id=1, source_target_pairs={{0,1},{1,0},{2,3},{3,2},{4,5},{5,4},{6,7},{7,6},{8,9},{9,8},{10,11... | collective-permute-start | bytes 393224 | tf_op jit(solution)/shard_map/ppermute | solution.py:362
  67.6 3.1 %collective-permute-start.25 = (bf16[384,256]{1,0:T(8,128)(2,1)S(1)}, bf16[384,256]{1,0:T(8,128)(2,1)S(1)}, u32[]{:S(2)}, u32[]{:S(2)}) collective-permute-start(bf16[384,256]{1,0:T(8,128)(2,1)S(1)} %get-tuple-element.115), channel_id=1, source_target_pairs={{0,1},{1,0},{2,3},{3,2},{4,5},{5,4},{6,7},{7,6},{8,9},{9,8},{10,11... | collective-permute-start | bytes 589832 | tf_op jit(solution)/shard_map/ppermute | solution.py:362
  67.7 3.0 %collective-permute-start.26 = (bf16[384,256]{1,0:T(8,128)(2,1)S(1)}, bf16[384,256]{1,0:T(8,128)(2,1)S(1)}, u32[]{:S(2)}, u32[]{:S(2)}) collective-permute-start(bf16[384,256]{1,0:T(8,128)(2,1)S(1)} %get-tuple-element.114), channel_id=1, source_target_pairs={{0,1},{1,0},{2,3},{3,2},{4,5},{5,4},{6,7},{7,6},{8,9},{9,8},{10,11... | collective-permute-start | bytes 589832 | tf_op jit(solution)/shard_map/ppermute | solution.py:362
  68.3 8.6 %collective-permute-start.22 = (bf16[2,2,2,2,32,256]{5,4,3,2,1,0:T(8,128)(2,1)S(1)}, bf16[2,2,2,2,32,256]{5,4,3,2,1,0:T(8,128)(2,1)S(1)}, u32[]{:S(2)}, u32[]{:S(2)}) collective-permute-start(bf16[2,2,2,2,32,256]{5,4,3,2,1,0:T(8,128)(2,1)S(1)} %get-tuple-element.95), channel_id=1, source_target_pairs={{0,2},{1,3},{2,0},{3,1},{4,6},{5,7},{6,4},{7,5},{8,10},{9,11},{10,... | collective-permute-start | bytes 786440 | tf_op jit(solution)/shard_map/ppermute | solution.py:495
  76.9 10.5 %collective-permute-start.31 = (bf16[2,2,2,2,32,256]{5,4,3,2,1,0:T(8,128)(2,1)S(1)}, bf16[2,2,2,2,32,256]{5,4,3,2,1,0:T(8,128)(2,1)S(1)}, u32[]{:S(2)}, u32[]{:S(2)}) collective-permute-start(bf16[2,2,2,2,32,256]{5,4,3,2,1,0:T(8,128)(2,1)S(1)} %get-tuple-element.111), channel_id=1, source_target_pairs={{0,2},{1,3},{2,0},{3,1},{4,6},{5,7},{6,4},{7,5},{8,10},{9,11},{10,... | collective-permute-start | bytes 786440 | tf_op jit(solution)/shard_map/ppermute | solution.py:495
  78.7 9.9 %collective-permute-start.23 = (bf16[2,2,2,32,256]{4,3,2,1,0:T(8,128)(2,1)S(1)}, bf16[2,2,2,32,256]{4,3,2,1,0:T(8,128)(2,1)S(1)}, u32[]{:S(2)}, u32[]{:S(2)}) collective-permute-start(bf16[2,2,2,32,256]{4,3,2,1,0:T(8,128)(2,1)S(1)} %get-tuple-element.97), channel_id=1, source_target_pairs={{0,4},{1,5},{2,6},{3,7},{4,0},{5,1},{6,2},{7,3},{8,12},{9,13},{10,... | collective-permute-start | bytes 393224 | tf_op jit(solution)/shard_map/ppermute | solution.py:502
  87.5 7.8 %collective-permute-start.32 = (bf16[2,2,2,32,256]{4,3,2,1,0:T(8,128)(2,1)S(1)}, bf16[2,2,2,32,256]{4,3,2,1,0:T(8,128)(2,1)S(1)}, u32[]{:S(2)}, u32[]{:S(2)}) collective-permute-start(bf16[2,2,2,32,256]{4,3,2,1,0:T(8,128)(2,1)S(1)} %get-tuple-element.113), channel_id=1, source_target_pairs={{0,4},{1,5},{2,6},{3,7},{4,0},{5,1},{6,2},{7,3},{8,12},{9,13},{10,... | collective-permute-start | bytes 393224 | tf_op jit(solution)/shard_map/ppermute | solution.py:502
  (11 other events, 33.1 us)

commit v9 on v8

--- a/solution.py
+++ b/solution.py
@@ -94,10 +94,30 @@
             copy_if(label_of(came[1 - h], held, half, j), found, sends[h].at[j])
 
 
+def pick_half_kernel(held, count, h, packed, came, labels, send):
+    owner = lax.axis_index("kp")
+    half = (packed.shape[0] - LABELS) // (2 * held)
+    found = entries(packed, owner, held, half)
+    found += entries(came, owner ^ BITS[h][0], held, half)
+    if len(send.shape) == 2:
+        send[2 * count * half :] = jnp.zeros((LABELS, send.shape[1]), BF16)
+    for j in range(count):
+        label = label_of(labels, held, half, j)
+        if len(send.shape) == 4:
+            copy_if(label, found, send.at[j])
+            continue
+        for name, message, real, imag in found:
+
+            @pl.when(label == name)
+            def _(j=j, message=message, real=real, imag=imag):
+                send[2 * j * half : (2 * j + 1) * half] = message[real : real + half]
+                send[(2 * j + 1) * half : (2 * j + 2) * half] = message[imag : imag + half]
+
+
 def near_kernel(held, packed_0, packed_1, came_0, came_1, picked_0, picked_1, near, *each):
     owner = lax.axis_index("kp")
     packed, came, picked = (packed_0, packed_1), (came_0, came_1), (picked_0, picked_1)
-    half = picked_0.shape[2]
+    half = picked_1.shape[2]
     for j in range(near.shape[0]):
         label = label_of(packed_0, held, half, j)
         for h in range(2):
@@ -108,7 +128,11 @@
 
             @pl.when(jnp.logical_not(hit))
             def _(h=h, j=j, out=out):
-                out[...] = picked[h][j]
+                if len(picked[h].shape) == 4:
+                    out[...] = picked[h][j]
+                else:
+                    out[0] = picked[h][2 * j * half : (2 * j + 1) * half]
+                    out[1] = picked[h][(2 * j + 1) * half : (2 * j + 2) * half]
 
     for j, out in enumerate(each):
         out[...] = near[j]
@@ -428,8 +452,18 @@
     total = product(first_kernel, 1, near, coulomb[None, :])
 
     came_before = [across(packed_before[h], BITS[h][0]) for h in range(2)]
-    came_before, total = tie((came_before, total))
-    picked_before = pick(packed_before, came_before)
+    picked_before, sent = [None, None], total
+    for h in range(2):
+        came_h, _ = tie((came_before[h], sent))
+        sent = run(
+            functools.partial(pick_half_kernel, held, count, h),
+            shape((count, 2, half, t) if h else (2 * count * half + LABELS, t), BF16),
+            packed_before[h],
+            came_h,
+            came[1 - h],
+            name="pick_half",
+        )
+        picked_before[h] = across(sent, BITS[h][1])
     near_before, before_each = near_of(packed_before, came_before, picked_before, True)
     behind = [along(x, FORTH) for x in before_each]
 

time: 96.3 us -> 96.4 us (level)
    pallas_call x22 -> x23, Pallas kernels: 24.1 us -> 24 us  [run(): pl.pallas_call(body, in_specs=specs or [VMEM] * len(args), out_specs=[VME...]
  transfers between devices with their start and end apart: 33 -> 33, of which waited for: 18 -> 17; matrix products, arithmetic and copies ran while one was open for 0% -> 0% of each run, Pallas kernels for 23% -> 23%
where the time goes in v9:
time: 96.4 us; the launch traced here: 96.2 us
  waiting for transfers between devices  37.9 us (39%)
  starting transfers between devices  32.7 us (34%)
  Pallas kernels  24 us (25%)
    pallas_call x23, Pallas kernels, run(): pl.pallas_call(body, in_specs=specs or [VMEM] * len(args), out_specs=[VME...  24 us
    ppermute x10, waiting for transfers between devices, across(): return lax.ppermute(x, 'kp', [(i, i ^ bit) for i in range(n_kp)])  12.5 us
    ppermute x10, starting transfers between devices, across(): return lax.ppermute(x, 'kp', [(i, i ^ bit) for i in range(n_kp)])  11.1 us
    ppermute x5, starting transfers between devices, along(): lax.ppermute(x, 'ga', [(i, 2 * chips_on[i // 2] + i % 2) for i in range(n...  11 us
    ppermute x2, waiting for transfers between devices, quick(): came_j = lax.ppermute(sends, 'ga', [(i, i ^ 2) for i in range(n_ga)])  8.32 us
    ppermute x5, waiting for transfers between devices, along(): lax.ppermute(x, 'ga', [(i, 2 * chips_on[i // 2] + i % 2) for i in range(n...  7.86 us
    ppermute x2, waiting for transfers between devices, quick(): lax.ppermute(sends, 'ga', [(i, i ^ 4) for i in range(n_ga)])  6.82 us
    ppermute x14, starting transfers between devices, other_core(): return lax.ppermute(x, 'ga', [(i, i ^ 1) for i in range(n_ga)])  3.87 us
  transfers between devices with their start and end apart: 33, of which 17 were waited for; matrix products, arithmetic and copies ran while one was open for 0% of the time, Pallas kernels for 23%

profile of v9, /device:TPU:0, one launch (start us, length us, event | category | flops | bytes accessed | tf_op | source)
XLA Modules:
  0.0 96.2 jit_solution(9609551352179709187)
XLA Ops:
  2.5 3.0 %collective-permute-start = (bf16[784,256]{1,0:T(8,128)(2,1)S(1)}, bf16[784,256]{1,0:T(8,128)(2,1)S(1)}, u32[]{:S(2)}, u32[]{:S(2)}) collective-permute-start(bf16[784,256]{1,0:T(8,128)(2,1)S(1)} %get-tuple-element.59.packed_0), channel_id=1, source_target_pairs={{0,8},{8,0},{16,24},{24,16},{1,9},{9,1},{17,25},{25,17},{2,10},{10... | collective-permute-start | bytes 1204232 | tf_op jit(solution)/shard_map/ppermute | solution.py:383
  5.5 1.5 %collective-permute-start.1 = (bf16[784,256]{1,0:T(8,128)(2,1)S(1)}, bf16[784,256]{1,0:T(8,128)(2,1)S(1)}, u32[]{:S(2)}, u32[]{:S(2)}) collective-permute-start(bf16[784,256]{1,0:T(8,128)(2,1)S(1)} %get-tuple-element.60.packed_1), channel_id=1, source_target_pairs={{0,16},{8,24},{16,0},{24,8},{1,17},{9,25},{17,1},{25,9},{2,18},{10... | collective-permute-start | bytes 1204232 | tf_op jit(solution)/shard_map/ppermute | solution.py:383
  7.0 1.6 %collective-permute-start.2 = (bf16[784,256]{1,0:T(8,128)(2,1)S(1)}, bf16[784,256]{1,0:T(8,128)(2,1)S(1)}, u32[]{:S(2)}, u32[]{:S(2)}) collective-permute-start(bf16[784,256]{1,0:T(8,128)(2,1)S(1)} %get-tuple-element.59.packed_0), channel_id=1, source_target_pairs={{0,2},{1,3},{2,6},{3,7},{4,0},{5,1},{6,4},{7,5},{8,10},{9,11},{10,... | collective-permute-start | bytes 1204232 | tf_op jit(solution)/shard_map/ppermute | solution.py:389
  8.6 2.6 %collective-permute-start.3 = (bf16[784,256]{1,0:T(8,128)(2,1)S(1)}, bf16[784,256]{1,0:T(8,128)(2,1)S(1)}, u32[]{:S(2)}, u32[]{:S(2)}) collective-permute-start(bf16[784,256]{1,0:T(8,128)(2,1)S(1)} %get-tuple-element.60.packed_1), channel_id=1, source_target_pairs={{0,2},{1,3},{2,6},{3,7},{4,0},{5,1},{6,4},{7,5},{8,10},{9,11},{10,... | collective-permute-start | bytes 1204232 | tf_op jit(solution)/shard_map/ppermute | solution.py:389
  11.2 3.8 %load.1.screened = bf16[2,2,384,3072]{3,2,1,0:T(8,128)(2,1)S(1)} custom-call(bf16[2,2,384,3072]{3,2,1,0:T(8,128)(2,1)} %source), custom_call_target="tpu_custom_call" | custom-call | tf_op jit(solution)/shard_map/load/pallas_call | solution.py:30
  16.8 1.6 %collective-permute-start.6 = (bf16[2,2,192,256]{3,2,1,0:T(8,128)(2,1)S(1)}, bf16[2,2,192,256]{3,2,1,0:T(8,128)(2,1)S(1)}, u32[]{:S(2)}, u32[]{:S(2)}) collective-permute-start(bf16[2,2,192,256]{3,2,1,0:T(8,128)(2,1)S(1)} %get-tuple-element.63), channel_id=1, source_target_pairs={{0,16},{8,24},{16,0},{24,8},{1,17},{9,25},{17,1},{25,9},{2,18},{10... | collective-permute-start | bytes 1179656 | tf_op jit(solution)/shard_map/ppermute | solution.py:383
  20.7 6.3 %collective-permute-done.3.packed.packed_1 = bf16[784,256]{1,0:T(8,128)(2,1)S(1)} collective-permute-done((bf16[784,256]{1,0:T(8,128)(2,1)S(1)}, bf16[784,256]{1,0:T(8,128)(2,1)S(1)}, u32[]{:S(2)}, u32[]{:S(2)}) %collective-permute-start.3) | collective-permute-done | bytes 401440 | tf_op jit(solution)/shard_map/ppermute | solution.py:389
  27.9 2.6 %collective-permute-done.7.picked_1 = bf16[2,2,192,256]{3,2,1,0:T(8,128)(2,1)S(1)} collective-permute-done((bf16[2,2,192,256]{3,2,1,0:T(8,128)(2,1)S(1)}, bf16[2,2,192,256]{3,2,1,0:T(8,128)(2,1)S(1)}, u32[]{:S(2)}, u32[]{:S(2)}) %collective-permute-start.7) | collective-permute-done | bytes 393248 | tf_op jit(solution)/shard_map/ppermute | solution.py:383
  30.9 2.6 %collective-permute-start.11 = (bf16[2,2,384,256]{3,2,1,0:T(8,128)(2,1)S(1)}, bf16[2,2,384,256]{3,2,1,0:T(8,128)(2,1)S(1)}, u32[]{:S(2)}, u32[]{:S(2)}) collective-permute-start(bf16[2,2,384,256]{3,2,1,0:T(8,128)(2,1)S(1)} %near.2.own.refs_0_), channel_id=1, source_target_pairs={{0,4},{1,5},{2,0},{3,1},{4,6},{5,7},{6,2},{7,3},{8,12},{9,13},{10,... | collective-permute-start | bytes 2359304 | tf_op jit(solution)/shard_map/ppermute | solution.py:389
  33.5 1.8 %product.3.before = f32[2,384,1024]{2,1,0:T(8,128)S(1)} custom-call(bf16[2,2,384,3072]{3,2,1,0:T(8,128)(2,1)S(1)} %load.1.screened, bf16[2,2,384,256]{3,2,1,0:T(8,128)(2,1)S(1)} %near.2.own.refs_0_, f32[1,384]{1,0:T(1,128)S(1)} %broadcast_in_dim.3.coulomb), custom_call_target="tpu_custom_call" | custom-call | tf_op jit(solution)/shard_map/product/pallas_call | solution.py:30
  38.3 7.5 %collective-permute-done.9.picked_1 = bf16[2,2,192,256]{3,2,1,0:T(8,128)(2,1)S(1)} collective-permute-done((bf16[2,2,192,256]{3,2,1,0:T(8,128)(2,1)S(1)}, bf16[2,2,192,256]{3,2,1,0:T(8,128)(2,1)S(1)}, u32[]{:S(2)}, u32[]{:S(2)}) %collective-permute-start.9) | collective-permute-done | bytes 393248 | tf_op jit(solution)/shard_map/ppermute | solution.py:383
  47.0 2.0 %collective-permute-start.10 = (bf16[2,384,256]{2,1,0:T(8,128)(2,1)S(1)}, bf16[2,384,256]{2,1,0:T(8,128)(2,1)S(1)}, u32[]{:S(2)}, u32[]{:S(2)}) collective-permute-start(bf16[2,384,256]{2,1,0:T(8,128)(2,1)S(1)} %get-tuple-element.71), channel_id=1, source_target_pairs={{0,2},{1,3},{2,6},{3,7},{4,0},{5,1},{6,4},{7,5},{8,10},{9,11},{10,... | collective-permute-start | bytes 1179656 | tf_op jit(solution)/shard_map/ppermute | solution.py:389
  49.0 1.5 %collective-permute-start.16 = (bf16[3,2,192,256]{3,2,1,0:T(8,128)(2,1)S(1)}, bf16[3,2,192,256]{3,2,1,0:T(8,128)(2,1)S(1)}, u32[]{:S(2)}, u32[]{:S(2)}) collective-permute-start(bf16[3,2,192,256]{3,2,1,0:T(8,128)(2,1)S(1)} %get-tuple-element.78), channel_id=1, source_target_pairs={{0,16},{8,24},{16,0},{24,8},{1,17},{9,25},{17,1},{25,9},{2,18},{10... | collective-permute-start | bytes 1769480 | tf_op jit(solution)/shard_map/ppermute | solution.py:383
  50.5 2.2 %collective-permute-start.24 = (bf16[2,384,256]{2,1,0:T(8,128)(2,1)S(1)}, bf16[2,384,256]{2,1,0:T(8,128)(2,1)S(1)}, u32[]{:S(2)}, u32[]{:S(2)}) collective-permute-start(bf16[2,384,256]{2,1,0:T(8,128)(2,1)S(1)} %get-tuple-element.92), channel_id=1, source_target_pairs={{0,2},{1,3},{2,6},{3,7},{4,0},{5,1},{6,4},{7,5},{8,10},{9,11},{10,... | collective-permute-start | bytes 1179656 | tf_op jit(solution)/shard_map/ppermute | solution.py:389
  53.3 3.0 %product.4.before = f32[2,384,1024]{2,1,0:T(8,128)S(1)} custom-call(bf16[2,2,384,3072]{3,2,1,0:T(8,128)(2,1)S(1)} %load.1.screened, bf16[2,2,384,256]{3,2,1,0:T(8,128)(2,1)S(1)} %collective-permute-done.11.own, bf16[2,2,384,256]{3,2,1,0:T(8,128)(2,1)S(1)} %collective-permute-done.13.pair, ...), custom_call_target="tpu_custom_call", output_to_operand_aliasing={{}: (3, {})} | custom-call | tf_op jit(solution)/shard_map/product/pallas_call | solution.py:30
  56.3 4.6 %product.5.before = f32[2,384,1024]{2,1,0:T(8,128)S(1)} custom-call(bf16[2,2,384,3072]{3,2,1,0:T(8,128)(2,1)S(1)} %load.1.screened, bf16[2,2,384,256]{3,2,1,0:T(8,128)(2,1)S(1)} %get-tuple-element.75.refs_1_.own, bf16[2,2,2,384,256]{4,3,2,1,0:T(8,128)(2,1)S(1)} %collective-permute-done.12.pairs, ...), custom_call_target="tpu_custom_call", output_to_operand_aliasing={{}: (3, {})} | custom-call | tf_op jit(solution)/shard_map/product/pallas_call | solution.py:30
  62.8 1.5 %image.2 = bf16[2,384,512]{2,1,0:T(8,128)(2,1)S(1)} custom-call(bf16[2,2,384,3072]{3,2,1,0:T(8,128)(2,1)S(1)} %load.1.screened, bf16[2,384,256]{2,1,0:T(8,128)(2,1)S(1)} %collective-permute-done.10.own, bf16[384,256]{1,0:T(8,128)(2,1)S(1)} %collective-permute-done.14.pair_real, bf16[384,256]{1,0:T(8,128)(2,1)S(1)} %collective-permute-done.15.pair_imag, ...), custom_call_target="tpu_custom_call" | custom-call | tf_op jit(solution)/shard_map/image/pallas_call | solution.py:30
  68.2 1.9 %collective-permute-start.22 = (bf16[2,2,2,2,32,256]{5,4,3,2,1,0:T(8,128)(2,1)S(1)}, bf16[2,2,2,2,32,256]{5,4,3,2,1,0:T(8,128)(2,1)S(1)}, u32[]{:S(2)}, u32[]{:S(2)}) collective-permute-start(bf16[2,2,2,2,32,256]{5,4,3,2,1,0:T(8,128)(2,1)S(1)} %get-tuple-element.89), channel_id=1, source_target_pairs={{0,2},{1,3},{2,0},{3,1},{4,6},{5,7},{6,4},{7,5},{8,10},{9,11},{10,... | collective-permute-start | bytes 786440 | tf_op jit(solution)/shard_map/ppermute | solution.py:529
  70.7 1.5 %image.3 = bf16[2,384,512]{2,1,0:T(8,128)(2,1)S(1)} custom-call(bf16[2,2,384,3072]{3,2,1,0:T(8,128)(2,1)S(1)} %load.1.screened, bf16[2,384,256]{2,1,0:T(8,128)(2,1)S(1)} %collective-permute-done.24.own, bf16[384,256]{1,0:T(8,128)(2,1)S(1)} %collective-permute-done.25.pair_real, bf16[384,256]{1,0:T(8,128)(2,1)S(1)} %collective-permute-done.26.pair_imag, ...), custom_call_target="tpu_custom_call" | custom-call | tf_op jit(solution)/shard_map/image/pallas_call | solution.py:30
  75.3 1.6 %collective-permute-done.22.came = bf16[2,2,2,2,32,256]{5,4,3,2,1,0:T(8,128)(2,1)S(1)} collective-permute-done((bf16[2,2,2,2,32,256]{5,4,3,2,1,0:T(8,128)(2,1)S(1)}, bf16[2,2,2,2,32,256]{5,4,3,2,1,0:T(8,128)(2,1)S(1)}, u32[]{:S(2)}, u32[]{:S(2)}) %collective-permute-start.22) | collective-permute-done | bytes 262176 | tf_op jit(solution)/shard_map/ppermute | solution.py:529
  76.9 1.7 %collective-permute-start.31 = (bf16[2,2,2,2,32,256]{5,4,3,2,1,0:T(8,128)(2,1)S(1)}, bf16[2,2,2,2,32,256]{5,4,3,2,1,0:T(8,128)(2,1)S(1)}, u32[]{:S(2)}, u32[]{:S(2)}) collective-permute-start(bf16[2,2,2,2,32,256]{5,4,3,2,1,0:T(8,128)(2,1)S(1)} %get-tuple-element.105), channel_id=1, source_target_pairs={{0,2},{1,3},{2,0},{3,1},{4,6},{5,7},{6,4},{7,5},{8,10},{9,11},{10,... | collective-permute-start | bytes 786440 | tf_op jit(solution)/shard_map/ppermute | solution.py:529
  78.7 2.1 %collective-permute-start.23 = (bf16[2,2,2,32,256]{4,3,2,1,0:T(8,128)(2,1)S(1)}, bf16[2,2,2,32,256]{4,3,2,1,0:T(8,128)(2,1)S(1)}, u32[]{:S(2)}, u32[]{:S(2)}) collective-permute-start(bf16[2,2,2,32,256]{4,3,2,1,0:T(8,128)(2,1)S(1)} %get-tuple-element.91), channel_id=1, source_target_pairs={{0,4},{1,5},{2,6},{3,7},{4,0},{5,1},{6,2},{7,3},{8,12},{9,13},{10,... | collective-permute-start | bytes 393224 | tf_op jit(solution)/shard_map/ppermute | solution.py:536
  80.8 6.7 %collective-permute-done.31.came = bf16[2,2,2,2,32,256]{5,4,3,2,1,0:T(8,128)(2,1)S(1)} collective-permute-done((bf16[2,2,2,2,32,256]{5,4,3,2,1,0:T(8,128)(2,1)S(1)}, bf16[2,2,2,2,32,256]{5,4,3,2,1,0:T(8,128)(2,1)S(1)}, u32[]{:S(2)}, u32[]{:S(2)}) %collective-permute-start.31) | collective-permute-done | bytes 262176 | tf_op jit(solution)/shard_map/ppermute | solution.py:529
  88.5 6.8 %collective-permute-done.32.refs_3_ = bf16[2,2,2,32,256]{4,3,2,1,0:T(8,128)(2,1)S(1)} collective-permute-done((bf16[2,2,2,32,256]{4,3,2,1,0:T(8,128)(2,1)S(1)}, bf16[2,2,2,32,256]{4,3,2,1,0:T(8,128)(2,1)S(1)}, u32[]{:S(2)}, u32[]{:S(2)}) %collective-permute-start.32) | collective-permute-done | bytes 131104 | tf_op jit(solution)/shard_map/ppermute | solution.py:536
  (72 shorter events, 23.2 us)
Async XLA Ops:
  2.5 12.5 %collective-permute-start = (bf16[784,256]{1,0:T(8,128)(2,1)S(1)}, bf16[784,256]{1,0:T(8,128)(2,1)S(1)}, u32[]{:S(2)}, u32[]{:S(2)}) collective-permute-start(bf16[784,256]{1,0:T(8,128)(2,1)S(1)} %get-tuple-element.59.packed_0), channel_id=1, source_target_pairs={{0,8},{8,0},{16,24},{24,16},{1,9},{9,1},{17,25},{25,17},{2,10},{10... | collective-permute-start | bytes 1204232 | tf_op jit(solution)/shard_map/ppermute | solution.py:383
  5.5 10.8 %collective-permute-start.1 = (bf16[784,256]{1,0:T(8,128)(2,1)S(1)}, bf16[784,256]{1,0:T(8,128)(2,1)S(1)}, u32[]{:S(2)}, u32[]{:S(2)}) collective-permute-start(bf16[784,256]{1,0:T(8,128)(2,1)S(1)} %get-tuple-element.60.packed_1), channel_id=1, source_target_pairs={{0,16},{8,24},{16,0},{24,8},{1,17},{9,25},{17,1},{25,9},{2,18},{10... | collective-permute-start | bytes 1204232 | tf_op jit(solution)/shard_map/ppermute | solution.py:383
  7.0 13.1 %collective-permute-start.2 = (bf16[784,256]{1,0:T(8,128)(2,1)S(1)}, bf16[784,256]{1,0:T(8,128)(2,1)S(1)}, u32[]{:S(2)}, u32[]{:S(2)}) collective-permute-start(bf16[784,256]{1,0:T(8,128)(2,1)S(1)} %get-tuple-element.59.packed_0), channel_id=1, source_target_pairs={{0,2},{1,3},{2,6},{3,7},{4,0},{5,1},{6,4},{7,5},{8,10},{9,11},{10,... | collective-permute-start | bytes 1204232 | tf_op jit(solution)/shard_map/ppermute | solution.py:389
  8.6 18.4 %collective-permute-start.3 = (bf16[784,256]{1,0:T(8,128)(2,1)S(1)}, bf16[784,256]{1,0:T(8,128)(2,1)S(1)}, u32[]{:S(2)}, u32[]{:S(2)}) collective-permute-start(bf16[784,256]{1,0:T(8,128)(2,1)S(1)} %get-tuple-element.60.packed_1), channel_id=1, source_target_pairs={{0,2},{1,3},{2,6},{3,7},{4,0},{5,1},{6,4},{7,5},{8,10},{9,11},{10,... | collective-permute-start | bytes 1204232 | tf_op jit(solution)/shard_map/ppermute | solution.py:389
  16.8 11.0 %collective-permute-start.6 = (bf16[2,2,192,256]{3,2,1,0:T(8,128)(2,1)S(1)}, bf16[2,2,192,256]{3,2,1,0:T(8,128)(2,1)S(1)}, u32[]{:S(2)}, u32[]{:S(2)}) collective-permute-start(bf16[2,2,192,256]{3,2,1,0:T(8,128)(2,1)S(1)} %get-tuple-element.63), channel_id=1, source_target_pairs={{0,16},{8,24},{16,0},{24,8},{1,17},{9,25},{17,1},{25,9},{2,18},{10... | collective-permute-start | bytes 1179656 | tf_op jit(solution)/shard_map/ppermute | solution.py:383
  18.4 12.1 %collective-permute-start.7 = (bf16[2,2,192,256]{3,2,1,0:T(8,128)(2,1)S(1)}, bf16[2,2,192,256]{3,2,1,0:T(8,128)(2,1)S(1)}, u32[]{:S(2)}, u32[]{:S(2)}) collective-permute-start(bf16[2,2,192,256]{3,2,1,0:T(8,128)(2,1)S(1)} %get-tuple-element.64), channel_id=1, source_target_pairs={{0,8},{8,0},{16,24},{24,16},{1,9},{9,1},{17,25},{25,17},{2,10},{10... | collective-permute-start | bytes 1179656 | tf_op jit(solution)/shard_map/ppermute | solution.py:383
  20.1 16.3 %collective-permute-start.4 = (bf16[784,256]{1,0:T(8,128)(2,1)S(1)}, bf16[784,256]{1,0:T(8,128)(2,1)S(1)}, u32[]{:S(2)}, u32[]{:S(2)}) collective-permute-start(bf16[784,256]{1,0:T(8,128)(2,1)S(1)} %collective-permute-done.2.packed.packed_0), channel_id=1, source_target_pairs={{0,8},{8,0},{16,24},{24,16},{1,9},{9,1},{17,25},{25,17},{2,10},{10... | collective-permute-start | bytes 1204232 | tf_op jit(solution)/shard_map/ppermute | solution.py:383
  27.0 10.3 %collective-permute-start.5 = (bf16[784,256]{1,0:T(8,128)(2,1)S(1)}, bf16[784,256]{1,0:T(8,128)(2,1)S(1)}, u32[]{:S(2)}, u32[]{:S(2)}) collective-permute-start(bf16[784,256]{1,0:T(8,128)(2,1)S(1)} %collective-permute-done.3.packed.packed_1), channel_id=1, source_target_pairs={{0,16},{8,24},{16,0},{24,8},{1,17},{9,25},{17,1},{25,9},{2,18},{10... | collective-permute-start | bytes 1204232 | tf_op jit(solution)/shard_map/ppermute | solution.py:383
  30.9 15.4 %collective-permute-start.11 = (bf16[2,2,384,256]{3,2,1,0:T(8,128)(2,1)S(1)}, bf16[2,2,384,256]{3,2,1,0:T(8,128)(2,1)S(1)}, u32[]{:S(2)}, u32[]{:S(2)}) collective-permute-start(bf16[2,2,384,256]{3,2,1,0:T(8,128)(2,1)S(1)} %near.2.own.refs_0_), channel_id=1, source_target_pairs={{0,4},{1,5},{2,0},{3,1},{4,6},{5,7},{6,2},{7,3},{8,12},{9,13},{10,... | collective-permute-start | bytes 2359304 | tf_op jit(solution)/shard_map/ppermute | solution.py:389
  36.7 9.1 %collective-permute-start.8 = (bf16[784,256]{1,0:T(8,128)(2,1)S(1)}, bf16[784,256]{1,0:T(8,128)(2,1)S(1)}, u32[]{:S(2)}, u32[]{:S(2)}) collective-permute-start(bf16[784,256]{1,0:T(8,128)(2,1)S(1)} %pick_half.2), channel_id=1, source_target_pairs={{0,16},{8,24},{16,0},{24,8},{1,17},{9,25},{17,1},{25,9},{2,18},{10... | collective-permute-start | bytes 1204232 | tf_op jit(solution)/shard_map/ppermute | solution.py:383
  37.6 8.2 %collective-permute-start.9 = (bf16[2,2,192,256]{3,2,1,0:T(8,128)(2,1)S(1)}, bf16[2,2,192,256]{3,2,1,0:T(8,128)(2,1)S(1)}, u32[]{:S(2)}, u32[]{:S(2)}) collective-permute-start(bf16[2,2,192,256]{3,2,1,0:T(8,128)(2,1)S(1)} %pick_half.3), channel_id=1, source_target_pairs={{0,8},{8,0},{16,24},{24,16},{1,9},{9,1},{17,25},{25,17},{2,10},{10... | collective-permute-start | bytes 1179656 | tf_op jit(solution)/shard_map/ppermute | solution.py:383
  46.4 9.9 %collective-permute-start.12 = (bf16[2,2,2,384,256]{4,3,2,1,0:T(8,128)(2,1)S(1)}, bf16[2,2,2,384,256]{4,3,2,1,0:T(8,128)(2,1)S(1)}, u32[]{:S(2)}, u32[]{:S(2)}) collective-permute-start(bf16[2,2,2,384,256]{4,3,2,1,0:T(8,128)(2,1)S(1)} %stack.1), channel_id=1, source_target_pairs={{0,1},{1,0},{2,3},{3,2},{4,5},{5,4},{6,7},{7,6},{8,9},{9,8},{10,11... | collective-permute-start | bytes 4718600 | tf_op jit(solution)/shard_map/ppermute | solution.py:386
  46.5 6.2 %collective-permute-start.13 = (bf16[2,2,384,256]{3,2,1,0:T(8,128)(2,1)S(1)}, bf16[2,2,384,256]{3,2,1,0:T(8,128)(2,1)S(1)}, u32[]{:S(2)}, u32[]{:S(2)}) collective-permute-start(bf16[2,2,384,256]{3,2,1,0:T(8,128)(2,1)S(1)} %collective-permute-done.11.own), channel_id=1, source_target_pairs={{0,1},{1,0},{2,3},{3,2},{4,5},{5,4},{6,7},{7,6},{8,9},{9,8},{10,11... | collective-permute-start | bytes 2359304 | tf_op jit(solution)/shard_map/ppermute | solution.py:386
  47.0 14.0 %collective-permute-start.10 = (bf16[2,384,256]{2,1,0:T(8,128)(2,1)S(1)}, bf16[2,384,256]{2,1,0:T(8,128)(2,1)S(1)}, u32[]{:S(2)}, u32[]{:S(2)}) collective-permute-start(bf16[2,384,256]{2,1,0:T(8,128)(2,1)S(1)} %get-tuple-element.71), channel_id=1, source_target_pairs={{0,2},{1,3},{2,6},{3,7},{4,0},{5,1},{6,4},{7,5},{8,10},{9,11},{10,... | collective-permute-start | bytes 1179656 | tf_op jit(solution)/shard_map/ppermute | solution.py:389
  49.0 15.4 %collective-permute-start.16 = (bf16[3,2,192,256]{3,2,1,0:T(8,128)(2,1)S(1)}, bf16[3,2,192,256]{3,2,1,0:T(8,128)(2,1)S(1)}, u32[]{:S(2)}, u32[]{:S(2)}) collective-permute-start(bf16[3,2,192,256]{3,2,1,0:T(8,128)(2,1)S(1)} %get-tuple-element.78), channel_id=1, source_target_pairs={{0,16},{8,24},{16,0},{24,8},{1,17},{9,25},{17,1},{25,9},{2,18},{10... | collective-permute-start | bytes 1769480 | tf_op jit(solution)/shard_map/ppermute | solution.py:383
  50.5 16.9 %collective-permute-start.24 = (bf16[2,384,256]{2,1,0:T(8,128)(2,1)S(1)}, bf16[2,384,256]{2,1,0:T(8,128)(2,1)S(1)}, u32[]{:S(2)}, u32[]{:S(2)}) collective-permute-start(bf16[2,384,256]{2,1,0:T(8,128)(2,1)S(1)} %get-tuple-element.92), channel_id=1, source_target_pairs={{0,2},{1,3},{2,6},{3,7},{4,0},{5,1},{6,4},{7,5},{8,10},{9,11},{10,... | collective-permute-start | bytes 1179656 | tf_op jit(solution)/shard_map/ppermute | solution.py:389
  52.7 11.6 %collective-permute-start.17 = (bf16[2,2,192,256]{3,2,1,0:T(8,128)(2,1)S(1)}, bf16[2,2,192,256]{3,2,1,0:T(8,128)(2,1)S(1)}, u32[]{:S(2)}, u32[]{:S(2)}) collective-permute-start(bf16[2,2,192,256]{3,2,1,0:T(8,128)(2,1)S(1)} %get-tuple-element.79), channel_id=1, source_target_pairs={{0,8},{8,0},{16,24},{24,16},{1,9},{9,1},{17,25},{25,17},{2,10},{10... | collective-permute-start | bytes 1179656 | tf_op jit(solution)/shard_map/ppermute | solution.py:383
  66.3 1.7 %collective-permute-start.19 = (bf16[4,2,32,256]{3,2,1,0:T(8,128)(2,1)S(1)}, bf16[4,2,32,256]{3,2,1,0:T(8,128)(2,1)S(1)}, u32[]{:S(2)}, u32[]{:S(2)}) collective-permute-start(bf16[4,2,32,256]{3,2,1,0:T(8,128)(2,1)S(1)} %get-tuple-element.84), channel_id=1, source_target_pairs={{0,1},{1,0},{2,3},{3,2},{4,5},{5,4},{6,7},{7,6},{8,9},{9,8},{10,11... | collective-permute-start | bytes 393224 | tf_op jit(solution)/shard_map/ppermute | solution.py:386
  67.4 3.3 %collective-permute-start.25 = (bf16[384,256]{1,0:T(8,128)(2,1)S(1)}, bf16[384,256]{1,0:T(8,128)(2,1)S(1)}, u32[]{:S(2)}, u32[]{:S(2)}) collective-permute-start(bf16[384,256]{1,0:T(8,128)(2,1)S(1)} %get-tuple-element.109), channel_id=1, source_target_pairs={{0,1},{1,0},{2,3},{3,2},{4,5},{5,4},{6,7},{7,6},{8,9},{9,8},{10,11... | collective-permute-start | bytes 589832 | tf_op jit(solution)/shard_map/ppermute | solution.py:386
  67.5 3.2 %collective-permute-start.26 = (bf16[384,256]{1,0:T(8,128)(2,1)S(1)}, bf16[384,256]{1,0:T(8,128)(2,1)S(1)}, u32[]{:S(2)}, u32[]{:S(2)}) collective-permute-start(bf16[384,256]{1,0:T(8,128)(2,1)S(1)} %get-tuple-element.108), channel_id=1, source_target_pairs={{0,1},{1,0},{2,3},{3,2},{4,5},{5,4},{6,7},{7,6},{8,9},{9,8},{10,11... | collective-permute-start | bytes 589832 | tf_op jit(solution)/shard_map/ppermute | solution.py:386
  68.2 8.7 %collective-permute-start.22 = (bf16[2,2,2,2,32,256]{5,4,3,2,1,0:T(8,128)(2,1)S(1)}, bf16[2,2,2,2,32,256]{5,4,3,2,1,0:T(8,128)(2,1)S(1)}, u32[]{:S(2)}, u32[]{:S(2)}) collective-permute-start(bf16[2,2,2,2,32,256]{5,4,3,2,1,0:T(8,128)(2,1)S(1)} %get-tuple-element.89), channel_id=1, source_target_pairs={{0,2},{1,3},{2,0},{3,1},{4,6},{5,7},{6,4},{7,5},{8,10},{9,11},{10,... | collective-permute-start | bytes 786440 | tf_op jit(solution)/shard_map/ppermute | solution.py:529
  76.9 10.6 %collective-permute-start.31 = (bf16[2,2,2,2,32,256]{5,4,3,2,1,0:T(8,128)(2,1)S(1)}, bf16[2,2,2,2,32,256]{5,4,3,2,1,0:T(8,128)(2,1)S(1)}, u32[]{:S(2)}, u32[]{:S(2)}) collective-permute-start(bf16[2,2,2,2,32,256]{5,4,3,2,1,0:T(8,128)(2,1)S(1)} %get-tuple-element.105), channel_id=1, source_target_pairs={{0,2},{1,3},{2,0},{3,1},{4,6},{5,7},{6,4},{7,5},{8,10},{9,11},{10,... | collective-permute-start | bytes 786440 | tf_op jit(solution)/shard_map/ppermute | solution.py:529
  78.7 9.9 %collective-permute-start.23 = (bf16[2,2,2,32,256]{4,3,2,1,0:T(8,128)(2,1)S(1)}, bf16[2,2,2,32,256]{4,3,2,1,0:T(8,128)(2,1)S(1)}, u32[]{:S(2)}, u32[]{:S(2)}) collective-permute-start(bf16[2,2,2,32,256]{4,3,2,1,0:T(8,128)(2,1)S(1)} %get-tuple-element.91), channel_id=1, source_target_pairs={{0,4},{1,5},{2,6},{3,7},{4,0},{5,1},{6,2},{7,3},{8,12},{9,13},{10,... | collective-permute-start | bytes 393224 | tf_op jit(solution)/shard_map/ppermute | solution.py:536
  87.5 7.8 %collective-permute-start.32 = (bf16[2,2,2,32,256]{4,3,2,1,0:T(8,128)(2,1)S(1)}, bf16[2,2,2,32,256]{4,3,2,1,0:T(8,128)(2,1)S(1)}, u32[]{:S(2)}, u32[]{:S(2)}) collective-permute-start(bf16[2,2,2,32,256]{4,3,2,1,0:T(8,128)(2,1)S(1)} %get-tuple-element.107), channel_id=1, source_target_pairs={{0,4},{1,5},{2,6},{3,7},{4,0},{5,1},{6,2},{7,3},{8,12},{9,13},{10,... | collective-permute-start | bytes 393224 | tf_op jit(solution)/shard_map/ppermute | solution.py:536
  (11 other events, 32.4 us)

commit v10 on v9

--- a/solution.py
+++ b/solution.py
@@ -340,7 +340,8 @@
 
 
 def split_kernel(keep, *refs):
-    *came, own, cross, sends = refs
+    count = 2 * keep.shape[1]
+    came, (own, cross, *sends) = refs[:count], refs[count:]
     z = lax.axis_index("ga") // 2
     for s in range(keep.shape[1]):
         for which in range(2):
@@ -351,12 +352,15 @@
             own[s, which] = chip(z)
             cross[s, which] = chip(z ^ 2)
             for i, at in enumerate((z ^ 1, z ^ 3)):
-                sends[i, s, which] = chip(at).astype(BF16)
-
-
-def merge_kernel(own, cross, came, total, sends):
-    total[...] = own[...] + came[0].astype(F32)
-    sends[...] = (cross[...] + came[1].astype(F32)).astype(BF16)
+                out = sends[0].at[i] if len(sends) == 1 else sends[i]
+                out[s, which] = chip(at).astype(BF16)
+
+
+def merge_kernel(own, cross, *refs):
+    *came, total, sends = refs
+    shares = came if len(came) == 2 else (came[0].at[0], came[0].at[1])
+    total[...] = own[...] + shares[0][...].astype(F32)
+    sends[...] = (cross[...] + shares[1][...].astype(F32)).astype(BF16)
 
 
 def finish_kernel(count, chips, scale, *refs):
@@ -514,24 +518,22 @@
             name="mirror",
             mib=24,
         )
-        own, cross, sends = run(
+        own, cross, *sends = run(
             split_kernel,
-            [shape(part, F32), shape(part, F32), shape((2, *part), BF16)],
+            [shape(part, F32)] * 2 + ([shape(part, BF16)] * 2 if j else [shape((2, *part), BF16)]),
             keep,
             *[other_core(x) for x in gives],
             name="split",
         )
-        if j + 1 < count:
-            behind[j + 1], _ = tie((behind[j + 1], keep))
-        if stages:
-            sends, _ = tie((sends, stages[-1][2]))
         done = own
-        came_j = lax.ppermute(sends, "ga", [(i, i ^ 2) for i in range(n_ga)])
+        came_j = [lax.ppermute(x, "ga", [(i, i ^ 2) for i in range(n_ga)]) for x in sends]
         stages.append((own, cross, came_j))
     groups = []
     for own, cross, came_j in stages:
+        if groups:
+            groups[-1], came_j = tie((groups[-1], came_j))
         own, sends = run(
-            merge_kernel, [shape(part, F32), shape(part, BF16)], own, cross, came_j, name="merge"
+            merge_kernel, [shape(part, F32), shape(part, BF16)], own, cross, *came_j, name="merge"
         )
         groups += [own, lax.ppermute(sends, "ga", [(i, i ^ 4) for i in range(n_ga)])]
     result = shape((count, transfers, 2, t // n_ga, t), F32)

time: 96.4 us -> 96.5 us (level)
    ppermute x2 -> x3, waiting for transfers between devices: 8.32 us -> 6.92 us  [quick(): lax.ppermute(x, 'ga', [(i, i ^ 2) for i in range(n_ga)])]
    ppermute x2 -> x3, starting transfers between devices: 3.6 us -> 3.93 us  [quick(): lax.ppermute(x, 'ga', [(i, i ^ 2) for i in range(n_ga)])]
  transfers between devices with their start and end apart: 33 -> 34, of which waited for: 17 -> 17; matrix products, arithmetic and copies ran while one was open for 0% -> 0% of each run, Pallas kernels for 23% -> 23%
where the time goes in v10:
time: 96.5 us; the launch traced here: 96.3 us
  waiting for transfers between devices  37 us (38%)
  starting transfers between devices  33.6 us (35%)
  Pallas kernels  24.1 us (25%)
    pallas_call x23, Pallas kernels, run(): pl.pallas_call(body, in_specs=specs or [VMEM] * len(args), out_specs=[VME...  24.1 us
    ppermute x10, waiting for transfers between devices, across(): return lax.ppermute(x, 'kp', [(i, i ^ bit) for i in range(n_kp)])  12.5 us
    ppermute x10, starting transfers between devices, across(): return lax.ppermute(x, 'kp', [(i, i ^ bit) for i in range(n_kp)])  11.1 us
    ppermute x5, starting transfers between devices, along(): lax.ppermute(x, 'ga', [(i, 2 * chips_on[i // 2] + i % 2) for i in range(n...  11 us
    ppermute x5, waiting for transfers between devices, along(): lax.ppermute(x, 'ga', [(i, 2 * chips_on[i // 2] + i % 2) for i in range(n...  7.81 us
    ppermute x2, waiting for transfers between devices, quick(): lax.ppermute(sends, 'ga', [(i, i ^ 4) for i in range(n_ga)])  7.38 us
    ppermute x3, waiting for transfers between devices, quick(): lax.ppermute(x, 'ga', [(i, i ^ 2) for i in range(n_ga)])  6.92 us
    ppermute x3, starting transfers between devices, quick(): lax.ppermute(x, 'ga', [(i, i ^ 2) for i in range(n_ga)])  3.93 us
  transfers between devices with their start and end apart: 34, of which 17 were waited for; matrix products, arithmetic and copies ran while one was open for 0% of the time, Pallas kernels for 23%

profile of v10, /device:TPU:0, one launch (start us, length us, event | category | flops | bytes accessed | tf_op | source)
XLA Modules:
  0.0 96.3 jit_solution(9118629453760298491)
XLA Ops:
  2.5 3.0 %collective-permute-start = (bf16[784,256]{1,0:T(8,128)(2,1)S(1)}, bf16[784,256]{1,0:T(8,128)(2,1)S(1)}, u32[]{:S(2)}, u32[]{:S(2)}) collective-permute-start(bf16[784,256]{1,0:T(8,128)(2,1)S(1)} %get-tuple-element.61.packed_0), channel_id=1, source_target_pairs={{0,8},{8,0},{16,24},{24,16},{1,9},{9,1},{17,25},{25,17},{2,10},{10... | collective-permute-start | bytes 1204232 | tf_op jit(solution)/shard_map/ppermute | solution.py:387
  5.5 1.5 %collective-permute-start.1 = (bf16[784,256]{1,0:T(8,128)(2,1)S(1)}, bf16[784,256]{1,0:T(8,128)(2,1)S(1)}, u32[]{:S(2)}, u32[]{:S(2)}) collective-permute-start(bf16[784,256]{1,0:T(8,128)(2,1)S(1)} %get-tuple-element.62.packed_1), channel_id=1, source_target_pairs={{0,16},{8,24},{16,0},{24,8},{1,17},{9,25},{17,1},{25,9},{2,18},{10... | collective-permute-start | bytes 1204232 | tf_op jit(solution)/shard_map/ppermute | solution.py:387
  7.0 1.6 %collective-permute-start.2 = (bf16[784,256]{1,0:T(8,128)(2,1)S(1)}, bf16[784,256]{1,0:T(8,128)(2,1)S(1)}, u32[]{:S(2)}, u32[]{:S(2)}) collective-permute-start(bf16[784,256]{1,0:T(8,128)(2,1)S(1)} %get-tuple-element.61.packed_0), channel_id=1, source_target_pairs={{0,2},{1,3},{2,6},{3,7},{4,0},{5,1},{6,4},{7,5},{8,10},{9,11},{10,... | collective-permute-start | bytes 1204232 | tf_op jit(solution)/shard_map/ppermute | solution.py:393
  8.6 2.6 %collective-permute-start.3 = (bf16[784,256]{1,0:T(8,128)(2,1)S(1)}, bf16[784,256]{1,0:T(8,128)(2,1)S(1)}, u32[]{:S(2)}, u32[]{:S(2)}) collective-permute-start(bf16[784,256]{1,0:T(8,128)(2,1)S(1)} %get-tuple-element.62.packed_1), channel_id=1, source_target_pairs={{0,2},{1,3},{2,6},{3,7},{4,0},{5,1},{6,4},{7,5},{8,10},{9,11},{10,... | collective-permute-start | bytes 1204232 | tf_op jit(solution)/shard_map/ppermute | solution.py:393
  11.2 3.8 %load.1.screened = bf16[2,2,384,3072]{3,2,1,0:T(8,128)(2,1)S(1)} custom-call(bf16[2,2,384,3072]{3,2,1,0:T(8,128)(2,1)} %source), custom_call_target="tpu_custom_call" | custom-call | tf_op jit(solution)/shard_map/load/pallas_call | solution.py:30
  16.8 1.6 %collective-permute-start.6 = (bf16[2,2,192,256]{3,2,1,0:T(8,128)(2,1)S(1)}, bf16[2,2,192,256]{3,2,1,0:T(8,128)(2,1)S(1)}, u32[]{:S(2)}, u32[]{:S(2)}) collective-permute-start(bf16[2,2,192,256]{3,2,1,0:T(8,128)(2,1)S(1)} %get-tuple-element.65), channel_id=1, source_target_pairs={{0,16},{8,24},{16,0},{24,8},{1,17},{9,25},{17,1},{25,9},{2,18},{10... | collective-permute-start | bytes 1179656 | tf_op jit(solution)/shard_map/ppermute | solution.py:387
  20.7 6.3 %collective-permute-done.3.packed.packed_1 = bf16[784,256]{1,0:T(8,128)(2,1)S(1)} collective-permute-done((bf16[784,256]{1,0:T(8,128)(2,1)S(1)}, bf16[784,256]{1,0:T(8,128)(2,1)S(1)}, u32[]{:S(2)}, u32[]{:S(2)}) %collective-permute-start.3) | collective-permute-done | bytes 401440 | tf_op jit(solution)/shard_map/ppermute | solution.py:393
  27.9 2.6 %collective-permute-done.7.picked_1 = bf16[2,2,192,256]{3,2,1,0:T(8,128)(2,1)S(1)} collective-permute-done((bf16[2,2,192,256]{3,2,1,0:T(8,128)(2,1)S(1)}, bf16[2,2,192,256]{3,2,1,0:T(8,128)(2,1)S(1)}, u32[]{:S(2)}, u32[]{:S(2)}) %collective-permute-start.7) | collective-permute-done | bytes 393248 | tf_op jit(solution)/shard_map/ppermute | solution.py:387
  30.8 2.6 %collective-permute-start.11 = (bf16[2,2,384,256]{3,2,1,0:T(8,128)(2,1)S(1)}, bf16[2,2,384,256]{3,2,1,0:T(8,128)(2,1)S(1)}, u32[]{:S(2)}, u32[]{:S(2)}) collective-permute-start(bf16[2,2,384,256]{3,2,1,0:T(8,128)(2,1)S(1)} %near.2.own.refs_0_), channel_id=1, source_target_pairs={{0,4},{1,5},{2,0},{3,1},{4,6},{5,7},{6,2},{7,3},{8,12},{9,13},{10,... | collective-permute-start | bytes 2359304 | tf_op jit(solution)/shard_map/ppermute | solution.py:393
  33.5 1.8 %product.3.before = f32[2,384,1024]{2,1,0:T(8,128)S(1)} custom-call(bf16[2,2,384,3072]{3,2,1,0:T(8,128)(2,1)S(1)} %load.1.screened, bf16[2,2,384,256]{3,2,1,0:T(8,128)(2,1)S(1)} %near.2.own.refs_0_, f32[1,384]{1,0:T(1,128)S(1)} %broadcast_in_dim.3.coulomb), custom_call_target="tpu_custom_call" | custom-call | tf_op jit(solution)/shard_map/product/pallas_call | solution.py:30
  38.3 7.5 %collective-permute-done.9.picked_1 = bf16[2,2,192,256]{3,2,1,0:T(8,128)(2,1)S(1)} collective-permute-done((bf16[2,2,192,256]{3,2,1,0:T(8,128)(2,1)S(1)}, bf16[2,2,192,256]{3,2,1,0:T(8,128)(2,1)S(1)}, u32[]{:S(2)}, u32[]{:S(2)}) %collective-permute-start.9) | collective-permute-done | bytes 393248 | tf_op jit(solution)/shard_map/ppermute | solution.py:387
  47.0 2.0 %collective-permute-start.10 = (bf16[2,384,256]{2,1,0:T(8,128)(2,1)S(1)}, bf16[2,384,256]{2,1,0:T(8,128)(2,1)S(1)}, u32[]{:S(2)}, u32[]{:S(2)}) collective-permute-start(bf16[2,384,256]{2,1,0:T(8,128)(2,1)S(1)} %get-tuple-element.73), channel_id=1, source_target_pairs={{0,2},{1,3},{2,6},{3,7},{4,0},{5,1},{6,4},{7,5},{8,10},{9,11},{10,... | collective-permute-start | bytes 1179656 | tf_op jit(solution)/shard_map/ppermute | solution.py:393
  48.9 1.5 %collective-permute-start.16 = (bf16[3,2,192,256]{3,2,1,0:T(8,128)(2,1)S(1)}, bf16[3,2,192,256]{3,2,1,0:T(8,128)(2,1)S(1)}, u32[]{:S(2)}, u32[]{:S(2)}) collective-permute-start(bf16[3,2,192,256]{3,2,1,0:T(8,128)(2,1)S(1)} %get-tuple-element.80), channel_id=1, source_target_pairs={{0,16},{8,24},{16,0},{24,8},{1,17},{9,25},{17,1},{25,9},{2,18},{10... | collective-permute-start | bytes 1769480 | tf_op jit(solution)/shard_map/ppermute | solution.py:387
  50.5 2.2 %collective-permute-start.24 = (bf16[2,384,256]{2,1,0:T(8,128)(2,1)S(1)}, bf16[2,384,256]{2,1,0:T(8,128)(2,1)S(1)}, u32[]{:S(2)}, u32[]{:S(2)}) collective-permute-start(bf16[2,384,256]{2,1,0:T(8,128)(2,1)S(1)} %get-tuple-element.94), channel_id=1, source_target_pairs={{0,2},{1,3},{2,6},{3,7},{4,0},{5,1},{6,4},{7,5},{8,10},{9,11},{10,... | collective-permute-start | bytes 1179656 | tf_op jit(solution)/shard_map/ppermute | solution.py:393
  53.3 3.0 %product.4.before = f32[2,384,1024]{2,1,0:T(8,128)S(1)} custom-call(bf16[2,2,384,3072]{3,2,1,0:T(8,128)(2,1)S(1)} %load.1.screened, bf16[2,2,384,256]{3,2,1,0:T(8,128)(2,1)S(1)} %collective-permute-done.11.own, bf16[2,2,384,256]{3,2,1,0:T(8,128)(2,1)S(1)} %collective-permute-done.13.pair, ...), custom_call_target="tpu_custom_call", output_to_operand_aliasing={{}: (3, {})} | custom-call | tf_op jit(solution)/shard_map/product/pallas_call | solution.py:30
  56.4 4.6 %product.5.before = f32[2,384,1024]{2,1,0:T(8,128)S(1)} custom-call(bf16[2,2,384,3072]{3,2,1,0:T(8,128)(2,1)S(1)} %load.1.screened, bf16[2,2,384,256]{3,2,1,0:T(8,128)(2,1)S(1)} %get-tuple-element.77.refs_1_.own, bf16[2,2,2,384,256]{4,3,2,1,0:T(8,128)(2,1)S(1)} %collective-permute-done.12.pairs, ...), custom_call_target="tpu_custom_call", output_to_operand_aliasing={{}: (3, {})} | custom-call | tf_op jit(solution)/shard_map/product/pallas_call | solution.py:30
  62.8 1.5 %image.2 = bf16[2,384,512]{2,1,0:T(8,128)(2,1)S(1)} custom-call(bf16[2,2,384,3072]{3,2,1,0:T(8,128)(2,1)S(1)} %load.1.screened, bf16[2,384,256]{2,1,0:T(8,128)(2,1)S(1)} %collective-permute-done.10.own, bf16[384,256]{1,0:T(8,128)(2,1)S(1)} %collective-permute-done.14.pair_real, bf16[384,256]{1,0:T(8,128)(2,1)S(1)} %collective-permute-done.15.pair_imag, ...), custom_call_target="tpu_custom_call" | custom-call | tf_op jit(solution)/shard_map/image/pallas_call | solution.py:30
  68.2 1.8 %collective-permute-start.22 = (bf16[2,2,2,2,32,256]{5,4,3,2,1,0:T(8,128)(2,1)S(1)}, bf16[2,2,2,2,32,256]{5,4,3,2,1,0:T(8,128)(2,1)S(1)}, u32[]{:S(2)}, u32[]{:S(2)}) collective-permute-start(bf16[2,2,2,2,32,256]{5,4,3,2,1,0:T(8,128)(2,1)S(1)} %get-tuple-element.91), channel_id=1, source_target_pairs={{0,2},{1,3},{2,0},{3,1},{4,6},{5,7},{6,4},{7,5},{8,10},{9,11},{10,... | collective-permute-start | bytes 786440 | tf_op jit(solution)/shard_map/ppermute | solution.py:529
  70.7 1.5 %image.3 = bf16[2,384,512]{2,1,0:T(8,128)(2,1)S(1)} custom-call(bf16[2,2,384,3072]{3,2,1,0:T(8,128)(2,1)S(1)} %load.1.screened, bf16[2,384,256]{2,1,0:T(8,128)(2,1)S(1)} %collective-permute-done.24.own, bf16[384,256]{1,0:T(8,128)(2,1)S(1)} %collective-permute-done.25.pair_real, bf16[384,256]{1,0:T(8,128)(2,1)S(1)} %collective-permute-done.26.pair_imag, ...), custom_call_target="tpu_custom_call" | custom-call | tf_op jit(solution)/shard_map/image/pallas_call | solution.py:30
  75.6 1.8 %collective-permute-start.32 = (bf16[2,2,2,32,256]{4,3,2,1,0:T(8,128)(2,1)S(1)}, bf16[2,2,2,32,256]{4,3,2,1,0:T(8,128)(2,1)S(1)}, u32[]{:S(2)}, u32[]{:S(2)}) collective-permute-start(bf16[2,2,2,32,256]{4,3,2,1,0:T(8,128)(2,1)S(1)} %get-tuple-element.104), channel_id=1, source_target_pairs={{0,2},{1,3},{2,0},{3,1},{4,6},{5,7},{6,4},{7,5},{8,10},{9,11},{10,... | collective-permute-start | bytes 393224 | tf_op jit(solution)/shard_map/ppermute | solution.py:529
  77.4 2.3 %collective-permute-start.23 = (bf16[2,2,2,32,256]{4,3,2,1,0:T(8,128)(2,1)S(1)}, bf16[2,2,2,32,256]{4,3,2,1,0:T(8,128)(2,1)S(1)}, u32[]{:S(2)}, u32[]{:S(2)}) collective-permute-start(bf16[2,2,2,32,256]{4,3,2,1,0:T(8,128)(2,1)S(1)} %get-tuple-element.93), channel_id=1, source_target_pairs={{0,4},{1,5},{2,6},{3,7},{4,0},{5,1},{6,2},{7,3},{8,12},{9,13},{10,... | collective-permute-start | bytes 393224 | tf_op jit(solution)/shard_map/ppermute | solution.py:538
  79.8 4.7 %collective-permute-done.31.refs_0_ = bf16[2,2,2,32,256]{4,3,2,1,0:T(8,128)(2,1)S(1)} collective-permute-done((bf16[2,2,2,32,256]{4,3,2,1,0:T(8,128)(2,1)S(1)}, bf16[2,2,2,32,256]{4,3,2,1,0:T(8,128)(2,1)S(1)}, u32[]{:S(2)}, u32[]{:S(2)}) %collective-permute-start.31) | collective-permute-done | bytes 131104 | tf_op jit(solution)/shard_map/ppermute | solution.py:529
  84.5 2.2 %collective-permute-done.32.refs_1_ = bf16[2,2,2,32,256]{4,3,2,1,0:T(8,128)(2,1)S(1)} collective-permute-done((bf16[2,2,2,32,256]{4,3,2,1,0:T(8,128)(2,1)S(1)}, bf16[2,2,2,32,256]{4,3,2,1,0:T(8,128)(2,1)S(1)}, u32[]{:S(2)}, u32[]{:S(2)}) %collective-permute-start.32) | collective-permute-done | bytes 131104 | tf_op jit(solution)/shard_map/ppermute | solution.py:529
  88.1 7.4 %collective-permute-done.33.refs_3_ = bf16[2,2,2,32,256]{4,3,2,1,0:T(8,128)(2,1)S(1)} collective-permute-done((bf16[2,2,2,32,256]{4,3,2,1,0:T(8,128)(2,1)S(1)}, bf16[2,2,2,32,256]{4,3,2,1,0:T(8,128)(2,1)S(1)}, u32[]{:S(2)}, u32[]{:S(2)}) %collective-permute-start.33) | collective-permute-done | bytes 131104 | tf_op jit(solution)/shard_map/ppermute | solution.py:538
  (74 shorter events, 23.9 us)
Async XLA Ops:
  2.5 12.5 %collective-permute-start = (bf16[784,256]{1,0:T(8,128)(2,1)S(1)}, bf16[784,256]{1,0:T(8,128)(2,1)S(1)}, u32[]{:S(2)}, u32[]{:S(2)}) collective-permute-start(bf16[784,256]{1,0:T(8,128)(2,1)S(1)} %get-tuple-element.61.packed_0), channel_id=1, source_target_pairs={{0,8},{8,0},{16,24},{24,16},{1,9},{9,1},{17,25},{25,17},{2,10},{10... | collective-permute-start | bytes 1204232 | tf_op jit(solution)/shard_map/ppermute | solution.py:387
  5.5 10.8 %collective-permute-start.1 = (bf16[784,256]{1,0:T(8,128)(2,1)S(1)}, bf16[784,256]{1,0:T(8,128)(2,1)S(1)}, u32[]{:S(2)}, u32[]{:S(2)}) collective-permute-start(bf16[784,256]{1,0:T(8,128)(2,1)S(1)} %get-tuple-element.62.packed_1), channel_id=1, source_target_pairs={{0,16},{8,24},{16,0},{24,8},{1,17},{9,25},{17,1},{25,9},{2,18},{10... | collective-permute-start | bytes 1204232 | tf_op jit(solution)/shard_map/ppermute | solution.py:387
  7.0 13.1 %collective-permute-start.2 = (bf16[784,256]{1,0:T(8,128)(2,1)S(1)}, bf16[784,256]{1,0:T(8,128)(2,1)S(1)}, u32[]{:S(2)}, u32[]{:S(2)}) collective-permute-start(bf16[784,256]{1,0:T(8,128)(2,1)S(1)} %get-tuple-element.61.packed_0), channel_id=1, source_target_pairs={{0,2},{1,3},{2,6},{3,7},{4,0},{5,1},{6,4},{7,5},{8,10},{9,11},{10,... | collective-permute-start | bytes 1204232 | tf_op jit(solution)/shard_map/ppermute | solution.py:393
  8.6 18.4 %collective-permute-start.3 = (bf16[784,256]{1,0:T(8,128)(2,1)S(1)}, bf16[784,256]{1,0:T(8,128)(2,1)S(1)}, u32[]{:S(2)}, u32[]{:S(2)}) collective-permute-start(bf16[784,256]{1,0:T(8,128)(2,1)S(1)} %get-tuple-element.62.packed_1), channel_id=1, source_target_pairs={{0,2},{1,3},{2,6},{3,7},{4,0},{5,1},{6,4},{7,5},{8,10},{9,11},{10,... | collective-permute-start | bytes 1204232 | tf_op jit(solution)/shard_map/ppermute | solution.py:393
  16.8 11.0 %collective-permute-start.6 = (bf16[2,2,192,256]{3,2,1,0:T(8,128)(2,1)S(1)}, bf16[2,2,192,256]{3,2,1,0:T(8,128)(2,1)S(1)}, u32[]{:S(2)}, u32[]{:S(2)}) collective-permute-start(bf16[2,2,192,256]{3,2,1,0:T(8,128)(2,1)S(1)} %get-tuple-element.65), channel_id=1, source_target_pairs={{0,16},{8,24},{16,0},{24,8},{1,17},{9,25},{17,1},{25,9},{2,18},{10... | collective-permute-start | bytes 1179656 | tf_op jit(solution)/shard_map/ppermute | solution.py:387
  18.4 12.1 %collective-permute-start.7 = (bf16[2,2,192,256]{3,2,1,0:T(8,128)(2,1)S(1)}, bf16[2,2,192,256]{3,2,1,0:T(8,128)(2,1)S(1)}, u32[]{:S(2)}, u32[]{:S(2)}) collective-permute-start(bf16[2,2,192,256]{3,2,1,0:T(8,128)(2,1)S(1)} %get-tuple-element.66), channel_id=1, source_target_pairs={{0,8},{8,0},{16,24},{24,16},{1,9},{9,1},{17,25},{25,17},{2,10},{10... | collective-permute-start | bytes 1179656 | tf_op jit(solution)/shard_map/ppermute | solution.py:387
  20.1 16.3 %collective-permute-start.4 = (bf16[784,256]{1,0:T(8,128)(2,1)S(1)}, bf16[784,256]{1,0:T(8,128)(2,1)S(1)}, u32[]{:S(2)}, u32[]{:S(2)}) collective-permute-start(bf16[784,256]{1,0:T(8,128)(2,1)S(1)} %collective-permute-done.2.packed.packed_0), channel_id=1, source_target_pairs={{0,8},{8,0},{16,24},{24,16},{1,9},{9,1},{17,25},{25,17},{2,10},{10... | collective-permute-start | bytes 1204232 | tf_op jit(solution)/shard_map/ppermute | solution.py:387
  27.0 10.3 %collective-permute-start.5 = (bf16[784,256]{1,0:T(8,128)(2,1)S(1)}, bf16[784,256]{1,0:T(8,128)(2,1)S(1)}, u32[]{:S(2)}, u32[]{:S(2)}) collective-permute-start(bf16[784,256]{1,0:T(8,128)(2,1)S(1)} %collective-permute-done.3.packed.packed_1), channel_id=1, source_target_pairs={{0,16},{8,24},{16,0},{24,8},{1,17},{9,25},{17,1},{25,9},{2,18},{10... | collective-permute-start | bytes 1204232 | tf_op jit(solution)/shard_map/ppermute | solution.py:387
  30.8 15.4 %collective-permute-start.11 = (bf16[2,2,384,256]{3,2,1,0:T(8,128)(2,1)S(1)}, bf16[2,2,384,256]{3,2,1,0:T(8,128)(2,1)S(1)}, u32[]{:S(2)}, u32[]{:S(2)}) collective-permute-start(bf16[2,2,384,256]{3,2,1,0:T(8,128)(2,1)S(1)} %near.2.own.refs_0_), channel_id=1, source_target_pairs={{0,4},{1,5},{2,0},{3,1},{4,6},{5,7},{6,2},{7,3},{8,12},{9,13},{10,... | collective-permute-start | bytes 2359304 | tf_op jit(solution)/shard_map/ppermute | solution.py:393
  36.7 9.1 %collective-permute-start.8 = (bf16[784,256]{1,0:T(8,128)(2,1)S(1)}, bf16[784,256]{1,0:T(8,128)(2,1)S(1)}, u32[]{:S(2)}, u32[]{:S(2)}) collective-permute-start(bf16[784,256]{1,0:T(8,128)(2,1)S(1)} %pick_half.2), channel_id=1, source_target_pairs={{0,16},{8,24},{16,0},{24,8},{1,17},{9,25},{17,1},{25,9},{2,18},{10... | collective-permute-start | bytes 1204232 | tf_op jit(solution)/shard_map/ppermute | solution.py:387
  37.6 8.2 %collective-permute-start.9 = (bf16[2,2,192,256]{3,2,1,0:T(8,128)(2,1)S(1)}, bf16[2,2,192,256]{3,2,1,0:T(8,128)(2,1)S(1)}, u32[]{:S(2)}, u32[]{:S(2)}) collective-permute-start(bf16[2,2,192,256]{3,2,1,0:T(8,128)(2,1)S(1)} %pick_half.3), channel_id=1, source_target_pairs={{0,8},{8,0},{16,24},{24,16},{1,9},{9,1},{17,25},{25,17},{2,10},{10... | collective-permute-start | bytes 1179656 | tf_op jit(solution)/shard_map/ppermute | solution.py:387
  46.4 10.0 %collective-permute-start.12 = (bf16[2,2,2,384,256]{4,3,2,1,0:T(8,128)(2,1)S(1)}, bf16[2,2,2,384,256]{4,3,2,1,0:T(8,128)(2,1)S(1)}, u32[]{:S(2)}, u32[]{:S(2)}) collective-permute-start(bf16[2,2,2,384,256]{4,3,2,1,0:T(8,128)(2,1)S(1)} %stack.1), channel_id=1, source_target_pairs={{0,1},{1,0},{2,3},{3,2},{4,5},{5,4},{6,7},{7,6},{8,9},{9,8},{10,11... | collective-permute-start | bytes 4718600 | tf_op jit(solution)/shard_map/ppermute | solution.py:390
  46.5 6.2 %collective-permute-start.13 = (bf16[2,2,384,256]{3,2,1,0:T(8,128)(2,1)S(1)}, bf16[2,2,384,256]{3,2,1,0:T(8,128)(2,1)S(1)}, u32[]{:S(2)}, u32[]{:S(2)}) collective-permute-start(bf16[2,2,384,256]{3,2,1,0:T(8,128)(2,1)S(1)} %collective-permute-done.11.own), channel_id=1, source_target_pairs={{0,1},{1,0},{2,3},{3,2},{4,5},{5,4},{6,7},{7,6},{8,9},{9,8},{10,11... | collective-permute-start | bytes 2359304 | tf_op jit(solution)/shard_map/ppermute | solution.py:390
  47.0 14.0 %collective-permute-start.10 = (bf16[2,384,256]{2,1,0:T(8,128)(2,1)S(1)}, bf16[2,384,256]{2,1,0:T(8,128)(2,1)S(1)}, u32[]{:S(2)}, u32[]{:S(2)}) collective-permute-start(bf16[2,384,256]{2,1,0:T(8,128)(2,1)S(1)} %get-tuple-element.73), channel_id=1, source_target_pairs={{0,2},{1,3},{2,6},{3,7},{4,0},{5,1},{6,4},{7,5},{8,10},{9,11},{10,... | collective-permute-start | bytes 1179656 | tf_op jit(solution)/shard_map/ppermute | solution.py:393
  48.9 15.4 %collective-permute-start.16 = (bf16[3,2,192,256]{3,2,1,0:T(8,128)(2,1)S(1)}, bf16[3,2,192,256]{3,2,1,0:T(8,128)(2,1)S(1)}, u32[]{:S(2)}, u32[]{:S(2)}) collective-permute-start(bf16[3,2,192,256]{3,2,1,0:T(8,128)(2,1)S(1)} %get-tuple-element.80), channel_id=1, source_target_pairs={{0,16},{8,24},{16,0},{24,8},{1,17},{9,25},{17,1},{25,9},{2,18},{10... | collective-permute-start | bytes 1769480 | tf_op jit(solution)/shard_map/ppermute | solution.py:387
  50.5 16.9 %collective-permute-start.24 = (bf16[2,384,256]{2,1,0:T(8,128)(2,1)S(1)}, bf16[2,384,256]{2,1,0:T(8,128)(2,1)S(1)}, u32[]{:S(2)}, u32[]{:S(2)}) collective-permute-start(bf16[2,384,256]{2,1,0:T(8,128)(2,1)S(1)} %get-tuple-element.94), channel_id=1, source_target_pairs={{0,2},{1,3},{2,6},{3,7},{4,0},{5,1},{6,4},{7,5},{8,10},{9,11},{10,... | collective-permute-start | bytes 1179656 | tf_op jit(solution)/shard_map/ppermute | solution.py:393
  52.7 11.7 %collective-permute-start.17 = (bf16[2,2,192,256]{3,2,1,0:T(8,128)(2,1)S(1)}, bf16[2,2,192,256]{3,2,1,0:T(8,128)(2,1)S(1)}, u32[]{:S(2)}, u32[]{:S(2)}) collective-permute-start(bf16[2,2,192,256]{3,2,1,0:T(8,128)(2,1)S(1)} %get-tuple-element.81), channel_id=1, source_target_pairs={{0,8},{8,0},{16,24},{24,16},{1,9},{9,1},{17,25},{25,17},{2,10},{10... | collective-permute-start | bytes 1179656 | tf_op jit(solution)/shard_map/ppermute | solution.py:387
  67.4 3.3 %collective-permute-start.25 = (bf16[384,256]{1,0:T(8,128)(2,1)S(1)}, bf16[384,256]{1,0:T(8,128)(2,1)S(1)}, u32[]{:S(2)}, u32[]{:S(2)}) collective-permute-start(bf16[384,256]{1,0:T(8,128)(2,1)S(1)} %get-tuple-element.113), channel_id=1, source_target_pairs={{0,1},{1,0},{2,3},{3,2},{4,5},{5,4},{6,7},{7,6},{8,9},{9,8},{10,11... | collective-permute-start | bytes 589832 | tf_op jit(solution)/shard_map/ppermute | solution.py:390
  67.5 3.2 %collective-permute-start.26 = (bf16[384,256]{1,0:T(8,128)(2,1)S(1)}, bf16[384,256]{1,0:T(8,128)(2,1)S(1)}, u32[]{:S(2)}, u32[]{:S(2)}) collective-permute-start(bf16[384,256]{1,0:T(8,128)(2,1)S(1)} %get-tuple-element.112), channel_id=1, source_target_pairs={{0,1},{1,0},{2,3},{3,2},{4,5},{5,4},{6,7},{7,6},{8,9},{9,8},{10,11... | collective-permute-start | bytes 589832 | tf_op jit(solution)/shard_map/ppermute | solution.py:390
  68.2 9.1 %collective-permute-start.22 = (bf16[2,2,2,2,32,256]{5,4,3,2,1,0:T(8,128)(2,1)S(1)}, bf16[2,2,2,2,32,256]{5,4,3,2,1,0:T(8,128)(2,1)S(1)}, u32[]{:S(2)}, u32[]{:S(2)}) collective-permute-start(bf16[2,2,2,2,32,256]{5,4,3,2,1,0:T(8,128)(2,1)S(1)} %get-tuple-element.91), channel_id=1, source_target_pairs={{0,2},{1,3},{2,0},{3,1},{4,6},{5,7},{6,4},{7,5},{8,10},{9,11},{10,... | collective-permute-start | bytes 786440 | tf_op jit(solution)/shard_map/ppermute | solution.py:529
  75.3 9.2 %collective-permute-start.31 = (bf16[2,2,2,32,256]{4,3,2,1,0:T(8,128)(2,1)S(1)}, bf16[2,2,2,32,256]{4,3,2,1,0:T(8,128)(2,1)S(1)}, u32[]{:S(2)}, u32[]{:S(2)}) collective-permute-start(bf16[2,2,2,32,256]{4,3,2,1,0:T(8,128)(2,1)S(1)} %get-tuple-element.103), channel_id=1, source_target_pairs={{0,2},{1,3},{2,0},{3,1},{4,6},{5,7},{6,4},{7,5},{8,10},{9,11},{10,... | collective-permute-start | bytes 393224 | tf_op jit(solution)/shard_map/ppermute | solution.py:529
  75.6 11.1 %collective-permute-start.32 = (bf16[2,2,2,32,256]{4,3,2,1,0:T(8,128)(2,1)S(1)}, bf16[2,2,2,32,256]{4,3,2,1,0:T(8,128)(2,1)S(1)}, u32[]{:S(2)}, u32[]{:S(2)}) collective-permute-start(bf16[2,2,2,32,256]{4,3,2,1,0:T(8,128)(2,1)S(1)} %get-tuple-element.104), channel_id=1, source_target_pairs={{0,2},{1,3},{2,0},{3,1},{4,6},{5,7},{6,4},{7,5},{8,10},{9,11},{10,... | collective-permute-start | bytes 393224 | tf_op jit(solution)/shard_map/ppermute | solution.py:529
  77.4 9.3 %collective-permute-start.23 = (bf16[2,2,2,32,256]{4,3,2,1,0:T(8,128)(2,1)S(1)}, bf16[2,2,2,32,256]{4,3,2,1,0:T(8,128)(2,1)S(1)}, u32[]{:S(2)}, u32[]{:S(2)}) collective-permute-start(bf16[2,2,2,32,256]{4,3,2,1,0:T(8,128)(2,1)S(1)} %get-tuple-element.93), channel_id=1, source_target_pairs={{0,4},{1,5},{2,6},{3,7},{4,0},{5,1},{6,2},{7,3},{8,12},{9,13},{10,... | collective-permute-start | bytes 393224 | tf_op jit(solution)/shard_map/ppermute | solution.py:538
  86.7 8.7 %collective-permute-start.33 = (bf16[2,2,2,32,256]{4,3,2,1,0:T(8,128)(2,1)S(1)}, bf16[2,2,2,32,256]{4,3,2,1,0:T(8,128)(2,1)S(1)}, u32[]{:S(2)}, u32[]{:S(2)}) collective-permute-start(bf16[2,2,2,32,256]{4,3,2,1,0:T(8,128)(2,1)S(1)} %get-tuple-element.111), channel_id=1, source_target_pairs={{0,4},{1,5},{2,6},{3,7},{4,0},{5,1},{6,2},{7,3},{8,12},{9,13},{10,... | collective-permute-start | bytes 393224 | tf_op jit(solution)/shard_map/ppermute | solution.py:538
  (12 other events, 34.1 us)

commit v11 on v10

--- a/solution.py
+++ b/solution.py
@@ -339,28 +339,45 @@
                 gives[2 * s + which][:, part] = give.astype(BF16)
 
 
-def split_kernel(keep, *refs):
-    count = 2 * keep.shape[1]
-    came, (own, cross, *sends) = refs[:count], refs[count:]
+def split_kernel(near, keep, *refs):
+    transfers, _, _, rows, t = keep.shape[1:]
+    came, (own, cross, *sends) = refs[: 2 * transfers], refs[2 * transfers :]
     z = lax.axis_index("ga") // 2
-    for s in range(keep.shape[1]):
+    for s in range(transfers):
         for which in range(2):
 
             def chip(at):
                 return keep[at, s, which] + came[2 * s + which][at].astype(F32)
 
             own[s, which] = chip(z)
-            cross[s, which] = chip(z ^ 2)
-            for i, at in enumerate((z ^ 1, z ^ 3)):
-                out = sends[0].at[i] if len(sends) == 1 else sends[i]
-                out[s, which] = chip(at).astype(BF16)
+            cross[s, which] = chip(z ^ 3 ^ near)
+            for i, at in enumerate((z ^ near, z ^ 3)):
+                share = chip(at).astype(BF16)
+                if len(sends) == 2:
+                    sends[i][s, which] = share
+                else:
+                    first = ((i * transfers + s) * 2 + which) * 2 * rows
+                    sends[0][first : first + 2 * rows] = share.reshape(2 * rows, t)
+    if len(sends) == 1:
+        rest = sends[0].shape[0] - 8 * transfers * rows
+        sends[0][8 * transfers * rows :] = jnp.zeros((rest, t), BF16)
 
 
 def merge_kernel(own, cross, *refs):
     *came, total, sends = refs
-    shares = came if len(came) == 2 else (came[0].at[0], came[0].at[1])
-    total[...] = own[...] + shares[0][...].astype(F32)
-    sends[...] = (cross[...] + shares[1][...].astype(F32)).astype(BF16)
+    transfers, _, _, rows, t = own.shape
+    for s in range(transfers):
+        for which in range(2):
+            shares = []
+            for i in range(2):
+                if len(came) == 2:
+                    share = came[i][s, which]
+                else:
+                    first = ((i * transfers + s) * 2 + which) * 2 * rows
+                    share = came[0][first : first + 2 * rows].reshape(2, rows, t)
+                shares.append(share.astype(F32))
+            total[s, which] = own[s, which] + shares[0]
+            sends[s, which] = (cross[s, which] + shares[1]).astype(BF16)
 
 
 def finish_kernel(count, chips, scale, *refs):
@@ -518,24 +535,25 @@
             name="mirror",
             mib=24,
         )
+        near_z = 1 if j % 2 else 2
         own, cross, *sends = run(
-            split_kernel,
-            [shape(part, F32)] * 2 + ([shape(part, BF16)] * 2 if j else [shape((2, *part), BF16)]),
+            functools.partial(split_kernel, near_z),
+            [shape(part, F32)] * 2 + ([shape(part, BF16)] * 2 if j else [shape((8 * transfers * part[3] + 16, t), BF16)]),
             keep,
             *[other_core(x) for x in gives],
             name="split",
         )
         done = own
-        came_j = [lax.ppermute(x, "ga", [(i, i ^ 2) for i in range(n_ga)]) for x in sends]
-        stages.append((own, cross, came_j))
+        came_j = [lax.ppermute(x, "ga", [(i, i ^ (2 * near_z)) for i in range(n_ga)]) for x in sends]
+        stages.append((own, cross, came_j, 3 - near_z))
     groups = []
-    for own, cross, came_j in stages:
+    for own, cross, came_j, far_z in stages:
         if groups:
-            groups[-1], came_j = tie((groups[-1], came_j))
+            came_j, _ = tie((came_j, sends))
         own, sends = run(
             merge_kernel, [shape(part, F32), shape(part, BF16)], own, cross, *came_j, name="merge"
         )
-        groups += [own, lax.ppermute(sends, "ga", [(i, i ^ 4) for i in range(n_ga)])]
+        groups += [own, lax.ppermute(sends, "ga", [(i, i ^ (2 * far_z)) for i in range(n_ga)])]
     result = shape((count, transfers, 2, t // n_ga, t), F32)
     return tuple(
         run(

time: 96.5 us -> 101 us (1.047)
  waiting for transfers between devices: 37 us -> 41.7 us
    ppermute x5, waiting for transfers between devices: 14.3 us -> 17.2 us  [the longest x3 11.4 us: quick(): lax.ppermute(x, 'ga', [(i, i ^ 2 * near_z) for i in range(n_ga)])]
    ppermute x14, waiting for transfers between devices: 2.4 us -> 3.52 us  [other_core(): return lax.ppermute(x, 'ga', [(i, i ^ 1) for i in range(n_ga)])]
  transfers between devices with their start and end apart: 34 -> 34, of which waited for: 17 -> 21; matrix products, arithmetic and copies ran while one was open for 0% -> 0% of each run, Pallas kernels for 23% -> 22%
where the time goes in v11:
time: 101 us; the launch traced here: 100 us
  waiting for transfers between devices  41.7 us (41%)
  starting transfers between devices  33 us (33%)
  Pallas kernels  24 us (24%)
    pallas_call x23, Pallas kernels, run(): pl.pallas_call(body, in_specs=specs or [VMEM] * len(args), out_specs=[VME...  24 us
    ppermute x10, waiting for transfers between devices, across(): return lax.ppermute(x, 'kp', [(i, i ^ bit) for i in range(n_kp)])  12.4 us
    ppermute x3, waiting for transfers between devices, quick(): lax.ppermute(x, 'ga', [(i, i ^ 2 * near_z) for i in range(n_ga)])  11.4 us
    ppermute x10, starting transfers between devices, across(): return lax.ppermute(x, 'kp', [(i, i ^ bit) for i in range(n_kp)])  11.2 us
    ppermute x5, starting transfers between devices, along(): lax.ppermute(x, 'ga', [(i, 2 * chips_on[i // 2] + i % 2) for i in range(n...  11 us
    ppermute x5, waiting for transfers between devices, along(): lax.ppermute(x, 'ga', [(i, 2 * chips_on[i // 2] + i % 2) for i in range(n...  8.58 us
    ppermute x2, waiting for transfers between devices, quick(): lax.ppermute(sends, 'ga', [(i, i ^ 2 * far_z) for i in range(n_ga)])  5.85 us
    ppermute x3, starting transfers between devices, quick(): lax.ppermute(x, 'ga', [(i, i ^ 2 * near_z) for i in range(n_ga)])  4.34 us
  transfers between devices with their start and end apart: 34, of which 21 were waited for; matrix products, arithmetic and copies ran while one was open for 0% of the time, Pallas kernels for 22%

profile of v11, /device:TPU:0, one launch (start us, length us, event | category | flops | bytes accessed | tf_op | source)
XLA Modules:
  0.0 100.4 jit_solution(9928495309099509933)
XLA Ops:
  2.5 3.0 %collective-permute-start = (bf16[784,256]{1,0:T(8,128)(2,1)S(1)}, bf16[784,256]{1,0:T(8,128)(2,1)S(1)}, u32[]{:S(2)}, u32[]{:S(2)}) collective-permute-start(bf16[784,256]{1,0:T(8,128)(2,1)S(1)} %get-tuple-element.60.packed_0), channel_id=1, source_target_pairs={{0,8},{8,0},{16,24},{24,16},{1,9},{9,1},{17,25},{25,17},{2,10},{10... | collective-permute-start | bytes 1204232 | tf_op jit(solution)/shard_map/ppermute | solution.py:404
  5.5 1.5 %collective-permute-start.1 = (bf16[784,256]{1,0:T(8,128)(2,1)S(1)}, bf16[784,256]{1,0:T(8,128)(2,1)S(1)}, u32[]{:S(2)}, u32[]{:S(2)}) collective-permute-start(bf16[784,256]{1,0:T(8,128)(2,1)S(1)} %get-tuple-element.61.packed_1), channel_id=1, source_target_pairs={{0,16},{8,24},{16,0},{24,8},{1,17},{9,25},{17,1},{25,9},{2,18},{10... | collective-permute-start | bytes 1204232 | tf_op jit(solution)/shard_map/ppermute | solution.py:404
  7.0 1.6 %collective-permute-start.2 = (bf16[784,256]{1,0:T(8,128)(2,1)S(1)}, bf16[784,256]{1,0:T(8,128)(2,1)S(1)}, u32[]{:S(2)}, u32[]{:S(2)}) collective-permute-start(bf16[784,256]{1,0:T(8,128)(2,1)S(1)} %get-tuple-element.60.packed_0), channel_id=1, source_target_pairs={{0,2},{1,3},{2,6},{3,7},{4,0},{5,1},{6,4},{7,5},{8,10},{9,11},{10,... | collective-permute-start | bytes 1204232 | tf_op jit(solution)/shard_map/ppermute | solution.py:410
  8.6 2.6 %collective-permute-start.3 = (bf16[784,256]{1,0:T(8,128)(2,1)S(1)}, bf16[784,256]{1,0:T(8,128)(2,1)S(1)}, u32[]{:S(2)}, u32[]{:S(2)}) collective-permute-start(bf16[784,256]{1,0:T(8,128)(2,1)S(1)} %get-tuple-element.61.packed_1), channel_id=1, source_target_pairs={{0,2},{1,3},{2,6},{3,7},{4,0},{5,1},{6,4},{7,5},{8,10},{9,11},{10,... | collective-permute-start | bytes 1204232 | tf_op jit(solution)/shard_map/ppermute | solution.py:410
  11.2 3.8 %load.1.screened = bf16[2,2,384,3072]{3,2,1,0:T(8,128)(2,1)S(1)} custom-call(bf16[2,2,384,3072]{3,2,1,0:T(8,128)(2,1)} %source), custom_call_target="tpu_custom_call" | custom-call | tf_op jit(solution)/shard_map/load/pallas_call | solution.py:30
  16.8 1.6 %collective-permute-start.6 = (bf16[2,2,192,256]{3,2,1,0:T(8,128)(2,1)S(1)}, bf16[2,2,192,256]{3,2,1,0:T(8,128)(2,1)S(1)}, u32[]{:S(2)}, u32[]{:S(2)}) collective-permute-start(bf16[2,2,192,256]{3,2,1,0:T(8,128)(2,1)S(1)} %get-tuple-element.64), channel_id=1, source_target_pairs={{0,16},{8,24},{16,0},{24,8},{1,17},{9,25},{17,1},{25,9},{2,18},{10... | collective-permute-start | bytes 1179656 | tf_op jit(solution)/shard_map/ppermute | solution.py:404
  20.7 6.3 %collective-permute-done.3.packed.packed_1 = bf16[784,256]{1,0:T(8,128)(2,1)S(1)} collective-permute-done((bf16[784,256]{1,0:T(8,128)(2,1)S(1)}, bf16[784,256]{1,0:T(8,128)(2,1)S(1)}, u32[]{:S(2)}, u32[]{:S(2)}) %collective-permute-start.3) | collective-permute-done | bytes 401440 | tf_op jit(solution)/shard_map/ppermute | solution.py:410
  27.9 2.6 %collective-permute-done.7.picked_1 = bf16[2,2,192,256]{3,2,1,0:T(8,128)(2,1)S(1)} collective-permute-done((bf16[2,2,192,256]{3,2,1,0:T(8,128)(2,1)S(1)}, bf16[2,2,192,256]{3,2,1,0:T(8,128)(2,1)S(1)}, u32[]{:S(2)}, u32[]{:S(2)}) %collective-permute-start.7) | collective-permute-done | bytes 393248 | tf_op jit(solution)/shard_map/ppermute | solution.py:404
  30.8 2.6 %collective-permute-start.11 = (bf16[2,2,384,256]{3,2,1,0:T(8,128)(2,1)S(1)}, bf16[2,2,384,256]{3,2,1,0:T(8,128)(2,1)S(1)}, u32[]{:S(2)}, u32[]{:S(2)}) collective-permute-start(bf16[2,2,384,256]{3,2,1,0:T(8,128)(2,1)S(1)} %near.2.own.refs_0_), channel_id=1, source_target_pairs={{0,4},{1,5},{2,0},{3,1},{4,6},{5,7},{6,2},{7,3},{8,12},{9,13},{10,... | collective-permute-start | bytes 2359304 | tf_op jit(solution)/shard_map/ppermute | solution.py:410
  33.5 1.8 %product.3.before = f32[2,384,1024]{2,1,0:T(8,128)S(1)} custom-call(bf16[2,2,384,3072]{3,2,1,0:T(8,128)(2,1)S(1)} %load.1.screened, bf16[2,2,384,256]{3,2,1,0:T(8,128)(2,1)S(1)} %near.2.own.refs_0_, f32[1,384]{1,0:T(1,128)S(1)} %broadcast_in_dim.3.coulomb), custom_call_target="tpu_custom_call" | custom-call | tf_op jit(solution)/shard_map/product/pallas_call | solution.py:30
  38.3 7.5 %collective-permute-done.9.picked_1 = bf16[2,2,192,256]{3,2,1,0:T(8,128)(2,1)S(1)} collective-permute-done((bf16[2,2,192,256]{3,2,1,0:T(8,128)(2,1)S(1)}, bf16[2,2,192,256]{3,2,1,0:T(8,128)(2,1)S(1)}, u32[]{:S(2)}, u32[]{:S(2)}) %collective-permute-start.9) | collective-permute-done | bytes 393248 | tf_op jit(solution)/shard_map/ppermute | solution.py:404
  47.0 2.0 %collective-permute-start.10 = (bf16[2,384,256]{2,1,0:T(8,128)(2,1)S(1)}, bf16[2,384,256]{2,1,0:T(8,128)(2,1)S(1)}, u32[]{:S(2)}, u32[]{:S(2)}) collective-permute-start(bf16[2,384,256]{2,1,0:T(8,128)(2,1)S(1)} %get-tuple-element.72), channel_id=1, source_target_pairs={{0,2},{1,3},{2,6},{3,7},{4,0},{5,1},{6,4},{7,5},{8,10},{9,11},{10,... | collective-permute-start | bytes 1179656 | tf_op jit(solution)/shard_map/ppermute | solution.py:410
  49.0 1.5 %collective-permute-start.16 = (bf16[3,2,192,256]{3,2,1,0:T(8,128)(2,1)S(1)}, bf16[3,2,192,256]{3,2,1,0:T(8,128)(2,1)S(1)}, u32[]{:S(2)}, u32[]{:S(2)}) collective-permute-start(bf16[3,2,192,256]{3,2,1,0:T(8,128)(2,1)S(1)} %get-tuple-element.79), channel_id=1, source_target_pairs={{0,16},{8,24},{16,0},{24,8},{1,17},{9,25},{17,1},{25,9},{2,18},{10... | collective-permute-start | bytes 1769480 | tf_op jit(solution)/shard_map/ppermute | solution.py:404
  50.5 2.2 %collective-permute-start.24 = (bf16[2,384,256]{2,1,0:T(8,128)(2,1)S(1)}, bf16[2,384,256]{2,1,0:T(8,128)(2,1)S(1)}, u32[]{:S(2)}, u32[]{:S(2)}) collective-permute-start(bf16[2,384,256]{2,1,0:T(8,128)(2,1)S(1)} %get-tuple-element.93), channel_id=1, source_target_pairs={{0,2},{1,3},{2,6},{3,7},{4,0},{5,1},{6,4},{7,5},{8,10},{9,11},{10,... | collective-permute-start | bytes 1179656 | tf_op jit(solution)/shard_map/ppermute | solution.py:410
  53.3 3.0 %product.4.before = f32[2,384,1024]{2,1,0:T(8,128)S(1)} custom-call(bf16[2,2,384,3072]{3,2,1,0:T(8,128)(2,1)S(1)} %load.1.screened, bf16[2,2,384,256]{3,2,1,0:T(8,128)(2,1)S(1)} %collective-permute-done.11.own, bf16[2,2,384,256]{3,2,1,0:T(8,128)(2,1)S(1)} %collective-permute-done.13.pair, ...), custom_call_target="tpu_custom_call", output_to_operand_aliasing={{}: (3, {})} | custom-call | tf_op jit(solution)/shard_map/product/pallas_call | solution.py:30
  56.4 4.6 %product.5.before = f32[2,384,1024]{2,1,0:T(8,128)S(1)} custom-call(bf16[2,2,384,3072]{3,2,1,0:T(8,128)(2,1)S(1)} %load.1.screened, bf16[2,2,384,256]{3,2,1,0:T(8,128)(2,1)S(1)} %get-tuple-element.76.refs_1_.own, bf16[2,2,2,384,256]{4,3,2,1,0:T(8,128)(2,1)S(1)} %collective-permute-done.12.pairs, ...), custom_call_target="tpu_custom_call", output_to_operand_aliasing={{}: (3, {})} | custom-call | tf_op jit(solution)/shard_map/product/pallas_call | solution.py:30
  69.9 1.8 %collective-permute-start.22 = (bf16[528,256]{1,0:T(8,128)(2,1)S(1)}, bf16[528,256]{1,0:T(8,128)(2,1)S(1)}, u32[]{:S(2)}, u32[]{:S(2)}) collective-permute-start(bf16[528,256]{1,0:T(8,128)(2,1)S(1)} %get-tuple-element.90), channel_id=1, source_target_pairs={{0,4},{1,5},{2,6},{3,7},{4,0},{5,1},{6,2},{7,3},{8,12},{9,13},{10,... | collective-permute-start | bytes 811016 | tf_op jit(solution)/shard_map/ppermute | solution.py:547
  72.3 1.5 %image.3 = bf16[2,384,512]{2,1,0:T(8,128)(2,1)S(1)} custom-call(bf16[2,2,384,3072]{3,2,1,0:T(8,128)(2,1)S(1)} %load.1.screened, bf16[2,384,256]{2,1,0:T(8,128)(2,1)S(1)} %collective-permute-done.24.own, bf16[384,256]{1,0:T(8,128)(2,1)S(1)} %collective-permute-done.25.pair_real, bf16[384,256]{1,0:T(8,128)(2,1)S(1)} %collective-permute-done.26.pair_imag, ...), custom_call_target="tpu_custom_call" | custom-call | tf_op jit(solution)/shard_map/image/pallas_call | solution.py:30
  76.9 2.5 %collective-permute-start.31 = (bf16[2,2,2,32,256]{4,3,2,1,0:T(8,128)(2,1)S(1)}, bf16[2,2,2,32,256]{4,3,2,1,0:T(8,128)(2,1)S(1)}, u32[]{:S(2)}, u32[]{:S(2)}) collective-permute-start(bf16[2,2,2,32,256]{4,3,2,1,0:T(8,128)(2,1)S(1)} %get-tuple-element.104), channel_id=1, source_target_pairs={{0,2},{1,3},{2,0},{3,1},{4,6},{5,7},{6,4},{7,5},{8,10},{9,11},{10,... | collective-permute-start | bytes 393224 | tf_op jit(solution)/shard_map/ppermute | solution.py:547
  79.5 5.9 %collective-permute-done.22.refs_0_ = bf16[528,256]{1,0:T(8,128)(2,1)S(1)} collective-permute-done((bf16[528,256]{1,0:T(8,128)(2,1)S(1)}, bf16[528,256]{1,0:T(8,128)(2,1)S(1)}, u32[]{:S(2)}, u32[]{:S(2)}) %collective-permute-start.22) | collective-permute-done | bytes 270368 | tf_op jit(solution)/shard_map/ppermute | solution.py:547
  85.4 2.7 %collective-permute-done.31.refs_0_ = bf16[2,2,2,32,256]{4,3,2,1,0:T(8,128)(2,1)S(1)} collective-permute-done((bf16[2,2,2,32,256]{4,3,2,1,0:T(8,128)(2,1)S(1)}, bf16[2,2,2,32,256]{4,3,2,1,0:T(8,128)(2,1)S(1)}, u32[]{:S(2)}, u32[]{:S(2)}) %collective-permute-start.31) | collective-permute-done | bytes 131104 | tf_op jit(solution)/shard_map/ppermute | solution.py:547
  88.1 2.8 %collective-permute-done.32.refs_1_ = bf16[2,2,2,32,256]{4,3,2,1,0:T(8,128)(2,1)S(1)} collective-permute-done((bf16[2,2,2,32,256]{4,3,2,1,0:T(8,128)(2,1)S(1)}, bf16[2,2,2,32,256]{4,3,2,1,0:T(8,128)(2,1)S(1)}, u32[]{:S(2)}, u32[]{:S(2)}) %collective-permute-start.32) | collective-permute-done | bytes 131104 | tf_op jit(solution)/shard_map/ppermute | solution.py:547
  91.3 2.5 %collective-permute-start.23 = (bf16[2,2,2,32,256]{4,3,2,1,0:T(8,128)(2,1)S(1)}, bf16[2,2,2,32,256]{4,3,2,1,0:T(8,128)(2,1)S(1)}, u32[]{:S(2)}, u32[]{:S(2)}) collective-permute-start(bf16[2,2,2,32,256]{4,3,2,1,0:T(8,128)(2,1)S(1)} %get-tuple-element.92), channel_id=1, source_target_pairs={{0,2},{1,3},{2,0},{3,1},{4,6},{5,7},{6,4},{7,5},{8,10},{9,11},{10,... | collective-permute-start | bytes 393224 | tf_op jit(solution)/shard_map/ppermute | solution.py:556
  93.7 5.7 %collective-permute-done.33.refs_3_ = bf16[2,2,2,32,256]{4,3,2,1,0:T(8,128)(2,1)S(1)} collective-permute-done((bf16[2,2,2,32,256]{4,3,2,1,0:T(8,128)(2,1)S(1)}, bf16[2,2,2,32,256]{4,3,2,1,0:T(8,128)(2,1)S(1)}, u32[]{:S(2)}, u32[]{:S(2)}) %collective-permute-start.33) | collective-permute-done | bytes 131104 | tf_op jit(solution)/shard_map/ppermute | solution.py:556
  (74 shorter events, 26.0 us)
Async XLA Ops:
  2.5 12.5 %collective-permute-start = (bf16[784,256]{1,0:T(8,128)(2,1)S(1)}, bf16[784,256]{1,0:T(8,128)(2,1)S(1)}, u32[]{:S(2)}, u32[]{:S(2)}) collective-permute-start(bf16[784,256]{1,0:T(8,128)(2,1)S(1)} %get-tuple-element.60.packed_0), channel_id=1, source_target_pairs={{0,8},{8,0},{16,24},{24,16},{1,9},{9,1},{17,25},{25,17},{2,10},{10... | collective-permute-start | bytes 1204232 | tf_op jit(solution)/shard_map/ppermute | solution.py:404
  5.5 10.8 %collective-permute-start.1 = (bf16[784,256]{1,0:T(8,128)(2,1)S(1)}, bf16[784,256]{1,0:T(8,128)(2,1)S(1)}, u32[]{:S(2)}, u32[]{:S(2)}) collective-permute-start(bf16[784,256]{1,0:T(8,128)(2,1)S(1)} %get-tuple-element.61.packed_1), channel_id=1, source_target_pairs={{0,16},{8,24},{16,0},{24,8},{1,17},{9,25},{17,1},{25,9},{2,18},{10... | collective-permute-start | bytes 1204232 | tf_op jit(solution)/shard_map/ppermute | solution.py:404
  7.0 13.1 %collective-permute-start.2 = (bf16[784,256]{1,0:T(8,128)(2,1)S(1)}, bf16[784,256]{1,0:T(8,128)(2,1)S(1)}, u32[]{:S(2)}, u32[]{:S(2)}) collective-permute-start(bf16[784,256]{1,0:T(8,128)(2,1)S(1)} %get-tuple-element.60.packed_0), channel_id=1, source_target_pairs={{0,2},{1,3},{2,6},{3,7},{4,0},{5,1},{6,4},{7,5},{8,10},{9,11},{10,... | collective-permute-start | bytes 1204232 | tf_op jit(solution)/shard_map/ppermute | solution.py:410
  8.6 18.4 %collective-permute-start.3 = (bf16[784,256]{1,0:T(8,128)(2,1)S(1)}, bf16[784,256]{1,0:T(8,128)(2,1)S(1)}, u32[]{:S(2)}, u32[]{:S(2)}) collective-permute-start(bf16[784,256]{1,0:T(8,128)(2,1)S(1)} %get-tuple-element.61.packed_1), channel_id=1, source_target_pairs={{0,2},{1,3},{2,6},{3,7},{4,0},{5,1},{6,4},{7,5},{8,10},{9,11},{10,... | collective-permute-start | bytes 1204232 | tf_op jit(solution)/shard_map/ppermute | solution.py:410
  16.8 11.0 %collective-permute-start.6 = (bf16[2,2,192,256]{3,2,1,0:T(8,128)(2,1)S(1)}, bf16[2,2,192,256]{3,2,1,0:T(8,128)(2,1)S(1)}, u32[]{:S(2)}, u32[]{:S(2)}) collective-permute-start(bf16[2,2,192,256]{3,2,1,0:T(8,128)(2,1)S(1)} %get-tuple-element.64), channel_id=1, source_target_pairs={{0,16},{8,24},{16,0},{24,8},{1,17},{9,25},{17,1},{25,9},{2,18},{10... | collective-permute-start | bytes 1179656 | tf_op jit(solution)/shard_map/ppermute | solution.py:404
  18.4 12.1 %collective-permute-start.7 = (bf16[2,2,192,256]{3,2,1,0:T(8,128)(2,1)S(1)}, bf16[2,2,192,256]{3,2,1,0:T(8,128)(2,1)S(1)}, u32[]{:S(2)}, u32[]{:S(2)}) collective-permute-start(bf16[2,2,192,256]{3,2,1,0:T(8,128)(2,1)S(1)} %get-tuple-element.65), channel_id=1, source_target_pairs={{0,8},{8,0},{16,24},{24,16},{1,9},{9,1},{17,25},{25,17},{2,10},{10... | collective-permute-start | bytes 1179656 | tf_op jit(solution)/shard_map/ppermute | solution.py:404
  20.1 16.3 %collective-permute-start.4 = (bf16[784,256]{1,0:T(8,128)(2,1)S(1)}, bf16[784,256]{1,0:T(8,128)(2,1)S(1)}, u32[]{:S(2)}, u32[]{:S(2)}) collective-permute-start(bf16[784,256]{1,0:T(8,128)(2,1)S(1)} %collective-permute-done.2.packed.packed_0), channel_id=1, source_target_pairs={{0,8},{8,0},{16,24},{24,16},{1,9},{9,1},{17,25},{25,17},{2,10},{10... | collective-permute-start | bytes 1204232 | tf_op jit(solution)/shard_map/ppermute | solution.py:404
  27.0 10.3 %collective-permute-start.5 = (bf16[784,256]{1,0:T(8,128)(2,1)S(1)}, bf16[784,256]{1,0:T(8,128)(2,1)S(1)}, u32[]{:S(2)}, u32[]{:S(2)}) collective-permute-start(bf16[784,256]{1,0:T(8,128)(2,1)S(1)} %collective-permute-done.3.packed.packed_1), channel_id=1, source_target_pairs={{0,16},{8,24},{16,0},{24,8},{1,17},{9,25},{17,1},{25,9},{2,18},{10... | collective-permute-start | bytes 1204232 | tf_op jit(solution)/shard_map/ppermute | solution.py:404
  30.8 15.4 %collective-permute-start.11 = (bf16[2,2,384,256]{3,2,1,0:T(8,128)(2,1)S(1)}, bf16[2,2,384,256]{3,2,1,0:T(8,128)(2,1)S(1)}, u32[]{:S(2)}, u32[]{:S(2)}) collective-permute-start(bf16[2,2,384,256]{3,2,1,0:T(8,128)(2,1)S(1)} %near.2.own.refs_0_), channel_id=1, source_target_pairs={{0,4},{1,5},{2,0},{3,1},{4,6},{5,7},{6,2},{7,3},{8,12},{9,13},{10,... | collective-permute-start | bytes 2359304 | tf_op jit(solution)/shard_map/ppermute | solution.py:410
  36.7 9.1 %collective-permute-start.8 = (bf16[784,256]{1,0:T(8,128)(2,1)S(1)}, bf16[784,256]{1,0:T(8,128)(2,1)S(1)}, u32[]{:S(2)}, u32[]{:S(2)}) collective-permute-start(bf16[784,256]{1,0:T(8,128)(2,1)S(1)} %pick_half.2), channel_id=1, source_target_pairs={{0,16},{8,24},{16,0},{24,8},{1,17},{9,25},{17,1},{25,9},{2,18},{10... | collective-permute-start | bytes 1204232 | tf_op jit(solution)/shard_map/ppermute | solution.py:404
  37.6 8.2 %collective-permute-start.9 = (bf16[2,2,192,256]{3,2,1,0:T(8,128)(2,1)S(1)}, bf16[2,2,192,256]{3,2,1,0:T(8,128)(2,1)S(1)}, u32[]{:S(2)}, u32[]{:S(2)}) collective-permute-start(bf16[2,2,192,256]{3,2,1,0:T(8,128)(2,1)S(1)} %pick_half.3), channel_id=1, source_target_pairs={{0,8},{8,0},{16,24},{24,16},{1,9},{9,1},{17,25},{25,17},{2,10},{10... | collective-permute-start | bytes 1179656 | tf_op jit(solution)/shard_map/ppermute | solution.py:404
  46.4 10.0 %collective-permute-start.12 = (bf16[2,2,2,384,256]{4,3,2,1,0:T(8,128)(2,1)S(1)}, bf16[2,2,2,384,256]{4,3,2,1,0:T(8,128)(2,1)S(1)}, u32[]{:S(2)}, u32[]{:S(2)}) collective-permute-start(bf16[2,2,2,384,256]{4,3,2,1,0:T(8,128)(2,1)S(1)} %stack.1), channel_id=1, source_target_pairs={{0,1},{1,0},{2,3},{3,2},{4,5},{5,4},{6,7},{7,6},{8,9},{9,8},{10,11... | collective-permute-start | bytes 4718600 | tf_op jit(solution)/shard_map/ppermute | solution.py:407
  46.5 6.2 %collective-permute-start.13 = (bf16[2,2,384,256]{3,2,1,0:T(8,128)(2,1)S(1)}, bf16[2,2,384,256]{3,2,1,0:T(8,128)(2,1)S(1)}, u32[]{:S(2)}, u32[]{:S(2)}) collective-permute-start(bf16[2,2,384,256]{3,2,1,0:T(8,128)(2,1)S(1)} %collective-permute-done.11.own), channel_id=1, source_target_pairs={{0,1},{1,0},{2,3},{3,2},{4,5},{5,4},{6,7},{7,6},{8,9},{9,8},{10,11... | collective-permute-start | bytes 2359304 | tf_op jit(solution)/shard_map/ppermute | solution.py:407
  47.0 14.1 %collective-permute-start.10 = (bf16[2,384,256]{2,1,0:T(8,128)(2,1)S(1)}, bf16[2,384,256]{2,1,0:T(8,128)(2,1)S(1)}, u32[]{:S(2)}, u32[]{:S(2)}) collective-permute-start(bf16[2,384,256]{2,1,0:T(8,128)(2,1)S(1)} %get-tuple-element.72), channel_id=1, source_target_pairs={{0,2},{1,3},{2,6},{3,7},{4,0},{5,1},{6,4},{7,5},{8,10},{9,11},{10,... | collective-permute-start | bytes 1179656 | tf_op jit(solution)/shard_map/ppermute | solution.py:410
  49.0 15.4 %collective-permute-start.16 = (bf16[3,2,192,256]{3,2,1,0:T(8,128)(2,1)S(1)}, bf16[3,2,192,256]{3,2,1,0:T(8,128)(2,1)S(1)}, u32[]{:S(2)}, u32[]{:S(2)}) collective-permute-start(bf16[3,2,192,256]{3,2,1,0:T(8,128)(2,1)S(1)} %get-tuple-element.79), channel_id=1, source_target_pairs={{0,16},{8,24},{16,0},{24,8},{1,17},{9,25},{17,1},{25,9},{2,18},{10... | collective-permute-start | bytes 1769480 | tf_op jit(solution)/shard_map/ppermute | solution.py:404
  50.5 16.9 %collective-permute-start.24 = (bf16[2,384,256]{2,1,0:T(8,128)(2,1)S(1)}, bf16[2,384,256]{2,1,0:T(8,128)(2,1)S(1)}, u32[]{:S(2)}, u32[]{:S(2)}) collective-permute-start(bf16[2,384,256]{2,1,0:T(8,128)(2,1)S(1)} %get-tuple-element.93), channel_id=1, source_target_pairs={{0,2},{1,3},{2,6},{3,7},{4,0},{5,1},{6,4},{7,5},{8,10},{9,11},{10,... | collective-permute-start | bytes 1179656 | tf_op jit(solution)/shard_map/ppermute | solution.py:410
  52.7 11.7 %collective-permute-start.17 = (bf16[2,2,192,256]{3,2,1,0:T(8,128)(2,1)S(1)}, bf16[2,2,192,256]{3,2,1,0:T(8,128)(2,1)S(1)}, u32[]{:S(2)}, u32[]{:S(2)}) collective-permute-start(bf16[2,2,192,256]{3,2,1,0:T(8,128)(2,1)S(1)} %get-tuple-element.80), channel_id=1, source_target_pairs={{0,8},{8,0},{16,24},{24,16},{1,9},{9,1},{17,25},{25,17},{2,10},{10... | collective-permute-start | bytes 1179656 | tf_op jit(solution)/shard_map/ppermute | solution.py:404
  67.4 4.9 %collective-permute-start.25 = (bf16[384,256]{1,0:T(8,128)(2,1)S(1)}, bf16[384,256]{1,0:T(8,128)(2,1)S(1)}, u32[]{:S(2)}, u32[]{:S(2)}) collective-permute-start(bf16[384,256]{1,0:T(8,128)(2,1)S(1)} %get-tuple-element.111), channel_id=1, source_target_pairs={{0,1},{1,0},{2,3},{3,2},{4,5},{5,4},{6,7},{7,6},{8,9},{9,8},{10,11... | collective-permute-start | bytes 589832 | tf_op jit(solution)/shard_map/ppermute | solution.py:407
  67.5 4.8 %collective-permute-start.26 = (bf16[384,256]{1,0:T(8,128)(2,1)S(1)}, bf16[384,256]{1,0:T(8,128)(2,1)S(1)}, u32[]{:S(2)}, u32[]{:S(2)}) collective-permute-start(bf16[384,256]{1,0:T(8,128)(2,1)S(1)} %get-tuple-element.110), channel_id=1, source_target_pairs={{0,1},{1,0},{2,3},{3,2},{4,5},{5,4},{6,7},{7,6},{8,9},{9,8},{10,11... | collective-permute-start | bytes 589832 | tf_op jit(solution)/shard_map/ppermute | solution.py:407
  69.9 15.4 %collective-permute-start.22 = (bf16[528,256]{1,0:T(8,128)(2,1)S(1)}, bf16[528,256]{1,0:T(8,128)(2,1)S(1)}, u32[]{:S(2)}, u32[]{:S(2)}) collective-permute-start(bf16[528,256]{1,0:T(8,128)(2,1)S(1)} %get-tuple-element.90), channel_id=1, source_target_pairs={{0,4},{1,5},{2,6},{3,7},{4,0},{5,1},{6,2},{7,3},{8,12},{9,13},{10,... | collective-permute-start | bytes 811016 | tf_op jit(solution)/shard_map/ppermute | solution.py:547
  76.9 11.2 %collective-permute-start.31 = (bf16[2,2,2,32,256]{4,3,2,1,0:T(8,128)(2,1)S(1)}, bf16[2,2,2,32,256]{4,3,2,1,0:T(8,128)(2,1)S(1)}, u32[]{:S(2)}, u32[]{:S(2)}) collective-permute-start(bf16[2,2,2,32,256]{4,3,2,1,0:T(8,128)(2,1)S(1)} %get-tuple-element.104), channel_id=1, source_target_pairs={{0,2},{1,3},{2,0},{3,1},{4,6},{5,7},{6,4},{7,5},{8,10},{9,11},{10,... | collective-permute-start | bytes 393224 | tf_op jit(solution)/shard_map/ppermute | solution.py:547
  79.4 11.5 %collective-permute-start.32 = (bf16[2,2,2,32,256]{4,3,2,1,0:T(8,128)(2,1)S(1)}, bf16[2,2,2,32,256]{4,3,2,1,0:T(8,128)(2,1)S(1)}, u32[]{:S(2)}, u32[]{:S(2)}) collective-permute-start(bf16[2,2,2,32,256]{4,3,2,1,0:T(8,128)(2,1)S(1)} %get-tuple-element.105), channel_id=1, source_target_pairs={{0,2},{1,3},{2,0},{3,1},{4,6},{5,7},{6,4},{7,5},{8,10},{9,11},{10,... | collective-permute-start | bytes 393224 | tf_op jit(solution)/shard_map/ppermute | solution.py:547
  90.9 8.5 %collective-permute-start.33 = (bf16[2,2,2,32,256]{4,3,2,1,0:T(8,128)(2,1)S(1)}, bf16[2,2,2,32,256]{4,3,2,1,0:T(8,128)(2,1)S(1)}, u32[]{:S(2)}, u32[]{:S(2)}) collective-permute-start(bf16[2,2,2,32,256]{4,3,2,1,0:T(8,128)(2,1)S(1)} %get-tuple-element.109), channel_id=1, source_target_pairs={{0,4},{1,5},{2,6},{3,7},{4,0},{5,1},{6,2},{7,3},{8,12},{9,13},{10,... | collective-permute-start | bytes 393224 | tf_op jit(solution)/shard_map/ppermute | solution.py:556
  91.3 8.3 %collective-permute-start.23 = (bf16[2,2,2,32,256]{4,3,2,1,0:T(8,128)(2,1)S(1)}, bf16[2,2,2,32,256]{4,3,2,1,0:T(8,128)(2,1)S(1)}, u32[]{:S(2)}, u32[]{:S(2)}) collective-permute-start(bf16[2,2,2,32,256]{4,3,2,1,0:T(8,128)(2,1)S(1)} %get-tuple-element.92), channel_id=1, source_target_pairs={{0,2},{1,3},{2,0},{3,1},{4,6},{5,7},{6,4},{7,5},{8,10},{9,11},{10,... | collective-permute-start | bytes 393224 | tf_op jit(solution)/shard_map/ppermute | solution.py:556
  (12 other events, 34.9 us)

commit v12 on v9

--- a/solution.py
+++ b/solution.py
@@ -250,16 +250,13 @@
     return z if steps == 0 else 3 - z
 
 
-def lay(terms, upper, lower):
+def lay(terms, near):
     for ref, first in terms:
         *count, _, g_local, t = ref.shape
         rows = pl.ds(first if isinstance(first, int) else pl.multiple_of(first, 128), g_local)
         for j, panel in enumerate([ref.at[j] for j in range(count[0])] if count else [ref]):
-            real, imag = slice(2 * j * t, (2 * j + 1) * t), slice((2 * j + 1) * t, (2 * j + 2) * t)
-            upper[rows, real] = panel[0]
-            upper[rows, imag] = panel[1]
-            lower[rows, real] = -panel[1]
-            lower[rows, imag] = panel[0]
+            near[rows, 2 * j * t : (2 * j + 1) * t] = panel[0]
+            near[rows, (2 * j + 1) * t : (2 * j + 2) * t] = panel[1]
 
 
 def place():
@@ -267,59 +264,67 @@
     return slot // 2, lax.rem(slot, 2)
 
 
-def multiply(screened, s, span, width, upper, lower, first=0):
+def combine(by_real, by_imag, t):
+    parts = []
+    for real in range(0, by_real.shape[1], 2 * t):
+        imag = real + t
+        parts.append(by_real[:, real:imag] - by_imag[:, imag : imag + t])
+        parts.append(by_real[:, imag : imag + t] + by_imag[:, real:imag])
+    return jnp.concatenate(parts, axis=1)
+
+
+def multiply(screened, s, span, width, near, t, first=0):
     span = pl.ds(pl.multiple_of(span, 128), width)
     rows = slice(first, first + width)
-    return dot(screened[s, 0, :, span], upper[rows]) + dot(screened[s, 1, :, span], lower[rows])
-
-
-def first_kernel(screened, own, coulomb, total, upper, lower):
+    by_real, by_imag = dot(screened[s, 0, :, span], near[rows]), dot(screened[s, 1, :, span], near[rows])
+    return combine(by_real, by_imag, t)
+
+
+def first_kernel(screened, own, coulomb, total, near):
     z, core = place()
-    g = screened.shape[2]
-    lay([(own, 0)], upper, lower)
+    g, t = own.shape[2:]
+    lay([(own, 0)], near)
     span = pl.ds(pl.multiple_of((2 * z + core) * g, 128), g)
     line = lax.broadcasted_iota(jnp.int32, (g, g), 0)
     on = line == lax.broadcasted_iota(jnp.int32, (g, g), 1)
     for s in range(screened.shape[0]):
         real = screened[s, 0, :, span]
         real = jnp.where(on, (real.astype(F32) - 2.0 * coulomb[...]).astype(BF16), real)
-        total[s] = dot(real, upper[...]) + dot(screened[s, 1, :, span], lower[...])
-
-
-def step_kernel(steps, screened, own, pair, before, total, upper, lower):
+        total[s] = combine(dot(real, near[...]), dot(screened[s, 1, :, span], near[...]), t)
+
+
+def step_kernel(steps, screened, own, pair, before, total, near):
     z, core = place()
-    g = screened.shape[2]
-    lay([(own, core * g), (pair, (1 - core) * g)], upper, lower)
+    g, t = own.shape[2:]
+    lay([(own, core * g), (pair, (1 - core) * g)], near)
     span = 2 * chip_at(z, steps) * g
     for s in range(screened.shape[0]):
-        total[s] = before[s] + multiply(screened, s, span, 2 * g, upper, lower)
-
-
-def second_kernel(steps, screened, own, pairs, before, total, upper, lower):
+        total[s] = before[s] + multiply(screened, s, span, 2 * g, near, t)
+
+
+def second_kernel(steps, screened, own, pairs, before, total, near):
     z, core = place()
-    g = screened.shape[2]
-    lay([(own, core * g), (pairs.at[1], (1 - core) * g), (pairs.at[0], 2 * g)], upper, lower)
+    g, t = own.shape[2:]
+    lay([(own, core * g), (pairs.at[1], (1 - core) * g), (pairs.at[0], 2 * g)], near)
     span = 2 * chip_at(z, steps) * g
     left = (2 * z + 1 - core) * g
     for s in range(screened.shape[0]):
-        value = before[s] + multiply(screened, s, span, 2 * g, upper, lower)
-        total[s] = value + multiply(screened, s, left, g, upper, lower, 2 * g)
-
-
-def image_kernel(steps, j, screened, own, pair_real, pair_imag, before, image, upper, lower):
+        value = before[s] + multiply(screened, s, span, 2 * g, near, t)
+        total[s] = value + multiply(screened, s, left, g, near, t, 2 * g)
+
+
+def image_kernel(steps, j, screened, own, pair_real, pair_imag, before, image, near):
     z, core = place()
     g = screened.shape[2]
     t = own.shape[2]
-    lay([(own, core * g)], upper, lower)
+    lay([(own, core * g)], near)
     rows = pl.ds(pl.multiple_of((1 - core) * g, 128), g)
-    upper[rows, :t] = pair_real[...]
-    upper[rows, t:] = pair_imag[...]
-    lower[rows, :t] = -pair_imag[...]
-    lower[rows, t:] = pair_real[...]
+    near[rows, :t] = pair_real[...]
+    near[rows, t:] = pair_imag[...]
     span = 2 * chip_at(z, steps) * g
     for s in range(screened.shape[0]):
         value = before[s, :, 2 * j * t : 2 * (j + 1) * t]
-        image[s] = (value + multiply(screened, s, span, 2 * g, upper, lower)).astype(BF16)
+        image[s] = (value + multiply(screened, s, span, 2 * g, near, t)).astype(BF16)
 
 
 def mirror_kernel(chips, image, far, keep, *gives):
@@ -398,7 +403,7 @@
             sums,
             screened,
             *args,
-            scratch=[pltpu.VMEM((terms * g_local, 2 * count * t), BF16)] * 2,
+            scratch=[pltpu.VMEM((terms * g_local, 2 * count * t), BF16)],
             aliases={} if terms == 1 else {3: 0},
             name="product",
             mib=24,
@@ -492,7 +497,7 @@
             behind[j],
             *[other_core(behind[j][part]) for part in range(2)],
             total,
-            scratch=[pltpu.VMEM((2 * g_local, 2 * t), BF16)] * 2,
+            scratch=[pltpu.VMEM((2 * g_local, 2 * t), BF16)],
             name="image",
             mib=24,
         )

time: 96.4 us -> 96.1 us (level)
  no operation moved by 1% of the time
where the time goes in v12:
time: 96.1 us; the launch traced here: 95.9 us
  waiting for transfers between devices  37.3 us (39%)
  starting transfers between devices  32.6 us (34%)
  Pallas kernels  24.3 us (25%)
    pallas_call x23, Pallas kernels, run(): pl.pallas_call(body, in_specs=specs or [VMEM] * len(args), out_specs=[VME...  24.3 us
    ppermute x10, waiting for transfers between devices, across(): return lax.ppermute(x, 'kp', [(i, i ^ bit) for i in range(n_kp)])  12.5 us
    ppermute x10, starting transfers between devices, across(): return lax.ppermute(x, 'kp', [(i, i ^ bit) for i in range(n_kp)])  11.2 us
    ppermute x5, starting transfers between devices, along(): lax.ppermute(x, 'ga', [(i, 2 * chips_on[i // 2] + i % 2) for i in range(n...  11 us
    ppermute x2, waiting for transfers between devices, quick(): came_j = lax.ppermute(sends, 'ga', [(i, i ^ 2) for i in range(n_ga)])  8.12 us
    ppermute x5, waiting for transfers between devices, along(): lax.ppermute(x, 'ga', [(i, 2 * chips_on[i // 2] + i % 2) for i in range(n...  7.74 us
    ppermute x2, waiting for transfers between devices, quick(): lax.ppermute(sends, 'ga', [(i, i ^ 4) for i in range(n_ga)])  6.54 us
    ppermute x14, starting transfers between devices, other_core(): return lax.ppermute(x, 'ga', [(i, i ^ 1) for i in range(n_ga)])  3.88 us
  transfers between devices with their start and end apart: 33, of which 17 were waited for; matrix products, arithmetic and copies ran while one was open for 0% of the time, Pallas kernels for 23%

profile of v12, /device:TPU:0, one launch (start us, length us, event | category | flops | bytes accessed | tf_op | source)
XLA Modules:
  0.0 95.9 jit_solution(9021803183926049511)
XLA Ops:
  2.5 3.0 %collective-permute-start = (bf16[784,256]{1,0:T(8,128)(2,1)S(1)}, bf16[784,256]{1,0:T(8,128)(2,1)S(1)}, u32[]{:S(2)}, u32[]{:S(2)}) collective-permute-start(bf16[784,256]{1,0:T(8,128)(2,1)S(1)} %get-tuple-element.59.packed_0), channel_id=1, source_target_pairs={{0,8},{8,0},{16,24},{24,16},{1,9},{9,1},{17,25},{25,17},{2,10},{10... | collective-permute-start | bytes 1204232 | tf_op jit(solution)/shard_map/ppermute | solution.py:388
  5.5 1.5 %collective-permute-start.1 = (bf16[784,256]{1,0:T(8,128)(2,1)S(1)}, bf16[784,256]{1,0:T(8,128)(2,1)S(1)}, u32[]{:S(2)}, u32[]{:S(2)}) collective-permute-start(bf16[784,256]{1,0:T(8,128)(2,1)S(1)} %get-tuple-element.60.packed_1), channel_id=1, source_target_pairs={{0,16},{8,24},{16,0},{24,8},{1,17},{9,25},{17,1},{25,9},{2,18},{10... | collective-permute-start | bytes 1204232 | tf_op jit(solution)/shard_map/ppermute | solution.py:388
  7.0 1.6 %collective-permute-start.2 = (bf16[784,256]{1,0:T(8,128)(2,1)S(1)}, bf16[784,256]{1,0:T(8,128)(2,1)S(1)}, u32[]{:S(2)}, u32[]{:S(2)}) collective-permute-start(bf16[784,256]{1,0:T(8,128)(2,1)S(1)} %get-tuple-element.59.packed_0), channel_id=1, source_target_pairs={{0,2},{1,3},{2,6},{3,7},{4,0},{5,1},{6,4},{7,5},{8,10},{9,11},{10,... | collective-permute-start | bytes 1204232 | tf_op jit(solution)/shard_map/ppermute | solution.py:394
  8.6 2.6 %collective-permute-start.3 = (bf16[784,256]{1,0:T(8,128)(2,1)S(1)}, bf16[784,256]{1,0:T(8,128)(2,1)S(1)}, u32[]{:S(2)}, u32[]{:S(2)}) collective-permute-start(bf16[784,256]{1,0:T(8,128)(2,1)S(1)} %get-tuple-element.60.packed_1), channel_id=1, source_target_pairs={{0,2},{1,3},{2,6},{3,7},{4,0},{5,1},{6,4},{7,5},{8,10},{9,11},{10,... | collective-permute-start | bytes 1204232 | tf_op jit(solution)/shard_map/ppermute | solution.py:394
  11.2 3.8 %load.1.screened = bf16[2,2,384,3072]{3,2,1,0:T(8,128)(2,1)S(1)} custom-call(bf16[2,2,384,3072]{3,2,1,0:T(8,128)(2,1)} %source), custom_call_target="tpu_custom_call" | custom-call | tf_op jit(solution)/shard_map/load/pallas_call | solution.py:30
  16.8 1.6 %collective-permute-start.6 = (bf16[2,2,192,256]{3,2,1,0:T(8,128)(2,1)S(1)}, bf16[2,2,192,256]{3,2,1,0:T(8,128)(2,1)S(1)}, u32[]{:S(2)}, u32[]{:S(2)}) collective-permute-start(bf16[2,2,192,256]{3,2,1,0:T(8,128)(2,1)S(1)} %get-tuple-element.63), channel_id=1, source_target_pairs={{0,16},{8,24},{16,0},{24,8},{1,17},{9,25},{17,1},{25,9},{2,18},{10... | collective-permute-start | bytes 1179656 | tf_op jit(solution)/shard_map/ppermute | solution.py:388
  20.7 6.3 %collective-permute-done.3.packed.packed_1 = bf16[784,256]{1,0:T(8,128)(2,1)S(1)} collective-permute-done((bf16[784,256]{1,0:T(8,128)(2,1)S(1)}, bf16[784,256]{1,0:T(8,128)(2,1)S(1)}, u32[]{:S(2)}, u32[]{:S(2)}) %collective-permute-start.3) | collective-permute-done | bytes 401440 | tf_op jit(solution)/shard_map/ppermute | solution.py:394
  27.9 2.6 %collective-permute-done.7.picked_1 = bf16[2,2,192,256]{3,2,1,0:T(8,128)(2,1)S(1)} collective-permute-done((bf16[2,2,192,256]{3,2,1,0:T(8,128)(2,1)S(1)}, bf16[2,2,192,256]{3,2,1,0:T(8,128)(2,1)S(1)}, u32[]{:S(2)}, u32[]{:S(2)}) %collective-permute-start.7) | collective-permute-done | bytes 393248 | tf_op jit(solution)/shard_map/ppermute | solution.py:388
  30.8 2.6 %collective-permute-start.11 = (bf16[2,2,384,256]{3,2,1,0:T(8,128)(2,1)S(1)}, bf16[2,2,384,256]{3,2,1,0:T(8,128)(2,1)S(1)}, u32[]{:S(2)}, u32[]{:S(2)}) collective-permute-start(bf16[2,2,384,256]{3,2,1,0:T(8,128)(2,1)S(1)} %near.2.own.refs_0_), channel_id=1, source_target_pairs={{0,4},{1,5},{2,0},{3,1},{4,6},{5,7},{6,2},{7,3},{8,12},{9,13},{10,... | collective-permute-start | bytes 2359304 | tf_op jit(solution)/shard_map/ppermute | solution.py:394
  33.5 1.8 %product.3.before = f32[2,384,1024]{2,1,0:T(8,128)S(1)} custom-call(bf16[2,2,384,3072]{3,2,1,0:T(8,128)(2,1)S(1)} %load.1.screened, bf16[2,2,384,256]{3,2,1,0:T(8,128)(2,1)S(1)} %near.2.own.refs_0_, f32[1,384]{1,0:T(1,128)S(1)} %broadcast_in_dim.3.coulomb), custom_call_target="tpu_custom_call" | custom-call | tf_op jit(solution)/shard_map/product/pallas_call | solution.py:30
  38.3 7.5 %collective-permute-done.9.picked_1 = bf16[2,2,192,256]{3,2,1,0:T(8,128)(2,1)S(1)} collective-permute-done((bf16[2,2,192,256]{3,2,1,0:T(8,128)(2,1)S(1)}, bf16[2,2,192,256]{3,2,1,0:T(8,128)(2,1)S(1)}, u32[]{:S(2)}, u32[]{:S(2)}) %collective-permute-start.9) | collective-permute-done | bytes 393248 | tf_op jit(solution)/shard_map/ppermute | solution.py:388
  47.0 2.0 %collective-permute-start.10 = (bf16[2,384,256]{2,1,0:T(8,128)(2,1)S(1)}, bf16[2,384,256]{2,1,0:T(8,128)(2,1)S(1)}, u32[]{:S(2)}, u32[]{:S(2)}) collective-permute-start(bf16[2,384,256]{2,1,0:T(8,128)(2,1)S(1)} %get-tuple-element.71), channel_id=1, source_target_pairs={{0,2},{1,3},{2,6},{3,7},{4,0},{5,1},{6,4},{7,5},{8,10},{9,11},{10,... | collective-permute-start | bytes 1179656 | tf_op jit(solution)/shard_map/ppermute | solution.py:394
  49.0 1.5 %collective-permute-start.16 = (bf16[3,2,192,256]{3,2,1,0:T(8,128)(2,1)S(1)}, bf16[3,2,192,256]{3,2,1,0:T(8,128)(2,1)S(1)}, u32[]{:S(2)}, u32[]{:S(2)}) collective-permute-start(bf16[3,2,192,256]{3,2,1,0:T(8,128)(2,1)S(1)} %get-tuple-element.78), channel_id=1, source_target_pairs={{0,16},{8,24},{16,0},{24,8},{1,17},{9,25},{17,1},{25,9},{2,18},{10... | collective-permute-start | bytes 1769480 | tf_op jit(solution)/shard_map/ppermute | solution.py:388
  50.5 2.2 %collective-permute-start.24 = (bf16[2,384,256]{2,1,0:T(8,128)(2,1)S(1)}, bf16[2,384,256]{2,1,0:T(8,128)(2,1)S(1)}, u32[]{:S(2)}, u32[]{:S(2)}) collective-permute-start(bf16[2,384,256]{2,1,0:T(8,128)(2,1)S(1)} %get-tuple-element.92), channel_id=1, source_target_pairs={{0,2},{1,3},{2,6},{3,7},{4,0},{5,1},{6,4},{7,5},{8,10},{9,11},{10,... | collective-permute-start | bytes 1179656 | tf_op jit(solution)/shard_map/ppermute | solution.py:394
  53.3 3.0 %product.4.before = f32[2,384,1024]{2,1,0:T(8,128)S(1)} custom-call(bf16[2,2,384,3072]{3,2,1,0:T(8,128)(2,1)S(1)} %load.1.screened, bf16[2,2,384,256]{3,2,1,0:T(8,128)(2,1)S(1)} %collective-permute-done.11.own, bf16[2,2,384,256]{3,2,1,0:T(8,128)(2,1)S(1)} %collective-permute-done.13.pair, ...), custom_call_target="tpu_custom_call", output_to_operand_aliasing={{}: (3, {})} | custom-call | tf_op jit(solution)/shard_map/product/pallas_call | solution.py:30
  56.3 4.9 %product.5.before = f32[2,384,1024]{2,1,0:T(8,128)S(1)} custom-call(bf16[2,2,384,3072]{3,2,1,0:T(8,128)(2,1)S(1)} %load.1.screened, bf16[2,2,384,256]{3,2,1,0:T(8,128)(2,1)S(1)} %get-tuple-element.75.refs_1_.own, bf16[2,2,2,384,256]{4,3,2,1,0:T(8,128)(2,1)S(1)} %collective-permute-done.12.pairs, ...), custom_call_target="tpu_custom_call", output_to_operand_aliasing={{}: (3, {})} | custom-call | tf_op jit(solution)/shard_map/product/pallas_call | solution.py:30
  63.1 1.5 %image.2 = bf16[2,384,512]{2,1,0:T(8,128)(2,1)S(1)} custom-call(bf16[2,2,384,3072]{3,2,1,0:T(8,128)(2,1)S(1)} %load.1.screened, bf16[2,384,256]{2,1,0:T(8,128)(2,1)S(1)} %collective-permute-done.10.own, bf16[384,256]{1,0:T(8,128)(2,1)S(1)} %collective-permute-done.14.pair_real, bf16[384,256]{1,0:T(8,128)(2,1)S(1)} %collective-permute-done.15.pair_imag, ...), custom_call_target="tpu_custom_call" | custom-call | tf_op jit(solution)/shard_map/image/pallas_call | solution.py:30
  68.3 1.6 %collective-permute-start.22 = (bf16[2,2,2,2,32,256]{5,4,3,2,1,0:T(8,128)(2,1)S(1)}, bf16[2,2,2,2,32,256]{5,4,3,2,1,0:T(8,128)(2,1)S(1)}, u32[]{:S(2)}, u32[]{:S(2)}) collective-permute-start(bf16[2,2,2,2,32,256]{5,4,3,2,1,0:T(8,128)(2,1)S(1)} %get-tuple-element.89), channel_id=1, source_target_pairs={{0,2},{1,3},{2,0},{3,1},{4,6},{5,7},{6,4},{7,5},{8,10},{9,11},{10,... | collective-permute-start | bytes 786440 | tf_op jit(solution)/shard_map/ppermute | solution.py:534
  70.7 1.5 %image.3 = bf16[2,384,512]{2,1,0:T(8,128)(2,1)S(1)} custom-call(bf16[2,2,384,3072]{3,2,1,0:T(8,128)(2,1)S(1)} %load.1.screened, bf16[2,384,256]{2,1,0:T(8,128)(2,1)S(1)} %collective-permute-done.24.own, bf16[384,256]{1,0:T(8,128)(2,1)S(1)} %collective-permute-done.25.pair_real, bf16[384,256]{1,0:T(8,128)(2,1)S(1)} %collective-permute-done.26.pair_imag, ...), custom_call_target="tpu_custom_call" | custom-call | tf_op jit(solution)/shard_map/image/pallas_call | solution.py:30
  75.3 1.5 %collective-permute-done.22.came = bf16[2,2,2,2,32,256]{5,4,3,2,1,0:T(8,128)(2,1)S(1)} collective-permute-done((bf16[2,2,2,2,32,256]{5,4,3,2,1,0:T(8,128)(2,1)S(1)}, bf16[2,2,2,2,32,256]{5,4,3,2,1,0:T(8,128)(2,1)S(1)}, u32[]{:S(2)}, u32[]{:S(2)}) %collective-permute-start.22) | collective-permute-done | bytes 262176 | tf_op jit(solution)/shard_map/ppermute | solution.py:534
  76.9 1.6 %collective-permute-start.31 = (bf16[2,2,2,2,32,256]{5,4,3,2,1,0:T(8,128)(2,1)S(1)}, bf16[2,2,2,2,32,256]{5,4,3,2,1,0:T(8,128)(2,1)S(1)}, u32[]{:S(2)}, u32[]{:S(2)}) collective-permute-start(bf16[2,2,2,2,32,256]{5,4,3,2,1,0:T(8,128)(2,1)S(1)} %get-tuple-element.105), channel_id=1, source_target_pairs={{0,2},{1,3},{2,0},{3,1},{4,6},{5,7},{6,4},{7,5},{8,10},{9,11},{10,... | collective-permute-start | bytes 786440 | tf_op jit(solution)/shard_map/ppermute | solution.py:534
  78.5 2.3 %collective-permute-start.23 = (bf16[2,2,2,32,256]{4,3,2,1,0:T(8,128)(2,1)S(1)}, bf16[2,2,2,32,256]{4,3,2,1,0:T(8,128)(2,1)S(1)}, u32[]{:S(2)}, u32[]{:S(2)}) collective-permute-start(bf16[2,2,2,32,256]{4,3,2,1,0:T(8,128)(2,1)S(1)} %get-tuple-element.91), channel_id=1, source_target_pairs={{0,4},{1,5},{2,6},{3,7},{4,0},{5,1},{6,2},{7,3},{8,12},{9,13},{10,... | collective-permute-start | bytes 393224 | tf_op jit(solution)/shard_map/ppermute | solution.py:541
  80.7 6.6 %collective-permute-done.31.came = bf16[2,2,2,2,32,256]{5,4,3,2,1,0:T(8,128)(2,1)S(1)} collective-permute-done((bf16[2,2,2,2,32,256]{5,4,3,2,1,0:T(8,128)(2,1)S(1)}, bf16[2,2,2,2,32,256]{5,4,3,2,1,0:T(8,128)(2,1)S(1)}, u32[]{:S(2)}, u32[]{:S(2)}) %collective-permute-start.31) | collective-permute-done | bytes 262176 | tf_op jit(solution)/shard_map/ppermute | solution.py:534
  88.5 6.5 %collective-permute-done.32.refs_3_ = bf16[2,2,2,32,256]{4,3,2,1,0:T(8,128)(2,1)S(1)} collective-permute-done((bf16[2,2,2,32,256]{4,3,2,1,0:T(8,128)(2,1)S(1)}, bf16[2,2,2,32,256]{4,3,2,1,0:T(8,128)(2,1)S(1)}, u32[]{:S(2)}, u32[]{:S(2)}) %collective-permute-start.32) | collective-permute-done | bytes 131104 | tf_op jit(solution)/shard_map/ppermute | solution.py:541
  (72 shorter events, 23.4 us)
Async XLA Ops:
  2.5 12.5 %collective-permute-start = (bf16[784,256]{1,0:T(8,128)(2,1)S(1)}, bf16[784,256]{1,0:T(8,128)(2,1)S(1)}, u32[]{:S(2)}, u32[]{:S(2)}) collective-permute-start(bf16[784,256]{1,0:T(8,128)(2,1)S(1)} %get-tuple-element.59.packed_0), channel_id=1, source_target_pairs={{0,8},{8,0},{16,24},{24,16},{1,9},{9,1},{17,25},{25,17},{2,10},{10... | collective-permute-start | bytes 1204232 | tf_op jit(solution)/shard_map/ppermute | solution.py:388
  5.5 10.8 %collective-permute-start.1 = (bf16[784,256]{1,0:T(8,128)(2,1)S(1)}, bf16[784,256]{1,0:T(8,128)(2,1)S(1)}, u32[]{:S(2)}, u32[]{:S(2)}) collective-permute-start(bf16[784,256]{1,0:T(8,128)(2,1)S(1)} %get-tuple-element.60.packed_1), channel_id=1, source_target_pairs={{0,16},{8,24},{16,0},{24,8},{1,17},{9,25},{17,1},{25,9},{2,18},{10... | collective-permute-start | bytes 1204232 | tf_op jit(solution)/shard_map/ppermute | solution.py:388
  7.0 13.1 %collective-permute-start.2 = (bf16[784,256]{1,0:T(8,128)(2,1)S(1)}, bf16[784,256]{1,0:T(8,128)(2,1)S(1)}, u32[]{:S(2)}, u32[]{:S(2)}) collective-permute-start(bf16[784,256]{1,0:T(8,128)(2,1)S(1)} %get-tuple-element.59.packed_0), channel_id=1, source_target_pairs={{0,2},{1,3},{2,6},{3,7},{4,0},{5,1},{6,4},{7,5},{8,10},{9,11},{10,... | collective-permute-start | bytes 1204232 | tf_op jit(solution)/shard_map/ppermute | solution.py:394
  8.6 18.4 %collective-permute-start.3 = (bf16[784,256]{1,0:T(8,128)(2,1)S(1)}, bf16[784,256]{1,0:T(8,128)(2,1)S(1)}, u32[]{:S(2)}, u32[]{:S(2)}) collective-permute-start(bf16[784,256]{1,0:T(8,128)(2,1)S(1)} %get-tuple-element.60.packed_1), channel_id=1, source_target_pairs={{0,2},{1,3},{2,6},{3,7},{4,0},{5,1},{6,4},{7,5},{8,10},{9,11},{10,... | collective-permute-start | bytes 1204232 | tf_op jit(solution)/shard_map/ppermute | solution.py:394
  16.8 11.0 %collective-permute-start.6 = (bf16[2,2,192,256]{3,2,1,0:T(8,128)(2,1)S(1)}, bf16[2,2,192,256]{3,2,1,0:T(8,128)(2,1)S(1)}, u32[]{:S(2)}, u32[]{:S(2)}) collective-permute-start(bf16[2,2,192,256]{3,2,1,0:T(8,128)(2,1)S(1)} %get-tuple-element.63), channel_id=1, source_target_pairs={{0,16},{8,24},{16,0},{24,8},{1,17},{9,25},{17,1},{25,9},{2,18},{10... | collective-permute-start | bytes 1179656 | tf_op jit(solution)/shard_map/ppermute | solution.py:388
  18.4 12.1 %collective-permute-start.7 = (bf16[2,2,192,256]{3,2,1,0:T(8,128)(2,1)S(1)}, bf16[2,2,192,256]{3,2,1,0:T(8,128)(2,1)S(1)}, u32[]{:S(2)}, u32[]{:S(2)}) collective-permute-start(bf16[2,2,192,256]{3,2,1,0:T(8,128)(2,1)S(1)} %get-tuple-element.64), channel_id=1, source_target_pairs={{0,8},{8,0},{16,24},{24,16},{1,9},{9,1},{17,25},{25,17},{2,10},{10... | collective-permute-start | bytes 1179656 | tf_op jit(solution)/shard_map/ppermute | solution.py:388
  20.1 16.3 %collective-permute-start.4 = (bf16[784,256]{1,0:T(8,128)(2,1)S(1)}, bf16[784,256]{1,0:T(8,128)(2,1)S(1)}, u32[]{:S(2)}, u32[]{:S(2)}) collective-permute-start(bf16[784,256]{1,0:T(8,128)(2,1)S(1)} %collective-permute-done.2.packed.packed_0), channel_id=1, source_target_pairs={{0,8},{8,0},{16,24},{24,16},{1,9},{9,1},{17,25},{25,17},{2,10},{10... | collective-permute-start | bytes 1204232 | tf_op jit(solution)/shard_map/ppermute | solution.py:388
  27.0 10.3 %collective-permute-start.5 = (bf16[784,256]{1,0:T(8,128)(2,1)S(1)}, bf16[784,256]{1,0:T(8,128)(2,1)S(1)}, u32[]{:S(2)}, u32[]{:S(2)}) collective-permute-start(bf16[784,256]{1,0:T(8,128)(2,1)S(1)} %collective-permute-done.3.packed.packed_1), channel_id=1, source_target_pairs={{0,16},{8,24},{16,0},{24,8},{1,17},{9,25},{17,1},{25,9},{2,18},{10... | collective-permute-start | bytes 1204232 | tf_op jit(solution)/shard_map/ppermute | solution.py:388
  30.8 15.4 %collective-permute-start.11 = (bf16[2,2,384,256]{3,2,1,0:T(8,128)(2,1)S(1)}, bf16[2,2,384,256]{3,2,1,0:T(8,128)(2,1)S(1)}, u32[]{:S(2)}, u32[]{:S(2)}) collective-permute-start(bf16[2,2,384,256]{3,2,1,0:T(8,128)(2,1)S(1)} %near.2.own.refs_0_), channel_id=1, source_target_pairs={{0,4},{1,5},{2,0},{3,1},{4,6},{5,7},{6,2},{7,3},{8,12},{9,13},{10,... | collective-permute-start | bytes 2359304 | tf_op jit(solution)/shard_map/ppermute | solution.py:394
  36.7 9.1 %collective-permute-start.8 = (bf16[784,256]{1,0:T(8,128)(2,1)S(1)}, bf16[784,256]{1,0:T(8,128)(2,1)S(1)}, u32[]{:S(2)}, u32[]{:S(2)}) collective-permute-start(bf16[784,256]{1,0:T(8,128)(2,1)S(1)} %pick_half.2), channel_id=1, source_target_pairs={{0,16},{8,24},{16,0},{24,8},{1,17},{9,25},{17,1},{25,9},{2,18},{10... | collective-permute-start | bytes 1204232 | tf_op jit(solution)/shard_map/ppermute | solution.py:388
  37.6 8.2 %collective-permute-start.9 = (bf16[2,2,192,256]{3,2,1,0:T(8,128)(2,1)S(1)}, bf16[2,2,192,256]{3,2,1,0:T(8,128)(2,1)S(1)}, u32[]{:S(2)}, u32[]{:S(2)}) collective-permute-start(bf16[2,2,192,256]{3,2,1,0:T(8,128)(2,1)S(1)} %pick_half.3), channel_id=1, source_target_pairs={{0,8},{8,0},{16,24},{24,16},{1,9},{9,1},{17,25},{25,17},{2,10},{10... | collective-permute-start | bytes 1179656 | tf_op jit(solution)/shard_map/ppermute | solution.py:388
  46.4 10.0 %collective-permute-start.12 = (bf16[2,2,2,384,256]{4,3,2,1,0:T(8,128)(2,1)S(1)}, bf16[2,2,2,384,256]{4,3,2,1,0:T(8,128)(2,1)S(1)}, u32[]{:S(2)}, u32[]{:S(2)}) collective-permute-start(bf16[2,2,2,384,256]{4,3,2,1,0:T(8,128)(2,1)S(1)} %stack.1), channel_id=1, source_target_pairs={{0,1},{1,0},{2,3},{3,2},{4,5},{5,4},{6,7},{7,6},{8,9},{9,8},{10,11... | collective-permute-start | bytes 4718600 | tf_op jit(solution)/shard_map/ppermute | solution.py:391
  46.5 6.2 %collective-permute-start.13 = (bf16[2,2,384,256]{3,2,1,0:T(8,128)(2,1)S(1)}, bf16[2,2,384,256]{3,2,1,0:T(8,128)(2,1)S(1)}, u32[]{:S(2)}, u32[]{:S(2)}) collective-permute-start(bf16[2,2,384,256]{3,2,1,0:T(8,128)(2,1)S(1)} %collective-permute-done.11.own), channel_id=1, source_target_pairs={{0,1},{1,0},{2,3},{3,2},{4,5},{5,4},{6,7},{7,6},{8,9},{9,8},{10,11... | collective-permute-start | bytes 2359304 | tf_op jit(solution)/shard_map/ppermute | solution.py:391
  47.0 14.3 %collective-permute-start.10 = (bf16[2,384,256]{2,1,0:T(8,128)(2,1)S(1)}, bf16[2,384,256]{2,1,0:T(8,128)(2,1)S(1)}, u32[]{:S(2)}, u32[]{:S(2)}) collective-permute-start(bf16[2,384,256]{2,1,0:T(8,128)(2,1)S(1)} %get-tuple-element.71), channel_id=1, source_target_pairs={{0,2},{1,3},{2,6},{3,7},{4,0},{5,1},{6,4},{7,5},{8,10},{9,11},{10,... | collective-permute-start | bytes 1179656 | tf_op jit(solution)/shard_map/ppermute | solution.py:394
  49.0 15.6 %collective-permute-start.16 = (bf16[3,2,192,256]{3,2,1,0:T(8,128)(2,1)S(1)}, bf16[3,2,192,256]{3,2,1,0:T(8,128)(2,1)S(1)}, u32[]{:S(2)}, u32[]{:S(2)}) collective-permute-start(bf16[3,2,192,256]{3,2,1,0:T(8,128)(2,1)S(1)} %get-tuple-element.78), channel_id=1, source_target_pairs={{0,16},{8,24},{16,0},{24,8},{1,17},{9,25},{17,1},{25,9},{2,18},{10... | collective-permute-start | bytes 1769480 | tf_op jit(solution)/shard_map/ppermute | solution.py:388
  50.5 16.9 %collective-permute-start.24 = (bf16[2,384,256]{2,1,0:T(8,128)(2,1)S(1)}, bf16[2,384,256]{2,1,0:T(8,128)(2,1)S(1)}, u32[]{:S(2)}, u32[]{:S(2)}) collective-permute-start(bf16[2,384,256]{2,1,0:T(8,128)(2,1)S(1)} %get-tuple-element.92), channel_id=1, source_target_pairs={{0,2},{1,3},{2,6},{3,7},{4,0},{5,1},{6,4},{7,5},{8,10},{9,11},{10,... | collective-permute-start | bytes 1179656 | tf_op jit(solution)/shard_map/ppermute | solution.py:394
  52.7 11.9 %collective-permute-start.17 = (bf16[2,2,192,256]{3,2,1,0:T(8,128)(2,1)S(1)}, bf16[2,2,192,256]{3,2,1,0:T(8,128)(2,1)S(1)}, u32[]{:S(2)}, u32[]{:S(2)}) collective-permute-start(bf16[2,2,192,256]{3,2,1,0:T(8,128)(2,1)S(1)} %get-tuple-element.79), channel_id=1, source_target_pairs={{0,8},{8,0},{16,24},{24,16},{1,9},{9,1},{17,25},{25,17},{2,10},{10... | collective-permute-start | bytes 1179656 | tf_op jit(solution)/shard_map/ppermute | solution.py:388
  61.4 1.7 %collective-permute-start.15 = (bf16[384,256]{1,0:T(8,128)(2,1)S(1)}, bf16[384,256]{1,0:T(8,128)(2,1)S(1)}, u32[]{:S(2)}, u32[]{:S(2)}) collective-permute-start(bf16[384,256]{1,0:T(8,128)(2,1)S(1)} %get-tuple-element.110), channel_id=1, source_target_pairs={{0,1},{1,0},{2,3},{3,2},{4,5},{5,4},{6,7},{7,6},{8,9},{9,8},{10,11... | collective-permute-start | bytes 589832 | tf_op jit(solution)/shard_map/ppermute | solution.py:391
  67.4 3.3 %collective-permute-start.25 = (bf16[384,256]{1,0:T(8,128)(2,1)S(1)}, bf16[384,256]{1,0:T(8,128)(2,1)S(1)}, u32[]{:S(2)}, u32[]{:S(2)}) collective-permute-start(bf16[384,256]{1,0:T(8,128)(2,1)S(1)} %get-tuple-element.109), channel_id=1, source_target_pairs={{0,1},{1,0},{2,3},{3,2},{4,5},{5,4},{6,7},{7,6},{8,9},{9,8},{10,11... | collective-permute-start | bytes 589832 | tf_op jit(solution)/shard_map/ppermute | solution.py:391
  67.5 3.2 %collective-permute-start.26 = (bf16[384,256]{1,0:T(8,128)(2,1)S(1)}, bf16[384,256]{1,0:T(8,128)(2,1)S(1)}, u32[]{:S(2)}, u32[]{:S(2)}) collective-permute-start(bf16[384,256]{1,0:T(8,128)(2,1)S(1)} %get-tuple-element.108), channel_id=1, source_target_pairs={{0,1},{1,0},{2,3},{3,2},{4,5},{5,4},{6,7},{7,6},{8,9},{9,8},{10,11... | collective-permute-start | bytes 589832 | tf_op jit(solution)/shard_map/ppermute | solution.py:391
  68.3 8.5 %collective-permute-start.22 = (bf16[2,2,2,2,32,256]{5,4,3,2,1,0:T(8,128)(2,1)S(1)}, bf16[2,2,2,2,32,256]{5,4,3,2,1,0:T(8,128)(2,1)S(1)}, u32[]{:S(2)}, u32[]{:S(2)}) collective-permute-start(bf16[2,2,2,2,32,256]{5,4,3,2,1,0:T(8,128)(2,1)S(1)} %get-tuple-element.89), channel_id=1, source_target_pairs={{0,2},{1,3},{2,0},{3,1},{4,6},{5,7},{6,4},{7,5},{8,10},{9,11},{10,... | collective-permute-start | bytes 786440 | tf_op jit(solution)/shard_map/ppermute | solution.py:534
  76.9 10.5 %collective-permute-start.31 = (bf16[2,2,2,2,32,256]{5,4,3,2,1,0:T(8,128)(2,1)S(1)}, bf16[2,2,2,2,32,256]{5,4,3,2,1,0:T(8,128)(2,1)S(1)}, u32[]{:S(2)}, u32[]{:S(2)}) collective-permute-start(bf16[2,2,2,2,32,256]{5,4,3,2,1,0:T(8,128)(2,1)S(1)} %get-tuple-element.105), channel_id=1, source_target_pairs={{0,2},{1,3},{2,0},{3,1},{4,6},{5,7},{6,4},{7,5},{8,10},{9,11},{10,... | collective-permute-start | bytes 786440 | tf_op jit(solution)/shard_map/ppermute | solution.py:534
  78.5 10.1 %collective-permute-start.23 = (bf16[2,2,2,32,256]{4,3,2,1,0:T(8,128)(2,1)S(1)}, bf16[2,2,2,32,256]{4,3,2,1,0:T(8,128)(2,1)S(1)}, u32[]{:S(2)}, u32[]{:S(2)}) collective-permute-start(bf16[2,2,2,32,256]{4,3,2,1,0:T(8,128)(2,1)S(1)} %get-tuple-element.91), channel_id=1, source_target_pairs={{0,4},{1,5},{2,6},{3,7},{4,0},{5,1},{6,2},{7,3},{8,12},{9,13},{10,... | collective-permute-start | bytes 393224 | tf_op jit(solution)/shard_map/ppermute | solution.py:541
  87.4 7.7 %collective-permute-start.32 = (bf16[2,2,2,32,256]{4,3,2,1,0:T(8,128)(2,1)S(1)}, bf16[2,2,2,32,256]{4,3,2,1,0:T(8,128)(2,1)S(1)}, u32[]{:S(2)}, u32[]{:S(2)}) collective-permute-start(bf16[2,2,2,32,256]{4,3,2,1,0:T(8,128)(2,1)S(1)} %get-tuple-element.107), channel_id=1, source_target_pairs={{0,4},{1,5},{2,6},{3,7},{4,0},{5,1},{6,2},{7,3},{8,12},{9,13},{10,... | collective-permute-start | bytes 393224 | tf_op jit(solution)/shard_map/ppermute | solution.py:541
  (11 other events, 32.2 us)

commit v13 on v11

--- a/solution.py
+++ b/solution.py
@@ -377,18 +377,30 @@
                     share = came[0][first : first + 2 * rows].reshape(2, rows, t)
                 shares.append(share.astype(F32))
             total[s, which] = own[s, which] + shares[0]
-            sends[s, which] = (cross[s, which] + shares[1]).astype(BF16)
-
-
-def finish_kernel(count, chips, scale, *refs):
+            share = (cross[s, which] + shares[1]).astype(BF16)
+            if len(sends.shape) > 2:
+                sends[s, which] = share
+            else:
+                first = (2 * s + which) * 2 * rows
+                sends[first : first + 2 * rows] = share.reshape(2 * rows, t)
+    if len(sends.shape) == 2:
+        rest = sends.shape[0] - 4 * transfers * rows
+        sends[4 * transfers * rows :] = jnp.zeros((rest, t), BF16)
+
+
+def finish_kernel(count, scale, *refs):
     kernel, mirror = refs[-2:]
     for j in range(count):
-        terms = refs[j * chips : (j + 1) * chips]
-        total = terms[0][...]
-        for term in terms[1:]:
-            total = total + term[...].astype(F32)
-        mirror[j] = total[:, 0] * scale
-        kernel[j] = total[:, 1] * scale
+        own, came = refs[2 * j : 2 * j + 2]
+        transfers, _, _, rows, t = own.shape
+        for s in range(transfers):
+            for which, out in enumerate((mirror, kernel)):
+                first = (2 * s + which) * 2 * rows
+                if len(came.shape) > 2:
+                    share = came[s, which]
+                else:
+                    share = came[first : first + 2 * rows].reshape(2, rows, t)
+                out[j, s] = (own[s, which] + share.astype(F32)) * scale
 
 
 def quick(n_kp, n_ga, densities, screened, coulomb, block_rows):
@@ -535,7 +547,7 @@
             name="mirror",
             mib=24,
         )
-        near_z = 1 if j % 2 else 2
+        near_z = 1
         own, cross, *sends = run(
             functools.partial(split_kernel, near_z),
             [shape(part, F32)] * 2 + ([shape(part, BF16)] * 2 if j else [shape((8 * transfers * part[3] + 16, t), BF16)]),
@@ -551,13 +563,21 @@
         if groups:
             came_j, _ = tie((came_j, sends))
         own, sends = run(
-            merge_kernel, [shape(part, F32), shape(part, BF16)], own, cross, *came_j, name="merge"
+            merge_kernel,
+            [
+                shape(part, F32),
+                shape(part, BF16) if groups else shape((4 * transfers * part[3] + 16, t), BF16),
+            ],
+            own,
+            cross,
+            *came_j,
+            name="merge",
         )
         groups += [own, lax.ppermute(sends, "ga", [(i, i ^ (2 * far_z)) for i in range(n_ga)])]
     result = shape((count, transfers, 2, t // n_ga, t), F32)
     return tuple(
         run(
-            functools.partial(finish_kernel, count, 2, -1.0 / math.sqrt(g_total)),
+            functools.partial(finish_kernel, count, -1.0 / math.sqrt(g_total)),
             [result] * 2,
             *groups,
             name="finish",

time: 101 us -> 97.6 us (0.966)
  waiting for transfers between devices: 41.7 us -> 39 us
    ppermute x3, waiting for transfers between devices: 11.4 us -> 6.5 us  [quick(): lax.ppermute(x, 'ga', [(i, i ^ 2 * near_z) for i in range(n_ga)])]
    ppermute x2, waiting for transfers between devices: 5.85 us -> 7.94 us  [quick(): lax.ppermute(sends, 'ga', [(i, i ^ 2 * far_z) for i in range(n_ga)])]
    ppermute x3, starting transfers between devices: 4.34 us -> 3.23 us  [quick(): lax.ppermute(x, 'ga', [(i, i ^ 2 * near_z) for i in range(n_ga)])]
  transfers between devices with their start and end apart: 34 -> 34, of which waited for: 21 -> 20; matrix products, arithmetic and copies ran while one was open for 0% -> 0% of each run, Pallas kernels for 22% -> 22%
where the time goes in v13:
time: 97.6 us; the launch traced here: 97.5 us
  waiting for transfers between devices  39 us (40%)
  starting transfers between devices  32.7 us (34%)
  Pallas kernels  24.1 us (25%)
    pallas_call x23, Pallas kernels, run(): pl.pallas_call(body, in_specs=specs or [VMEM] * len(args), out_specs=[VME...  24.1 us
    ppermute x10, waiting for transfers between devices, across(): return lax.ppermute(x, 'kp', [(i, i ^ bit) for i in range(n_kp)])  12.5 us
    ppermute x10, starting transfers between devices, across(): return lax.ppermute(x, 'kp', [(i, i ^ bit) for i in range(n_kp)])  11.2 us
    ppermute x5, starting transfers between devices, along(): lax.ppermute(x, 'ga', [(i, 2 * chips_on[i // 2] + i % 2) for i in range(n...  11 us
    ppermute x5, waiting for transfers between devices, along(): lax.ppermute(x, 'ga', [(i, 2 * chips_on[i // 2] + i % 2) for i in range(n...  8.6 us
    ppermute x2, waiting for transfers between devices, quick(): lax.ppermute(sends, 'ga', [(i, i ^ 2 * far_z) for i in range(n_ga)])  7.94 us
    ppermute x3, waiting for transfers between devices, quick(): lax.ppermute(x, 'ga', [(i, i ^ 2 * near_z) for i in range(n_ga)])  6.5 us
    ppermute x2, starting transfers between devices, quick(): lax.ppermute(sends, 'ga', [(i, i ^ 2 * far_z) for i in range(n_ga)])  3.7 us
  transfers between devices with their start and end apart: 34, of which 20 were waited for; matrix products, arithmetic and copies ran while one was open for 0% of the time, Pallas kernels for 22%

profile of v13, /device:TPU:0, one launch (start us, length us, event | category | flops | bytes accessed | tf_op | source)
XLA Modules:
  0.0 97.5 jit_solution(5975062605706003340)
XLA Ops:
  2.5 3.0 %collective-permute-start = (bf16[784,256]{1,0:T(8,128)(2,1)S(1)}, bf16[784,256]{1,0:T(8,128)(2,1)S(1)}, u32[]{:S(2)}, u32[]{:S(2)}) collective-permute-start(bf16[784,256]{1,0:T(8,128)(2,1)S(1)} %get-tuple-element.60.packed_0), channel_id=1, source_target_pairs={{0,8},{8,0},{16,24},{24,16},{1,9},{9,1},{17,25},{25,17},{2,10},{10... | collective-permute-start | bytes 1204232 | tf_op jit(solution)/shard_map/ppermute | solution.py:416
  5.5 1.5 %collective-permute-start.1 = (bf16[784,256]{1,0:T(8,128)(2,1)S(1)}, bf16[784,256]{1,0:T(8,128)(2,1)S(1)}, u32[]{:S(2)}, u32[]{:S(2)}) collective-permute-start(bf16[784,256]{1,0:T(8,128)(2,1)S(1)} %get-tuple-element.61.packed_1), channel_id=1, source_target_pairs={{0,16},{8,24},{16,0},{24,8},{1,17},{9,25},{17,1},{25,9},{2,18},{10... | collective-permute-start | bytes 1204232 | tf_op jit(solution)/shard_map/ppermute | solution.py:416
  7.0 1.6 %collective-permute-start.2 = (bf16[784,256]{1,0:T(8,128)(2,1)S(1)}, bf16[784,256]{1,0:T(8,128)(2,1)S(1)}, u32[]{:S(2)}, u32[]{:S(2)}) collective-permute-start(bf16[784,256]{1,0:T(8,128)(2,1)S(1)} %get-tuple-element.60.packed_0), channel_id=1, source_target_pairs={{0,2},{1,3},{2,6},{3,7},{4,0},{5,1},{6,4},{7,5},{8,10},{9,11},{10,... | collective-permute-start | bytes 1204232 | tf_op jit(solution)/shard_map/ppermute | solution.py:422
  8.6 2.6 %collective-permute-start.3 = (bf16[784,256]{1,0:T(8,128)(2,1)S(1)}, bf16[784,256]{1,0:T(8,128)(2,1)S(1)}, u32[]{:S(2)}, u32[]{:S(2)}) collective-permute-start(bf16[784,256]{1,0:T(8,128)(2,1)S(1)} %get-tuple-element.61.packed_1), channel_id=1, source_target_pairs={{0,2},{1,3},{2,6},{3,7},{4,0},{5,1},{6,4},{7,5},{8,10},{9,11},{10,... | collective-permute-start | bytes 1204232 | tf_op jit(solution)/shard_map/ppermute | solution.py:422
  11.2 3.8 %load.1.screened = bf16[2,2,384,3072]{3,2,1,0:T(8,128)(2,1)S(1)} custom-call(bf16[2,2,384,3072]{3,2,1,0:T(8,128)(2,1)} %source), custom_call_target="tpu_custom_call" | custom-call | tf_op jit(solution)/shard_map/load/pallas_call | solution.py:30
  15.0 1.2 %collective-permute-done.1.came_1.labels = bf16[784,256]{1,0:T(8,128)(2,1)S(1)} collective-permute-done((bf16[784,256]{1,0:T(8,128)(2,1)S(1)}, bf16[784,256]{1,0:T(8,128)(2,1)S(1)}, u32[]{:S(2)}, u32[]{:S(2)}) %collective-permute-start.1) | collective-permute-done | bytes 401440 | tf_op jit(solution)/shard_map/ppermute | solution.py:416
  16.8 1.6 %collective-permute-start.6 = (bf16[2,2,192,256]{3,2,1,0:T(8,128)(2,1)S(1)}, bf16[2,2,192,256]{3,2,1,0:T(8,128)(2,1)S(1)}, u32[]{:S(2)}, u32[]{:S(2)}) collective-permute-start(bf16[2,2,192,256]{3,2,1,0:T(8,128)(2,1)S(1)} %get-tuple-element.64), channel_id=1, source_target_pairs={{0,16},{8,24},{16,0},{24,8},{1,17},{9,25},{17,1},{25,9},{2,18},{10... | collective-permute-start | bytes 1179656 | tf_op jit(solution)/shard_map/ppermute | solution.py:416
  18.9 1.2 %collective-permute-done.2.packed.packed_0 = bf16[784,256]{1,0:T(8,128)(2,1)S(1)} collective-permute-done((bf16[784,256]{1,0:T(8,128)(2,1)S(1)}, bf16[784,256]{1,0:T(8,128)(2,1)S(1)}, u32[]{:S(2)}, u32[]{:S(2)}) %collective-permute-start.2) | collective-permute-done | bytes 401440 | tf_op jit(solution)/shard_map/ppermute | solution.py:422
  20.7 6.3 %collective-permute-done.3.packed.packed_1 = bf16[784,256]{1,0:T(8,128)(2,1)S(1)} collective-permute-done((bf16[784,256]{1,0:T(8,128)(2,1)S(1)}, bf16[784,256]{1,0:T(8,128)(2,1)S(1)}, u32[]{:S(2)}, u32[]{:S(2)}) %collective-permute-start.3) | collective-permute-done | bytes 401440 | tf_op jit(solution)/shard_map/ppermute | solution.py:422
  27.9 2.6 %collective-permute-done.7.picked_1 = bf16[2,2,192,256]{3,2,1,0:T(8,128)(2,1)S(1)} collective-permute-done((bf16[2,2,192,256]{3,2,1,0:T(8,128)(2,1)S(1)}, bf16[2,2,192,256]{3,2,1,0:T(8,128)(2,1)S(1)}, u32[]{:S(2)}, u32[]{:S(2)}) %collective-permute-start.7) | collective-permute-done | bytes 393248 | tf_op jit(solution)/shard_map/ppermute | solution.py:416
  30.8 2.6 %collective-permute-start.11 = (bf16[2,2,384,256]{3,2,1,0:T(8,128)(2,1)S(1)}, bf16[2,2,384,256]{3,2,1,0:T(8,128)(2,1)S(1)}, u32[]{:S(2)}, u32[]{:S(2)}) collective-permute-start(bf16[2,2,384,256]{3,2,1,0:T(8,128)(2,1)S(1)} %near.2.own.refs_0_), channel_id=1, source_target_pairs={{0,4},{1,5},{2,0},{3,1},{4,6},{5,7},{6,2},{7,3},{8,12},{9,13},{10,... | collective-permute-start | bytes 2359304 | tf_op jit(solution)/shard_map/ppermute | solution.py:422
  33.5 1.8 %product.3.before = f32[2,384,1024]{2,1,0:T(8,128)S(1)} custom-call(bf16[2,2,384,3072]{3,2,1,0:T(8,128)(2,1)S(1)} %load.1.screened, bf16[2,2,384,256]{3,2,1,0:T(8,128)(2,1)S(1)} %near.2.own.refs_0_, f32[1,384]{1,0:T(1,128)S(1)} %broadcast_in_dim.3.coulomb), custom_call_target="tpu_custom_call" | custom-call | tf_op jit(solution)/shard_map/product/pallas_call | solution.py:30
  38.3 7.5 %collective-permute-done.9.picked_1 = bf16[2,2,192,256]{3,2,1,0:T(8,128)(2,1)S(1)} collective-permute-done((bf16[2,2,192,256]{3,2,1,0:T(8,128)(2,1)S(1)}, bf16[2,2,192,256]{3,2,1,0:T(8,128)(2,1)S(1)}, u32[]{:S(2)}, u32[]{:S(2)}) %collective-permute-start.9) | collective-permute-done | bytes 393248 | tf_op jit(solution)/shard_map/ppermute | solution.py:416
  47.0 2.0 %collective-permute-start.10 = (bf16[2,384,256]{2,1,0:T(8,128)(2,1)S(1)}, bf16[2,384,256]{2,1,0:T(8,128)(2,1)S(1)}, u32[]{:S(2)}, u32[]{:S(2)}) collective-permute-start(bf16[2,384,256]{2,1,0:T(8,128)(2,1)S(1)} %get-tuple-element.72), channel_id=1, source_target_pairs={{0,2},{1,3},{2,6},{3,7},{4,0},{5,1},{6,4},{7,5},{8,10},{9,11},{10,... | collective-permute-start | bytes 1179656 | tf_op jit(solution)/shard_map/ppermute | solution.py:422
  48.9 1.5 %collective-permute-start.16 = (bf16[3,2,192,256]{3,2,1,0:T(8,128)(2,1)S(1)}, bf16[3,2,192,256]{3,2,1,0:T(8,128)(2,1)S(1)}, u32[]{:S(2)}, u32[]{:S(2)}) collective-permute-start(bf16[3,2,192,256]{3,2,1,0:T(8,128)(2,1)S(1)} %get-tuple-element.79), channel_id=1, source_target_pairs={{0,16},{8,24},{16,0},{24,8},{1,17},{9,25},{17,1},{25,9},{2,18},{10... | collective-permute-start | bytes 1769480 | tf_op jit(solution)/shard_map/ppermute | solution.py:416
  50.5 2.2 %collective-permute-start.24 = (bf16[2,384,256]{2,1,0:T(8,128)(2,1)S(1)}, bf16[2,384,256]{2,1,0:T(8,128)(2,1)S(1)}, u32[]{:S(2)}, u32[]{:S(2)}) collective-permute-start(bf16[2,384,256]{2,1,0:T(8,128)(2,1)S(1)} %get-tuple-element.93), channel_id=1, source_target_pairs={{0,2},{1,3},{2,6},{3,7},{4,0},{5,1},{6,4},{7,5},{8,10},{9,11},{10,... | collective-permute-start | bytes 1179656 | tf_op jit(solution)/shard_map/ppermute | solution.py:422
  53.3 3.0 %product.4.before = f32[2,384,1024]{2,1,0:T(8,128)S(1)} custom-call(bf16[2,2,384,3072]{3,2,1,0:T(8,128)(2,1)S(1)} %load.1.screened, bf16[2,2,384,256]{3,2,1,0:T(8,128)(2,1)S(1)} %collective-permute-done.11.own, bf16[2,2,384,256]{3,2,1,0:T(8,128)(2,1)S(1)} %collective-permute-done.13.pair, ...), custom_call_target="tpu_custom_call", output_to_operand_aliasing={{}: (3, {})} | custom-call | tf_op jit(solution)/shard_map/product/pallas_call | solution.py:30
  56.4 4.6 %product.5.before = f32[2,384,1024]{2,1,0:T(8,128)S(1)} custom-call(bf16[2,2,384,3072]{3,2,1,0:T(8,128)(2,1)S(1)} %load.1.screened, bf16[2,2,384,256]{3,2,1,0:T(8,128)(2,1)S(1)} %get-tuple-element.76.refs_1_.own, bf16[2,2,2,384,256]{4,3,2,1,0:T(8,128)(2,1)S(1)} %collective-permute-done.12.pairs, ...), custom_call_target="tpu_custom_call", output_to_operand_aliasing={{}: (3, {})} | custom-call | tf_op jit(solution)/shard_map/product/pallas_call | solution.py:30
  62.8 1.5 %image.2 = bf16[2,384,512]{2,1,0:T(8,128)(2,1)S(1)} custom-call(bf16[2,2,384,3072]{3,2,1,0:T(8,128)(2,1)S(1)} %load.1.screened, bf16[2,384,256]{2,1,0:T(8,128)(2,1)S(1)} %collective-permute-done.10.own, bf16[384,256]{1,0:T(8,128)(2,1)S(1)} %collective-permute-done.14.pair_real, bf16[384,256]{1,0:T(8,128)(2,1)S(1)} %collective-permute-done.15.pair_imag, ...), custom_call_target="tpu_custom_call" | custom-call | tf_op jit(solution)/shard_map/image/pallas_call | solution.py:30
  71.7 1.5 %image.3 = bf16[2,384,512]{2,1,0:T(8,128)(2,1)S(1)} custom-call(bf16[2,2,384,3072]{3,2,1,0:T(8,128)(2,1)S(1)} %load.1.screened, bf16[2,384,256]{2,1,0:T(8,128)(2,1)S(1)} %collective-permute-done.24.own, bf16[384,256]{1,0:T(8,128)(2,1)S(1)} %collective-permute-done.25.pair_real, bf16[384,256]{1,0:T(8,128)(2,1)S(1)} %collective-permute-done.26.pair_imag, ...), custom_call_target="tpu_custom_call" | custom-call | tf_op jit(solution)/shard_map/image/pallas_call | solution.py:30
  78.6 2.9 %collective-permute-start.23 = (bf16[272,256]{1,0:T(8,128)(2,1)S(1)}, bf16[272,256]{1,0:T(8,128)(2,1)S(1)}, u32[]{:S(2)}, u32[]{:S(2)}) collective-permute-start(bf16[272,256]{1,0:T(8,128)(2,1)S(1)} %get-tuple-element.92), channel_id=1, source_target_pairs={{0,4},{1,5},{2,6},{3,7},{4,0},{5,1},{6,2},{7,3},{8,12},{9,13},{10,... | collective-permute-start | bytes 417800 | tf_op jit(solution)/shard_map/ppermute | solution.py:576
  81.6 4.1 %collective-permute-done.31.refs_0_ = bf16[2,2,2,32,256]{4,3,2,1,0:T(8,128)(2,1)S(1)} collective-permute-done((bf16[2,2,2,32,256]{4,3,2,1,0:T(8,128)(2,1)S(1)}, bf16[2,2,2,32,256]{4,3,2,1,0:T(8,128)(2,1)S(1)}, u32[]{:S(2)}, u32[]{:S(2)}) %collective-permute-start.31) | collective-permute-done | bytes 131104 | tf_op jit(solution)/shard_map/ppermute | solution.py:559
  85.7 2.2 %collective-permute-done.32.refs_1_ = bf16[2,2,2,32,256]{4,3,2,1,0:T(8,128)(2,1)S(1)} collective-permute-done((bf16[2,2,2,32,256]{4,3,2,1,0:T(8,128)(2,1)S(1)}, bf16[2,2,2,32,256]{4,3,2,1,0:T(8,128)(2,1)S(1)}, u32[]{:S(2)}, u32[]{:S(2)}) %collective-permute-start.32) | collective-permute-done | bytes 131104 | tf_op jit(solution)/shard_map/ppermute | solution.py:559
  88.7 7.9 %collective-permute-done.33.refs_3_ = bf16[2,2,2,32,256]{4,3,2,1,0:T(8,128)(2,1)S(1)} collective-permute-done((bf16[2,2,2,32,256]{4,3,2,1,0:T(8,128)(2,1)S(1)}, bf16[2,2,2,32,256]{4,3,2,1,0:T(8,128)(2,1)S(1)}, u32[]{:S(2)}, u32[]{:S(2)}) %collective-permute-start.33) | collective-permute-done | bytes 131104 | tf_op jit(solution)/shard_map/ppermute | solution.py:576
  (74 shorter events, 25.7 us)
Async XLA Ops:
  2.5 12.5 %collective-permute-start = (bf16[784,256]{1,0:T(8,128)(2,1)S(1)}, bf16[784,256]{1,0:T(8,128)(2,1)S(1)}, u32[]{:S(2)}, u32[]{:S(2)}) collective-permute-start(bf16[784,256]{1,0:T(8,128)(2,1)S(1)} %get-tuple-element.60.packed_0), channel_id=1, source_target_pairs={{0,8},{8,0},{16,24},{24,16},{1,9},{9,1},{17,25},{25,17},{2,10},{10... | collective-permute-start | bytes 1204232 | tf_op jit(solution)/shard_map/ppermute | solution.py:416
  5.5 10.8 %collective-permute-start.1 = (bf16[784,256]{1,0:T(8,128)(2,1)S(1)}, bf16[784,256]{1,0:T(8,128)(2,1)S(1)}, u32[]{:S(2)}, u32[]{:S(2)}) collective-permute-start(bf16[784,256]{1,0:T(8,128)(2,1)S(1)} %get-tuple-element.61.packed_1), channel_id=1, source_target_pairs={{0,16},{8,24},{16,0},{24,8},{1,17},{9,25},{17,1},{25,9},{2,18},{10... | collective-permute-start | bytes 1204232 | tf_op jit(solution)/shard_map/ppermute | solution.py:416
  7.0 13.1 %collective-permute-start.2 = (bf16[784,256]{1,0:T(8,128)(2,1)S(1)}, bf16[784,256]{1,0:T(8,128)(2,1)S(1)}, u32[]{:S(2)}, u32[]{:S(2)}) collective-permute-start(bf16[784,256]{1,0:T(8,128)(2,1)S(1)} %get-tuple-element.60.packed_0), channel_id=1, source_target_pairs={{0,2},{1,3},{2,6},{3,7},{4,0},{5,1},{6,4},{7,5},{8,10},{9,11},{10,... | collective-permute-start | bytes 1204232 | tf_op jit(solution)/shard_map/ppermute | solution.py:422
  8.6 18.4 %collective-permute-start.3 = (bf16[784,256]{1,0:T(8,128)(2,1)S(1)}, bf16[784,256]{1,0:T(8,128)(2,1)S(1)}, u32[]{:S(2)}, u32[]{:S(2)}) collective-permute-start(bf16[784,256]{1,0:T(8,128)(2,1)S(1)} %get-tuple-element.61.packed_1), channel_id=1, source_target_pairs={{0,2},{1,3},{2,6},{3,7},{4,0},{5,1},{6,4},{7,5},{8,10},{9,11},{10,... | collective-permute-start | bytes 1204232 | tf_op jit(solution)/shard_map/ppermute | solution.py:422
  16.8 11.0 %collective-permute-start.6 = (bf16[2,2,192,256]{3,2,1,0:T(8,128)(2,1)S(1)}, bf16[2,2,192,256]{3,2,1,0:T(8,128)(2,1)S(1)}, u32[]{:S(2)}, u32[]{:S(2)}) collective-permute-start(bf16[2,2,192,256]{3,2,1,0:T(8,128)(2,1)S(1)} %get-tuple-element.64), channel_id=1, source_target_pairs={{0,16},{8,24},{16,0},{24,8},{1,17},{9,25},{17,1},{25,9},{2,18},{10... | collective-permute-start | bytes 1179656 | tf_op jit(solution)/shard_map/ppermute | solution.py:416
  18.4 12.1 %collective-permute-start.7 = (bf16[2,2,192,256]{3,2,1,0:T(8,128)(2,1)S(1)}, bf16[2,2,192,256]{3,2,1,0:T(8,128)(2,1)S(1)}, u32[]{:S(2)}, u32[]{:S(2)}) collective-permute-start(bf16[2,2,192,256]{3,2,1,0:T(8,128)(2,1)S(1)} %get-tuple-element.65), channel_id=1, source_target_pairs={{0,8},{8,0},{16,24},{24,16},{1,9},{9,1},{17,25},{25,17},{2,10},{10... | collective-permute-start | bytes 1179656 | tf_op jit(solution)/shard_map/ppermute | solution.py:416
  20.1 16.3 %collective-permute-start.4 = (bf16[784,256]{1,0:T(8,128)(2,1)S(1)}, bf16[784,256]{1,0:T(8,128)(2,1)S(1)}, u32[]{:S(2)}, u32[]{:S(2)}) collective-permute-start(bf16[784,256]{1,0:T(8,128)(2,1)S(1)} %collective-permute-done.2.packed.packed_0), channel_id=1, source_target_pairs={{0,8},{8,0},{16,24},{24,16},{1,9},{9,1},{17,25},{25,17},{2,10},{10... | collective-permute-start | bytes 1204232 | tf_op jit(solution)/shard_map/ppermute | solution.py:416
  27.0 10.3 %collective-permute-start.5 = (bf16[784,256]{1,0:T(8,128)(2,1)S(1)}, bf16[784,256]{1,0:T(8,128)(2,1)S(1)}, u32[]{:S(2)}, u32[]{:S(2)}) collective-permute-start(bf16[784,256]{1,0:T(8,128)(2,1)S(1)} %collective-permute-done.3.packed.packed_1), channel_id=1, source_target_pairs={{0,16},{8,24},{16,0},{24,8},{1,17},{9,25},{17,1},{25,9},{2,18},{10... | collective-permute-start | bytes 1204232 | tf_op jit(solution)/shard_map/ppermute | solution.py:416
  30.8 15.4 %collective-permute-start.11 = (bf16[2,2,384,256]{3,2,1,0:T(8,128)(2,1)S(1)}, bf16[2,2,384,256]{3,2,1,0:T(8,128)(2,1)S(1)}, u32[]{:S(2)}, u32[]{:S(2)}) collective-permute-start(bf16[2,2,384,256]{3,2,1,0:T(8,128)(2,1)S(1)} %near.2.own.refs_0_), channel_id=1, source_target_pairs={{0,4},{1,5},{2,0},{3,1},{4,6},{5,7},{6,2},{7,3},{8,12},{9,13},{10,... | collective-permute-start | bytes 2359304 | tf_op jit(solution)/shard_map/ppermute | solution.py:422
  36.7 9.1 %collective-permute-start.8 = (bf16[784,256]{1,0:T(8,128)(2,1)S(1)}, bf16[784,256]{1,0:T(8,128)(2,1)S(1)}, u32[]{:S(2)}, u32[]{:S(2)}) collective-permute-start(bf16[784,256]{1,0:T(8,128)(2,1)S(1)} %pick_half.2), channel_id=1, source_target_pairs={{0,16},{8,24},{16,0},{24,8},{1,17},{9,25},{17,1},{25,9},{2,18},{10... | collective-permute-start | bytes 1204232 | tf_op jit(solution)/shard_map/ppermute | solution.py:416
  37.6 8.2 %collective-permute-start.9 = (bf16[2,2,192,256]{3,2,1,0:T(8,128)(2,1)S(1)}, bf16[2,2,192,256]{3,2,1,0:T(8,128)(2,1)S(1)}, u32[]{:S(2)}, u32[]{:S(2)}) collective-permute-start(bf16[2,2,192,256]{3,2,1,0:T(8,128)(2,1)S(1)} %pick_half.3), channel_id=1, source_target_pairs={{0,8},{8,0},{16,24},{24,16},{1,9},{9,1},{17,25},{25,17},{2,10},{10... | collective-permute-start | bytes 1179656 | tf_op jit(solution)/shard_map/ppermute | solution.py:416
  46.4 10.0 %collective-permute-start.12 = (bf16[2,2,2,384,256]{4,3,2,1,0:T(8,128)(2,1)S(1)}, bf16[2,2,2,384,256]{4,3,2,1,0:T(8,128)(2,1)S(1)}, u32[]{:S(2)}, u32[]{:S(2)}) collective-permute-start(bf16[2,2,2,384,256]{4,3,2,1,0:T(8,128)(2,1)S(1)} %stack.1), channel_id=1, source_target_pairs={{0,1},{1,0},{2,3},{3,2},{4,5},{5,4},{6,7},{7,6},{8,9},{9,8},{10,11... | collective-permute-start | bytes 4718600 | tf_op jit(solution)/shard_map/ppermute | solution.py:419
  46.5 6.2 %collective-permute-start.13 = (bf16[2,2,384,256]{3,2,1,0:T(8,128)(2,1)S(1)}, bf16[2,2,384,256]{3,2,1,0:T(8,128)(2,1)S(1)}, u32[]{:S(2)}, u32[]{:S(2)}) collective-permute-start(bf16[2,2,384,256]{3,2,1,0:T(8,128)(2,1)S(1)} %collective-permute-done.11.own), channel_id=1, source_target_pairs={{0,1},{1,0},{2,3},{3,2},{4,5},{5,4},{6,7},{7,6},{8,9},{9,8},{10,11... | collective-permute-start | bytes 2359304 | tf_op jit(solution)/shard_map/ppermute | solution.py:419
  47.0 14.0 %collective-permute-start.10 = (bf16[2,384,256]{2,1,0:T(8,128)(2,1)S(1)}, bf16[2,384,256]{2,1,0:T(8,128)(2,1)S(1)}, u32[]{:S(2)}, u32[]{:S(2)}) collective-permute-start(bf16[2,384,256]{2,1,0:T(8,128)(2,1)S(1)} %get-tuple-element.72), channel_id=1, source_target_pairs={{0,2},{1,3},{2,6},{3,7},{4,0},{5,1},{6,4},{7,5},{8,10},{9,11},{10,... | collective-permute-start | bytes 1179656 | tf_op jit(solution)/shard_map/ppermute | solution.py:422
  48.9 15.4 %collective-permute-start.16 = (bf16[3,2,192,256]{3,2,1,0:T(8,128)(2,1)S(1)}, bf16[3,2,192,256]{3,2,1,0:T(8,128)(2,1)S(1)}, u32[]{:S(2)}, u32[]{:S(2)}) collective-permute-start(bf16[3,2,192,256]{3,2,1,0:T(8,128)(2,1)S(1)} %get-tuple-element.79), channel_id=1, source_target_pairs={{0,16},{8,24},{16,0},{24,8},{1,17},{9,25},{17,1},{25,9},{2,18},{10... | collective-permute-start | bytes 1769480 | tf_op jit(solution)/shard_map/ppermute | solution.py:416
  50.5 16.9 %collective-permute-start.24 = (bf16[2,384,256]{2,1,0:T(8,128)(2,1)S(1)}, bf16[2,384,256]{2,1,0:T(8,128)(2,1)S(1)}, u32[]{:S(2)}, u32[]{:S(2)}) collective-permute-start(bf16[2,384,256]{2,1,0:T(8,128)(2,1)S(1)} %get-tuple-element.93), channel_id=1, source_target_pairs={{0,2},{1,3},{2,6},{3,7},{4,0},{5,1},{6,4},{7,5},{8,10},{9,11},{10,... | collective-permute-start | bytes 1179656 | tf_op jit(solution)/shard_map/ppermute | solution.py:422
  52.7 11.7 %collective-permute-start.17 = (bf16[2,2,192,256]{3,2,1,0:T(8,128)(2,1)S(1)}, bf16[2,2,192,256]{3,2,1,0:T(8,128)(2,1)S(1)}, u32[]{:S(2)}, u32[]{:S(2)}) collective-permute-start(bf16[2,2,192,256]{3,2,1,0:T(8,128)(2,1)S(1)} %get-tuple-element.80), channel_id=1, source_target_pairs={{0,8},{8,0},{16,24},{24,16},{1,9},{9,1},{17,25},{25,17},{2,10},{10... | collective-permute-start | bytes 1179656 | tf_op jit(solution)/shard_map/ppermute | solution.py:416
  67.4 4.3 %collective-permute-start.25 = (bf16[384,256]{1,0:T(8,128)(2,1)S(1)}, bf16[384,256]{1,0:T(8,128)(2,1)S(1)}, u32[]{:S(2)}, u32[]{:S(2)}) collective-permute-start(bf16[384,256]{1,0:T(8,128)(2,1)S(1)} %get-tuple-element.111), channel_id=1, source_target_pairs={{0,1},{1,0},{2,3},{3,2},{4,5},{5,4},{6,7},{7,6},{8,9},{9,8},{10,11... | collective-permute-start | bytes 589832 | tf_op jit(solution)/shard_map/ppermute | solution.py:419
  67.5 4.2 %collective-permute-start.26 = (bf16[384,256]{1,0:T(8,128)(2,1)S(1)}, bf16[384,256]{1,0:T(8,128)(2,1)S(1)}, u32[]{:S(2)}, u32[]{:S(2)}) collective-permute-start(bf16[384,256]{1,0:T(8,128)(2,1)S(1)} %get-tuple-element.110), channel_id=1, source_target_pairs={{0,1},{1,0},{2,3},{3,2},{4,5},{5,4},{6,7},{7,6},{8,9},{9,8},{10,11... | collective-permute-start | bytes 589832 | tf_op jit(solution)/shard_map/ppermute | solution.py:419
  70.0 8.6 %collective-permute-start.22 = (bf16[528,256]{1,0:T(8,128)(2,1)S(1)}, bf16[528,256]{1,0:T(8,128)(2,1)S(1)}, u32[]{:S(2)}, u32[]{:S(2)}) collective-permute-start(bf16[528,256]{1,0:T(8,128)(2,1)S(1)} %get-tuple-element.90), channel_id=1, source_target_pairs={{0,2},{1,3},{2,0},{3,1},{4,6},{5,7},{6,4},{7,5},{8,10},{9,11},{10,... | collective-permute-start | bytes 811016 | tf_op jit(solution)/shard_map/ppermute | solution.py:559
  76.3 9.4 %collective-permute-start.31 = (bf16[2,2,2,32,256]{4,3,2,1,0:T(8,128)(2,1)S(1)}, bf16[2,2,2,32,256]{4,3,2,1,0:T(8,128)(2,1)S(1)}, u32[]{:S(2)}, u32[]{:S(2)}) collective-permute-start(bf16[2,2,2,32,256]{4,3,2,1,0:T(8,128)(2,1)S(1)} %get-tuple-element.104), channel_id=1, source_target_pairs={{0,2},{1,3},{2,0},{3,1},{4,6},{5,7},{6,4},{7,5},{8,10},{9,11},{10,... | collective-permute-start | bytes 393224 | tf_op jit(solution)/shard_map/ppermute | solution.py:559
  77.3 10.6 %collective-permute-start.32 = (bf16[2,2,2,32,256]{4,3,2,1,0:T(8,128)(2,1)S(1)}, bf16[2,2,2,32,256]{4,3,2,1,0:T(8,128)(2,1)S(1)}, u32[]{:S(2)}, u32[]{:S(2)}) collective-permute-start(bf16[2,2,2,32,256]{4,3,2,1,0:T(8,128)(2,1)S(1)} %get-tuple-element.105), channel_id=1, source_target_pairs={{0,2},{1,3},{2,0},{3,1},{4,6},{5,7},{6,4},{7,5},{8,10},{9,11},{10,... | collective-permute-start | bytes 393224 | tf_op jit(solution)/shard_map/ppermute | solution.py:559
  78.6 18.0 %collective-permute-start.23 = (bf16[272,256]{1,0:T(8,128)(2,1)S(1)}, bf16[272,256]{1,0:T(8,128)(2,1)S(1)}, u32[]{:S(2)}, u32[]{:S(2)}) collective-permute-start(bf16[272,256]{1,0:T(8,128)(2,1)S(1)} %get-tuple-element.92), channel_id=1, source_target_pairs={{0,4},{1,5},{2,6},{3,7},{4,0},{5,1},{6,2},{7,3},{8,12},{9,13},{10,... | collective-permute-start | bytes 417800 | tf_op jit(solution)/shard_map/ppermute | solution.py:576
  87.9 8.7 %collective-permute-start.33 = (bf16[2,2,2,32,256]{4,3,2,1,0:T(8,128)(2,1)S(1)}, bf16[2,2,2,32,256]{4,3,2,1,0:T(8,128)(2,1)S(1)}, u32[]{:S(2)}, u32[]{:S(2)}) collective-permute-start(bf16[2,2,2,32,256]{4,3,2,1,0:T(8,128)(2,1)S(1)} %get-tuple-element.109), channel_id=1, source_target_pairs={{0,4},{1,5},{2,6},{3,7},{4,0},{5,1},{6,2},{7,3},{8,12},{9,13},{10,... | collective-permute-start | bytes 393224 | tf_op jit(solution)/shard_map/ppermute | solution.py:576
  (12 other events, 34.9 us)

commit v14 on v9

--- a/solution.py
+++ b/solution.py
@@ -336,7 +336,10 @@
                 block = block.reshape(chips, 2, t // (2 * chips), t)
                 keep[:, s, which, part] = jnp.where(first, block[:, 0], block[:, 1])
                 give = jnp.where(first, block[:, 1], block[:, 0])
-                gives[2 * s + which][:, part] = give.astype(BF16)
+                if len(gives) == 2:
+                    gives[which][:, s, part] = give.astype(BF16)
+                else:
+                    gives[2 * s + which][:, part] = give.astype(BF16)
 
 
 def split_kernel(keep, *refs):
@@ -346,6 +349,8 @@
         for which in range(2):
 
             def chip(at):
+                if len(came) == 2:
+                    return keep[at, s, which] + came[which][at, s].astype(F32)
                 return keep[at, s, which] + came[2 * s + which][at].astype(F32)
 
             own[s, which] = chip(z)
@@ -508,7 +513,12 @@
         )
         keep, *gives = run(
             functools.partial(mirror_kernel, chips),
-            [parts] + [shape((chips, 2, t // n_ga, t), BF16)] * (2 * transfers),
+            [parts]
+            + (
+                [shape((chips, 2, t // n_ga, t), BF16)] * (2 * transfers)
+                if j
+                else [shape((chips, transfers, 2, t // n_ga, t), BF16)] * 2
+            ),
             image,
             far,
             name="mirror",

time: 96.4 us -> 95.6 us (level)
  waiting for transfers between devices: 37.9 us -> 36.8 us
    ppermute x14 -> x12, starting transfers between devices: 3.87 us -> 3.36 us  [other_core(): return lax.ppermute(x, 'ga', [(i, i ^ 1) for i in range(n_ga)])]
    ppermute x14 -> x12, waiting for transfers between devices: 2.38 us -> 2.25 us  [other_core(): return lax.ppermute(x, 'ga', [(i, i ^ 1) for i in range(n_ga)])]
  transfers between devices with their start and end apart: 33 -> 31, of which waited for: 17 -> 16; matrix products, arithmetic and copies ran while one was open for 0% -> 0% of each run, Pallas kernels for 23% -> 23%
where the time goes in v14:
time: 95.6 us; the launch traced here: 95.4 us
  waiting for transfers between devices  36.8 us (38%)
  starting transfers between devices  32.9 us (34%)
  Pallas kernels  24.1 us (25%)
    pallas_call x23, Pallas kernels, run(): pl.pallas_call(body, in_specs=specs or [VMEM] * len(args), out_specs=[VME...  24.1 us
    ppermute x10, waiting for transfers between devices, across(): return lax.ppermute(x, 'kp', [(i, i ^ bit) for i in range(n_kp)])  12.5 us
    ppermute x10, starting transfers between devices, across(): return lax.ppermute(x, 'kp', [(i, i ^ bit) for i in range(n_kp)])  11.1 us
    ppermute x5, starting transfers between devices, along(): lax.ppermute(x, 'ga', [(i, 2 * chips_on[i // 2] + i % 2) for i in range(n...  11 us
    ppermute x5, waiting for transfers between devices, along(): lax.ppermute(x, 'ga', [(i, 2 * chips_on[i // 2] + i % 2) for i in range(n...  8.38 us
    ppermute x2, waiting for transfers between devices, quick(): came_j = lax.ppermute(sends, 'ga', [(i, i ^ 2) for i in range(n_ga)])  7.61 us
    ppermute x2, waiting for transfers between devices, quick(): lax.ppermute(sends, 'ga', [(i, i ^ 4) for i in range(n_ga)])  6.09 us
    ppermute x2, starting transfers between devices, quick(): lax.ppermute(sends, 'ga', [(i, i ^ 4) for i in range(n_ga)])  3.91 us
  transfers between devices with their start and end apart: 31, of which 16 were waited for; matrix products, arithmetic and copies ran while one was open for 0% of the time, Pallas kernels for 23%

profile of v14, /device:TPU:0, one launch (start us, length us, event | category | flops | bytes accessed | tf_op | source)
XLA Modules:
  0.0 95.4 jit_solution(392824992379815696)
XLA Ops:
  2.5 3.0 %collective-permute-start = (bf16[784,256]{1,0:T(8,128)(2,1)S(1)}, bf16[784,256]{1,0:T(8,128)(2,1)S(1)}, u32[]{:S(2)}, u32[]{:S(2)}) collective-permute-start(bf16[784,256]{1,0:T(8,128)(2,1)S(1)} %get-tuple-element.57.packed_0), channel_id=1, source_target_pairs={{0,8},{8,0},{16,24},{24,16},{1,9},{9,1},{17,25},{25,17},{2,10},{10... | collective-permute-start | bytes 1204232 | tf_op jit(solution)/shard_map/ppermute | solution.py:388
  5.5 1.5 %collective-permute-start.1 = (bf16[784,256]{1,0:T(8,128)(2,1)S(1)}, bf16[784,256]{1,0:T(8,128)(2,1)S(1)}, u32[]{:S(2)}, u32[]{:S(2)}) collective-permute-start(bf16[784,256]{1,0:T(8,128)(2,1)S(1)} %get-tuple-element.58.packed_1), channel_id=1, source_target_pairs={{0,16},{8,24},{16,0},{24,8},{1,17},{9,25},{17,1},{25,9},{2,18},{10... | collective-permute-start | bytes 1204232 | tf_op jit(solution)/shard_map/ppermute | solution.py:388
  7.0 1.6 %collective-permute-start.2 = (bf16[784,256]{1,0:T(8,128)(2,1)S(1)}, bf16[784,256]{1,0:T(8,128)(2,1)S(1)}, u32[]{:S(2)}, u32[]{:S(2)}) collective-permute-start(bf16[784,256]{1,0:T(8,128)(2,1)S(1)} %get-tuple-element.57.packed_0), channel_id=1, source_target_pairs={{0,2},{1,3},{2,6},{3,7},{4,0},{5,1},{6,4},{7,5},{8,10},{9,11},{10,... | collective-permute-start | bytes 1204232 | tf_op jit(solution)/shard_map/ppermute | solution.py:394
  8.6 2.6 %collective-permute-start.3 = (bf16[784,256]{1,0:T(8,128)(2,1)S(1)}, bf16[784,256]{1,0:T(8,128)(2,1)S(1)}, u32[]{:S(2)}, u32[]{:S(2)}) collective-permute-start(bf16[784,256]{1,0:T(8,128)(2,1)S(1)} %get-tuple-element.58.packed_1), channel_id=1, source_target_pairs={{0,2},{1,3},{2,6},{3,7},{4,0},{5,1},{6,4},{7,5},{8,10},{9,11},{10,... | collective-permute-start | bytes 1204232 | tf_op jit(solution)/shard_map/ppermute | solution.py:394
  11.2 3.8 %load.1.screened = bf16[2,2,384,3072]{3,2,1,0:T(8,128)(2,1)S(1)} custom-call(bf16[2,2,384,3072]{3,2,1,0:T(8,128)(2,1)} %source), custom_call_target="tpu_custom_call" | custom-call | tf_op jit(solution)/shard_map/load/pallas_call | solution.py:30
  16.8 1.6 %collective-permute-start.6 = (bf16[2,2,192,256]{3,2,1,0:T(8,128)(2,1)S(1)}, bf16[2,2,192,256]{3,2,1,0:T(8,128)(2,1)S(1)}, u32[]{:S(2)}, u32[]{:S(2)}) collective-permute-start(bf16[2,2,192,256]{3,2,1,0:T(8,128)(2,1)S(1)} %get-tuple-element.61), channel_id=1, source_target_pairs={{0,16},{8,24},{16,0},{24,8},{1,17},{9,25},{17,1},{25,9},{2,18},{10... | collective-permute-start | bytes 1179656 | tf_op jit(solution)/shard_map/ppermute | solution.py:388
  20.7 6.3 %collective-permute-done.3.packed.packed_1 = bf16[784,256]{1,0:T(8,128)(2,1)S(1)} collective-permute-done((bf16[784,256]{1,0:T(8,128)(2,1)S(1)}, bf16[784,256]{1,0:T(8,128)(2,1)S(1)}, u32[]{:S(2)}, u32[]{:S(2)}) %collective-permute-start.3) | collective-permute-done | bytes 401440 | tf_op jit(solution)/shard_map/ppermute | solution.py:394
  27.9 2.6 %collective-permute-done.7.picked_1 = bf16[2,2,192,256]{3,2,1,0:T(8,128)(2,1)S(1)} collective-permute-done((bf16[2,2,192,256]{3,2,1,0:T(8,128)(2,1)S(1)}, bf16[2,2,192,256]{3,2,1,0:T(8,128)(2,1)S(1)}, u32[]{:S(2)}, u32[]{:S(2)}) %collective-permute-start.7) | collective-permute-done | bytes 393248 | tf_op jit(solution)/shard_map/ppermute | solution.py:388
  30.9 2.6 %collective-permute-start.11 = (bf16[2,2,384,256]{3,2,1,0:T(8,128)(2,1)S(1)}, bf16[2,2,384,256]{3,2,1,0:T(8,128)(2,1)S(1)}, u32[]{:S(2)}, u32[]{:S(2)}) collective-permute-start(bf16[2,2,384,256]{3,2,1,0:T(8,128)(2,1)S(1)} %near.2.own.refs_0_), channel_id=1, source_target_pairs={{0,4},{1,5},{2,0},{3,1},{4,6},{5,7},{6,2},{7,3},{8,12},{9,13},{10,... | collective-permute-start | bytes 2359304 | tf_op jit(solution)/shard_map/ppermute | solution.py:394
  33.5 1.8 %product.3.before = f32[2,384,1024]{2,1,0:T(8,128)S(1)} custom-call(bf16[2,2,384,3072]{3,2,1,0:T(8,128)(2,1)S(1)} %load.1.screened, bf16[2,2,384,256]{3,2,1,0:T(8,128)(2,1)S(1)} %near.2.own.refs_0_, f32[1,384]{1,0:T(1,128)S(1)} %broadcast_in_dim.3.coulomb), custom_call_target="tpu_custom_call" | custom-call | tf_op jit(solution)/shard_map/product/pallas_call | solution.py:30
  38.3 7.5 %collective-permute-done.9.picked_1 = bf16[2,2,192,256]{3,2,1,0:T(8,128)(2,1)S(1)} collective-permute-done((bf16[2,2,192,256]{3,2,1,0:T(8,128)(2,1)S(1)}, bf16[2,2,192,256]{3,2,1,0:T(8,128)(2,1)S(1)}, u32[]{:S(2)}, u32[]{:S(2)}) %collective-permute-start.9) | collective-permute-done | bytes 393248 | tf_op jit(solution)/shard_map/ppermute | solution.py:388
  47.0 2.0 %collective-permute-start.10 = (bf16[2,384,256]{2,1,0:T(8,128)(2,1)S(1)}, bf16[2,384,256]{2,1,0:T(8,128)(2,1)S(1)}, u32[]{:S(2)}, u32[]{:S(2)}) collective-permute-start(bf16[2,384,256]{2,1,0:T(8,128)(2,1)S(1)} %get-tuple-element.69), channel_id=1, source_target_pairs={{0,2},{1,3},{2,6},{3,7},{4,0},{5,1},{6,4},{7,5},{8,10},{9,11},{10,... | collective-permute-start | bytes 1179656 | tf_op jit(solution)/shard_map/ppermute | solution.py:394
  49.0 1.5 %collective-permute-start.16 = (bf16[3,2,192,256]{3,2,1,0:T(8,128)(2,1)S(1)}, bf16[3,2,192,256]{3,2,1,0:T(8,128)(2,1)S(1)}, u32[]{:S(2)}, u32[]{:S(2)}) collective-permute-start(bf16[3,2,192,256]{3,2,1,0:T(8,128)(2,1)S(1)} %get-tuple-element.76), channel_id=1, source_target_pairs={{0,16},{8,24},{16,0},{24,8},{1,17},{9,25},{17,1},{25,9},{2,18},{10... | collective-permute-start | bytes 1769480 | tf_op jit(solution)/shard_map/ppermute | solution.py:388
  50.5 2.2 %collective-permute-start.22 = (bf16[2,384,256]{2,1,0:T(8,128)(2,1)S(1)}, bf16[2,384,256]{2,1,0:T(8,128)(2,1)S(1)}, u32[]{:S(2)}, u32[]{:S(2)}) collective-permute-start(bf16[2,384,256]{2,1,0:T(8,128)(2,1)S(1)} %get-tuple-element.88), channel_id=1, source_target_pairs={{0,2},{1,3},{2,6},{3,7},{4,0},{5,1},{6,4},{7,5},{8,10},{9,11},{10,... | collective-permute-start | bytes 1179656 | tf_op jit(solution)/shard_map/ppermute | solution.py:394
  53.3 3.0 %product.4.before = f32[2,384,1024]{2,1,0:T(8,128)S(1)} custom-call(bf16[2,2,384,3072]{3,2,1,0:T(8,128)(2,1)S(1)} %load.1.screened, bf16[2,2,384,256]{3,2,1,0:T(8,128)(2,1)S(1)} %collective-permute-done.11.own, bf16[2,2,384,256]{3,2,1,0:T(8,128)(2,1)S(1)} %collective-permute-done.13.pair, ...), custom_call_target="tpu_custom_call", output_to_operand_aliasing={{}: (3, {})} | custom-call | tf_op jit(solution)/shard_map/product/pallas_call | solution.py:30
  56.3 4.6 %product.5.before = f32[2,384,1024]{2,1,0:T(8,128)S(1)} custom-call(bf16[2,2,384,3072]{3,2,1,0:T(8,128)(2,1)S(1)} %load.1.screened, bf16[2,2,384,256]{3,2,1,0:T(8,128)(2,1)S(1)} %get-tuple-element.73.refs_1_.own, bf16[2,2,2,384,256]{4,3,2,1,0:T(8,128)(2,1)S(1)} %collective-permute-done.12.pairs, ...), custom_call_target="tpu_custom_call", output_to_operand_aliasing={{}: (3, {})} | custom-call | tf_op jit(solution)/shard_map/product/pallas_call | solution.py:30
  62.8 1.5 %image.2 = bf16[2,384,512]{2,1,0:T(8,128)(2,1)S(1)} custom-call(bf16[2,2,384,3072]{3,2,1,0:T(8,128)(2,1)S(1)} %load.1.screened, bf16[2,384,256]{2,1,0:T(8,128)(2,1)S(1)} %collective-permute-done.10.own, bf16[384,256]{1,0:T(8,128)(2,1)S(1)} %collective-permute-done.14.pair_real, bf16[384,256]{1,0:T(8,128)(2,1)S(1)} %collective-permute-done.15.pair_imag, ...), custom_call_target="tpu_custom_call" | custom-call | tf_op jit(solution)/shard_map/image/pallas_call | solution.py:30
  68.1 1.9 %collective-permute-start.20 = (bf16[2,2,2,2,32,256]{5,4,3,2,1,0:T(8,128)(2,1)S(1)}, bf16[2,2,2,2,32,256]{5,4,3,2,1,0:T(8,128)(2,1)S(1)}, u32[]{:S(2)}, u32[]{:S(2)}) collective-permute-start(bf16[2,2,2,2,32,256]{5,4,3,2,1,0:T(8,128)(2,1)S(1)} %get-tuple-element.85), channel_id=1, source_target_pairs={{0,2},{1,3},{2,0},{3,1},{4,6},{5,7},{6,4},{7,5},{8,10},{9,11},{10,... | collective-permute-start | bytes 786440 | tf_op jit(solution)/shard_map/ppermute | solution.py:539
  70.6 1.5 %image.3 = bf16[2,384,512]{2,1,0:T(8,128)(2,1)S(1)} custom-call(bf16[2,2,384,3072]{3,2,1,0:T(8,128)(2,1)S(1)} %load.1.screened, bf16[2,384,256]{2,1,0:T(8,128)(2,1)S(1)} %collective-permute-done.22.own, bf16[384,256]{1,0:T(8,128)(2,1)S(1)} %collective-permute-done.23.pair_real, bf16[384,256]{1,0:T(8,128)(2,1)S(1)} %collective-permute-done.24.pair_imag, ...), custom_call_target="tpu_custom_call" | custom-call | tf_op jit(solution)/shard_map/image/pallas_call | solution.py:30
  76.6 1.7 %collective-permute-start.29 = (bf16[2,2,2,2,32,256]{5,4,3,2,1,0:T(8,128)(2,1)S(1)}, bf16[2,2,2,2,32,256]{5,4,3,2,1,0:T(8,128)(2,1)S(1)}, u32[]{:S(2)}, u32[]{:S(2)}) collective-permute-start(bf16[2,2,2,2,32,256]{5,4,3,2,1,0:T(8,128)(2,1)S(1)} %get-tuple-element.101), channel_id=1, source_target_pairs={{0,2},{1,3},{2,0},{3,1},{4,6},{5,7},{6,4},{7,5},{8,10},{9,11},{10,... | collective-permute-start | bytes 786440 | tf_op jit(solution)/shard_map/ppermute | solution.py:539
  78.4 2.4 %collective-permute-start.21 = (bf16[2,2,2,32,256]{4,3,2,1,0:T(8,128)(2,1)S(1)}, bf16[2,2,2,32,256]{4,3,2,1,0:T(8,128)(2,1)S(1)}, u32[]{:S(2)}, u32[]{:S(2)}) collective-permute-start(bf16[2,2,2,32,256]{4,3,2,1,0:T(8,128)(2,1)S(1)} %get-tuple-element.87), channel_id=1, source_target_pairs={{0,4},{1,5},{2,6},{3,7},{4,0},{5,1},{6,2},{7,3},{8,12},{9,13},{10,... | collective-permute-start | bytes 393224 | tf_op jit(solution)/shard_map/ppermute | solution.py:546
  80.7 6.2 %collective-permute-done.29.came = bf16[2,2,2,2,32,256]{5,4,3,2,1,0:T(8,128)(2,1)S(1)} collective-permute-done((bf16[2,2,2,2,32,256]{5,4,3,2,1,0:T(8,128)(2,1)S(1)}, bf16[2,2,2,2,32,256]{5,4,3,2,1,0:T(8,128)(2,1)S(1)}, u32[]{:S(2)}, u32[]{:S(2)}) %collective-permute-start.29) | collective-permute-done | bytes 262176 | tf_op jit(solution)/shard_map/ppermute | solution.py:539
  87.0 1.5 %collective-permute-start.30 = (bf16[2,2,2,32,256]{4,3,2,1,0:T(8,128)(2,1)S(1)}, bf16[2,2,2,32,256]{4,3,2,1,0:T(8,128)(2,1)S(1)}, u32[]{:S(2)}, u32[]{:S(2)}) collective-permute-start(bf16[2,2,2,32,256]{4,3,2,1,0:T(8,128)(2,1)S(1)} %get-tuple-element.103), channel_id=1, source_target_pairs={{0,4},{1,5},{2,6},{3,7},{4,0},{5,1},{6,2},{7,3},{8,12},{9,13},{10,... | collective-permute-start | bytes 393224 | tf_op jit(solution)/shard_map/ppermute | solution.py:546
  88.5 6.1 %collective-permute-done.30.refs_3_ = bf16[2,2,2,32,256]{4,3,2,1,0:T(8,128)(2,1)S(1)} collective-permute-done((bf16[2,2,2,32,256]{4,3,2,1,0:T(8,128)(2,1)S(1)}, bf16[2,2,2,32,256]{4,3,2,1,0:T(8,128)(2,1)S(1)}, u32[]{:S(2)}, u32[]{:S(2)}) %collective-permute-start.30) | collective-permute-done | bytes 131104 | tf_op jit(solution)/shard_map/ppermute | solution.py:546
  (68 shorter events, 23.5 us)
Async XLA Ops:
  2.5 12.5 %collective-permute-start = (bf16[784,256]{1,0:T(8,128)(2,1)S(1)}, bf16[784,256]{1,0:T(8,128)(2,1)S(1)}, u32[]{:S(2)}, u32[]{:S(2)}) collective-permute-start(bf16[784,256]{1,0:T(8,128)(2,1)S(1)} %get-tuple-element.57.packed_0), channel_id=1, source_target_pairs={{0,8},{8,0},{16,24},{24,16},{1,9},{9,1},{17,25},{25,17},{2,10},{10... | collective-permute-start | bytes 1204232 | tf_op jit(solution)/shard_map/ppermute | solution.py:388
  5.5 10.8 %collective-permute-start.1 = (bf16[784,256]{1,0:T(8,128)(2,1)S(1)}, bf16[784,256]{1,0:T(8,128)(2,1)S(1)}, u32[]{:S(2)}, u32[]{:S(2)}) collective-permute-start(bf16[784,256]{1,0:T(8,128)(2,1)S(1)} %get-tuple-element.58.packed_1), channel_id=1, source_target_pairs={{0,16},{8,24},{16,0},{24,8},{1,17},{9,25},{17,1},{25,9},{2,18},{10... | collective-permute-start | bytes 1204232 | tf_op jit(solution)/shard_map/ppermute | solution.py:388
  7.0 13.1 %collective-permute-start.2 = (bf16[784,256]{1,0:T(8,128)(2,1)S(1)}, bf16[784,256]{1,0:T(8,128)(2,1)S(1)}, u32[]{:S(2)}, u32[]{:S(2)}) collective-permute-start(bf16[784,256]{1,0:T(8,128)(2,1)S(1)} %get-tuple-element.57.packed_0), channel_id=1, source_target_pairs={{0,2},{1,3},{2,6},{3,7},{4,0},{5,1},{6,4},{7,5},{8,10},{9,11},{10,... | collective-permute-start | bytes 1204232 | tf_op jit(solution)/shard_map/ppermute | solution.py:394
  8.6 18.4 %collective-permute-start.3 = (bf16[784,256]{1,0:T(8,128)(2,1)S(1)}, bf16[784,256]{1,0:T(8,128)(2,1)S(1)}, u32[]{:S(2)}, u32[]{:S(2)}) collective-permute-start(bf16[784,256]{1,0:T(8,128)(2,1)S(1)} %get-tuple-element.58.packed_1), channel_id=1, source_target_pairs={{0,2},{1,3},{2,6},{3,7},{4,0},{5,1},{6,4},{7,5},{8,10},{9,11},{10,... | collective-permute-start | bytes 1204232 | tf_op jit(solution)/shard_map/ppermute | solution.py:394
  16.8 11.0 %collective-permute-start.6 = (bf16[2,2,192,256]{3,2,1,0:T(8,128)(2,1)S(1)}, bf16[2,2,192,256]{3,2,1,0:T(8,128)(2,1)S(1)}, u32[]{:S(2)}, u32[]{:S(2)}) collective-permute-start(bf16[2,2,192,256]{3,2,1,0:T(8,128)(2,1)S(1)} %get-tuple-element.61), channel_id=1, source_target_pairs={{0,16},{8,24},{16,0},{24,8},{1,17},{9,25},{17,1},{25,9},{2,18},{10... | collective-permute-start | bytes 1179656 | tf_op jit(solution)/shard_map/ppermute | solution.py:388
  18.4 12.1 %collective-permute-start.7 = (bf16[2,2,192,256]{3,2,1,0:T(8,128)(2,1)S(1)}, bf16[2,2,192,256]{3,2,1,0:T(8,128)(2,1)S(1)}, u32[]{:S(2)}, u32[]{:S(2)}) collective-permute-start(bf16[2,2,192,256]{3,2,1,0:T(8,128)(2,1)S(1)} %get-tuple-element.62), channel_id=1, source_target_pairs={{0,8},{8,0},{16,24},{24,16},{1,9},{9,1},{17,25},{25,17},{2,10},{10... | collective-permute-start | bytes 1179656 | tf_op jit(solution)/shard_map/ppermute | solution.py:388
  20.1 16.3 %collective-permute-start.4 = (bf16[784,256]{1,0:T(8,128)(2,1)S(1)}, bf16[784,256]{1,0:T(8,128)(2,1)S(1)}, u32[]{:S(2)}, u32[]{:S(2)}) collective-permute-start(bf16[784,256]{1,0:T(8,128)(2,1)S(1)} %collective-permute-done.2.packed.packed_0), channel_id=1, source_target_pairs={{0,8},{8,0},{16,24},{24,16},{1,9},{9,1},{17,25},{25,17},{2,10},{10... | collective-permute-start | bytes 1204232 | tf_op jit(solution)/shard_map/ppermute | solution.py:388
  27.0 10.3 %collective-permute-start.5 = (bf16[784,256]{1,0:T(8,128)(2,1)S(1)}, bf16[784,256]{1,0:T(8,128)(2,1)S(1)}, u32[]{:S(2)}, u32[]{:S(2)}) collective-permute-start(bf16[784,256]{1,0:T(8,128)(2,1)S(1)} %collective-permute-done.3.packed.packed_1), channel_id=1, source_target_pairs={{0,16},{8,24},{16,0},{24,8},{1,17},{9,25},{17,1},{25,9},{2,18},{10... | collective-permute-start | bytes 1204232 | tf_op jit(solution)/shard_map/ppermute | solution.py:388
  30.9 15.4 %collective-permute-start.11 = (bf16[2,2,384,256]{3,2,1,0:T(8,128)(2,1)S(1)}, bf16[2,2,384,256]{3,2,1,0:T(8,128)(2,1)S(1)}, u32[]{:S(2)}, u32[]{:S(2)}) collective-permute-start(bf16[2,2,384,256]{3,2,1,0:T(8,128)(2,1)S(1)} %near.2.own.refs_0_), channel_id=1, source_target_pairs={{0,4},{1,5},{2,0},{3,1},{4,6},{5,7},{6,2},{7,3},{8,12},{9,13},{10,... | collective-permute-start | bytes 2359304 | tf_op jit(solution)/shard_map/ppermute | solution.py:394
  36.7 9.1 %collective-permute-start.8 = (bf16[784,256]{1,0:T(8,128)(2,1)S(1)}, bf16[784,256]{1,0:T(8,128)(2,1)S(1)}, u32[]{:S(2)}, u32[]{:S(2)}) collective-permute-start(bf16[784,256]{1,0:T(8,128)(2,1)S(1)} %pick_half.2), channel_id=1, source_target_pairs={{0,16},{8,24},{16,0},{24,8},{1,17},{9,25},{17,1},{25,9},{2,18},{10... | collective-permute-start | bytes 1204232 | tf_op jit(solution)/shard_map/ppermute | solution.py:388
  37.6 8.2 %collective-permute-start.9 = (bf16[2,2,192,256]{3,2,1,0:T(8,128)(2,1)S(1)}, bf16[2,2,192,256]{3,2,1,0:T(8,128)(2,1)S(1)}, u32[]{:S(2)}, u32[]{:S(2)}) collective-permute-start(bf16[2,2,192,256]{3,2,1,0:T(8,128)(2,1)S(1)} %pick_half.3), channel_id=1, source_target_pairs={{0,8},{8,0},{16,24},{24,16},{1,9},{9,1},{17,25},{25,17},{2,10},{10... | collective-permute-start | bytes 1179656 | tf_op jit(solution)/shard_map/ppermute | solution.py:388
  46.4 9.9 %collective-permute-start.12 = (bf16[2,2,2,384,256]{4,3,2,1,0:T(8,128)(2,1)S(1)}, bf16[2,2,2,384,256]{4,3,2,1,0:T(8,128)(2,1)S(1)}, u32[]{:S(2)}, u32[]{:S(2)}) collective-permute-start(bf16[2,2,2,384,256]{4,3,2,1,0:T(8,128)(2,1)S(1)} %stack.1), channel_id=1, source_target_pairs={{0,1},{1,0},{2,3},{3,2},{4,5},{5,4},{6,7},{7,6},{8,9},{9,8},{10,11... | collective-permute-start | bytes 4718600 | tf_op jit(solution)/shard_map/ppermute | solution.py:391
  46.5 6.2 %collective-permute-start.13 = (bf16[2,2,384,256]{3,2,1,0:T(8,128)(2,1)S(1)}, bf16[2,2,384,256]{3,2,1,0:T(8,128)(2,1)S(1)}, u32[]{:S(2)}, u32[]{:S(2)}) collective-permute-start(bf16[2,2,384,256]{3,2,1,0:T(8,128)(2,1)S(1)} %collective-permute-done.11.own), channel_id=1, source_target_pairs={{0,1},{1,0},{2,3},{3,2},{4,5},{5,4},{6,7},{7,6},{8,9},{9,8},{10,11... | collective-permute-start | bytes 2359304 | tf_op jit(solution)/shard_map/ppermute | solution.py:391
  47.0 14.0 %collective-permute-start.10 = (bf16[2,384,256]{2,1,0:T(8,128)(2,1)S(1)}, bf16[2,384,256]{2,1,0:T(8,128)(2,1)S(1)}, u32[]{:S(2)}, u32[]{:S(2)}) collective-permute-start(bf16[2,384,256]{2,1,0:T(8,128)(2,1)S(1)} %get-tuple-element.69), channel_id=1, source_target_pairs={{0,2},{1,3},{2,6},{3,7},{4,0},{5,1},{6,4},{7,5},{8,10},{9,11},{10,... | collective-permute-start | bytes 1179656 | tf_op jit(solution)/shard_map/ppermute | solution.py:394
  49.0 15.4 %collective-permute-start.16 = (bf16[3,2,192,256]{3,2,1,0:T(8,128)(2,1)S(1)}, bf16[3,2,192,256]{3,2,1,0:T(8,128)(2,1)S(1)}, u32[]{:S(2)}, u32[]{:S(2)}) collective-permute-start(bf16[3,2,192,256]{3,2,1,0:T(8,128)(2,1)S(1)} %get-tuple-element.76), channel_id=1, source_target_pairs={{0,16},{8,24},{16,0},{24,8},{1,17},{9,25},{17,1},{25,9},{2,18},{10... | collective-permute-start | bytes 1769480 | tf_op jit(solution)/shard_map/ppermute | solution.py:388
  50.5 16.9 %collective-permute-start.22 = (bf16[2,384,256]{2,1,0:T(8,128)(2,1)S(1)}, bf16[2,384,256]{2,1,0:T(8,128)(2,1)S(1)}, u32[]{:S(2)}, u32[]{:S(2)}) collective-permute-start(bf16[2,384,256]{2,1,0:T(8,128)(2,1)S(1)} %get-tuple-element.88), channel_id=1, source_target_pairs={{0,2},{1,3},{2,6},{3,7},{4,0},{5,1},{6,4},{7,5},{8,10},{9,11},{10,... | collective-permute-start | bytes 1179656 | tf_op jit(solution)/shard_map/ppermute | solution.py:394
  52.7 11.6 %collective-permute-start.17 = (bf16[2,2,192,256]{3,2,1,0:T(8,128)(2,1)S(1)}, bf16[2,2,192,256]{3,2,1,0:T(8,128)(2,1)S(1)}, u32[]{:S(2)}, u32[]{:S(2)}) collective-permute-start(bf16[2,2,192,256]{3,2,1,0:T(8,128)(2,1)S(1)} %get-tuple-element.77), channel_id=1, source_target_pairs={{0,8},{8,0},{16,24},{24,16},{1,9},{9,1},{17,25},{25,17},{2,10},{10... | collective-permute-start | bytes 1179656 | tf_op jit(solution)/shard_map/ppermute | solution.py:388
  66.0 2.0 %collective-permute-start.18 = (bf16[4,2,2,32,256]{4,3,2,1,0:T(8,128)(2,1)S(1)}, bf16[4,2,2,32,256]{4,3,2,1,0:T(8,128)(2,1)S(1)}, u32[]{:S(2)}, u32[]{:S(2)}) collective-permute-start(bf16[4,2,2,32,256]{4,3,2,1,0:T(8,128)(2,1)S(1)} %get-tuple-element.81), channel_id=1, source_target_pairs={{0,1},{1,0},{2,3},{3,2},{4,5},{5,4},{6,7},{7,6},{8,9},{9,8},{10,11... | collective-permute-start | bytes 786440 | tf_op jit(solution)/shard_map/ppermute | solution.py:391
  67.4 3.1 %collective-permute-start.23 = (bf16[384,256]{1,0:T(8,128)(2,1)S(1)}, bf16[384,256]{1,0:T(8,128)(2,1)S(1)}, u32[]{:S(2)}, u32[]{:S(2)}) collective-permute-start(bf16[384,256]{1,0:T(8,128)(2,1)S(1)} %get-tuple-element.105), channel_id=1, source_target_pairs={{0,1},{1,0},{2,3},{3,2},{4,5},{5,4},{6,7},{7,6},{8,9},{9,8},{10,11... | collective-permute-start | bytes 589832 | tf_op jit(solution)/shard_map/ppermute | solution.py:391
  67.5 3.0 %collective-permute-start.24 = (bf16[384,256]{1,0:T(8,128)(2,1)S(1)}, bf16[384,256]{1,0:T(8,128)(2,1)S(1)}, u32[]{:S(2)}, u32[]{:S(2)}) collective-permute-start(bf16[384,256]{1,0:T(8,128)(2,1)S(1)} %get-tuple-element.104), channel_id=1, source_target_pairs={{0,1},{1,0},{2,3},{3,2},{4,5},{5,4},{6,7},{7,6},{8,9},{9,8},{10,11... | collective-permute-start | bytes 589832 | tf_op jit(solution)/shard_map/ppermute | solution.py:391
  68.1 8.5 %collective-permute-start.20 = (bf16[2,2,2,2,32,256]{5,4,3,2,1,0:T(8,128)(2,1)S(1)}, bf16[2,2,2,2,32,256]{5,4,3,2,1,0:T(8,128)(2,1)S(1)}, u32[]{:S(2)}, u32[]{:S(2)}) collective-permute-start(bf16[2,2,2,2,32,256]{5,4,3,2,1,0:T(8,128)(2,1)S(1)} %get-tuple-element.85), channel_id=1, source_target_pairs={{0,2},{1,3},{2,0},{3,1},{4,6},{5,7},{6,4},{7,5},{8,10},{9,11},{10,... | collective-permute-start | bytes 786440 | tf_op jit(solution)/shard_map/ppermute | solution.py:539
  76.6 10.4 %collective-permute-start.29 = (bf16[2,2,2,2,32,256]{5,4,3,2,1,0:T(8,128)(2,1)S(1)}, bf16[2,2,2,2,32,256]{5,4,3,2,1,0:T(8,128)(2,1)S(1)}, u32[]{:S(2)}, u32[]{:S(2)}) collective-permute-start(bf16[2,2,2,2,32,256]{5,4,3,2,1,0:T(8,128)(2,1)S(1)} %get-tuple-element.101), channel_id=1, source_target_pairs={{0,2},{1,3},{2,0},{3,1},{4,6},{5,7},{6,4},{7,5},{8,10},{9,11},{10,... | collective-permute-start | bytes 786440 | tf_op jit(solution)/shard_map/ppermute | solution.py:539
  78.4 10.2 %collective-permute-start.21 = (bf16[2,2,2,32,256]{4,3,2,1,0:T(8,128)(2,1)S(1)}, bf16[2,2,2,32,256]{4,3,2,1,0:T(8,128)(2,1)S(1)}, u32[]{:S(2)}, u32[]{:S(2)}) collective-permute-start(bf16[2,2,2,32,256]{4,3,2,1,0:T(8,128)(2,1)S(1)} %get-tuple-element.87), channel_id=1, source_target_pairs={{0,4},{1,5},{2,6},{3,7},{4,0},{5,1},{6,2},{7,3},{8,12},{9,13},{10,... | collective-permute-start | bytes 393224 | tf_op jit(solution)/shard_map/ppermute | solution.py:546
  87.0 7.6 %collective-permute-start.30 = (bf16[2,2,2,32,256]{4,3,2,1,0:T(8,128)(2,1)S(1)}, bf16[2,2,2,32,256]{4,3,2,1,0:T(8,128)(2,1)S(1)}, u32[]{:S(2)}, u32[]{:S(2)}) collective-permute-start(bf16[2,2,2,32,256]{4,3,2,1,0:T(8,128)(2,1)S(1)} %get-tuple-element.103), channel_id=1, source_target_pairs={{0,4},{1,5},{2,6},{3,7},{4,0},{5,1},{6,2},{7,3},{8,12},{9,13},{10,... | collective-permute-start | bytes 393224 | tf_op jit(solution)/shard_map/ppermute | solution.py:546
  (9 other events, 29.9 us)
